TPU v7x, 32 devices: a whole 2x2x4 slice. The times are simulated.
32 devices in a mesh: dp: 4 (over y, x), fsdp: 8 (over z, core).
Axes of the slice: x: 2, y: 2, z: 4, core: 2. Of those that a mesh axis runs over, the one named last changes fastest.
Arguments:
- block_input: bfloat16 [2, 128, 128, 768], P(None, ('dp', 'fsdp')), may hold values from -6 to 6
- out_grad: bfloat16 [2, 128, 128, 768], P(None, ('dp', 'fsdp')), may hold values from -6 to 6
- timestep: int32 [2, 128], P(None, ('dp', 'fsdp')), may hold values from 0 to 1999
- dataset: int32 [2, 128], P(None, ('dp', 'fsdp')), may hold values from 0 to 1, as said below
- lengths: int32 [2, 128], P(None, ('dp', 'fsdp')), may hold values from 16 to 128, as said below
- norm1_gain: bfloat16 [768], P(('dp', 'fsdp')), may hold values from 0.099609375 to 1.8984375
- qkv_weight: bfloat16 [768, 2304], P(('dp', 'fsdp')), may hold values from -0.21875 to 0.21875
- out_weight: bfloat16 [768, 768], P(('dp', 'fsdp')), may hold values from -0.875 to 0.875
- norm2_gain: bfloat16 [768], P(('dp', 'fsdp')), may hold values from 0.099609375 to 1.8984375
- up_weight: bfloat16 [768, 3072], P(('dp', 'fsdp')), may hold values from -0.21875 to 0.21875
- down_weight: bfloat16 [3072, 768], P(('dp', 'fsdp')), may hold values from -0.109375 to 0.109375
- time_in: bfloat16 [512, 128], P(('dp', 'fsdp')), may hold values from -0.5 to 0.5
- time_out: bfloat16 [512, 768], P(('dp', 'fsdp')), may hold values from -0.25 to 0.25
- data_embed: bfloat16 [768, 2], P(('dp', 'fsdp')), may hold values from -3 to 3
Outputs:
- block_output: bfloat16 [2, 128, 128, 768], P(None, ('dp', 'fsdp'))
- input_grad: bfloat16 [2, 128, 128, 768], P(None, ('dp', 'fsdp'))
- norm1_gain_grad: float32 [768], P(('dp', 'fsdp'))
- qkv_weight_grad: float32 [768, 2304], P(('dp', 'fsdp'))
- out_weight_grad: float32 [768, 768], P(('dp', 'fsdp'))
- norm2_gain_grad: float32 [768], P(('dp', 'fsdp'))
- up_weight_grad: float32 [768, 3072], P(('dp', 'fsdp'))
- down_weight_grad: float32 [3072, 768], P(('dp', 'fsdp'))
- time_in_grad: float32 [512, 128], P(('dp', 'fsdp'))
- time_out_grad: float32 [512, 768], P(('dp', 'fsdp'))
- data_embed_grad: float32 [768, 2], P(('dp', 'fsdp'))
Inputs may be any that keep to these rules, and one draw needn't show every extreme that they name: In every micro-batch the first of each device's 4 sequences is of dataset 1. `lengths`: a sequence of dataset 0 has at most 64 tokens; in every micro-batch the first of each device's 4 sequences has 128.
All inputs are finite; a program needn't handle non-finite values.
Results may differ from a plain program's by a relative error of at most 0.013.
Values may be sent and summed in bfloat16 or wider, within the bound.
No kernel may reach another device: no remote copies, remote signals or barrier semaphores. Data moves between devices by JAX's collectives and lax.ppermute only.
A program may use at most 192 MiB of HBM per device.

v0:
```python
from functools import partial
import math

import jax
import jax.numpy as jnp
from jax import lax
from jax.sharding import PartitionSpec as P

HEAD_DIM = 64


def layer_norm(tok_rows, gain):
    center = tok_rows - jnp.mean(tok_rows, axis=-1, keepdims=True)
    spread = jnp.mean(center * center, axis=-1, keepdims=True)
    return center * lax.rsqrt(spread + 1e-05) * gain


def sinusoid(timestep, half_width):
    frequency = jnp.exp(-math.log(10000.0) * jnp.arange(half_width, dtype=jnp.float32) / half_width)
    angles = timestep.astype(jnp.float32)[:, None] * frequency[None, :]
    return jnp.concatenate([jnp.cos(angles), jnp.sin(angles)], axis=-1)


def contract_first(left, right):
    return lax.dot_general(
        left, right, (((0,), (0,)), ((), ())), preferred_element_type=jnp.float32
    )


def contract_last(left, right):
    return lax.dot_general(
        left, right, (((1,), (1,)), ((), ())), preferred_element_type=jnp.float32
    )


def split_heads(qkv_rows, seq_count, seq_len):
    heads_count = qkv_rows.shape[1] // (3 * HEAD_DIM)
    split_view = qkv_rows.reshape(seq_count, seq_len, 3, heads_count, HEAD_DIM)
    return (split_view[:, :, 0], split_view[:, :, 1], split_view[:, :, 2])


def score_block(query_rows, key_rows, key_mask):
    raw_scores = jnp.einsum(
        "slhd,smhd->shlm", query_rows, key_rows, preferred_element_type=jnp.float32
    ) * HEAD_DIM ** (-0.5)
    return jnp.where(key_mask[:, None, None, :], raw_scores, -1000000000.0)


def forward_pass(full_weights, inputs, timestep, dataset, lengths):
    gain_first, w_qkv, w_out, gain_second, w_up, w_down, time_in, time_out, data_embed = (
        full_weights
    )
    seq_count, seq_len, model_width = inputs.shape
    features = sinusoid(timestep, time_in.shape[1] // 2).astype(jnp.bfloat16)
    time_pre = contract_last(features, time_in)
    time_hidden = jax.nn.silu(time_pre).astype(jnp.bfloat16)
    set_onehot = (dataset[:, None] == jnp.arange(data_embed.shape[1])[None, :]).astype(jnp.float32)
    time_embed = jnp.dot(time_hidden, time_out, preferred_element_type=jnp.float32) + jnp.dot(
        set_onehot, data_embed.astype(jnp.float32).T, precision=lax.Precision.HIGHEST
    )
    resid_in = (inputs.astype(jnp.float32) + time_embed[:, None, :]).reshape(
        seq_count * seq_len, model_width
    )
    normed = layer_norm(resid_in, gain_first.astype(jnp.float32)).astype(jnp.bfloat16)
    qkv_rows = jnp.dot(normed, w_qkv, preferred_element_type=jnp.float32).astype(jnp.bfloat16)
    key_mask = jnp.arange(seq_len)[None, :] < lengths[:, None]
    query_rows, key_rows, value_rows = split_heads(qkv_rows, seq_count, seq_len)
    scores = score_block(query_rows, key_rows, key_mask)
    log_total = jax.nn.logsumexp(scores, axis=-1, keepdims=True)
    probs_low = jnp.exp(scores - log_total).astype(jnp.bfloat16)
    attended = jnp.einsum(
        "shlm,smhd->slhd", probs_low, value_rows, preferred_element_type=jnp.float32
    )
    attended = attended.astype(jnp.bfloat16).reshape(seq_count * seq_len, model_width)
    resid_mid = resid_in + jnp.dot(attended, w_out, preferred_element_type=jnp.float32)
    normed_two = layer_norm(resid_mid, gain_second.astype(jnp.float32)).astype(jnp.bfloat16)
    up_proj = jnp.dot(normed_two, w_up, preferred_element_type=jnp.float32)
    activated = jax.nn.gelu(up_proj, approximate=False).astype(jnp.bfloat16)
    result = resid_mid + jnp.dot(activated, w_down, preferred_element_type=jnp.float32)
    stored = (
        features,
        time_pre,
        time_hidden,
        set_onehot,
        resid_in,
        normed,
        qkv_rows,
        key_mask,
        log_total,
        attended,
        resid_mid,
        normed_two,
        up_proj,
        activated,
    )
    return (result.astype(jnp.bfloat16).reshape(inputs.shape), stored)


def backward_pass(full_weights, stored, cotangent):
    gain_first, w_qkv, w_out, gain_second, w_up, w_down, time_in, time_out, data_embed = (
        full_weights
    )
    (
        features,
        time_pre,
        time_hidden,
        set_onehot,
        resid_in,
        normed,
        qkv_rows,
        key_mask,
        log_total,
        attended,
        resid_mid,
        normed_two,
        up_proj,
        activated,
    ) = stored
    seq_count, seq_len, model_width = cotangent.shape
    highest = lax.Precision.HIGHEST
    out_rows = cotangent.astype(jnp.float32).reshape(seq_count * seq_len, model_width)
    grad_mlp = out_rows.astype(jnp.bfloat16)
    grad_down = contract_first(activated, grad_mlp)
    grad_act = contract_last(grad_mlp, w_down)
    unused_gelu, gelu_back = jax.vjp(partial(jax.nn.gelu, approximate=False), up_proj)
    grad_upin = gelu_back(grad_act)[0].astype(jnp.bfloat16)
    grad_up = contract_first(normed_two, grad_upin)
    grad_norm_two = contract_last(grad_upin, w_up)
    unused_two, second_back = jax.vjp(layer_norm, resid_mid, gain_second.astype(jnp.float32))
    grad_mid_norm, grad_gain_two = second_back(grad_norm_two)
    grad_mid = out_rows + grad_mid_norm
    grad_branch = grad_mid.astype(jnp.bfloat16)
    grad_wout = contract_first(attended, grad_branch)
    query_rows, key_rows, value_rows = split_heads(qkv_rows, seq_count, seq_len)
    grad_attended = contract_last(grad_branch, w_out).astype(jnp.bfloat16).reshape(value_rows.shape)
    scores = score_block(query_rows, key_rows, key_mask)
    probs = jnp.exp(scores - log_total)
    probs_low = probs.astype(jnp.bfloat16)
    grad_probs = jnp.einsum(
        "slhd,smhd->shlm", grad_attended, value_rows, preferred_element_type=jnp.float32
    )
    grad_scores = probs * (grad_probs - jnp.sum(probs * grad_probs, axis=-1, keepdims=True))
    grad_scores = grad_scores.astype(jnp.bfloat16)
    scale_factor = HEAD_DIM ** (-0.5)
    grad_query = (
        jnp.einsum("shlm,smhd->slhd", grad_scores, key_rows, preferred_element_type=jnp.float32)
        * scale_factor
    )
    grad_key = (
        jnp.einsum("shlm,slhd->smhd", grad_scores, query_rows, preferred_element_type=jnp.float32)
        * scale_factor
    )
    grad_value = jnp.einsum(
        "shlm,slhd->smhd", probs_low, grad_attended, preferred_element_type=jnp.float32
    )
    grad_qkv = jnp.stack([grad_query, grad_key, grad_value], axis=2).astype(jnp.bfloat16)
    grad_qkv = grad_qkv.reshape(seq_count * seq_len, 3 * model_width)
    grad_wqkv = contract_first(normed, grad_qkv)
    grad_normed = contract_last(grad_qkv, w_qkv)
    unused_one, first_back = jax.vjp(layer_norm, resid_in, gain_first.astype(jnp.float32))
    grad_in_norm, grad_gain_one = first_back(grad_normed)
    grad_resid = grad_mid + grad_in_norm
    grad_embed = jnp.sum(grad_resid.reshape(seq_count, seq_len, model_width), axis=1)
    grad_data = jnp.dot(grad_embed.T, set_onehot, precision=highest)
    grad_tout = jnp.dot(time_hidden.astype(jnp.float32).T, grad_embed, precision=highest)
    grad_thid = jnp.dot(grad_embed, time_out.astype(jnp.float32).T, precision=highest)
    unused_silu, silu_back = jax.vjp(jax.nn.silu, time_pre)
    grad_tpre = silu_back(grad_thid)[0]
    grad_tin = jnp.dot(grad_tpre.T, features.astype(jnp.float32), precision=highest)
    gradients = (
        grad_gain_one,
        grad_wqkv,
        grad_wout,
        grad_gain_two,
        grad_up,
        grad_down,
        grad_tin,
        grad_tout,
        grad_data,
    )
    return (gradients, grad_resid.astype(jnp.bfloat16).reshape(cotangent.shape))


def shards(
    block_input,
    out_grad,
    timestep,
    dataset,
    lengths,
    norm1_gain,
    qkv_weight,
    out_weight,
    norm2_gain,
    up_weight,
    down_weight,
    time_in,
    time_out,
    data_embed,
):
    results = []
    grad_inputs = []
    running = None
    for micro_index in range(block_input.shape[0]):
        full_weights = (
            lax.all_gather(norm1_gain, ("dp", "fsdp"), axis=0, tiled=True),
            lax.all_gather(qkv_weight, ("dp", "fsdp"), axis=0, tiled=True),
            lax.all_gather(out_weight, ("dp", "fsdp"), axis=0, tiled=True),
            lax.all_gather(norm2_gain, ("dp", "fsdp"), axis=0, tiled=True),
            lax.all_gather(up_weight, ("dp", "fsdp"), axis=0, tiled=True),
            lax.all_gather(down_weight, ("dp", "fsdp"), axis=0, tiled=True),
            lax.all_gather(time_in, ("dp", "fsdp"), axis=0, tiled=True),
            lax.all_gather(time_out, ("dp", "fsdp"), axis=0, tiled=True),
            lax.all_gather(data_embed, ("dp", "fsdp"), axis=0, tiled=True),
        )
        result, stored = forward_pass(
            full_weights,
            block_input[micro_index],
            timestep[micro_index],
            dataset[micro_index],
            lengths[micro_index],
        )
        full_weights = (
            lax.all_gather(norm1_gain, ("dp", "fsdp"), axis=0, tiled=True),
            lax.all_gather(qkv_weight, ("dp", "fsdp"), axis=0, tiled=True),
            lax.all_gather(out_weight, ("dp", "fsdp"), axis=0, tiled=True),
            lax.all_gather(norm2_gain, ("dp", "fsdp"), axis=0, tiled=True),
            lax.all_gather(up_weight, ("dp", "fsdp"), axis=0, tiled=True),
            lax.all_gather(down_weight, ("dp", "fsdp"), axis=0, tiled=True),
            lax.all_gather(time_in, ("dp", "fsdp"), axis=0, tiled=True),
            lax.all_gather(time_out, ("dp", "fsdp"), axis=0, tiled=True),
            lax.all_gather(data_embed, ("dp", "fsdp"), axis=0, tiled=True),
        )
        gradients, grad_input = backward_pass(full_weights, stored, out_grad[micro_index])
        gradients = (
            lax.psum_scatter(gradients[0], ("dp", "fsdp"), scatter_dimension=0, tiled=True),
            lax.psum_scatter(gradients[1], ("dp", "fsdp"), scatter_dimension=0, tiled=True),
            lax.psum_scatter(gradients[2], ("dp", "fsdp"), scatter_dimension=0, tiled=True),
            lax.psum_scatter(gradients[3], ("dp", "fsdp"), scatter_dimension=0, tiled=True),
            lax.psum_scatter(gradients[4], ("dp", "fsdp"), scatter_dimension=0, tiled=True),
            lax.psum_scatter(gradients[5], ("dp", "fsdp"), scatter_dimension=0, tiled=True),
            lax.psum_scatter(gradients[6], ("dp", "fsdp"), scatter_dimension=0, tiled=True),
            lax.psum_scatter(gradients[7], ("dp", "fsdp"), scatter_dimension=0, tiled=True),
            lax.psum_scatter(gradients[8], ("dp", "fsdp"), scatter_dimension=0, tiled=True),
        )
        running = gradients if running is None else jax.tree.map(jnp.add, running, gradients)
        results.append(result)
        grad_inputs.append(grad_input)
    return (
        jnp.stack(results),
        jnp.stack(grad_inputs),
        running[0],
        running[1],
        running[2],
        running[3],
        running[4],
        running[5],
        running[6],
        running[7],
        running[8],
    )


def solution(mesh):
    in_specs = (
        P(None, ("dp", "fsdp"), None, None),
        P(None, ("dp", "fsdp"), None, None),
        P(None, ("dp", "fsdp")),
        P(None, ("dp", "fsdp")),
        P(None, ("dp", "fsdp")),
        P(("dp", "fsdp")),
        P(("dp", "fsdp"), None),
        P(("dp", "fsdp"), None),
        P(("dp", "fsdp")),
        P(("dp", "fsdp"), None),
        P(("dp", "fsdp"), None),
        P(("dp", "fsdp"), None),
        P(("dp", "fsdp"), None),
        P(("dp", "fsdp"), None),
    )
    out_specs = (
        P(None, ("dp", "fsdp"), None, None),
        P(None, ("dp", "fsdp"), None, None),
        P(("dp", "fsdp")),
        P(("dp", "fsdp"), None),
        P(("dp", "fsdp"), None),
        P(("dp", "fsdp")),
        P(("dp", "fsdp"), None),
        P(("dp", "fsdp"), None),
        P(("dp", "fsdp"), None),
        P(("dp", "fsdp"), None),
        P(("dp", "fsdp"), None),
    )
    return jax.shard_map(shards, mesh=mesh, in_specs=in_specs, out_specs=out_specs, check_vma=False)
```

profile of v0, /device:TPU:0, one launch (start us, length us, event | category | flops | bytes accessed | tf_op | source)
XLA Modules:
  0.0 1119.8 jit_solution(7563039078659546609)
XLA Ops:
  11.8 42.1 %all-reduce.6 = (bf16[768]{0:T(1024)(128)(2,1)S(1)}, bf16[768]{0:T(1024)(128)(2,1)S(1)}) all-reduce(bf16[768]{0:T(1024)(128)(2,1)S(1)} %dynamic-update-slice, bf16[768]{0:T(1024)(128)(2,1)S(1)} %dynamic-update-slice.1), channel_id=1, replica_groups=mesh['dp'=4,'fsdp'=8] {'dp','fsdp'}, use_global_device_ids=true, to_apply=%add | all-reduce | flops 1536 | bytes 6144
  53.9 44.9 %all_gather.19 = bf16[512,768]{1,0:T(8,128)(2,1)S(1)} all-gather(bf16[16,768]{1,0:T(8,128)(2,1)} %param.26), channel_id=1, replica_groups=mesh['dp'=4,'fsdp'=8] {'dp','fsdp'}, dimensions={0}, use_global_device_ids=true | all-gather | bytes 811008 | tf_op jit(solution)/shard_map/all_gather | solution.py:212
  98.8 37.5 %all_gather.18 = bf16[512,128]{1,0:T(8,128)(2,1)S(1)} all-gather(bf16[16,128]{1,0:T(8,128)(2,1)} %param.25), channel_id=1, replica_groups=mesh['dp'=4,'fsdp'=8] {'dp','fsdp'}, dimensions={0}, use_global_device_ids=true | all-gather | bytes 135168 | tf_op jit(solution)/shard_map/all_gather | solution.py:211
  137.0 37.8 %all-gather = bf16[32,24,2]{1,2,0:T(2,128)(2,1)S(1)} all-gather(bf16[1,24,2]{1,2,0:T(2,128)(2,1)} %bitcast.335), channel_id=1, replica_groups=mesh['dp'=4,'fsdp'=8] {'dp','fsdp'}, dimensions={0}, use_global_device_ids=true | all-gather | bytes 3168 | tf_op jit(solution)/shard_map/all_gather | solution.py:213
  221.8 7.3 fusion.105
  233.9 28.2 %all-gather.12.cloned.1.call-done = bf16[3072,768]{1,0:T(8,128)(2,1)} async-done(((bf16[96,768]{1,0:T(8,128)(2,1)}), bf16[3072,768]{1,0:T(8,128)(2,1)}) %all-gather.12.cloned.1.call-update) | async-done | bytes 4718608 | tf_op jit(solution)/shard_map/all_gather | solution.py:210
  262.0 19.4 %add_convert_fusion.1 = (bf16[512,3072]{1,0:T(8,128)(2,1)S(1)}, f32[512,3072]{1,0:T(8,128)}) fusion(f32[512,3072]{1,0:T(8,128)} %fusion.104, bf16[512,768]{1,0:T(8,128)(2,1)S(1)} %bitcast.325, bf16[3072,768]{1,0:T(8,128)(2,1)} %all-gather.12.cloned.1.call-done), kind=kOutput, calls=%fused_computation.5 | convolution fusion | flops 2529165312 | bytes 21233664 | tf_op jit(solution)/shard_map/dot_general | solution.py:31
  281.4 6.2 fusion.117
  288.4 18.0 %add_convert_fusion = (bf16[512,3072]{1,0:T(8,128)(2,1)S(1)}, f32[512,3072]{1,0:T(8,128)}) fusion(f32[512,3072]{1,0:T(8,128)S(1)} %copy-done.30, bf16[512,768]{1,0:T(8,128)(2,1)S(1)} %bitcast.317, bf16[3072,768]{1,0:T(8,128)(2,1)S(1)} %copy-done.130), kind=kOutput, calls=%fused_computation.4 | convolution fusion | flops 2529165312 | bytes 21233664 | tf_op jit(solution)/shard_map/dot_general | solution.py:31
  379.4 5.0 convolution_add_fusion
  384.7 4.9 fusion.103
  389.6 5.5 convolution_add_fusion.2
  395.2 6.2 multiply_convert_fusion.1
  404.1 6.2 multiply_convert_fusion
  412.0 5.4 convolution_add_fusion.1
  418.5 40.1 %all-reduce.5 = (f32[768]{0:T(1024)S(1)}, f32[768]{0:T(1024)S(1)}, f32[768,2]{0,1:T(2,128)S(1)}) all-reduce(f32[768]{0:T(1024)S(1)} %add.252, f32[768]{0:T(1024)S(1)} %add.255, f32[768,2]{0,1:T(2,128)S(1)} %convolution_add_fusion.10), channel_id=11, replica_groups=mesh['dp'=4,'fsdp'=8] {'dp','fsdp'}, use_global_device_ids=true, to_apply=%region_23.24.clone | all-reduce | flops 3072 | bytes 24576
  460.4 6.0 add_convert_fusion.2
  466.5 5.0 add_convert_fusion.3
  474.7 25.6 %reduce-scatter.16.cloned.1.call-done = f32[16,128]{1,0:T(8,128)} async-done(((f32[512,128]{1,0:T(8,128)}), f32[16,128]{1,0:T(8,128)}) %reduce-scatter.16.cloned.1.call-update) | async-done | bytes 8208 | tf_op jit(solution)/shard_map/reduce_scatter | solution.py:241
  500.3 99.9 %reduce-scatter.18.cloned.1.call-done = f32[16,768]{1,0:T(8,128)} async-done(((f32[512,768]{1,0:T(8,128)}), f32[16,768]{1,0:T(8,128)}) %reduce-scatter.18.cloned.1.call-update) | async-done | bytes 49168 | tf_op jit(solution)/shard_map/reduce_scatter | solution.py:242
  600.1 104.8 %reduce-scatter.10.cloned.1.call-done = f32[24,768]{1,0:T(8,128)} async-done(((f32[768,768]{1,0:T(8,128)}), f32[24,768]{1,0:T(8,128)}) %reduce-scatter.10.cloned.1.call-update) | async-done | bytes 73744 | tf_op jit(solution)/shard_map/reduce_scatter | solution.py:237
  704.9 124.4 %reduce-scatter.8.cloned.1.call-done = f32[24,2304]{1,0:T(8,128)} async-done(((f32[768,2304]{1,0:T(8,128)}), f32[24,2304]{1,0:T(8,128)}) %reduce-scatter.8.cloned.1.call-update) | async-done | bytes 221200 | tf_op jit(solution)/shard_map/reduce_scatter | solution.py:236
  829.4 142.4 %reduce-scatter.12.cloned.1.call-done = f32[24,3072]{1,0:T(8,128)} async-done(((f32[768,3072]{1,0:T(8,128)}), f32[24,3072]{1,0:T(8,128)}) %reduce-scatter.12.cloned.1.call-update) | async-done | bytes 294928 | tf_op jit(solution)/shard_map/reduce_scatter | solution.py:239
  971.8 141.0 %reduce-scatter.14.cloned.1.call-done = f32[96,768]{1,0:T(8,128)} async-done(((f32[3072,768]{1,0:T(8,128)}), f32[96,768]{1,0:T(8,128)}) %reduce-scatter.14.cloned.1.call-update) | async-done | bytes 294928 | tf_op jit(solution)/shard_map/reduce_scatter | solution.py:240
  (407 shorter events, 139.9 us)
Async XLA Ops:
  7.2 171.9 %copy-start = (bf16[2,4,128,768]{3,2,1,0:T(8,128)(2,1)S(1)}, bf16[2,4,128,768]{3,2,1,0:T(8,128)(2,1)}, u32[]{:S(2)}) copy-start(bf16[2,4,128,768]{3,2,1,0:T(8,128)(2,1)} %param.14) | copy-start | bytes 4718596
  7.2 178.2 %all-gather.6.cloned.1.call-start = ((), (), s32[]{:S(2)}) async-start(), calls=%async_computation.6 | async-start | bytes 3649536 | tf_op jit(solution)/shard_map/all_gather | solution.py:206
  7.9 208.6 %all-gather.8.cloned.1.call-start = ((), (), s32[]{:S(2)}) async-start(), calls=%async_computation.7 | async-start | bytes 1216512 | tf_op jit(solution)/shard_map/all_gather | solution.py:207
  8.7 213.1 %all-gather.10.cloned.1.call-start = ((), (), s32[]{:S(2)}) async-start(), calls=%async_computation.8 | async-start | bytes 4866048 | tf_op jit(solution)/shard_map/all_gather | solution.py:209
  9.4 252.6 %all-gather.12.cloned.1.call-start = ((), (), s32[]{:S(2)}) async-start(), calls=%async_computation.9 | async-start | bytes 4866048 | tf_op jit(solution)/shard_map/all_gather | solution.py:210
  10.0 490.3 %reduce-scatter.16.cloned.1.call-start = ((), (), s32[]{:S(2)}) async-start(), calls=%async_computation.14 | async-start | bytes 270336 | tf_op jit(solution)/shard_map/reduce_scatter | solution.py:241
  53.9 126.4 %copy-start.77 = (f32[768]{0:T(1024)}, f32[768]{0:T(1024)S(1)}, u32[]{:S(2)}) copy-start(f32[768]{0:T(1024)S(1)} %convert_element_type.239) | copy-start | bytes 9220
  98.8 84.0 %copy-start.10 = (bf16[512,768]{1,0:T(8,128)(2,1)}, bf16[512,768]{1,0:T(8,128)(2,1)S(1)}, u32[]{:S(2)}) copy-start(bf16[512,768]{1,0:T(8,128)(2,1)S(1)} %all_gather.19) | copy-start | bytes 2359300
  180.2 48.9 %copy-start.67 = (f32[768]{0:T(1024)}, f32[768]{0:T(1024)S(1)}, u32[]{:S(2)}) copy-start(f32[768]{0:T(1024)S(1)} %convert_element_type.245) | copy-start | bytes 9220
  182.9 31.1 %copy-start.121 = (pred[4,128]{1,0:T(4,128)(4,1)}, pred[4,128]{1,0:T(4,128)(4,1)S(1)}, u32[]{:S(2)}) copy-start(pred[4,128]{1,0:T(4,128)(4,1)S(1)} %get-tuple-element.95) | copy-start | bytes 1540
  229.1 32.9 %copy-start.25 = (bf16[1,4,128,768]{3,2,1,0:T(8,128)(2,1)S(1)}, bf16[1,4,128,768]{3,2,1,0:T(8,128)(2,1)}, u32[]{:S(2)}) copy-start(bf16[1,4,128,768]{3,2,1,0:T(8,128)(2,1)} %get-tuple-element.56) | copy-start | bytes 2359300
  281.4 24.9 %slice-start = ((s8[4718592]{0:T(1024)(128)(4,1)}), s8[4194304]{0:T(1024)(128)(4,1)S(1)}, s32[]{:S(2)}) async-start(s8[4718592]{0:T(1024)(128)(4,1)} %bitcast.336), calls=%async_computation.16 | async-start | bytes 8388608
  288.3 18.0 %copy-start.9 = (f32[512,768]{1,0:T(8,128)S(1)}, f32[512,768]{1,0:T(8,128)}, u32[]{:S(2)}) copy-start(f32[512,768]{1,0:T(8,128)} %copy-done.8) | copy-start | bytes 4718596
  288.3 18.1 %copy-start.68 = (f32[768]{0:T(1024)S(1)}, f32[768]{0:T(1024)}, u32[]{:S(2)}) copy-start(f32[768]{0:T(1024)} %copy-done.67) | copy-start | bytes 9220
  288.3 18.1 %copy-start.84 = (f32[512]{0:T(512)S(1)}, f32[512]{0:T(512)}, u32[]{:S(2)}) copy-start(f32[512]{0:T(512)} %copy-done.83) | copy-start | bytes 6148
  288.3 18.1 %copy-start.90 = (f32[512]{0:T(512)S(1)}, f32[512]{0:T(512)}, u32[]{:S(2)}) copy-start(f32[512]{0:T(512)} %copy-done.89) | copy-start | bytes 6148
  288.3 18.1 %copy-start.92 = (f32[512]{0:T(512)S(1)}, f32[512]{0:T(512)}, u32[]{:S(2)}) copy-start(f32[512]{0:T(512)} %copy-done.91) | copy-start | bytes 6148
  288.4 18.1 %copy-start.102 = (f32[512]{0:T(512)S(1)}, f32[512]{0:T(512)}, u32[]{:S(2)}) copy-start(f32[512]{0:T(512)} %copy-done.101) | copy-start | bytes 6148
  288.4 18.1 %slice-start.1 = ((s8[4718592]{0:T(1024)(128)(4,1)}), s8[524288]{0:T(1024)(128)(4,1)S(1)}, s32[]{:S(2)}) async-start(s8[4718592]{0:T(1024)(128)(4,1)} %bitcast.336), calls=%async_computation.17 | async-start | bytes 1048576
  367.8 232.4 %reduce-scatter.18.cloned.1.call-start = ((), (), s32[]{:S(2)}) async-start(), calls=%async_computation.15 | async-start | bytes 1622016 | tf_op jit(solution)/shard_map/reduce_scatter | solution.py:242
  370.7 334.3 %reduce-scatter.10.cloned.1.call-start = ((), (), s32[]{:S(2)}) async-start(), calls=%async_computation.11 | async-start | bytes 2433024 | tf_op jit(solution)/shard_map/reduce_scatter | solution.py:237
  375.2 454.1 %reduce-scatter.8.cloned.1.call-start = ((), (), s32[]{:S(2)}) async-start(), calls=%async_computation.10 | async-start | bytes 7299072 | tf_op jit(solution)/shard_map/reduce_scatter | solution.py:236
  384.4 587.3 %reduce-scatter.12.cloned.1.call-start = ((), (), s32[]{:S(2)}) async-start(), calls=%async_computation.12 | async-start | bytes 9732096 | tf_op jit(solution)/shard_map/reduce_scatter | solution.py:239
  395.1 717.6 %reduce-scatter.14.cloned.1.call-start = ((), (), s32[]{:S(2)}) async-start(), calls=%async_computation.13 | async-start | bytes 9732096 | tf_op jit(solution)/shard_map/reduce_scatter | solution.py:240
  (120 other events, 419.3 us)
Sparse Core Ops, SparseCore 0:
  11.0 63.3 all-gather.5
  77.5 53.3 all-gather.7
  133.9 62.6 all-gather.9
  199.5 62.4 all-gather.11
  367.9 132.3 reduce-scatter.15
  506.8 93.2 reduce-scatter.17
  606.8 98.0 reduce-scatter.9
  711.2 118.1 reduce-scatter.7
  836.8 134.8 reduce-scatter.11
  978.1 134.5 reduce-scatter.13
where the time goes:
time: 1130 us; the launch traced here: 1120 us
  waiting for transfers between devices  669 us (59%)
  blocking collectives  202 us (18%)
  matrix products  148 us (13%)
  local copies, waits for them, and re-layouts  47.6 us (4%)
  other arithmetic  36.1 us (3%)
  between operations  16.4 us (1%)
    reduce_scatter x1, waiting for transfers between devices, shards(): lax.psum_scatter(gradients[4], ('dp', 'fsdp'), scatter_dimension=0, tiled...  142 us
    reduce_scatter x1, waiting for transfers between devices, shards(): lax.psum_scatter(gradients[5], ('dp', 'fsdp'), scatter_dimension=0, tiled...  141 us
    reduce_scatter x1, waiting for transfers between devices, shards(): lax.psum_scatter(gradients[1], ('dp', 'fsdp'), scatter_dimension=0, tiled...  124 us
    reduce_scatter x1, waiting for transfers between devices, shards(): lax.psum_scatter(gradients[2], ('dp', 'fsdp'), scatter_dimension=0, tiled...  105 us
    reduce_scatter x1, waiting for transfers between devices, shards(): lax.psum_scatter(gradients[7], ('dp', 'fsdp'), scatter_dimension=0, tiled...  99.9 us
    unnamed x2, blocking collectives  82.2 us
    dot_general x10, matrix products, contract_last(): lax.dot_general(left, right, (((1,), (1,)), ((), ())), preferred_element_...  55.5 us
    all_gather x1, blocking collectives, shards(): lax.all_gather(time_out, ('dp', 'fsdp'), axis=0, tiled=True)  44.9 us
  transfers between devices with their start and end apart: 10, of which 7 were waited for; matrix products, arithmetic and copies ran while one was open for 11% of the time, Pallas kernels for 0%

commit v1 on v0

v1 whole, which is shorter than its diff:
```python
from functools import partial
import math

import jax
import jax.numpy as jnp
from jax import lax
from jax.experimental import pallas as pl
from jax.experimental.pallas import tpu as pltpu
from jax.sharding import PartitionSpec as P

HEAD_DIM = 64
AXES = ("dp", "fsdp")
LANES = 384
CHIPS = 16
WIDTH = 768
FF = 3072
VMEM_MIB = 58
F32 = jnp.float32
BF16 = jnp.bfloat16
NEG = -1000000000.0
PHI_RATE = 0.4 / math.sqrt(2.0)
PHI_POLY = (
    0.2256758619023266,
    0.22566959976942397,
    0.20784266147672614,
    0.16854232328082183,
    0.14142988763898146,
    -0.005603842501456246,
    0.16908061566688656,
    -0.18289823607849773,
    0.05026125371366006,
)


def sinusoid(timestep, half_width):
    frequency = jnp.exp(-math.log(10000.0) * jnp.arange(half_width, dtype=F32) / half_width)
    angles = timestep.astype(F32)[:, None] * frequency[None, :]
    return jnp.concatenate([jnp.cos(angles), jnp.sin(angles)], axis=-1)


def dot(left, right):
    return jnp.dot(left, right, preferred_element_type=F32)


def dot_last(left, right):
    return lax.dot_general(left, right, (((1,), (1,)), ((), ())), preferred_element_type=F32)


def dot_first(left, right):
    return lax.dot_general(left, right, (((0,), (0,)), ((), ())), preferred_element_type=F32)


def position_bits(core, masks):
    return [sum(masks[core][b] for b in range(4) if (p >> b) & 1) for p in range(CHIPS)]


CHIP_MASKS = ((2, 1, 8, 4), (2, 1, 4, 8))
ORDER = [position_bits(core, CHIP_MASKS) for core in (0, 1)]
INVERSE = [[ORDER[core].index(k) for k in range(CHIPS)] for core in (0, 1)]


def core_swap(x):
    return lax.ppermute(x, AXES, [(i, i ^ 1) for i in range(2 * CHIPS)])


def chip_swap(x, step):
    return lax.ppermute(
        x, AXES, [(i, i ^ (CHIP_MASKS[i & 1][step] * 2)) for i in range(2 * CHIPS)]
    )


def gather_pieces(piece):
    held = piece
    for step in range(3):
        held = jnp.concatenate([held, chip_swap(held, step)], axis=0)
    far = chip_swap(held, 3)
    return held, far, core_swap(held), core_swap(far)


def add_parts(parts, start, stop):
    total = parts[0][start:stop].astype(F32)
    for part in parts[1:]:
        total = total + part[start:stop].astype(F32)
    return total


def scatter_pieces(mine, theirs):
    parts = [mine, core_swap(theirs)]
    for step, size in ((3, 8), (2, 4), (1, 2), (0, 1)):
        parts.append(chip_swap(add_parts(parts, size, 2 * size).astype(BF16), step))
    return add_parts(parts, 0, 1)[0]


def vmem(count):
    return [pl.BlockSpec(memory_space=pltpu.VMEM)] * count


def smem(count):
    return [pl.BlockSpec(memory_space=pltpu.SMEM)] * count


def anywhere(count):
    return [pl.BlockSpec(memory_space=pl.ANY)] * count


def params():
    return pltpu.CompilerParams(vmem_limit_bytes=VMEM_MIB * 1024 * 1024)


def cost(flops, nbytes, transcendentals=0):
    return pl.CostEstimate(flops=flops, bytes_accessed=nbytes, transcendentals=transcendentals)


def ln_stats(v):
    center = v - jnp.mean(v, axis=-1, keepdims=True)
    scale = lax.rsqrt(jnp.mean(center * center, axis=-1, keepdims=True) + 1e-05)
    return center * scale, scale


def ln_back(y, gain, xhat, scale):
    yg = y * gain
    return scale * (
        yg - jnp.mean(yg, axis=-1, keepdims=True) - xhat * jnp.mean(yg * xhat, axis=-1, keepdims=True)
    )


def first_core(tab):
    return tab[64]


def each_piece(tab, parts, fn):
    core = first_core(tab)
    for side in (0, 1):
        half = core if side == 0 else 1 - core
        for group in (0, 1):
            part = parts[side * 2 + group]

            def body(q, _, part=part, side=side, group=group, half=half):
                chip = tab[side * CHIPS + group * 8 + q]
                fn(part.at[q], chip, half)
                return 0

            lax.fori_loop(0, 8, body, 0)


def rows_of(chip, size):
    return pl.ds(pl.multiple_of(chip * size, size), size)


def lanes_of(half, size, base=0):
    return pl.ds(pl.multiple_of(half * size + base, 128), LANES)


def attention_forward_kernel(
    tab, lens, g_a, g_b, g_c, g_d, x_ref, feat_ref, set_ref,
    normed_ref, qkv_ref, probs_ref, att_ref, mid_ref, two_ref, te_ref, vec_ref,
    w_qkv, w_out, w_time, extra, sem_qkv, sem_out, sem_time, sem_extra,
):
    def fetch(src, chip, half):
        for sec in range(3):
            pltpu.make_async_copy(
                src.at[pl.ds(48 * sec, 48), :],
                w_qkv.at[rows_of(chip, 48), lanes_of(half, 3 * LANES, sec * LANES)],
                sem_qkv,
            ).start()
        pltpu.make_async_copy(
            src.at[pl.ds(144, 48), :], w_out.at[rows_of(chip, 48), lanes_of(half, LANES)], sem_out
        ).start()
        for owner in (0, 1):
            pltpu.make_async_copy(
                src.at[pl.ds(192 + 16 * owner, 16), :],
                w_time.at[owner, rows_of(chip, 16), lanes_of(half, LANES)],
                sem_time,
            ).start()
        pltpu.make_async_copy(
            src.at[pl.ds(224, 16), :], extra.at[half, rows_of(chip, 16), :], sem_extra
        ).start()

    each_piece(tab, (g_a, g_b, g_c, g_d), fetch)
    pltpu.make_async_copy(extra, extra, sem_extra).wait()
    pltpu.make_async_copy(w_time, w_time, sem_time).wait()

    lane = lax.broadcasted_iota(jnp.int32, (128, WIDTH), 1)
    spread = (lax.broadcasted_iota(jnp.int32, (128, WIDTH), 0) == lane % 24).astype(BF16)
    vectors = jnp.zeros((16, WIDTH), F32)
    embed = jnp.zeros((8, WIDTH), F32)
    for owner in (0, 1):
        wide = dot(extra[owner, :, 128:256], spread)
        chip = lax.broadcasted_iota(jnp.int32, (256, WIDTH), 0) // 16
        place = lax.broadcasted_iota(jnp.int32, (256, WIDTH), 1) // 24
        wide = jnp.where(place == chip * 2 + owner, wide, 0.0)
        vectors = vectors + jnp.sum(wide.reshape(CHIPS, 16, WIDTH), axis=0)
        pre = dot_last(feat_ref[...], extra[owner, :, 0:128])
        hidden = (pre / (1.0 + jnp.exp(-pre))).astype(BF16)
        embed = embed + dot(hidden, w_time[owner])
    vec_ref[...] = vectors
    chosen = set_ref[...]
    embed = embed + jnp.where(chosen > 0.5, vectors[3:4, :], vectors[2:3, :])
    te_ref[...] = embed
    gain_one = vectors[0:1, :]
    gain_two = vectors[1:2, :]

    def norm_body(s, _):
        rows = pl.ds(pl.multiple_of(s * 128, 128), 128)
        xhat, _unused = ln_stats(x_ref[rows, :].astype(F32) + te_ref[pl.ds(s, 1), :])
        normed_ref[rows, :] = (xhat * gain_one).astype(BF16)
        return 0

    lax.fori_loop(0, 8, norm_body, 0)
    pltpu.make_async_copy(w_qkv, w_qkv, sem_qkv).wait()

    def qkv_body(i, _):
        rows = pl.ds(pl.multiple_of(i * 256, 256), 256)
        qkv_ref[rows, :] = dot(normed_ref[rows, :], w_qkv[...]).astype(BF16)
        return 0

    lax.fori_loop(0, 4, qkv_body, 0)

    def attend_body(s, _):
        rows = pl.ds(pl.multiple_of(s * 128, 128), 128)
        low_half = lax.broadcasted_iota(jnp.int32, (128, 128), 1) < HEAD_DIM
        keep = lax.broadcasted_iota(jnp.int32, (256, 128), 1) < lens[s]
        for pair in range(6):
            base = (pair // 3) * 3 * LANES + (pair % 3) * 128
            query = qkv_ref[rows, base : base + 128]
            key = qkv_ref[rows, base + LANES : base + LANES + 128]
            value = qkv_ref[rows, base + 2 * LANES : base + 2 * LANES + 128]
            none = jnp.zeros_like(query)
            stacked = jnp.concatenate(
                [jnp.where(low_half, query, none), jnp.where(low_half, none, query)], axis=0
            )
            scores = jnp.where(keep, dot_last(stacked, key) * HEAD_DIM ** (-0.5), NEG)
            shifted = jnp.exp(scores - jnp.max(scores, axis=-1, keepdims=True))
            probs = (shifted / jnp.sum(shifted, axis=-1, keepdims=True)).astype(BF16)
            probs_ref[pl.ds(pl.multiple_of((s * 6 + pair) * 256, 256), 256), :] = probs
            values = jnp.concatenate(
                [jnp.where(low_half, value, none), jnp.where(low_half, none, value)], axis=0
            )
            both = jnp.concatenate([probs[:128], probs[128:]], axis=1)
            att_ref[rows, pair * 128 : pair * 128 + 128] = dot(both, values).astype(BF16)
        return 0

    lax.fori_loop(0, 8, attend_body, 0)
    pltpu.make_async_copy(w_out, w_out, sem_out).wait()

    def out_body(s, _):
        rows = pl.ds(pl.multiple_of(s * 128, 128), 128)
        mid = (
            x_ref[rows, :].astype(F32)
            + te_ref[pl.ds(s, 1), :]
            + dot(att_ref[rows, :], w_out[...])
        )
        mid_ref[rows, :] = mid
        xhat, _unused = ln_stats(mid)
        two_ref[rows, :] = (xhat * gain_two).astype(BF16)
        return 0

    lax.fori_loop(0, 8, out_body, 0)


def attention_forward(tab, lens, pieces, rows, features, sets):
    shape = jax.ShapeDtypeStruct
    return pl.pallas_call(
        attention_forward_kernel,
        out_shape=(
            shape((1024, WIDTH), BF16),
            shape((1024, 3 * WIDTH), BF16),
            shape((48 * 256, 128), BF16),
            shape((1024, WIDTH), BF16),
            shape((1024, WIDTH), F32),
            shape((1024, WIDTH), BF16),
            shape((8, WIDTH), F32),
            shape((16, WIDTH), F32),
        ),
        in_specs=smem(2) + anywhere(4) + vmem(3),
        out_specs=tuple(vmem(8)),
        scratch_shapes=[
            pltpu.VMEM((WIDTH, 3 * WIDTH), BF16),
            pltpu.VMEM((WIDTH, WIDTH), BF16),
            pltpu.VMEM((2, 256, WIDTH), BF16),
            pltpu.VMEM((2, 256, LANES), BF16),
        ]
        + [pltpu.SemaphoreType.DMA] * 4,
        compiler_params=params(),
        cost_estimate=cost(8_000_000_000, 24_000_000, 2_000_000),
        name="attention_forward",
    )(tab, lens, *pieces, rows, features, sets)


def gelu_parts(u):
    size = jnp.abs(u)
    t = 1.0 / (1.0 + PHI_RATE * size)
    poly = jnp.full_like(t, PHI_POLY[-1])
    for coefficient in PHI_POLY[-2::-1]:
        poly = poly * t + coefficient
    bell = jnp.exp(u * u * -0.5)
    tail = bell * (t * poly * 0.5)
    return jnp.where(u > 0, 1.0 - tail, tail), bell * (1.0 / math.sqrt(2.0 * math.pi))


def mlp_kernel(
    tab, g_a, g_b, g_c, g_d, two_ref, out_grad_ref, mid_ref, vec_ref,
    mine_ref, theirs_ref, result_ref, grad_mid_ref, branch_ref, gain_ref,
    w_up, w_down, act, grad_up, back, part, sem_up, sem_down,
):
    core = first_core(tab)

    def fetch(src, chip, half):
        pltpu.make_async_copy(
            src.at[pl.ds(0, 192), :], w_down.at[rows_of(chip, 192), lanes_of(half, LANES)], sem_down
        ).start()
        for block in range(4):
            pltpu.make_async_copy(
                src.at[pl.ds(192 + 48 * block, 48), :],
                w_up.at[rows_of(chip, 48), lanes_of(half, 4 * LANES, block * LANES)],
                sem_up,
            ).start()

    each_piece(tab, (g_a, g_b, g_c, g_d), fetch)
    pltpu.make_async_copy(w_up, w_up, sem_up).wait()
    pltpu.make_async_copy(w_down, w_down, sem_down).wait()

    def chunk_body(j, _):
        cols = pl.ds(pl.multiple_of(j * WIDTH, WIDTH), WIDTH)

        def row_body(i, _):
            rows = pl.ds(pl.multiple_of(i * 256, 256), 256)
            up = dot(two_ref[rows, :], w_up[:, cols])
            grad_act = dot_last(out_grad_ref[rows, :], w_down[cols, :])
            cdf, density = gelu_parts(up)
            activated = (up * cdf).astype(BF16)
            act[rows, :] = activated
            grad = (grad_act * (cdf + up * density)).astype(BF16)
            grad_up[rows, :] = grad
            down = dot(activated, w_down[cols, :])
            normed_back = dot_last(grad, w_up[:, cols])

            @pl.when(j == 0)
            def _():
                grad_mid_ref[rows, :] = mid_ref[rows, :] + down
                back[rows, :] = normed_back

            @pl.when(j > 0)
            def _():
                grad_mid_ref[rows, :] = grad_mid_ref[rows, :] + down
                back[rows, :] = back[rows, :] + normed_back

            return 0

        lax.fori_loop(0, 4, row_body, 0)
        part[...] = dot_first(act[...], out_grad_ref[...]).astype(BF16)
        for side, target in ((0, mine_ref), (1, theirs_ref)):
            half = core if side == 0 else 1 - core
            for k in range(4):
                place = tab[32 + side * CHIPS + j * 4 + k]
                target[place, 0:192, :] = part[192 * k : 192 * k + 192, lanes_of(half, LANES)]
        part[...] = dot_first(two_ref[...], grad_up[...]).astype(BF16)
        for side, target in ((0, mine_ref), (1, theirs_ref)):
            half = core if side == 0 else 1 - core

            @pl.when(j // 2 == half)
            def _(side=side, target=target):
                def store_body(chip, _):
                    place = tab[32 + side * CHIPS + chip]
                    for b in range(2):
                        row = pl.multiple_of(192 + 48 * (2 * (j % 2) + b), 48)
                        target[place, pl.ds(row, 48), :] = part[
                            rows_of(chip, 48), b * LANES : (b + 1) * LANES
                        ]
                    return 0

                lax.fori_loop(0, CHIPS, store_body, 0)

        return 0

    lax.fori_loop(0, 4, chunk_body, 0)
    gain_two = vec_ref[1:2, :]

    def norm_body(s, total):
        rows = pl.ds(pl.multiple_of(s * 128, 128), 128)
        result_ref[rows, :] = grad_mid_ref[rows, :].astype(BF16)
        xhat, scale = ln_stats(mid_ref[rows, :])
        y = back[rows, :]
        grad = out_grad_ref[rows, :].astype(F32) + ln_back(y, gain_two, xhat, scale)
        grad_mid_ref[rows, :] = grad
        branch_ref[rows, :] = grad.astype(BF16)
        return total + jnp.sum(y * xhat, axis=0, keepdims=True)

    gain_ref[...] = lax.fori_loop(0, 8, norm_body, jnp.zeros((1, WIDTH), F32))


def mlp(tab, pieces, two, out_grad, mid, vectors):
    shape = jax.ShapeDtypeStruct
    return pl.pallas_call(
        mlp_kernel,
        out_shape=(
            shape((CHIPS, 384, LANES), BF16),
            shape((CHIPS, 384, LANES), BF16),
            shape((1024, WIDTH), BF16),
            shape((1024, WIDTH), F32),
            shape((1024, WIDTH), BF16),
            shape((1, WIDTH), F32),
        ),
        in_specs=smem(1) + anywhere(4) + vmem(4),
        out_specs=tuple(vmem(6)),
        scratch_shapes=[
            pltpu.VMEM((WIDTH, FF), BF16),
            pltpu.VMEM((FF, WIDTH), BF16),
            pltpu.VMEM((1024, WIDTH), BF16),
            pltpu.VMEM((1024, WIDTH), BF16),
            pltpu.VMEM((1024, WIDTH), F32),
            pltpu.VMEM((WIDTH, WIDTH), BF16),
            pltpu.SemaphoreType.DMA,
            pltpu.SemaphoreType.DMA,
        ],
        compiler_params=params(),
        cost_estimate=cost(30_000_000_000, 40_000_000, 3_000_000),
        name="mlp",
    )(tab, *pieces, two, out_grad, mid, vectors)


def attention_backward_kernel(
    tab, g_a, g_b, g_c, g_d, branch_ref, att_ref, qkv_ref, probs_ref, normed_ref,
    mine_ref, theirs_ref, grad_qkv_ref,
    w_out, grad_att, part, sem,
):
    core = first_core(tab)

    def fetch(src, chip, half):
        pltpu.make_async_copy(
            src.at[pl.ds(144, 48), :], w_out.at[rows_of(chip, 48), lanes_of(half, LANES)], sem
        ).start()

    each_piece(tab, (g_a, g_b, g_c, g_d), fetch)
    pltpu.make_async_copy(w_out, w_out, sem).wait()

    def grad_att_body(i, _):
        rows = pl.ds(pl.multiple_of(i * 256, 256), 256)
        grad_att[rows, :] = dot_last(branch_ref[rows, :], w_out[...]).astype(BF16)
        return 0

    lax.fori_loop(0, 4, grad_att_body, 0)

    def store(side, target, block, columns):
        def store_body(chip, _):
            place = tab[32 + side * CHIPS + chip]
            target[place, 48 * block : 48 * block + 48, :] = part[rows_of(chip, 48), columns]
            return 0

        lax.fori_loop(0, CHIPS, store_body, 0)

    part[...] = dot_first(att_ref[...], branch_ref[...]).astype(BF16)
    store(0, mine_ref, 3, lanes_of(core, LANES))
    store(1, theirs_ref, 3, lanes_of(1 - core, LANES))

    def attend_body(s, _):
        rows = pl.ds(pl.multiple_of(s * 128, 128), 128)
        low_half = lax.broadcasted_iota(jnp.int32, (128, 128), 1) < HEAD_DIM

        def heads(x):
            none = jnp.zeros_like(x)
            return jnp.concatenate(
                [jnp.where(low_half, x, none), jnp.where(low_half, none, x)], axis=0
            )

        for pair in range(6):
            base = (pair // 3) * 3 * LANES + (pair % 3) * 128
            query = heads(qkv_ref[rows, base : base + 128])
            key = heads(qkv_ref[rows, base + LANES : base + LANES + 128])
            value = qkv_ref[rows, base + 2 * LANES : base + 2 * LANES + 128]
            up = heads(grad_att[rows, pair * 128 : pair * 128 + 128])
            probs_low = probs_ref[pl.ds(pl.multiple_of((s * 6 + pair) * 256, 256), 256), :]
            probs = probs_low.astype(F32)
            grad_probs = dot_last(up, value)
            inner = jnp.sum(probs * grad_probs, axis=-1, keepdims=True)
            grad_scores = (probs * (grad_probs - inner)).astype(BF16)
            both = jnp.concatenate([grad_scores[:128], grad_scores[128:]], axis=1)
            grad_query = dot(both, key) * HEAD_DIM ** (-0.5)
            grad_key = dot_first(grad_scores, query) * HEAD_DIM ** (-0.5)
            grad_value = dot_first(probs_low, up)
            grad_qkv_ref[rows, base : base + 128] = grad_query.astype(BF16)
            grad_qkv_ref[rows, base + LANES : base + LANES + 128] = grad_key.astype(BF16)
            grad_qkv_ref[rows, base + 2 * LANES : base + 2 * LANES + 128] = grad_value.astype(BF16)
        return 0

    lax.fori_loop(0, 8, attend_body, 0)

    for half in (0, 1):
        for sec in range(3):
            col = half * 3 * LANES + sec * LANES
            part[:, 0:LANES] = dot_first(
                normed_ref[...], grad_qkv_ref[:, col : col + LANES]
            ).astype(BF16)

            @pl.when(core == half)
            def _(sec=sec):
                store(0, mine_ref, sec, slice(0, LANES))

            @pl.when(core != half)
            def _(sec=sec):
                store(1, theirs_ref, sec, slice(0, LANES))


def attention_backward(tab, pieces, branch, att, qkv, probs, normed):
    shape = jax.ShapeDtypeStruct
    return pl.pallas_call(
        attention_backward_kernel,
        out_shape=(
            shape((CHIPS, 192, LANES), BF16),
            shape((CHIPS, 192, LANES), BF16),
            shape((1024, 3 * WIDTH), BF16),
        ),
        in_specs=smem(1) + anywhere(4) + vmem(5),
        out_specs=tuple(vmem(3)),
        scratch_shapes=[
            pltpu.VMEM((WIDTH, WIDTH), BF16),
            pltpu.VMEM((1024, WIDTH), BF16),
            pltpu.VMEM((WIDTH, WIDTH), BF16),
            pltpu.SemaphoreType.DMA,
        ],
        compiler_params=params(),
        cost_estimate=cost(10_000_000_000, 20_000_000),
        name="attention_backward",
    )(tab, *pieces, branch, att, qkv, probs, normed)


def input_backward_kernel(
    tab, g_a, g_b, g_c, g_d, grad_qkv_ref, x_ref, te_ref, vec_ref, grad_mid_ref, gain_two_ref,
    input_ref, small_ref,
    w_qkv, sem,
):
    def fetch(src, chip, half):
        for sec in range(3):
            pltpu.make_async_copy(
                src.at[pl.ds(48 * sec, 48), :],
                w_qkv.at[rows_of(chip, 48), lanes_of(half, 3 * LANES, sec * LANES)],
                sem,
            ).start()

    each_piece(tab, (g_a, g_b, g_c, g_d), fetch)
    pltpu.make_async_copy(w_qkv, w_qkv, sem).wait()
    gain = vec_ref[0:1, :]

    def body(s, total):
        rows = pl.ds(pl.multiple_of(s * 128, 128), 128)
        y = dot_last(grad_qkv_ref[rows, :], w_qkv[...])
        xhat, scale = ln_stats(x_ref[rows, :].astype(F32) + te_ref[pl.ds(s, 1), :])
        grad = grad_mid_ref[rows, :] + ln_back(y, gain, xhat, scale)
        input_ref[rows, :] = grad.astype(BF16)
        small_ref[pl.ds(s, 1), :] = jnp.sum(grad, axis=0, keepdims=True)
        return total + jnp.sum(y * xhat, axis=0, keepdims=True)

    small_ref[8:9, :] = lax.fori_loop(0, 8, body, jnp.zeros((1, WIDTH), F32))
    small_ref[9:10, :] = gain_two_ref[...]
    small_ref[10:16, :] = jnp.zeros((6, WIDTH), F32)


def input_backward(tab, pieces, grad_qkv, rows, embed, vectors, grad_mid, gain_two):
    shape = jax.ShapeDtypeStruct
    return pl.pallas_call(
        input_backward_kernel,
        out_shape=(shape((1024, WIDTH), BF16), shape((16, WIDTH), F32)),
        in_specs=smem(1) + anywhere(4) + vmem(6),
        out_specs=tuple(vmem(2)),
        scratch_shapes=[pltpu.VMEM((WIDTH, 3 * WIDTH), BF16), pltpu.SemaphoreType.DMA],
        compiler_params=params(),
        cost_estimate=cost(4_000_000_000, 18_000_000),
        name="input_backward",
    )(tab, *pieces, grad_qkv, rows, embed, vectors, grad_mid, gain_two)


def pick(stacked, index):
    return lax.dynamic_index_in_dim(stacked, index, 0, keepdims=False)


def in_core_order(core, own, other, axis):
    return jnp.where(
        core == 0,
        jnp.concatenate([own, other], axis=axis),
        jnp.concatenate([other, own], axis=axis),
    )


def pack_extra(time_in, vectors, ints):
    rows = time_in.shape[0]
    filler = jnp.zeros((rows, 128), BF16)
    vec = lax.dynamic_update_slice(filler, vectors, (0, 0))
    num = lax.dynamic_update_slice(filler, ints[None, :], (0, 0))
    return jnp.concatenate([time_in, vec, num], axis=1)


def split_time(timestep, dataset):
    steps = timestep.reshape(-1)
    return jnp.concatenate([steps // 64, steps % 64, dataset.reshape(-1)]).astype(BF16)


def gather_all(x):
    return lax.all_gather(x, AXES, axis=0, tiled=True)


def shards(
    block_input,
    out_grad,
    timestep,
    dataset,
    lengths,
    norm1_gain,
    qkv_weight,
    out_weight,
    norm2_gain,
    up_weight,
    down_weight,
    time_in,
    time_out,
    data_embed,
    devices,
):
    flat = lax.axis_index(AXES)
    exchange = devices == 2 * CHIPS
    vectors = jnp.concatenate([norm1_gain[None], norm2_gain[None], data_embed.T], axis=0)
    numbers = split_time(timestep, dataset)
    count = numbers.shape[0] // 3
    if exchange:
        core = flat & 1
        chip = flat >> 1
        order = jnp.array(ORDER, jnp.int32)
        inverse = jnp.array(INVERSE, jnp.int32)
        where = jnp.bitwise_xor(chip, jnp.arange(CHIPS, dtype=jnp.int32))
        first = core == 0
        tab = jnp.concatenate(
            [
                jnp.bitwise_xor(chip, jnp.where(first, order[0], order[1])),
                jnp.bitwise_xor(chip, jnp.where(first, order[1], order[0])),
                jnp.where(first, inverse[0][where], inverse[1][where]),
                jnp.where(first, inverse[1][where], inverse[0][where]),
                jnp.full((8,), core, jnp.int32),
            ]
        )
        wide = jnp.concatenate(
            [qkv_weight.reshape(24, 3, 2, LANES), out_weight.reshape(24, 1, 2, LANES)], axis=1
        ).transpose(2, 1, 0, 3)
        time_halves = time_out.reshape(16, 2, LANES).transpose(1, 0, 2)
        both = jnp.concatenate([wide.reshape(2, 96, LANES), time_halves], axis=1)
        own = pick(both, core)
        other = core_swap(pick(both, 1 - core))
        blocks = in_core_order(
            core, own[:96].reshape(4, 24, LANES), other[:96].reshape(4, 24, LANES), 1
        )
        attention_piece = jnp.concatenate(
            [
                blocks.reshape(192, LANES),
                in_core_order(core, own[96:], other[96:], 0),
                pack_extra(time_in, vectors, numbers),
            ],
            axis=0,
        )[None]
        up_halves = up_weight.reshape(24, 2, 4, LANES).transpose(1, 2, 0, 3)
        down_halves = down_weight.reshape(96, 2, LANES).transpose(1, 0, 2)
        both = jnp.concatenate([down_halves, up_halves.reshape(2, 96, LANES)], axis=1)
        own = pick(both, core)
        other = core_swap(pick(both, 1 - core))
        blocks = in_core_order(
            core, own[96:].reshape(4, 24, LANES), other[96:].reshape(4, 24, LANES), 1
        )
        mlp_piece = jnp.concatenate(
            [in_core_order(core, own[:96], other[:96], 0), blocks.reshape(192, LANES)], axis=0
        )[None]
        attention_pieces = gather_pieces(attention_piece)
        mlp_pieces = gather_pieces(mlp_piece)
        seen = jnp.concatenate([g[:, 224, 256 : 256 + 3 * count] for g in attention_pieces], axis=0)
    else:
        tab = jnp.concatenate(
            [jnp.tile(jnp.arange(CHIPS, dtype=jnp.int32), 4), jnp.zeros((8,), jnp.int32)]
        )
        full_qkv = gather_all(qkv_weight).reshape(CHIPS, 48, 3, 2, LANES)
        full_out = gather_all(out_weight).reshape(CHIPS, 48, 1, 2, LANES)
        full_up = gather_all(up_weight).reshape(CHIPS, 48, 2, 4, LANES)
        full_down = gather_all(down_weight).reshape(CHIPS, 192, 2, LANES)
        full_tin = gather_all(time_in).reshape(CHIPS, 2, 16, 128)
        full_tout = gather_all(time_out).reshape(CHIPS, 32, 2, LANES)
        full_vec = lax.all_gather(vectors, AXES, axis=1, tiled=True).reshape(4, CHIPS, 2, 24)
        seen = gather_all(numbers[None])
        extra = jnp.zeros((CHIPS, 2, 16, LANES), BF16)
        extra = extra.at[:, :, :, :128].set(full_tin)
        extra = extra.at[:, :, 0:4, 128:152].set(full_vec.transpose(1, 2, 0, 3))
        attention_pieces = []
        mlp_pieces = []
        for half in (0, 1):
            wide = jnp.concatenate([full_qkv[:, :, :, half], full_out[:, :, :, half]], axis=2)
            whole = jnp.concatenate(
                [
                    wide.transpose(0, 2, 1, 3).reshape(CHIPS, 192, LANES),
                    full_tout[:, :, half],
                    extra[:, half],
                ],
                axis=1,
            )
            attention_pieces += [whole[:8], whole[8:]]
            whole = jnp.concatenate(
                [
                    full_down[:, :, half],
                    full_up[:, :, half].transpose(0, 2, 1, 3).reshape(CHIPS, 192, LANES),
                ],
                axis=1,
            )
            mlp_pieces += [whole[:8], whole[8:]]

    micros, seqs, seq_len, width = block_input.shape
    tokens = micros * seqs * seq_len
    x_rows = block_input.reshape(tokens, width)
    grad_rows = out_grad.reshape(tokens, width)
    features = sinusoid(timestep.reshape(-1), time_in.shape[1] // 2).astype(BF16)
    sets = dataset.reshape(-1, 1).astype(F32)
    normed, qkv, probs, att, mid, two, embed, vecs = attention_forward(
        tab, lengths.reshape(-1), attention_pieces, x_rows, features, sets
    )
    mlp_mine, mlp_theirs, result, grad_mid, branch, gain_two = mlp(
        tab, mlp_pieces, two, grad_rows, mid, vecs
    )
    att_mine, att_theirs, grad_qkv = attention_backward(
        tab, attention_pieces, branch, att, qkv, probs, normed
    )
    grad_input, small = input_backward(
        tab, attention_pieces, grad_qkv, x_rows, embed, vecs, grad_mid, gain_two
    )

    small = small.astype(BF16)[None]
    if exchange:
        every = jnp.concatenate(gather_pieces(small), axis=0)
    else:
        every = gather_all(small)
    every = every.reshape(devices * 16, width)
    steps = seen[:, :count] * 64 + seen[:, count : 2 * count].astype(F32)
    wave = sinusoid(steps.reshape(-1), time_in.shape[1] // 2).astype(BF16)
    wave = jnp.pad(wave.reshape(devices, count, -1), ((0, 0), (0, 16 - count), (0, 0)))
    wave = wave.reshape(devices * 16, -1)
    which = jnp.pad(seen[:, 2 * count :], ((0, 0), (0, 16 - count))).reshape(-1)
    place = jnp.tile(jnp.arange(16), devices)
    hot = jnp.stack(
        [(place < count) & (which == 0), (place < count) & (which == 1), place == 8, place == 9]
    ).astype(BF16)
    pre = dot_last(wave, time_in)
    gate = 1.0 / (1.0 + jnp.exp(-pre))
    hidden = (pre * gate).astype(BF16)
    grad_tout = dot_first(hidden, every)
    grad_pre = dot_last(every, time_out) * (gate * (1.0 + pre * (1.0 - gate)))
    grad_tin = dot_first(grad_pre.astype(BF16), wave)
    sums = dot(hot, every)
    own_cols = norm1_gain.shape[0]
    sums = lax.dynamic_slice_in_dim(sums, flat * own_cols, own_cols, 1)

    if exchange:
        piece = scatter_pieces(mlp_mine, mlp_theirs)
        down = piece[:192].reshape(2, 96, LANES)
        up = piece[192:].reshape(4, 2, 24, LANES).transpose(1, 0, 2, 3).reshape(2, 96, LANES)
        both = jnp.concatenate([down, up], axis=1)
        own = pick(both, core)
        other = core_swap(pick(both, 1 - core))
        grad_down = in_core_order(core, own[:96], other[:96], 1)
        grad_up = in_core_order(
            core, own[96:].reshape(4, 24, LANES), other[96:].reshape(4, 24, LANES), 0
        )
        grad_up = grad_up.transpose(1, 0, 2).reshape(24, FF)
        piece = scatter_pieces(att_mine, att_theirs)
        both = piece.reshape(4, 2, 24, LANES).transpose(1, 0, 2, 3)
        own = pick(both, core)
        other = core_swap(pick(both, 1 - core))
        joined = in_core_order(core, own[:, None], other[:, None], 1)
        joined = joined.transpose(2, 0, 1, 3).reshape(24, 4 * WIDTH)
        grad_qkv_weight = joined[:, : 3 * WIDTH]
        grad_out_weight = joined[:, 3 * WIDTH :]
    else:
        scatter = partial(lax.psum_scatter, axis_name=AXES, scatter_dimension=0, tiled=True)
        both = jnp.stack([mlp_mine, mlp_theirs]).astype(F32)
        grad_down = scatter(both[:, :, :192].transpose(1, 2, 0, 3).reshape(FF, WIDTH))
        grad_up = scatter(
            both[:, :, 192:].reshape(2, CHIPS, 4, 48, LANES).transpose(1, 3, 0, 2, 4).reshape(WIDTH, FF)
        )
        both = jnp.stack([att_mine, att_theirs]).astype(F32).reshape(2, CHIPS, 4, 48, LANES)
        both = scatter(both.transpose(1, 3, 2, 0, 4).reshape(WIDTH, 4 * WIDTH))
        grad_qkv_weight = both[:, : 3 * WIDTH]
        grad_out_weight = both[:, 3 * WIDTH :]

    return (
        result.reshape(block_input.shape),
        grad_input.reshape(block_input.shape),
        sums[2],
        grad_qkv_weight,
        grad_out_weight,
        sums[3],
        grad_up,
        grad_down,
        grad_tin,
        grad_tout,
        sums[:2].T,
    )


def solution(mesh):
    devices = mesh.shape["dp"] * mesh.shape["fsdp"]
    seq_spec = P(None, AXES, None, None)
    int_spec = P(None, AXES)
    row_spec = P(AXES, None)
    in_specs = (seq_spec, seq_spec, int_spec, int_spec, int_spec, P(AXES), row_spec, row_spec, P(AXES))
    in_specs = in_specs + (row_spec,) * 5
    out_specs = (seq_spec, seq_spec, P(AXES), row_spec, row_spec, P(AXES)) + (row_spec,) * 5
    return jax.shard_map(
        partial(shards, devices=devices),
        mesh=mesh,
        in_specs=in_specs,
        out_specs=out_specs,
        check_vma=False,
    )
```

time: 1130 us -> 371 us (0.33)
  waiting for transfers between devices: 669 us -> 145 us
  blocking collectives: 202 us -> 0 us
  matrix products: 148 us -> 2.22 us
  Pallas kernels: 0 us -> 145 us
  starting transfers between devices: 0.61 us -> 31.8 us
  local copies, waits for them, and re-layouts: 47.6 us -> 17.6 us
  between operations: 16.4 us -> 1.23 us
    reduce_scatter x6 -> x0, waiting for transfers between devices: 638 us -> none  [the longest x1 142 us: shards(): lax.psum_scatter(gradients[4], ('dp', 'fsdp'), scatter_dimension=0, tiled...]
    dot_general x50 -> x4, matrix products: 148 us -> 2.22 us  [the longest x2 1.87 us: dot_first(): lax.dot_general(left, right, (((0,), (0,)), ((), ())), preferred_element_...]
    pallas_call x0 -> x4, Pallas kernels: none -> 145 us  [the longest x1 60.6 us: mlp(): pl.pallas_call(mlp_kernel, out_shape=(shape((CHIPS, 384, LANES), BF16), s...]
    ppermute x0 -> x32, waiting for transfers between devices: none -> 145 us  [the longest x20 142 us: chip_swap(): lax.ppermute(x, AXES, [(i, i ^ CHIP_MASKS[i & 1][step] * 2) for i in rang...]
    all_gather x3 -> x0, blocking collectives: 120 us -> none  [the longest x1 44.9 us: shards(): lax.all_gather(time_out, ('dp', 'fsdp'), axis=0, tiled=True)]
    unnamed x2 -> x0, blocking collectives: 82.2 us -> none
    ppermute x0 -> x32, starting transfers between devices: none -> 31.8 us  [the longest x20 30 us: chip_swap(): lax.ppermute(x, AXES, [(i, i ^ CHIP_MASKS[i & 1][step] * 2) for i in rang...]
    all_gather x4 -> x0, waiting for transfers between devices: 28.2 us -> none  [the longest x1 28.2 us: shards(): lax.all_gather(down_weight, ('dp', 'fsdp'), axis=0, tiled=True)]
  transfers between devices with their start and end apart: 10 -> 32, of which waited for: 7 -> 16; matrix products, arithmetic and copies ran while one was open for 11% -> 12% of each run, Pallas kernels for 0% -> 23%
where the time goes in v1:
time: 371 us; the launch traced here: 370 us
  waiting for transfers between devices  145 us (39%)
  Pallas kernels  145 us (39%)
  starting transfers between devices  31.8 us (9%)
  other arithmetic  27.4 us (7%)
  local copies, waits for them, and re-layouts  17.6 us (5%)
    ppermute x20, waiting for transfers between devices, chip_swap(): lax.ppermute(x, AXES, [(i, i ^ CHIP_MASKS[i & 1][step] * 2) for i in rang...  142 us
    pallas_call x1, Pallas kernels, mlp(): pl.pallas_call(mlp_kernel, out_shape=(shape((CHIPS, 384, LANES), BF16), s...  60.6 us
    pallas_call x1, Pallas kernels, attention_backward(): pl.pallas_call(attention_backward_kernel, out_shape=(shape((CHIPS, 192, L...  36.4 us
    ppermute x20, starting transfers between devices, chip_swap(): lax.ppermute(x, AXES, [(i, i ^ CHIP_MASKS[i & 1][step] * 2) for i in rang...  30 us
    pallas_call x1, Pallas kernels, attention_forward(): pl.pallas_call(attention_forward_kernel, out_shape=(shape((1024, WIDTH),...  29.2 us
    pallas_call x1, Pallas kernels, input_backward(): pl.pallas_call(input_backward_kernel, out_shape=(shape((1024, WIDTH), BF1...  18.8 us
    convert_element_type x8, other arithmetic, scatter_pieces(): parts.append(chip_swap(add_parts(parts, size, 2 * size).astype(BF16), step))  16.5 us
  transfers between devices with their start and end apart: 32, of which 16 were waited for; matrix products, arithmetic and copies ran while one was open for 12% of the time, Pallas kernels for 23%

profile of v1, /device:TPU:0, one launch (start us, length us, event | category | flops | bytes accessed | tf_op | source)
XLA Modules:
  0.0 370.0 jit_solution(5169965433548959594)
XLA Ops:
  4.4 4.0 %collective-permute-start.1 = (bf16[1,384,384]{2,1,0:T(8,128)(2,1)S(1)}, bf16[1,384,384]{2,1,0:T(8,128)(2,1)S(1)}, u32[]{:S(2)}, u32[]{:S(2)}) collective-permute-start(bf16[1,384,384]{2,1,0:T(8,128)(2,1)S(1)} %maximum_bitcast_fusion), channel_id=1, source_target_pairs={{0,4},{1,5},{2,6},{3,7},{4,0},{5,1},{6,2},{7,3},{8,12},{9,13},{10,... | collective-permute-start | bytes 884744 | tf_op jit(solution)/shard_map/ppermute | solution.py:67
  8.4 13.6 %collective-permute-done.1 = bf16[1,384,384]{2,1,0:T(8,128)(2,1)S(1)} collective-permute-done((bf16[1,384,384]{2,1,0:T(8,128)(2,1)S(1)}, bf16[1,384,384]{2,1,0:T(8,128)(2,1)S(1)}, u32[]{:S(2)}, u32[]{:S(2)}) %collective-permute-start.1) | collective-permute-done | bytes 294944 | tf_op jit(solution)/shard_map/ppermute | solution.py:67
  24.9 12.1 %collective-permute-done.2 = bf16[2,384,384]{2,1,0:T(8,128)(2,1)S(1)} collective-permute-done((bf16[2,384,384]{2,1,0:T(8,128)(2,1)S(1)}, bf16[2,384,384]{2,1,0:T(8,128)(2,1)S(1)}, u32[]{:S(2)}, u32[]{:S(2)}) %collective-permute-start.2) | collective-permute-done | bytes 589856 | tf_op jit(solution)/shard_map/ppermute | solution.py:67
  44.4 3.1 collective-permute-start.8
  47.5 8.0 %collective-permute-done.8 = bf16[1,240,384]{2,1,0:T(8,128)(2,1)S(1)} collective-permute-done((bf16[1,240,384]{2,1,0:T(8,128)(2,1)S(1)}, bf16[1,240,384]{2,1,0:T(8,128)(2,1)S(1)}, u32[]{:S(2)}, u32[]{:S(2)}) %collective-permute-start.8) | collective-permute-done | bytes 184352 | tf_op jit(solution)/shard_map/ppermute | solution.py:67
  58.6 6.6 %collective-permute-done.9 = bf16[2,240,384]{2,1,0:T(8,128)(2,1)S(1)} collective-permute-done((bf16[2,240,384]{2,1,0:T(8,128)(2,1)S(1)}, bf16[2,240,384]{2,1,0:T(8,128)(2,1)S(1)}, u32[]{:S(2)}, u32[]{:S(2)}) %collective-permute-start.9) | collective-permute-done | bytes 368672 | tf_op jit(solution)/shard_map/ppermute | solution.py:67
  67.4 17.4 %collective-permute-done.10 = bf16[4,240,384]{2,1,0:T(8,128)(2,1)S(1)} collective-permute-done((bf16[4,240,384]{2,1,0:T(8,128)(2,1)S(1)}, bf16[4,240,384]{2,1,0:T(8,128)(2,1)S(1)}, u32[]{:S(2)}, u32[]{:S(2)}) %collective-permute-start.10) | collective-permute-done | bytes 737312 | tf_op jit(solution)/shard_map/ppermute | solution.py:67
  85.6 9.5 %collective-permute-done.4.g_b = bf16[8,384,384]{2,1,0:T(8,128)(2,1)} collective-permute-done((bf16[8,384,384]{2,1,0:T(8,128)(2,1)}, bf16[8,384,384]{2,1,0:T(8,128)(2,1)}, u32[]{:S(2)}, u32[]{:S(2)}) %collective-permute-start.4) | collective-permute-done | bytes 2359328 | tf_op jit(solution)/shard_map/ppermute | solution.py:67
  95.6 15.2 %collective-permute-done.11.g_b = bf16[8,240,384]{2,1,0:T(8,128)(2,1)S(1)} collective-permute-done((bf16[8,240,384]{2,1,0:T(8,128)(2,1)S(1)}, bf16[8,240,384]{2,1,0:T(8,128)(2,1)S(1)}, u32[]{:S(2)}, u32[]{:S(2)}) %collective-permute-start.11) | collective-permute-done | bytes 1474592 | tf_op jit(solution)/shard_map/ppermute | solution.py:67
  114.9 29.2 %attention_forward.1 = (bf16[1024,768]{1,0:T(8,128)(2,1)}, bf16[1024,2304]{1,0:T(8,128)(2,1)}, bf16[12288,128]{1,0:T(8,128)(2,1)}, bf16[1024,768]{1,0:T(8,128)(2...) custom-call(s32[72]{0:T(128)} %concatenate.135.tab, ...), custom_call_target="tpu_custom_call" | custom-call | flops 8000000000 | bytes 24000000 | tf_op jit(solution)/shard_map/attention_forward/pallas_call | solution.py:263
  144.1 60.6 %mlp.1 = (bf16[16,384,384]{2,1,0:T(8,128)(2,1)}, bf16[16,384,384]{2,1,0:T(8,128)(2,1)}, bf16[1024,768]{1,0:T(8,128)(2,1)}, f32[1024,768]{1,0:T(8,128)}, bf16[1024,768]{1,0:T(8,128)(2,1)}, /*index=5*/f32[1,768]{1,0:T(1,128)}) custom-call(s32[72]{0:T(128)} %concatenate.135.tab, bf16[8,384,384]{2,1,0:T(8,128)(2,1)} %pad_maximum_fusion.g_a, ...), custom_call_target="tpu_custom_call" | custom-call | flops 30000001024 | bytes 40000000 | tf_op jit(solution)/shard_map/mlp/pallas_call | solution.py:394
  205.3 36.4 %attention_backward.1 = (bf16[16,192,384]{2,1,0:T(8,128)(2,1)}, bf16[16,192,384]{2,1,0:T(8,128)(2,1)}, bf16[1024,2304]{1,0:T(8,128)(2,1)}) custom-call(s32[72]{0:T(128)} %concatenate.135.tab, bf16[8,240,384]{2,1,0:T(8,128)(2,1)} %copy-done.2, bf16[8,240,384]{2,1,0:T(8,128)(2,1)} %copy-done.3, bf16[8,240,384]{2,1,0:T(8,128)(2,1)} %collective-permute-done.12.g_c, ...), custom_call_target="tpu_custom_call" | custom-call | flops 10000000000 | bytes 20000000 | tf_op jit(solution)/shard_map/attention_backward/pallas_call | solution.py:506
  245.6 3.0 add_convert_fusion
  249.4 18.8 %input_backward.1 = (bf16[1024,768]{1,0:T(8,128)(2,1)}, f32[16,768]{1,0:T(8,128)}) custom-call(s32[72]{0:T(128)} %concatenate.135.tab, bf16[8,240,384]{2,1,0:T(8,128)(2,1)} %copy-done.2, bf16[8,240,384]{2,1,0:T(8,128)(2,1)} %copy-done.3, bf16[8,240,384]{2,1,0:T(8,128)(2,1)} %collective-permute-done.12.g_c, bf16[8,240,384]{2,1,0:T(8,128)(2,1)} %collective-permute-done.13.g_d, ...), custom_call_target="tpu_custom_call" | custom-call | flops 4000000000 | bytes 18000000 | tf_op jit(solution)/shard_map/input_backward/pallas_call | solution.py:560
  269.0 3.4 collective-permute-start.14
  280.1 4.2 %collective-permute-done.16 = bf16[4,16,768]{2,1,0:T(8,128)(2,1)S(1)} collective-permute-done((bf16[4,16,768]{2,1,0:T(8,128)(2,1)S(1)}, bf16[4,16,768]{2,1,0:T(8,128)(2,1)S(1)}, u32[]{:S(2)}, u32[]{:S(2)}) %collective-permute-start.16) | collective-permute-done | bytes 98336 | tf_op jit(solution)/shard_map/ppermute | solution.py:67
  286.0 10.4 %collective-permute-done.17 = bf16[8,16,768]{2,1,0:T(8,128)(2,1)S(1)} collective-permute-done((bf16[8,16,768]{2,1,0:T(8,128)(2,1)S(1)}, bf16[8,16,768]{2,1,0:T(8,128)(2,1)S(1)}, u32[]{:S(2)}, u32[]{:S(2)}) %collective-permute-start.17) | collective-permute-done | bytes 196640 | tf_op jit(solution)/shard_map/ppermute | solution.py:67
  297.9 2.4 add_convert_fusion.1
  306.0 16.9 %collective-permute-done.22 = bf16[4,192,384]{2,1,0:T(8,128)(2,1)S(1)} collective-permute-done((bf16[4,192,384]{2,1,0:T(8,128)(2,1)S(1)}, bf16[4,192,384]{2,1,0:T(8,128)(2,1)S(1)}, u32[]{:S(2)}, u32[]{:S(2)}) %collective-permute-start.22) | collective-permute-done | bytes 589856 | tf_op jit(solution)/shard_map/ppermute | solution.py:67
  326.1 2.6 add_convert_fusion.3
  331.3 4.0 %collective-permute-done.23 = bf16[2,192,384]{2,1,0:T(8,128)(2,1)} collective-permute-done((bf16[2,192,384]{2,1,0:T(8,128)(2,1)}, bf16[2,192,384]{2,1,0:T(8,128)(2,1)}, u32[]{:S(2)}, u32[]{:S(2)}) %collective-permute-start.23) | collective-permute-done | bytes 294944 | tf_op jit(solution)/shard_map/ppermute | solution.py:67
  336.5 2.2 collective-permute-start.24
  338.7 10.6 %collective-permute-done.29 = bf16[2,384,384]{2,1,0:T(8,128)(2,1)S(1)} collective-permute-done((bf16[2,384,384]{2,1,0:T(8,128)(2,1)}, bf16[2,384,384]{2,1,0:T(8,128)(2,1)S(1)}, u32[]{:S(2)}, u32[]{:S(2)}) %collective-permute-start.29) | collective-permute-done | bytes 589856 | tf_op jit(solution)/shard_map/ppermute | solution.py:67
  352.8 12.3 %collective-permute-done.30 = bf16[1,384,384]{2,1,0:T(8,128)(2,1)S(1)} collective-permute-done((bf16[1,384,384]{2,1,0:T(8,128)(2,1)S(1)}, bf16[1,384,384]{2,1,0:T(8,128)(2,1)S(1)}, u32[]{:S(2)}, u32[]{:S(2)}) %collective-permute-start.30) | collective-permute-done | bytes 294944 | tf_op jit(solution)/shard_map/ppermute | solution.py:67
  (189 shorter events, 62.4 us)
Async XLA Ops:
  4.4 17.7 %collective-permute-start.1 = (bf16[1,384,384]{2,1,0:T(8,128)(2,1)S(1)}, bf16[1,384,384]{2,1,0:T(8,128)(2,1)S(1)}, u32[]{:S(2)}, u32[]{:S(2)}) collective-permute-start(bf16[1,384,384]{2,1,0:T(8,128)(2,1)S(1)} %maximum_bitcast_fusion), channel_id=1, source_target_pairs={{0,4},{1,5},{2,6},{3,7},{4,0},{5,1},{6,2},{7,3},{8,12},{9,13},{10,... | collective-permute-start | bytes 884744 | tf_op jit(solution)/shard_map/ppermute | solution.py:67
  22.2 14.9 %collective-permute-start.2 = (bf16[2,384,384]{2,1,0:T(8,128)(2,1)S(1)}, bf16[2,384,384]{2,1,0:T(8,128)(2,1)S(1)}, u32[]{:S(2)}, u32[]{:S(2)}) collective-permute-start(bf16[2,384,384]{2,1,0:T(8,128)(2,1)S(1)} %pad_maximum_fusion.4), channel_id=1, source_target_pairs={{0,2},{1,3},{2,0},{3,1},{4,6},{5,7},{6,4},{7,5},{8,10},{9,11},{10,... | collective-permute-start | bytes 1769480 | tf_op jit(solution)/shard_map/ppermute | solution.py:67
  23.8 18.9 %collective-permute-start.7 = (bf16[112,384]{1,0:T(8,128)(2,1)}, bf16[112,384]{1,0:T(8,128)(2,1)}, u32[]{:S(2)}, u32[]{:S(2)}) collective-permute-start(bf16[112,384]{1,0:T(8,128)(2,1)} %get-tuple-element.64), channel_id=1, source_target_pairs={{0,1},{1,0},{2,3},{3,2},{4,5},{5,4},{6,7},{7,6},{8,9},{9,8},{10,11... | collective-permute-start | bytes 258056 | tf_op jit(solution)/shard_map/ppermute | solution.py:63
  37.2 19.0 %collective-permute-start.3 = (bf16[4,384,384]{2,1,0:T(8,128)(2,1)S(1)}, bf16[4,384,384]{2,1,0:T(8,128)(2,1)S(1)}, u32[]{:S(2)}, u32[]{:S(2)}) collective-permute-start(bf16[4,384,384]{2,1,0:T(8,128)(2,1)S(1)} %pad_maximum_fusion.2), channel_id=1, source_target_pairs={{0,16},{1,9},{2,18},{3,11},{4,20},{5,13},{6,22},{7,15},{8,24},{9,1... | collective-permute-start | bytes 3538952 | tf_op jit(solution)/shard_map/ppermute | solution.py:67
  44.4 11.1 %collective-permute-start.8 = (bf16[1,240,384]{2,1,0:T(8,128)(2,1)S(1)}, bf16[1,240,384]{2,1,0:T(8,128)(2,1)S(1)}, u32[]{:S(2)}, u32[]{:S(2)}) collective-permute-start(bf16[1,240,384]{2,1,0:T(8,128)(2,1)S(1)} %maximum_bitcast_fusion.1), channel_id=1, source_target_pairs={{0,4},{1,5},{2,6},{3,7},{4,0},{5,1},{6,2},{7,3},{8,12},{9,13},{10,... | collective-permute-start | bytes 552968 | tf_op jit(solution)/shard_map/ppermute | solution.py:67
  58.1 37.1 %collective-permute-start.4 = (bf16[8,384,384]{2,1,0:T(8,128)(2,1)}, bf16[8,384,384]{2,1,0:T(8,128)(2,1)}, u32[]{:S(2)}, u32[]{:S(2)}) collective-permute-start(bf16[8,384,384]{2,1,0:T(8,128)(2,1)} %pad_maximum_fusion.g_a), channel_id=1, source_target_pairs={{0,8},{1,17},{2,10},{3,19},{4,12},{5,21},{6,14},{7,23},{8,0},{9,25... | collective-permute-start | bytes 7077896 | tf_op jit(solution)/shard_map/ppermute | solution.py:67
  65.3 19.5 %collective-permute-start.10 = (bf16[4,240,384]{2,1,0:T(8,128)(2,1)S(1)}, bf16[4,240,384]{2,1,0:T(8,128)(2,1)S(1)}, u32[]{:S(2)}, u32[]{:S(2)}) collective-permute-start(bf16[4,240,384]{2,1,0:T(8,128)(2,1)S(1)} %pad_maximum_fusion.3), channel_id=1, source_target_pairs={{0,16},{1,9},{2,18},{3,11},{4,20},{5,13},{6,22},{7,15},{8,24},{9,1... | collective-permute-start | bytes 2211848 | tf_op jit(solution)/shard_map/ppermute | solution.py:67
  85.0 25.8 %collective-permute-start.11 = (bf16[8,240,384]{2,1,0:T(8,128)(2,1)S(1)}, bf16[8,240,384]{2,1,0:T(8,128)(2,1)S(1)}, u32[]{:S(2)}, u32[]{:S(2)}) collective-permute-start(bf16[8,240,384]{2,1,0:T(8,128)(2,1)S(1)} %pad_maximum_fusion.1.g_a), channel_id=1, source_target_pairs={{0,8},{1,17},{2,10},{3,19},{4,12},{5,21},{6,14},{7,23},{8,0},{9,25... | collective-permute-start | bytes 4423688 | tf_op jit(solution)/shard_map/ppermute | solution.py:67
  85.6 58.5 %collective-permute-start.5 = (bf16[8,384,384]{2,1,0:T(8,128)(2,1)}, bf16[8,384,384]{2,1,0:T(8,128)(2,1)}, u32[]{:S(2)}, u32[]{:S(2)}) collective-permute-start(bf16[8,384,384]{2,1,0:T(8,128)(2,1)} %pad_maximum_fusion.g_a), channel_id=1, source_target_pairs={{0,1},{1,0},{2,3},{3,2},{4,5},{5,4},{6,7},{7,6},{8,9},{9,8},{10,11... | collective-permute-start | bytes 7077896 | tf_op jit(solution)/shard_map/ppermute | solution.py:63
  95.1 49.0 %collective-permute-start.6 = (bf16[8,384,384]{2,1,0:T(8,128)(2,1)}, bf16[8,384,384]{2,1,0:T(8,128)(2,1)}, u32[]{:S(2)}, u32[]{:S(2)}) collective-permute-start(bf16[8,384,384]{2,1,0:T(8,128)(2,1)} %collective-permute-done.4.g_b), channel_id=1, source_target_pairs={{0,1},{1,0},{2,3},{3,2},{4,5},{5,4},{6,7},{7,6},{8,9},{9,8},{10,11... | collective-permute-start | bytes 7077896 | tf_op jit(solution)/shard_map/ppermute | solution.py:63
  95.1 19.7 %collective-permute-start.12 = (bf16[8,240,384]{2,1,0:T(8,128)(2,1)S(1)}, bf16[8,240,384]{2,1,0:T(8,128)(2,1)}, u32[]{:S(2)}, u32[]{:S(2)}) collective-permute-start(bf16[8,240,384]{2,1,0:T(8,128)(2,1)S(1)} %pad_maximum_fusion.1.g_a), channel_id=1, source_target_pairs={{0,1},{1,0},{2,3},{3,2},{4,5},{5,4},{6,7},{7,6},{8,9},{9,8},{10,11... | collective-permute-start | bytes 4423688 | tf_op jit(solution)/shard_map/ppermute | solution.py:63
  204.7 40.9 %collective-permute-start.26 = (bf16[16,384,384]{2,1,0:T(8,128)(2,1)}, bf16[16,384,384]{2,1,0:T(8,128)(2,1)}, u32[]{:S(2)}, u32[]{:S(2)}) collective-permute-start(bf16[16,384,384]{2,1,0:T(8,128)(2,1)} %get-tuple-element.48), channel_id=1, source_target_pairs={{0,1},{1,0},{2,3},{3,2},{4,5},{5,4},{6,7},{7,6},{8,9},{9,8},{10,11... | collective-permute-start | bytes 14155784 | tf_op jit(solution)/shard_map/ppermute | solution.py:63
  241.7 33.4 %collective-permute-start.20 = (bf16[16,192,384]{2,1,0:T(8,128)(2,1)}, bf16[16,192,384]{2,1,0:T(8,128)(2,1)}, u32[]{:S(2)}, u32[]{:S(2)}) collective-permute-start(bf16[16,192,384]{2,1,0:T(8,128)(2,1)} %get-tuple-element.46), channel_id=1, source_target_pairs={{0,1},{1,0},{2,3},{3,2},{4,5},{5,4},{6,7},{7,6},{8,9},{9,8},{10,11... | collective-permute-start | bytes 7077896 | tf_op jit(solution)/shard_map/ppermute | solution.py:63
  248.6 49.3 %collective-permute-start.27 = (bf16[8,384,384]{2,1,0:T(8,128)(2,1)S(1)}, bf16[8,384,384]{2,1,0:T(8,128)(2,1)}, u32[]{:S(2)}, u32[]{:S(2)}) collective-permute-start(bf16[8,384,384]{2,1,0:T(8,128)(2,1)S(1)} %add_convert_fusion), channel_id=1, source_target_pairs={{0,8},{1,17},{2,10},{3,19},{4,12},{5,21},{6,14},{7,23},{8,0},{9,25... | collective-permute-start | bytes 7077896 | tf_op jit(solution)/shard_map/ppermute | solution.py:67
  277.0 24.4 %collective-permute-start.21 = (bf16[8,192,384]{2,1,0:T(8,128)(2,1)S(1)}, bf16[8,192,384]{2,1,0:T(8,128)(2,1)S(1)}, u32[]{:S(2)}, u32[]{:S(2)}) collective-permute-start(bf16[8,192,384]{2,1,0:T(8,128)(2,1)S(1)} %add_convert_fusion.2), channel_id=1, source_target_pairs={{0,8},{1,17},{2,10},{3,19},{4,12},{5,21},{6,14},{7,23},{8,0},{9,25... | collective-permute-start | bytes 3538952 | tf_op jit(solution)/shard_map/ppermute | solution.py:67
  284.4 12.0 %collective-permute-start.17 = (bf16[8,16,768]{2,1,0:T(8,128)(2,1)S(1)}, bf16[8,16,768]{2,1,0:T(8,128)(2,1)S(1)}, u32[]{:S(2)}, u32[]{:S(2)}) collective-permute-start(bf16[8,16,768]{2,1,0:T(8,128)(2,1)S(1)} %pad_maximum_fusion.6), channel_id=1, source_target_pairs={{0,8},{1,17},{2,10},{3,19},{4,12},{5,21},{6,14},{7,23},{8,0},{9,25... | collective-permute-start | bytes 589832 | tf_op jit(solution)/shard_map/ppermute | solution.py:67
  286.0 10.4 %collective-permute-start.18 = (bf16[8,16,768]{2,1,0:T(8,128)(2,1)S(1)}, bf16[8,16,768]{2,1,0:T(8,128)(2,1)S(1)}, u32[]{:S(2)}, u32[]{:S(2)}) collective-permute-start(bf16[8,16,768]{2,1,0:T(8,128)(2,1)S(1)} %pad_maximum_fusion.6), channel_id=1, source_target_pairs={{0,1},{1,0},{2,3},{3,2},{4,5},{5,4},{6,7},{7,6},{8,9},{9,8},{10,11... | collective-permute-start | bytes 589832 | tf_op jit(solution)/shard_map/ppermute | solution.py:63
  300.3 25.8 %collective-permute-start.28 = (bf16[4,384,384]{2,1,0:T(8,128)(2,1)S(1)}, bf16[4,384,384]{2,1,0:T(8,128)(2,1)S(1)}, u32[]{:S(2)}, u32[]{:S(2)}) collective-permute-start(bf16[4,384,384]{2,1,0:T(8,128)(2,1)S(1)} %add_convert_fusion.1), channel_id=1, source_target_pairs={{0,16},{1,9},{2,18},{3,11},{4,20},{5,13},{6,22},{7,15},{8,24},{9,1... | collective-permute-start | bytes 3538952 | tf_op jit(solution)/shard_map/ppermute | solution.py:67
  303.3 19.6 %collective-permute-start.22 = (bf16[4,192,384]{2,1,0:T(8,128)(2,1)S(1)}, bf16[4,192,384]{2,1,0:T(8,128)(2,1)S(1)}, u32[]{:S(2)}, u32[]{:S(2)}) collective-permute-start(bf16[4,192,384]{2,1,0:T(8,128)(2,1)S(1)} %add_convert_fusion.4), channel_id=1, source_target_pairs={{0,16},{1,9},{2,18},{3,11},{4,20},{5,13},{6,22},{7,15},{8,24},{9,1... | collective-permute-start | bytes 1769480 | tf_op jit(solution)/shard_map/ppermute | solution.py:67
  325.0 10.3 %collective-permute-start.23 = (bf16[2,192,384]{2,1,0:T(8,128)(2,1)}, bf16[2,192,384]{2,1,0:T(8,128)(2,1)}, u32[]{:S(2)}, u32[]{:S(2)}) collective-permute-start(bf16[2,192,384]{2,1,0:T(8,128)(2,1)} %add_convert_fusion.6), channel_id=1, source_target_pairs={{0,2},{1,3},{2,0},{3,1},{4,6},{5,7},{6,4},{7,5},{8,10},{9,11},{10,... | collective-permute-start | bytes 884744 | tf_op jit(solution)/shard_map/ppermute | solution.py:67
  328.7 20.5 %collective-permute-start.29 = (bf16[2,384,384]{2,1,0:T(8,128)(2,1)}, bf16[2,384,384]{2,1,0:T(8,128)(2,1)S(1)}, u32[]{:S(2)}, u32[]{:S(2)}) collective-permute-start(bf16[2,384,384]{2,1,0:T(8,128)(2,1)} %add_convert_fusion.3), channel_id=1, source_target_pairs={{0,2},{1,3},{2,0},{3,1},{4,6},{5,7},{6,4},{7,5},{8,10},{9,11},{10,... | collective-permute-start | bytes 1769480 | tf_op jit(solution)/shard_map/ppermute | solution.py:67
  336.5 14.9 %collective-permute-start.24 = (bf16[1,192,384]{2,1,0:T(8,128)(2,1)S(1)}, bf16[1,192,384]{2,1,0:T(8,128)(2,1)S(1)}, u32[]{:S(2)}, u32[]{:S(2)}) collective-permute-start(bf16[1,192,384]{2,1,0:T(8,128)(2,1)S(1)} %add_convert_fusion.7), channel_id=1, source_target_pairs={{0,4},{1,5},{2,6},{3,7},{4,0},{5,1},{6,2},{7,3},{8,12},{9,13},{10,... | collective-permute-start | bytes 442376 | tf_op jit(solution)/shard_map/ppermute | solution.py:67
  350.6 14.5 %collective-permute-start.30 = (bf16[1,384,384]{2,1,0:T(8,128)(2,1)S(1)}, bf16[1,384,384]{2,1,0:T(8,128)(2,1)S(1)}, u32[]{:S(2)}, u32[]{:S(2)}) collective-permute-start(bf16[1,384,384]{2,1,0:T(8,128)(2,1)S(1)} %add_convert_fusion.5), channel_id=1, source_target_pairs={{0,4},{1,5},{2,6},{3,7},{4,0},{5,1},{6,2},{7,3},{8,12},{9,13},{10,... | collective-permute-start | bytes 884744 | tf_op jit(solution)/shard_map/ppermute | solution.py:67
  352.7 14.0 %collective-permute-start.25 = (f32[4,24,384]{2,1,0:T(8,128)S(1)}, f32[4,24,384]{2,1,0:T(8,128)S(1)}, u32[]{:S(2)}, u32[]{:S(2)}) collective-permute-start(f32[4,24,384]{2,1,0:T(8,128)S(1)} %get-tuple-element.60), channel_id=1, source_target_pairs={{0,1},{1,0},{2,3},{3,2},{4,5},{5,4},{6,7},{7,6},{8,9},{9,8},{10,11... | collective-permute-start | bytes 442376 | tf_op jit(solution)/shard_map/ppermute | solution.py:63
  (26 other events, 523.0 us)

commit v2 on v0

v2 whole, which is shorter than its diff:
```python
from functools import partial
import math

import jax
import jax.numpy as jnp
from jax import lax
from jax.experimental import pallas as pl
from jax.experimental.pallas import tpu as pltpu
from jax.sharding import PartitionSpec as P

HEAD_DIM = 64
AXES = ("dp", "fsdp")
LANES = 384
CHIPS = 16
WIDTH = 768
FF = 3072
VMEM_MIB = 58
F32 = jnp.float32
BF16 = jnp.bfloat16
NEG = -1000000000.0


def sinusoid(timestep, half_width):
    frequency = jnp.exp(-math.log(10000.0) * jnp.arange(half_width, dtype=F32) / half_width)
    angles = timestep.astype(F32)[:, None] * frequency[None, :]
    return jnp.concatenate([jnp.cos(angles), jnp.sin(angles)], axis=-1)


def dot(left, right):
    return jnp.dot(left, right, preferred_element_type=F32)


def dot_last(left, right):
    return lax.dot_general(left, right, (((1,), (1,)), ((), ())), preferred_element_type=F32)


def dot_first(left, right):
    return lax.dot_general(left, right, (((0,), (0,)), ((), ())), preferred_element_type=F32)


def position_bits(core, masks):
    return [sum(masks[core][b] for b in range(4) if (p >> b) & 1) for p in range(CHIPS)]


CHIP_MASKS = ((2, 1, 8, 4), (2, 1, 4, 8))
ORDER = [position_bits(core, CHIP_MASKS) for core in (0, 1)]
INVERSE = [[ORDER[core].index(k) for k in range(CHIPS)] for core in (0, 1)]


def core_swap(x):
    return lax.ppermute(x, AXES, [(i, i ^ 1) for i in range(2 * CHIPS)])


def chip_swap(x, position):
    return lax.ppermute(
        x, AXES, [(i, i ^ (ORDER[i & 1][position] * 2)) for i in range(2 * CHIPS)]
    )


def after(x, *others):
    return lax.optimization_barrier((x,) + others)[0]


def gather_line(piece):
    return jnp.concatenate([piece] + [chip_swap(piece, p) for p in (1, 2, 3)], axis=0)


def gather_plane(held):
    return jnp.concatenate([held, chip_swap(held, 4)], axis=0)


def gather_pieces(piece):
    held = gather_plane(gather_line(piece))
    far = chip_swap(held, 8)
    return held, far, core_swap(held), core_swap(far)


class Scatter:
    def __init__(self, theirs):
        self.parts = [core_swap(theirs)]
        self.steps = [(8,), (4,), (1, 2, 3)]

    def sum(self, start, stop):
        total = self.parts[0][start:stop].astype(F32)
        for part in self.parts[1:]:
            total = total + part[start:stop].astype(F32)
        return total

    def send(self):
        self.positions = self.steps.pop(0)
        size = 1 if len(self.positions) == 3 else self.positions[0]
        self.sent = tuple(self.sum(p, p + size).astype(BF16) for p in self.positions)
        return self.sent

    def receive(self, *others):
        brought = [chip_swap(x, p) for x, p in zip(self.sent, self.positions)]
        self.parts += [after(x, *others) for x in brought] if others else brought

    def step(self, *others):
        self.receive(*others)
        return self.send()

    def total(self, *others):
        self.receive(*others)
        return self.sum(0, 1)[0]


VMEM_SPEC = pl.BlockSpec(memory_space=pltpu.VMEM)
SMEM_SPEC = pl.BlockSpec(memory_space=pltpu.SMEM)
ANY_SPEC = pl.BlockSpec(memory_space=pl.ANY)


def tiles(rows, cols):
    return pl.BlockSpec((rows, cols), lambda i: (i, 0))


def columns(rows, cols):
    return pl.BlockSpec((rows, cols), lambda i: (0, i))


def fixed(*shape):
    return pl.BlockSpec(shape, lambda i: (0,) * len(shape))


def shaped(shape, dtype=BF16):
    return jax.ShapeDtypeStruct(shape, dtype)


def params():
    return pltpu.CompilerParams(vmem_limit_bytes=VMEM_MIB * 1024 * 1024)


def cost(flops, nbytes, transcendentals=0):
    return pl.CostEstimate(flops=flops, bytes_accessed=nbytes, transcendentals=transcendentals)


def ln_stats(v):
    center = v - jnp.mean(v, axis=-1, keepdims=True)
    scale = lax.rsqrt(jnp.mean(center * center, axis=-1, keepdims=True) + 1e-05)
    return center * scale, scale


def ln_back(y, gain, xhat, scale):
    yg = y * gain
    return scale * (
        yg - jnp.mean(yg, axis=-1, keepdims=True) - xhat * jnp.mean(yg * xhat, axis=-1, keepdims=True)
    )


def first_core(tab):
    return tab[64]


def each_piece(tab, parts, fn):
    core = first_core(tab)
    for side in (0, 1):
        half = core if side == 0 else 1 - core
        for group in (0, 1):
            part = parts[side * 2 + group]

            def body(q, _, part=part, side=side, group=group, half=half):
                chip = tab[side * CHIPS + group * 8 + q]
                fn(part.at[q], chip, half)
                return 0

            lax.fori_loop(0, 8, body, 0)


def rows_of(chip, size):
    return pl.ds(pl.multiple_of(chip * size, size), size)


def lanes_of(half, size, base=0):
    return pl.ds(pl.multiple_of(half * size + base, 128), LANES)


def fetch_pieces(tab, parts, rows, dst, sem):
    each_piece(
        tab,
        parts,
        lambda src, chip, half: pltpu.make_async_copy(
            src.at[pl.ds(0, rows), :], dst.at[chip, half], sem
        ).start(),
    )


def block(pieces, half, first, rows=48):
    return pieces[:, half, first : first + rows, :].reshape(CHIPS * rows, LANES)


def both_halves(pieces, first, rows=48):
    return jnp.concatenate([block(pieces, h, first, rows) for h in (0, 1)], axis=1)


def down_rows(pieces, j):
    return jnp.concatenate(
        [pieces[4 * j : 4 * j + 4, h].reshape(WIDTH, LANES) for h in (0, 1)], axis=1
    )


def qkv_columns(pieces, half):
    return jnp.concatenate([block(pieces, half, 48 * sec) for sec in range(3)], axis=1)


def finish(ref, sem):
    pltpu.make_async_copy(ref, ref, sem).wait()


def add_embed(x, embed, i):
    seqs = x.shape[0] // 128
    parts = [
        x[128 * k : 128 * k + 128].astype(F32) + embed[pl.ds(i * seqs + k, 1), :]
        for k in range(seqs)
    ]
    return jnp.concatenate(parts, axis=0)


def qkv_kernel(
    tab, g_a, g_b, g_c, g_d, x_ref, feat_ref, set_ref,
    normed_ref, qkv_ref, te_ref, vec_ref,
    w, sem,
):
    i = pl.program_id(0)

    @pl.when(i == 0)
    def _():
        fetch_pieces(tab, (g_a, g_b, g_c, g_d), 192, w, sem)
        finish(w, sem)
        lane = lax.broadcasted_iota(jnp.int32, (128, WIDTH), 1)
        spread = (lax.broadcasted_iota(jnp.int32, (128, WIDTH), 0) == lane % 24).astype(BF16)
        vectors = jnp.zeros((16, WIDTH), F32)
        embed = jnp.zeros((8, WIDTH), F32)
        for owner in (0, 1):
            extra = block(w, owner, 176, 16)
            wide = dot(extra[:, 128:256], spread)
            chip = lax.broadcasted_iota(jnp.int32, (256, WIDTH), 0) // 16
            place = lax.broadcasted_iota(jnp.int32, (256, WIDTH), 1) // 24
            wide = jnp.where(place == chip * 2 + owner, wide, 0.0)
            vectors = vectors + jnp.sum(wide.reshape(CHIPS, 16, WIDTH), axis=0)
            pre = dot_last(feat_ref[...], extra[:, 0:128])
            hidden = (pre / (1.0 + jnp.exp(-pre))).astype(BF16)
            embed = embed + dot(hidden, both_halves(w, 144 + 16 * owner, 16))
        vec_ref[...] = vectors
        te_ref[...] = embed + jnp.where(set_ref[...] > 0.5, vectors[3:4, :], vectors[2:3, :])

    xhat, _unused = ln_stats(add_embed(x_ref[...], te_ref, i))
    normed_ref[...] = (xhat * vec_ref[0:1, :]).astype(BF16)
    for half in (0, 1):
        cols = slice(half * 3 * LANES, (half + 1) * 3 * LANES)
        qkv_ref[:, cols] = dot(normed_ref[...], qkv_columns(w, half)).astype(BF16)


def qkv_forward(tab, pieces, rows, features, sets):
    return pl.pallas_call(
        qkv_kernel,
        grid=(4,),
        out_shape=(
            shaped((1024, WIDTH)),
            shaped((1024, 3 * WIDTH)),
            shaped((8, WIDTH), F32),
            shaped((16, WIDTH), F32),
        ),
        in_specs=[SMEM_SPEC] + [ANY_SPEC] * 4 + [tiles(256, WIDTH), fixed(8, 128), fixed(8, 1)],
        out_specs=(tiles(256, WIDTH), tiles(256, 3 * WIDTH), fixed(8, WIDTH), fixed(16, WIDTH)),
        scratch_shapes=[pltpu.VMEM((CHIPS, 2, 192, LANES), BF16), pltpu.SemaphoreType.DMA],
        compiler_params=params(),
        cost_estimate=cost(4_000_000_000, 12_000_000),
        name="qkv_forward",
    )(tab, *pieces, rows, features, sets)


def two_heads(x, low_half):
    none = jnp.zeros_like(x)
    return jnp.concatenate([jnp.where(low_half, x, none), jnp.where(low_half, none, x)], axis=0)


def side_by_side(x):
    return jnp.concatenate([x[:128], x[128:]], axis=1)


def pair_base(pair):
    return (pair // 3) * 3 * LANES + (pair % 3) * 128


def attention_kernel(lens, qkv_ref, probs_ref, att_ref):
    low_half = lax.broadcasted_iota(jnp.int32, (128, 128), 1) < HEAD_DIM
    lane = lax.broadcasted_iota(jnp.int32, (256, 128), 1)
    for k in range(2):
        keep = lane < lens[pl.program_id(0) * 2 + k]
        rows = slice(128 * k, 128 * k + 128)
        scores = []
        for pair in range(6):
            base = pair_base(pair)
            query = two_heads(qkv_ref[rows, base : base + 128], low_half)
            key = qkv_ref[rows, base + LANES : base + LANES + 128]
            scores.append(jnp.where(keep, dot_last(query, key) * HEAD_DIM ** (-0.5), NEG))
        probs = []
        for pair in range(6):
            shifted = jnp.exp(scores[pair] - jnp.max(scores[pair], axis=-1, keepdims=True))
            total = jnp.sum(shifted, axis=-1, keepdims=True)
            probs.append((shifted * (1.0 / total)).astype(BF16))
            first = 256 * (6 * k + pair)
            probs_ref[first : first + 256, :] = probs[pair]
        for pair in range(6):
            base = pair_base(pair) + 2 * LANES
            value = two_heads(qkv_ref[rows, base : base + 128], low_half)
            att_ref[rows, pair * 128 : pair * 128 + 128] = dot(
                side_by_side(probs[pair]), value
            ).astype(BF16)


def attention(lens, qkv):
    return pl.pallas_call(
        attention_kernel,
        grid=(4,),
        out_shape=(shaped((48 * 256, 128)), shaped((1024, WIDTH))),
        in_specs=[SMEM_SPEC, tiles(256, 3 * WIDTH)],
        out_specs=(tiles(12 * 256, 128), tiles(256, WIDTH)),
        compiler_params=params(),
        cost_estimate=cost(4_000_000_000, 9_000_000, 1_600_000),
        name="attention",
    )(lens, qkv)


def gelu_parts(u):
    cdf = 0.5 + 0.5 * lax.erf(u * math.sqrt(0.5))
    return cdf, jnp.exp(u * u * -0.5) * (1.0 / math.sqrt(2.0 * math.pi))


def up_kernel(
    g_ref, att_ref, x_ref, te_ref, vec_ref,
    mid_ref, two_ref, act_ref, slope_ref,
    w, sem,
):
    i = pl.program_id(0)

    @pl.when(i == 0)
    def _():
        pltpu.make_async_copy(g_ref, w, sem).start()
        finish(w, sem)

    mid = add_embed(x_ref[...], te_ref, i) + dot(att_ref[...], w[:, FF:])
    mid_ref[...] = mid
    xhat, _unused = ln_stats(mid)
    two_ref[...] = (xhat * vec_ref[1:2, :]).astype(BF16)
    for j in range(4):
        cols = slice(j * WIDTH, (j + 1) * WIDTH)
        up = dot(two_ref[...], w[:, cols])
        cdf, density = gelu_parts(up)
        act_ref[:, cols] = (up * cdf).astype(BF16)
        slope_ref[:, cols] = (cdf + up * density).astype(BF16)


def up_forward(gathered, att, rows, embed, vectors):
    return pl.pallas_call(
        up_kernel,
        grid=(4,),
        out_shape=(
            shaped((1024, WIDTH), F32),
            shaped((1024, WIDTH)),
            shaped((1024, FF)),
            shaped((1024, FF)),
        ),
        in_specs=[ANY_SPEC, tiles(256, WIDTH), tiles(256, WIDTH), fixed(8, WIDTH), fixed(16, WIDTH)],
        out_specs=(tiles(256, WIDTH), tiles(256, WIDTH), tiles(256, FF), tiles(256, FF)),
        scratch_shapes=[pltpu.VMEM((WIDTH, FF + WIDTH), BF16), pltpu.SemaphoreType.DMA],
        compiler_params=params(),
        cost_estimate=cost(8_000_000_000, 26_000_000, 6_000_000),
        name="up_forward",
    )(gathered, att, rows, embed, vectors)


def half_of(tab, side):
    return first_core(tab) if side == 0 else 1 - first_core(tab)


def down_grad_kernel(act_ref, out_grad_ref, out_ref):
    out_ref[...] = dot_first(act_ref[...], out_grad_ref[...]).astype(BF16)


def down_grad(act, out_grad):
    return pl.pallas_call(
        down_grad_kernel,
        grid=(4,),
        out_shape=shaped((FF, WIDTH)),
        in_specs=[columns(1024, WIDTH), fixed(1024, WIDTH)],
        out_specs=tiles(WIDTH, WIDTH),
        compiler_params=params(),
        cost_estimate=cost(5_000_000_000, 13_000_000),
        name="down_grad",
    )(act, out_grad)


def store_blocks(tab, side, target, first, part, lanes):
    for chip in range(CHIPS):
        place = tab[32 + side * CHIPS + chip]
        target[place, pl.ds(first, 48), :] = part[48 * chip : 48 * chip + 48, lanes]


def up_grad_kernel(tab, two_ref, grad_up_ref, out_ref, part):
    j = pl.program_id(0)
    part[...] = dot_first(two_ref[...], grad_up_ref[...]).astype(BF16)
    for b in range(2):
        first = pl.multiple_of((2 * j + b) * 48, 48)
        store_blocks(tab, 0, out_ref, first, part, slice(b * LANES, (b + 1) * LANES))


def up_grad(tab, two, grad_up):
    return pl.pallas_call(
        up_grad_kernel,
        grid_spec=pltpu.PrefetchScalarGridSpec(
            num_scalar_prefetch=1,
            grid=(2,),
            in_specs=[
                pl.BlockSpec((1024, WIDTH), lambda j, tab: (0, 0)),
                pl.BlockSpec((1024, WIDTH), lambda j, tab: (0, half_of(tab, 0) * 2 + j)),
            ],
            out_specs=VMEM_SPEC,
            scratch_shapes=[pltpu.VMEM((WIDTH, WIDTH), BF16)],
        ),
        out_shape=shaped((CHIPS, 192, LANES)),
        compiler_params=params(),
        cost_estimate=cost(2_400_000_000, 8_000_000),
        name="up_grad",
    )(tab, two, grad_up)


def clamped(rows, cols):
    return pl.BlockSpec((rows, cols), lambda i: (jnp.minimum(i, 3), 0))


def mlp_backward_kernel(
    tab, g_ref, d_a, d_b, d_c, d_d, two_hbm, act_ref, slope_ref, out_grad_ref, mid_ref, vec_ref,
    result_ref, grad_mid_ref, branch_ref, grad_up_ref, grad_att_ref, gain_ref, theirs_ref,
    w, w_down, two, kept, part, sem, sem_down, sem_two,
):
    i = pl.program_id(0)

    @pl.when(i == 0)
    def _():
        fetch_pieces(tab, (d_a, d_b, d_c, d_d), 192, w_down, sem_down)
        gain_ref[...] = jnp.zeros_like(gain_ref)
        finish(w_down, sem_down)
        pltpu.make_async_copy(g_ref, w, sem).start()
        pltpu.make_async_copy(two_hbm, two, sem_two).start()

    @pl.when(i < 4)
    def _():
        total = mid_ref[...]
        for j in range(4):
            cols = slice(j * WIDTH, (j + 1) * WIDTH)
            total = total + dot(act_ref[:, cols], down_rows(w_down, j))
            grad_act = dot_last(out_grad_ref[...], down_rows(w_down, j))
            grad_up_ref[:, cols] = (grad_act * slope_ref[:, cols].astype(F32)).astype(BF16)
        result_ref[...] = total.astype(BF16)

        @pl.when(i == 0)
        def _():
            finish(w, sem)

        y = jnp.zeros_like(total)
        for j in range(4):
            cols = slice(j * WIDTH, (j + 1) * WIDTH)
            y = y + dot_last(grad_up_ref[:, cols], w[:, cols])
        theirs = pl.ds(pl.multiple_of(half_of(tab, 1) * 4 * LANES, 128), 4 * LANES)
        kept[rows_of(i, 256), :] = grad_up_ref[:, theirs]
        xhat, scale = ln_stats(mid_ref[...])
        grad = out_grad_ref[...].astype(F32) + ln_back(y, vec_ref[1:2, :], xhat, scale)
        grad_mid_ref[...] = grad
        branch_ref[...] = grad.astype(BF16)
        gain_ref[...] += jnp.sum(y * xhat, axis=0, keepdims=True)
        grad_att_ref[...] = dot_last(branch_ref[...], w[:, FF:]).astype(BF16)

    @pl.when(i == 4)
    def _():
        finish(two, sem_two)

    @pl.when(i >= 4)
    def _():
        cols = pl.ds(pl.multiple_of((i - 4) * WIDTH, WIDTH), WIDTH)
        part[...] = dot_first(two[...], kept[:, cols]).astype(BF16)
        for b in range(2):
            first = pl.multiple_of((2 * (i - 4) + b) * 48, 48)
            store_blocks(tab, 1, theirs_ref, first, part, slice(b * LANES, (b + 1) * LANES))


def mlp_backward(tab, gathered, pieces, two, act, slope, out_grad, mid, vectors):
    row = clamped(256, WIDTH)
    wide = clamped(256, FF)
    return pl.pallas_call(
        mlp_backward_kernel,
        grid=(6,),
        out_shape=(
            shaped((1024, WIDTH)),
            shaped((1024, WIDTH), F32),
            shaped((1024, WIDTH)),
            shaped((1024, FF)),
            shaped((1024, WIDTH)),
            shaped((1, WIDTH), F32),
            shaped((CHIPS, 192, LANES)),
        ),
        in_specs=[SMEM_SPEC] + [ANY_SPEC] * 6 + [wide, wide, row, row, fixed(16, WIDTH)],
        out_specs=(row, row, row, wide, row, fixed(1, WIDTH), VMEM_SPEC),
        scratch_shapes=[
            pltpu.VMEM((WIDTH, FF + WIDTH), BF16),
            pltpu.VMEM((CHIPS, 2, 192, LANES), BF16),
            pltpu.VMEM((1024, WIDTH), BF16),
            pltpu.VMEM((1024, 4 * LANES), BF16),
            pltpu.VMEM((WIDTH, WIDTH), BF16),
        ]
        + [pltpu.SemaphoreType.DMA] * 3,
        compiler_params=params(),
        cost_estimate=cost(18_000_000_000, 50_000_000),
        name="mlp_backward",
    )(tab, gathered, *pieces, two, act, slope, out_grad, mid, vectors)


def attention_backward_rows(k, qkv_ref, probs_ref, grad_att_ref, grad_qkv_ref):
    low_half = lax.broadcasted_iota(jnp.int32, (128, 128), 1) < HEAD_DIM
    rows = slice(128 * k, 128 * k + 128)

    def heads(ref, base):
        return two_heads(ref[rows, base : base + 128], low_half)

    def probs_of(pair):
        first = 256 * (6 * k + pair)
        return probs_ref[first : first + 256, :]

    grad_probs = []
    for pair in range(6):
        base = pair_base(pair) + 2 * LANES
        grad_probs.append(
            dot_last(heads(grad_att_ref, pair * 128), qkv_ref[rows, base : base + 128])
        )
    grad_scores = []
    for pair in range(6):
        probs = probs_of(pair).astype(F32)
        inner = jnp.sum(probs * grad_probs[pair], axis=-1, keepdims=True)
        grad_scores.append((probs * (grad_probs[pair] - inner)).astype(BF16))
    for pair in range(6):
        base = pair_base(pair)
        grad_query = dot(side_by_side(grad_scores[pair]), heads(qkv_ref, base + LANES))
        grad_key = dot_first(grad_scores[pair], heads(qkv_ref, base))
        grad_value = dot_first(probs_of(pair), heads(grad_att_ref, pair * 128))
        grad_query = (grad_query * HEAD_DIM ** (-0.5)).astype(BF16)
        grad_qkv_ref[rows, base : base + 128] = grad_query
        base = base + LANES
        grad_qkv_ref[rows, base : base + 128] = (grad_key * HEAD_DIM ** (-0.5)).astype(BF16)
        base = base + LANES
        grad_qkv_ref[rows, base : base + 128] = grad_value.astype(BF16)


def attention_grad_rows(tab, side, att, branch, normed, grad_qkv, out_ref, part, out_part):
    lanes = lanes_of(half_of(tab, side), LANES)
    out_part[...] = dot_first(att[...], branch[:, lanes]).astype(BF16)
    store_blocks(tab, side, out_ref, 144, out_part, slice(0, LANES))
    part[...] = dot_first(normed[...], grad_qkv[...]).astype(BF16)
    for sec in range(3):
        store_blocks(tab, side, out_ref, 48 * sec, part, slice(sec * LANES, (sec + 1) * LANES))


def attention_backward_kernel(
    tab, att_hbm, branch_hbm, normed_hbm, qkv_ref, probs_ref, grad_att_ref,
    grad_qkv_ref, theirs_ref,
    att, branch, normed, kept, part, out_part, sem_att, sem_branch, sem_normed,
):
    i = pl.program_id(0)
    fetched = (
        (att_hbm, att, sem_att), (branch_hbm, branch, sem_branch), (normed_hbm, normed, sem_normed)
    )

    @pl.when(i == 0)
    def _():
        for src, dst, sem in fetched:
            pltpu.make_async_copy(src, dst, sem).start()

    @pl.when(i < 4)
    def _():
        for k in range(2):
            attention_backward_rows(k, qkv_ref, probs_ref, grad_att_ref, grad_qkv_ref)
        theirs = pl.ds(pl.multiple_of(half_of(tab, 1) * 3 * LANES, 128), 3 * LANES)
        kept[rows_of(i, 256), :] = grad_qkv_ref[:, theirs]

    @pl.when(i == 4)
    def _():
        for _src, dst, sem in fetched:
            finish(dst, sem)
        attention_grad_rows(tab, 1, att, branch, normed, kept, theirs_ref, part, out_part)


def attention_backward(tab, att, branch, normed, qkv, probs, grad_att):
    wide = clamped(256, 3 * WIDTH)
    return pl.pallas_call(
        attention_backward_kernel,
        grid=(5,),
        out_shape=(shaped((1024, 3 * WIDTH)), shaped((CHIPS, 192, LANES))),
        in_specs=[SMEM_SPEC] + [ANY_SPEC] * 3 + [wide, clamped(12 * 256, 128), clamped(256, WIDTH)],
        out_specs=(wide, VMEM_SPEC),
        scratch_shapes=[pltpu.VMEM((1024, WIDTH), BF16)] * 3
        + [
            pltpu.VMEM((1024, 3 * LANES), BF16),
            pltpu.VMEM((WIDTH, 3 * LANES), BF16),
            pltpu.VMEM((WIDTH, LANES), BF16),
        ]
        + [pltpu.SemaphoreType.DMA] * 3,
        compiler_params=params(),
        cost_estimate=cost(11_000_000_000, 22_000_000),
        name="attention_backward",
    )(tab, att, branch, normed, qkv, probs, grad_att)


def attention_grad_kernel(
    tab, att_ref, branch_ref, normed_ref, grad_qkv_ref, out_ref, part, out_part
):
    attention_grad_rows(
        tab, 0, att_ref, branch_ref, normed_ref, grad_qkv_ref, out_ref, part, out_part
    )


def attention_grad(tab, att, branch, normed, grad_qkv):
    def whole(i, tab):
        return (0, 0)

    rows = pl.BlockSpec((1024, WIDTH), whole)
    chosen = pl.BlockSpec((1024, 3 * LANES), lambda i, tab: (0, half_of(tab, 0)))
    return pl.pallas_call(
        attention_grad_kernel,
        grid_spec=pltpu.PrefetchScalarGridSpec(
            num_scalar_prefetch=1,
            grid=(1,),
            in_specs=[rows, rows, rows, chosen],
            out_specs=VMEM_SPEC,
            scratch_shapes=[
                pltpu.VMEM((WIDTH, 3 * LANES), BF16),
                pltpu.VMEM((WIDTH, LANES), BF16),
            ],
        ),
        out_shape=shaped((CHIPS, 192, LANES)),
        compiler_params=params(),
        cost_estimate=cost(2_600_000_000, 10_000_000),
        name="attention_grad",
    )(tab, att, branch, normed, grad_qkv)


def input_backward_kernel(
    tab, g_a, g_b, g_c, g_d, grad_qkv_ref, x_ref, te_ref, vec_ref, grad_mid_ref, gain_two_ref,
    input_ref, small_ref,
    w, sem,
):
    i = pl.program_id(0)

    @pl.when(i == 0)
    def _():
        fetch_pieces(tab, (g_a, g_b, g_c, g_d), 144, w, sem)
        small_ref[8:9, :] = jnp.zeros((1, WIDTH), F32)
        small_ref[9:10, :] = gain_two_ref[...]
        small_ref[10:16, :] = jnp.zeros((6, WIDTH), F32)
        finish(w, sem)

    y = jnp.zeros((256, WIDTH), F32)
    for half in (0, 1):
        cols = slice(half * 3 * LANES, (half + 1) * 3 * LANES)
        y = y + dot_last(grad_qkv_ref[:, cols], qkv_columns(w, half))
    xhat, scale = ln_stats(add_embed(x_ref[...], te_ref, i))
    grad = grad_mid_ref[...] + ln_back(y, vec_ref[0:1, :], xhat, scale)
    input_ref[...] = grad.astype(BF16)
    for s in range(2):
        small_ref[pl.ds(i * 2 + s, 1), :] = jnp.sum(
            grad[128 * s : 128 * s + 128], axis=0, keepdims=True
        )
    small_ref[8:9, :] += jnp.sum(y * xhat, axis=0, keepdims=True)


def input_backward(tab, pieces, grad_qkv, rows, embed, vectors, grad_mid, gain_two):
    row = tiles(256, WIDTH)
    return pl.pallas_call(
        input_backward_kernel,
        grid=(4,),
        out_shape=(shaped((1024, WIDTH)), shaped((16, WIDTH), F32)),
        in_specs=[SMEM_SPEC]
        + [ANY_SPEC] * 4
        + [tiles(256, 3 * WIDTH), row, fixed(8, WIDTH), fixed(16, WIDTH), row, fixed(1, WIDTH)],
        out_specs=(row, fixed(16, WIDTH)),
        scratch_shapes=[pltpu.VMEM((CHIPS, 2, 144, LANES), BF16), pltpu.SemaphoreType.DMA],
        compiler_params=params(),
        cost_estimate=cost(4_000_000_000, 18_000_000),
        name="input_backward",
    )(tab, *pieces, grad_qkv, rows, embed, vectors, grad_mid, gain_two)


def pick(stacked, index):
    return lax.dynamic_index_in_dim(stacked, index, 0, keepdims=False)


def in_core_order(core, own, other, axis):
    return jnp.where(
        core == 0,
        jnp.concatenate([own, other], axis=axis),
        jnp.concatenate([other, own], axis=axis),
    )


def position_table(chip, core):
    index = jnp.arange(72, dtype=jnp.int32)
    order = jnp.bitwise_xor(core, (index // CHIPS) % 2)
    inner = index % CHIPS
    found = jnp.bitwise_xor(inner, chip)
    value = jnp.where(index < 32, inner, found)
    bits = [(value >> b) & 1 for b in range(4)]
    low = 2 * bits[0] + bits[1]
    straight = low + 4 * bits[2] + 8 * bits[3]
    crossed = low + 8 * bits[2] + 4 * bits[3]
    moved = jnp.where(order == 0, crossed, straight)
    moved = jnp.where(index < 32, jnp.bitwise_xor(moved, chip), moved)
    return jnp.where(index < 64, moved, core)


def swap_halves(halves, core):
    return pick(halves, core), core_swap(pick(halves, 1 - core))


def join_rows(own, other, core, blocks):
    shape = (blocks, own.shape[0] // blocks, LANES)
    return in_core_order(core, own.reshape(shape), other.reshape(shape), 1).reshape(-1, LANES)


def split_rows(piece):
    return piece.reshape(4, 2, 24, LANES).transpose(1, 0, 2, 3).reshape(2, 96, LANES)


def pack_extra(time_in, vectors, ints):
    rows = time_in.shape[0]
    filler = jnp.zeros((rows, 128), BF16)
    vec = lax.dynamic_update_slice(filler, vectors, (0, 0))
    num = lax.dynamic_update_slice(filler, ints[None, :], (0, 0))
    return jnp.concatenate([time_in, vec, num], axis=1)


def split_time(timestep, dataset):
    steps = timestep.reshape(-1)
    return jnp.concatenate([steps // 64, steps % 64, dataset.reshape(-1)]).astype(BF16)


def gather_all(x):
    return lax.all_gather(x, AXES, axis=0, tiled=True)


def shards(
    block_input,
    out_grad,
    timestep,
    dataset,
    lengths,
    norm1_gain,
    qkv_weight,
    out_weight,
    norm2_gain,
    up_weight,
    down_weight,
    time_in,
    time_out,
    data_embed,
    devices,
):
    flat = lax.axis_index(AXES)
    gathered = gather_all(jnp.concatenate([up_weight, out_weight], axis=1))
    exchange = devices == 2 * CHIPS
    vectors = jnp.concatenate([norm1_gain[None], norm2_gain[None], data_embed.T], axis=0)
    numbers = split_time(timestep, dataset)
    count = numbers.shape[0] // 3
    if exchange:
        core = flat & 1
        chip = flat >> 1
        tab = position_table(chip, core)
        wide = qkv_weight.reshape(24, 3, 2, LANES).transpose(2, 1, 0, 3).reshape(2, 72, LANES)
        time_halves = time_out.reshape(16, 2, LANES).transpose(1, 0, 2)
        own, other = swap_halves(jnp.concatenate([wide, time_halves], axis=1), core)
        attention_piece = jnp.concatenate(
            [
                join_rows(own[:72], other[:72], core, 3),
                join_rows(own[72:], other[72:], core, 1),
                pack_extra(time_in, vectors, numbers),
            ],
            axis=0,
        )[None]
        own, other = swap_halves(down_weight.reshape(96, 2, LANES).transpose(1, 0, 2), core)
        down_piece = join_rows(own, other, core, 1)[None]
        held = gather_plane(gather_line(attention_piece))
        far = chip_swap(held, 8)
        attention_pieces = (held, far, core_swap(held), core_swap(far))
        down_near = [chip_swap(after(down_piece, far), p) for p in (1, 2, 3)]
        seen = jnp.concatenate([g[:, 176, 256 : 256 + 3 * count] for g in attention_pieces], axis=0)
    else:
        tab = jnp.concatenate(
            [jnp.tile(jnp.arange(CHIPS, dtype=jnp.int32), 4), jnp.zeros((8,), jnp.int32)]
        )
        full_qkv = gather_all(qkv_weight).reshape(CHIPS, 48, 3, 2, LANES)
        full_down = gather_all(down_weight).reshape(CHIPS, 192, 2, LANES)
        full_tin = gather_all(time_in).reshape(CHIPS, 2, 16, 128)
        full_tout = gather_all(time_out).reshape(CHIPS, 32, 2, LANES)
        full_vec = lax.all_gather(vectors, AXES, axis=1, tiled=True).reshape(4, CHIPS, 2, 24)
        seen = gather_all(numbers[None])
        extra = jnp.zeros((CHIPS, 2, 16, LANES), BF16)
        extra = extra.at[:, :, :, :128].set(full_tin)
        extra = extra.at[:, :, 0:4, 128:152].set(full_vec.transpose(1, 2, 0, 3))
        attention_pieces = []
        down_pieces = []
        for half in (0, 1):
            wide = full_qkv[:, :, :, half].transpose(0, 2, 1, 3).reshape(CHIPS, 144, LANES)
            whole = jnp.concatenate([wide, full_tout[:, :, half], extra[:, half]], axis=1)
            attention_pieces += [whole[:8], whole[8:]]
            down_pieces += [full_down[:8, :, half], full_down[8:, :, half]]

    micros, seqs, seq_len, width = block_input.shape
    tokens = micros * seqs * seq_len
    x_rows = block_input.reshape(tokens, width)
    grad_rows = out_grad.reshape(tokens, width)
    features = sinusoid(timestep.reshape(-1), time_in.shape[1] // 2).astype(BF16)
    sets = dataset.reshape(-1, 1).astype(F32)
    normed, qkv, embed, vecs = qkv_forward(tab, attention_pieces, x_rows, features, sets)
    if exchange:
        down_line = jnp.concatenate([down_piece] + [after(x, embed) for x in down_near], axis=0)
        qkv = after(qkv, down_line)
        down_plane = chip_swap(down_line, 4)
    probs, att = attention(lengths.reshape(-1), qkv)
    if exchange:
        down_held = jnp.concatenate([down_line, after(down_plane, att)], axis=0)
        att = after(att, down_held)
        down_far = chip_swap(down_held, 8)
    mid, two, act, slope = up_forward(gathered, att, x_rows, embed, vecs)
    if exchange:
        down_far = after(down_far, two)
        act = after(act, down_far)
        down_pieces = (down_held, down_far, core_swap(down_held), core_swap(down_far))
    down_sum = down_grad(act, grad_rows)
    grad_down = lax.psum_scatter(down_sum, AXES, scatter_dimension=0, tiled=True)
    slope = after(slope, down_sum)

    def backward(slope):
        result, grad_mid, branch, grad_up, grad_att, gain_two, up_theirs = mlp_backward(
            tab, gathered, down_pieces, two, act, slope, grad_rows, mid, vecs
        )
        up_mine = up_grad(tab, two, grad_up)
        if exchange:
            up_sum = Scatter(up_theirs)
            up_sum.parts.append(up_mine)
            grad_att = after(grad_att, *up_sum.send())
        grad_qkv, att_theirs = attention_backward(tab, att, branch, normed, qkv, probs, grad_att)
        if exchange:
            att_sum = Scatter(att_theirs)
            grad_qkv = after(grad_qkv, *up_sum.step(att_theirs))
        att_mine = attention_grad(tab, att, branch, normed, grad_qkv)
        if exchange:
            att_sum.parts.append(att_mine)
            grad_qkv = after(grad_qkv, *att_sum.send(), *up_sum.step(att_mine))
        grad_input, small = input_backward(
            tab, attention_pieces, grad_qkv, x_rows, embed, vecs, grad_mid, gain_two
        )

        small = small.astype(BF16)[None]
        if exchange:
            small_line = gather_line(after(small, *att_sum.step(small)))
            small_line = after(small_line, *att_sum.step(small_line))
            held = gather_plane(small_line)
            far = chip_swap(held, 8)
            every = jnp.concatenate([held, far, core_swap(held), core_swap(far)], axis=0)
        else:
            every = gather_all(small)
        every = every.reshape(devices * 16, width)
        steps = seen[:, :count] * 64 + seen[:, count : 2 * count].astype(F32)
        wave = sinusoid(steps.reshape(-1), time_in.shape[1] // 2).astype(BF16)
        wave = jnp.pad(wave.reshape(devices, count, -1), ((0, 0), (0, 16 - count), (0, 0)))
        wave = wave.reshape(devices * 16, -1)
        which = jnp.pad(seen[:, 2 * count :], ((0, 0), (0, 16 - count))).reshape(-1)
        place = jnp.tile(jnp.arange(16), devices)
        hot = jnp.stack(
            [(place < count) & (which == 0), (place < count) & (which == 1), place == 8, place == 9]
        ).astype(BF16)
        pre = dot_last(wave, time_in)
        gate = 1.0 / (1.0 + jnp.exp(-pre))
        hidden = (pre * gate).astype(BF16)
        grad_tout = dot_first(hidden, every)
        grad_pre = dot_last(every, time_out) * (gate * (1.0 + pre * (1.0 - gate)))
        grad_tin = dot_first(grad_pre.astype(BF16), wave)
        sums = dot(hot, every)
        own_cols = norm1_gain.shape[0]
        sums = lax.dynamic_slice_in_dim(sums, flat * own_cols, own_cols, 1)

        if exchange:
            piece = up_sum.total()
            own, other = swap_halves(split_rows(piece), core)
            both = in_core_order(core, own.reshape(4, 24, LANES), other.reshape(4, 24, LANES), 0)
            grad_up_weight = both.transpose(1, 0, 2).reshape(24, FF)
            piece = att_sum.total()
            own, other = swap_halves(split_rows(piece), core)
            both = in_core_order(core, own.reshape(4, 1, 24, LANES), other.reshape(4, 1, 24, LANES), 1)
            both = both.transpose(2, 0, 1, 3).reshape(24, 4 * WIDTH)
        else:
            scatter = partial(lax.psum_scatter, axis_name=AXES, scatter_dimension=0, tiled=True)
            both = jnp.stack([up_mine, up_theirs]).astype(F32).reshape(2, CHIPS, 4, 48, LANES)
            grad_up_weight = scatter(both.transpose(1, 3, 0, 2, 4).reshape(WIDTH, FF))
            both = jnp.stack([att_mine, att_theirs]).astype(F32).reshape(2, CHIPS, 4, 48, LANES)
            both = scatter(both.transpose(1, 3, 2, 0, 4).reshape(WIDTH, 4 * WIDTH))
        return (
            result.reshape(block_input.shape),
            grad_input.reshape(block_input.shape),
            sums[2],
            both[:, : 3 * WIDTH],
            both[:, 3 * WIDTH :],
            sums[3],
            grad_up_weight,
            grad_tin,
            grad_tout,
            sums[:2].T,
        )

    shapes = jax.eval_shape(backward, slope)
    done = lax.cond(
        flat < devices,
        backward,
        lambda _: jax.tree.map(lambda x: jnp.zeros(x.shape, x.dtype), shapes),
        slope,
    )
    return done[:7] + (grad_down.astype(F32),) + done[7:]


def solution(mesh):
    devices = mesh.shape["dp"] * mesh.shape["fsdp"]
    seq_spec = P(None, AXES, None, None)
    int_spec = P(None, AXES)
    row_spec = P(AXES, None)
    in_specs = (seq_spec, seq_spec, int_spec, int_spec, int_spec, P(AXES), row_spec, row_spec, P(AXES))
    in_specs = in_specs + (row_spec,) * 5
    out_specs = (seq_spec, seq_spec, P(AXES), row_spec, row_spec, P(AXES)) + (row_spec,) * 5
    return jax.shard_map(
        partial(shards, devices=devices),
        mesh=mesh,
        in_specs=in_specs,
        out_specs=out_specs,
        check_vma=False,
    )
```

time: 1130 us -> 298 us (0.26)
  waiting for transfers between devices: 669 us -> 82.7 us
  blocking collectives: 202 us -> 0 us
  matrix products: 148 us -> 2.85 us
  Pallas kernels: 0 us -> 121 us
  starting transfers between devices: 0.61 us -> 37.5 us
  local copies, waits for them, and re-layouts: 47.6 us -> 17.6 us
  other arithmetic: 36.1 us -> 20.8 us
    reduce_scatter x6 -> x1, waiting for transfers between devices: 638 us -> 0.01 us  [shards(): lax.psum_scatter(down_sum, AXES, scatter_dimension=0, tiled=True)]
    dot_general x50 -> x4, matrix products: 148 us -> 2.85 us  [the longest x2 1.87 us: dot_first(): lax.dot_general(left, right, (((0,), (0,)), ((), ())), preferred_element_...]
    pallas_call x0 -> x9, Pallas kernels: none -> 121 us  [the longest x1 34 us: mlp_backward(): pl.pallas_call(mlp_backward_kernel, grid=(6,), out_shape=(shaped((1024, W...]
    all_gather x3 -> x0, blocking collectives: 120 us -> none  [the longest x1 44.9 us: shards(): lax.all_gather(time_out, ('dp', 'fsdp'), axis=0, tiled=True)]
    ppermute x0 -> x37, waiting for transfers between devices: none -> 82.6 us  [the longest x25 79 us: chip_swap(): lax.ppermute(x, AXES, [(i, i ^ ORDER[i & 1][position] * 2) for i in range...]
    unnamed x2 -> x0, blocking collectives: 82.2 us -> none
    ppermute x0 -> x37, starting transfers between devices: none -> 37.5 us  [the longest x25 35 us: chip_swap(): lax.ppermute(x, AXES, [(i, i ^ ORDER[i & 1][position] * 2) for i in range...]
    all_gather x4 -> x1, waiting for transfers between devices: 28.2 us -> 0.01 us  [gather_all(): return lax.all_gather(x, AXES, axis=0, tiled=True)]
  transfers between devices with their start and end apart: 10 -> 39, of which waited for: 7 -> 17; matrix products, arithmetic and copies ran while one was open for 11% -> 13% of each run, Pallas kernels for 0% -> 38%
where the time goes in v2:
time: 298 us; the launch traced here: 297 us
  Pallas kernels  121 us (41%)
  waiting for transfers between devices  82.7 us (28%)
  starting transfers between devices  37.5 us (13%)
  other arithmetic  20.8 us (7%)
  local copies, waits for them, and re-layouts  17.6 us (6%)
  between operations  14.4 us (5%)
    ppermute x25, waiting for transfers between devices, chip_swap(): lax.ppermute(x, AXES, [(i, i ^ ORDER[i & 1][position] * 2) for i in range...  79 us
    ppermute x25, starting transfers between devices, chip_swap(): lax.ppermute(x, AXES, [(i, i ^ ORDER[i & 1][position] * 2) for i in range...  35 us
    pallas_call x1, Pallas kernels, mlp_backward(): pl.pallas_call(mlp_backward_kernel, grid=(6,), out_shape=(shaped((1024, W...  34 us
    pallas_call x1, Pallas kernels, up_forward(): pl.pallas_call(up_kernel, grid=(4,), out_shape=(shaped((1024, WIDTH), F32...  16.5 us
    pallas_call x1, Pallas kernels, attention_backward(): pl.pallas_call(attention_backward_kernel, grid=(5,), out_shape=(shaped((1...  14.7 us
    pallas_call x1, Pallas kernels, qkv_forward(): pl.pallas_call(qkv_kernel, grid=(4,), out_shape=(shaped((1024, WIDTH)), s...  13.5 us
    convert_element_type x6, other arithmetic, send(): self.sum(p, p + size).astype(BF16)  11 us
    pallas_call x1, Pallas kernels, input_backward(): pl.pallas_call(input_backward_kernel, grid=(4,), out_shape=(shaped((1024,...  10.8 us
  transfers between devices with their start and end apart: 39, of which 17 were waited for; matrix products, arithmetic and copies ran while one was open for 13% of the time, Pallas kernels for 38%

profile of v2, /device:TPU:0, one launch (start us, length us, event | category | flops | bytes accessed | tf_op | source)
XLA Modules:
  0.0 297.0 jit_solution(9231734258927484056)
XLA Ops:
  12.3 5.0 %collective-permute-start.25 = (bf16[1,192,384]{2,1,0:T(8,128)(2,1)S(1)}, bf16[1,192,384]{2,1,0:T(8,128)(2,1)S(1)}, u32[]{:S(2)}, u32[]{:S(2)}) collective-permute-start(bf16[1,192,384]{2,1,0:T(8,128)(2,1)S(1)} %maximum_bitcast_fusion), channel_id=1, source_target_pairs={{0,6},{1,7},{2,4},{3,5},{4,2},{5,3},{6,0},{7,1},{8,14},{9,15},{10,... | collective-permute-start | bytes 442376 | tf_op jit(solution)/shard_map/ppermute | solution.py:55
  17.9 4.0 %collective-permute-done.25 = bf16[1,192,384]{2,1,0:T(8,128)(2,1)S(1)} collective-permute-done((bf16[1,192,384]{2,1,0:T(8,128)(2,1)S(1)}, bf16[1,192,384]{2,1,0:T(8,128)(2,1)S(1)}, u32[]{:S(2)}, u32[]{:S(2)}) %collective-permute-start.25) | collective-permute-done | bytes 147488 | tf_op jit(solution)/shard_map/ppermute | solution.py:55
  22.0 3.7 %collective-permute-done.24 = bf16[1,192,384]{2,1,0:T(8,128)(2,1)S(1)} collective-permute-done((bf16[1,192,384]{2,1,0:T(8,128)(2,1)S(1)}, bf16[1,192,384]{2,1,0:T(8,128)(2,1)S(1)}, u32[]{:S(2)}, u32[]{:S(2)}) %collective-permute-start.24) | collective-permute-done | bytes 147488 | tf_op jit(solution)/shard_map/ppermute | solution.py:55
  25.7 6.9 %collective-permute-done.23 = bf16[1,192,384]{2,1,0:T(8,128)(2,1)S(1)} collective-permute-done((bf16[1,192,384]{2,1,0:T(8,128)(2,1)S(1)}, bf16[1,192,384]{2,1,0:T(8,128)(2,1)S(1)}, u32[]{:S(2)}, u32[]{:S(2)}) %collective-permute-start.23) | collective-permute-done | bytes 147488 | tf_op jit(solution)/shard_map/ppermute | solution.py:55
  34.4 8.2 %collective-permute-done.26 = bf16[4,192,384]{2,1,0:T(8,128)(2,1)S(1)} collective-permute-done((bf16[4,192,384]{2,1,0:T(8,128)(2,1)S(1)}, bf16[4,192,384]{2,1,0:T(8,128)(2,1)S(1)}, u32[]{:S(2)}, u32[]{:S(2)}) %collective-permute-start.26) | collective-permute-done | bytes 589856 | tf_op jit(solution)/shard_map/ppermute | solution.py:55
  44.3 19.1 %collective-permute-done.27.g_b = bf16[8,192,384]{2,1,0:T(8,128)(2,1)S(1)} collective-permute-done((bf16[8,192,384]{2,1,0:T(8,128)(2,1)S(1)}, bf16[8,192,384]{2,1,0:T(8,128)(2,1)S(1)}, u32[]{:S(2)}, u32[]{:S(2)}) %collective-permute-start.27) | collective-permute-done | bytes 1179680 | tf_op jit(solution)/shard_map/ppermute | solution.py:55
  67.1 3.3 %collective-permute-start.32 = (bf16[1,192,384]{2,1,0:T(8,128)(2,1)S(1)}, bf16[1,192,384]{2,1,0:T(8,128)(2,1)S(1)}, u32[]{:S(2)}, u32[]{:S(2)}) collective-permute-start(bf16[1,192,384]{2,1,0:T(8,128)(2,1)S(1)} %get-tuple-element.142), channel_id=1, source_target_pairs={{0,6},{1,7},{2,4},{3,5},{4,2},{5,3},{6,0},{7,1},{8,14},{9,15},{10,... | collective-permute-start | bytes 442376 | tf_op jit(solution)/shard_map/ppermute | solution.py:55
  71.5 13.5 %qkv_forward.1 = (bf16[1024,768]{1,0:T(8,128)(2,1)}, bf16[1024,2304]{1,0:T(8,128)(2,1)}, f32[8,768]{1,0:T(8,128)S(1)}, f32[16,768]{1,0:T(8,128)S(1)}) custom-call(s32[72]{0:T(128)S(1)} %compare_select_fusion.3.tab, bf16[8,192,384]{2,1,0:T(8,128)(2,1)S(1)} %constant_dynamic-update-slice_fusion.11.g_a, bf16[8,192,384]{2,1,0:T(8,128)(2,1)S(1)} %collective-permute-done.27.g_b, ...), custom_call_target="tpu_custom_call" | custom-call | flops 4000000000 | bytes 12000000 | tf_op jit(solution)/shard_map/qkv_forward/pallas_call | solution.py:254
  85.5 10.4 %collective-permute-done.28 = bf16[1,192,384]{2,1,0:T(8,128)(2,1)S(1)} collective-permute-done((bf16[1,192,384]{2,1,0:T(8,128)(2,1)S(1)}, bf16[1,192,384]{2,1,0:T(8,128)(2,1)S(1)}, u32[]{:S(2)}, u32[]{:S(2)}) %collective-permute-start.28) | collective-permute-done | bytes 147488 | tf_op jit(solution)/shard_map/ppermute | solution.py:55
  99.5 7.9 %attention.1 = (bf16[12288,128]{1,0:T(8,128)(2,1)}, bf16[1024,768]{1,0:T(8,128)(2,1)S(1)}) custom-call(s32[8]{0:T(128)} %reshape.379.lens, bf16[1024,2304]{1,0:T(8,128)(2,1)} %get-tuple-element.148.qkv_ref), custom_call_target="tpu_custom_call" | custom-call | flops 4000000000 | bytes 9000000 | tf_op jit(solution)/shard_map/attention/pallas_call | solution.py:313
  109.8 16.5 %up_forward.1 = (f32[1024,768]{1,0:T(8,128)}, bf16[1024,768]{1,0:T(8,128)(2,1)S(1)}, bf16[1024,3072]{1,0:T(8,128)(2,1)}, bf16[1024,3072]{1,0:T(8,128)(2,1)}) custom-call(bf16[768,3840]{1,0:T(8,128)(2,1)} %all-gather.2.cloned.1.call-done.g_ref, bf16[1024,768]{1,0:T(8,128)(2,1)S(1)} %get-tuple-element.151.att_ref, bf16[1024,768]{1,0:T(8,128)(2,1)} %bitcast.114, ...), custom_call_target="tpu_custom_call" | custom-call | flops 8000000000 | bytes 26000000 | tf_op jit(solution)/shard_map/up_forward/pallas_call | solution.py:355
  126.3 8.7 %down_grad.1 = bf16[3072,768]{1,0:T(8,128)(2,1)} custom-call(bf16[1024,3072]{1,0:T(8,128)(2,1)} %get-tuple-element.156.act_ref, bf16[1024,768]{1,0:T(8,128)(2,1)S(1)} %bitcast.117), custom_call_target="tpu_custom_call" | custom-call | flops 5000000000 | bytes 13000000 | tf_op jit(solution)/shard_map/down_grad/pallas_call | solution.py:382
  140.2 148.3 %conditional.1 = (bf16[2,4,128,768]{3,2,1,0:T(8,128)(2,1)}, bf16[2,4,128,768]{3,2,1,0:T(8,128)(2,1)}, f32[24]{0:T(128)}, f32[24,2304]{1,0:T(8,128)}, f32[24,768]...) conditional(s32[]{:T(128)} %convert_element_type.223, () %tuple.35, ...), branch_computations={%region_0.1_spmd, %region_1.2_spmd} | conditional | flops 38047309824 | bytes 221182928 | solution.py:918
  140.2 34.0 %mlp_backward.1 = (bf16[1024,768]{1,0:T(8,128)(2,1)}, f32[1024,768]{1,0:T(8,128)}, bf16[1024,768]{1,0:T(8,128)(2,1)}, bf16[1024,3072]{1,0:T(8,128)(2,1)}, bf16[1...) custom-call(s32[72]{0:T(128)S(1)} %get-tuple-element.54.tab, ...), custom_call_target="tpu_custom_call" | custom-call | flops 17999998976 | bytes 50000000 | tf_op jit(solution)/shard_map/cond/branch_1_fun/mlp_backward/pallas_call | solution.py:490
  174.5 6.5 %up_grad.1 = bf16[16,192,384]{2,1,0:T(8,128)(2,1)} custom-call(s32[72]{0:T(128)S(1)} %get-tuple-element.54.tab, bf16[1024,768]{1,0:T(8,128)(2,1)S(1)} %get-tuple-element.60.two_hbm.two_ref, bf16[1024,3072]{1,0:T(8,128)(2,1)} %get-tuple-element.78.grad_up_ref), custom_call_target="tpu_custom_call" | custom-call | flops 2400000000 | bytes 8000000 | tf_op jit(solution)/shard_map/cond/branch_1_fun/up_grad/pallas_call | solution.py:409
  181.0 2.4 add_convert_fusion.1
  183.5 14.7 %attention_backward.1 = (bf16[1024,2304]{1,0:T(8,128)(2,1)}, bf16[16,192,384]{2,1,0:T(8,128)(2,1)}) custom-call(s32[72]{0:T(128)S(1)} %get-tuple-element.54.tab, bf16[1024,768]{1,0:T(8,128)(2,1)} %copy-done.4, bf16[1024,768]{1,0:T(8,128)(2,1)} %get-tuple-element.72.branch_hbm.branch_ref, bf16[1024,768]{1,0:T(8,128)(2,1)} %get-tuple-element.73.normed_hbm.normed_ref, ...), custom_call_target="tpu_custom_call" | custom-call | flops 11000000512 | bytes 22000000 | tf_op jit(solution)/shard_map/cond/branch_1_fun/attention_backward/pallas_call | solution.py:593
  203.5 13.6 %collective-permute-done.1 = bf16[8,192,384]{2,1,0:T(8,128)(2,1)} collective-permute-done((bf16[8,192,384]{2,1,0:T(8,128)(2,1)S(1)}, bf16[8,192,384]{2,1,0:T(8,128)(2,1)}, u32[]{:S(2)}, u32[]{:S(2)}) %collective-permute-start.1) | collective-permute-done | bytes 1179680 | tf_op jit(solution)/shard_map/cond/branch_1_fun/ppermute | solution.py:55
  218.7 8.0 %attention_grad.1 = bf16[16,192,384]{2,1,0:T(8,128)(2,1)} custom-call(s32[72]{0:T(128)S(1)} %copy-done.17, bf16[1024,768]{1,0:T(8,128)(2,1)} %copy-done.4, bf16[1024,768]{1,0:T(8,128)(2,1)} %get-tuple-element.72.branch_hbm.branch_ref, bf16[1024,768]{1,0:T(8,128)(2,1)S(1)} %copy-done.3, bf16[1024,2304]{1,0:T(8,128)(2,1)} %get-tuple-element.85.grad_qkv_ref), custom_call_target="tpu_custom_call" | custom-call | flops 2600000000 | bytes 10000000 | tf_op jit(solution)/shard_map/cond/branch_1_fun/attention_grad/pallas_call | solution.py:626
  233.9 3.7 %collective-permute-start.17 = (bf16[1,192,384]{2,1,0:T(8,128)(2,1)S(1)}, bf16[1,192,384]{2,1,0:T(8,128)(2,1)}, u32[]{:S(2)}, u32[]{:S(2)}) collective-permute-start(bf16[1,192,384]{2,1,0:T(8,128)(2,1)S(1)} %get-tuple-element.260), channel_id=1, source_target_pairs={{0,4},{1,5},{2,6},{3,7},{4,0},{5,1},{6,2},{7,3},{8,12},{9,13},{10,... | collective-permute-start | bytes 442376 | tf_op jit(solution)/shard_map/cond/branch_1_fun/ppermute | solution.py:55
  237.6 10.8 %input_backward.1 = (bf16[1024,768]{1,0:T(8,128)(2,1)}, f32[16,768]{1,0:T(8,128)}) custom-call(s32[72]{0:T(128)S(1)} %copy-done.17, bf16[8,192,384]{2,1,0:T(8,128)(2,1)} %get-tuple-element.67.g_a, bf16[8,192,384]{2,1,0:T(8,128)(2,1)} %get-tuple-element.68.g_b, bf16[8,192,384]{2,1,0:T(8,128)(2,1)} %get-tuple-element.69.g_c, ...), custom_call_target="tpu_custom_call" | custom-call | flops 4000000000 | bytes 18000000 | tf_op jit(solution)/shard_map/cond/branch_1_fun/input_backward/pallas_call | solution.py:676
  255.0 3.0 %collective-permute-start.5 = (bf16[1,16,768]{2,1,0:T(8,128)(2,1)S(1)}, bf16[1,16,768]{2,1,0:T(8,128)(2,1)S(1)}, u32[]{:S(2)}, u32[]{:S(2)}) collective-permute-start(bf16[1,16,768]{2,1,0:T(8,128)(2,1)S(1)} %convert_bitcast_fusion), channel_id=1, source_target_pairs={{0,4},{1,5},{2,6},{3,7},{4,0},{5,1},{6,2},{7,3},{8,12},{9,13},{10,... | collective-permute-start | bytes 73736 | tf_op jit(solution)/shard_map/cond/branch_1_fun/ppermute | solution.py:55
  268.1 2.7 collective-permute-done.15
  272.0 4.7 %collective-permute-done.13 = bf16[1,192,384]{2,1,0:T(8,128)(2,1)S(1)} collective-permute-done((bf16[1,192,384]{2,1,0:T(8,128)(2,1)S(1)}, bf16[1,192,384]{2,1,0:T(8,128)(2,1)S(1)}, u32[]{:S(2)}, u32[]{:S(2)}) %collective-permute-start.13) | collective-permute-done | bytes 147488 | tf_op jit(solution)/shard_map/cond/branch_1_fun/ppermute | solution.py:55
  (220 shorter events, 70.8 us)
Async XLA Ops:
  7.2 102.6 %all-gather.2.cloned.1.call-start = ((), (), s32[]{:S(2)}) async-start(), calls=%async_computation.1 | async-start | bytes 6082560 | tf_op jit(solution)/shard_map/all_gather | solution.py:745
  8.9 279.6 %reduce-scatter.2.cloned.1.call-start = ((), (), s32[]{:S(2)}) async-start(), calls=%async_computation.2 | async-start | bytes 4866048 | tf_op jit(solution)/shard_map/reduce_scatter | solution.py:836
  12.3 9.7 %collective-permute-start.25 = (bf16[1,192,384]{2,1,0:T(8,128)(2,1)S(1)}, bf16[1,192,384]{2,1,0:T(8,128)(2,1)S(1)}, u32[]{:S(2)}, u32[]{:S(2)}) collective-permute-start(bf16[1,192,384]{2,1,0:T(8,128)(2,1)S(1)} %maximum_bitcast_fusion), channel_id=1, source_target_pairs={{0,6},{1,7},{2,4},{3,5},{4,2},{5,3},{6,0},{7,1},{8,14},{9,15},{10,... | collective-permute-start | bytes 442376 | tf_op jit(solution)/shard_map/ppermute | solution.py:55
  17.3 15.3 %collective-permute-start.23 = (bf16[1,192,384]{2,1,0:T(8,128)(2,1)S(1)}, bf16[1,192,384]{2,1,0:T(8,128)(2,1)S(1)}, u32[]{:S(2)}, u32[]{:S(2)}) collective-permute-start(bf16[1,192,384]{2,1,0:T(8,128)(2,1)S(1)} %maximum_bitcast_fusion), channel_id=1, source_target_pairs={{0,4},{1,5},{2,6},{3,7},{4,0},{5,1},{6,2},{7,3},{8,12},{9,13},{10,... | collective-permute-start | bytes 442376 | tf_op jit(solution)/shard_map/ppermute | solution.py:55
  32.7 9.9 %collective-permute-start.26 = (bf16[4,192,384]{2,1,0:T(8,128)(2,1)S(1)}, bf16[4,192,384]{2,1,0:T(8,128)(2,1)S(1)}, u32[]{:S(2)}, u32[]{:S(2)}) collective-permute-start(bf16[4,192,384]{2,1,0:T(8,128)(2,1)S(1)} %pad_maximum_fusion), channel_id=1, source_target_pairs={{0,16},{1,9},{2,18},{3,11},{4,20},{5,13},{6,22},{7,15},{8,24},{9,1... | collective-permute-start | bytes 1769480 | tf_op jit(solution)/shard_map/ppermute | solution.py:55
  42.8 20.6 %collective-permute-start.27 = (bf16[8,192,384]{2,1,0:T(8,128)(2,1)S(1)}, bf16[8,192,384]{2,1,0:T(8,128)(2,1)S(1)}, u32[]{:S(2)}, u32[]{:S(2)}) collective-permute-start(bf16[8,192,384]{2,1,0:T(8,128)(2,1)S(1)} %constant_dynamic-update-slice_fusion.11.g_a), channel_id=1, source_target_pairs={{0,8},{1,17},{2,10},{3,19},{4,12},{5,21},{6,14},{7,23},{8,0},{9,25... | collective-permute-start | bytes 3538952 | tf_op jit(solution)/shard_map/ppermute | solution.py:55
  44.3 27.2 %collective-permute-start.29 = (bf16[8,192,384]{2,1,0:T(8,128)(2,1)S(1)}, bf16[8,192,384]{2,1,0:T(8,128)(2,1)}, u32[]{:S(2)}, u32[]{:S(2)}) collective-permute-start(bf16[8,192,384]{2,1,0:T(8,128)(2,1)S(1)} %constant_dynamic-update-slice_fusion.11.g_a), channel_id=1, source_target_pairs={{0,1},{1,0},{2,3},{3,2},{4,5},{5,4},{6,7},{7,6},{8,9},{9,8},{10,11... | collective-permute-start | bytes 3538952 | tf_op jit(solution)/shard_map/ppermute | solution.py:51
  67.1 17.9 %collective-permute-start.32 = (bf16[1,192,384]{2,1,0:T(8,128)(2,1)S(1)}, bf16[1,192,384]{2,1,0:T(8,128)(2,1)S(1)}, u32[]{:S(2)}, u32[]{:S(2)}) collective-permute-start(bf16[1,192,384]{2,1,0:T(8,128)(2,1)S(1)} %get-tuple-element.142), channel_id=1, source_target_pairs={{0,6},{1,7},{2,4},{3,5},{4,2},{5,3},{6,0},{7,1},{8,14},{9,15},{10,... | collective-permute-start | bytes 442376 | tf_op jit(solution)/shard_map/ppermute | solution.py:55
  70.5 15.0 %collective-permute-start.31 = (bf16[1,192,384]{2,1,0:T(8,128)(2,1)S(1)}, bf16[1,192,384]{2,1,0:T(8,128)(2,1)S(1)}, u32[]{:S(2)}, u32[]{:S(2)}) collective-permute-start(bf16[1,192,384]{2,1,0:T(8,128)(2,1)S(1)} %get-tuple-element.142), channel_id=1, source_target_pairs={{0,2},{1,3},{2,0},{3,1},{4,6},{5,7},{6,4},{7,5},{8,10},{9,11},{10,... | collective-permute-start | bytes 442376 | tf_op jit(solution)/shard_map/ppermute | solution.py:55
  70.5 25.4 %collective-permute-start.28 = (bf16[1,192,384]{2,1,0:T(8,128)(2,1)S(1)}, bf16[1,192,384]{2,1,0:T(8,128)(2,1)S(1)}, u32[]{:S(2)}, u32[]{:S(2)}) collective-permute-start(bf16[1,192,384]{2,1,0:T(8,128)(2,1)S(1)} %get-tuple-element.142), channel_id=1, source_target_pairs={{0,4},{1,5},{2,6},{3,7},{4,0},{5,1},{6,2},{7,3},{8,12},{9,13},{10,... | collective-permute-start | bytes 442376 | tf_op jit(solution)/shard_map/ppermute | solution.py:55
  96.0 11.4 %collective-permute-start.33 = (bf16[4,192,384]{2,1,0:T(8,128)(2,1)S(1)}, bf16[4,192,384]{2,1,0:T(8,128)(2,1)S(1)}, u32[]{:S(2)}, u32[]{:S(2)}) collective-permute-start(bf16[4,192,384]{2,1,0:T(8,128)(2,1)S(1)} %pad_maximum_fusion.1), channel_id=1, source_target_pairs={{0,16},{1,9},{2,18},{3,11},{4,20},{5,13},{6,22},{7,15},{8,24},{9,1... | collective-permute-start | bytes 1769480 | tf_op jit(solution)/shard_map/ppermute | solution.py:55
  108.3 17.9 %collective-permute-start.34 = (bf16[8,192,384]{2,1,0:T(8,128)(2,1)}, bf16[8,192,384]{2,1,0:T(8,128)(2,1)}, u32[]{:S(2)}, u32[]{:S(2)}) collective-permute-start(bf16[8,192,384]{2,1,0:T(8,128)(2,1)} %constant_dynamic-update-slice_fusion.16), channel_id=1, source_target_pairs={{0,8},{1,17},{2,10},{3,19},{4,12},{5,21},{6,14},{7,23},{8,0},{9,25... | collective-permute-start | bytes 3538952 | tf_op jit(solution)/shard_map/ppermute | solution.py:55
  198.2 28.5 %collective-permute-start.2 = (bf16[16,192,384]{2,1,0:T(8,128)(2,1)}, bf16[16,192,384]{2,1,0:T(8,128)(2,1)}, u32[]{:S(2)}, u32[]{:S(2)}) collective-permute-start(bf16[16,192,384]{2,1,0:T(8,128)(2,1)} %get-tuple-element.81), channel_id=1, source_target_pairs={{0,1},{1,0},{2,3},{3,2},{4,5},{5,4},{6,7},{7,6},{8,9},{9,8},{10,11... | collective-permute-start | bytes 7077896 | tf_op jit(solution)/shard_map/cond/branch_1_fun/ppermute | solution.py:51
  198.6 18.4 %collective-permute-start.1 = (bf16[8,192,384]{2,1,0:T(8,128)(2,1)S(1)}, bf16[8,192,384]{2,1,0:T(8,128)(2,1)}, u32[]{:S(2)}, u32[]{:S(2)}) collective-permute-start(bf16[8,192,384]{2,1,0:T(8,128)(2,1)S(1)} %add_convert_fusion.1), channel_id=1, source_target_pairs={{0,8},{1,17},{2,10},{3,19},{4,12},{5,21},{6,14},{7,23},{8,0},{9,25... | collective-permute-start | bytes 3538952 | tf_op jit(solution)/shard_map/cond/branch_1_fun/ppermute | solution.py:55
  218.5 12.4 %collective-permute-start.3 = (bf16[4,192,384]{2,1,0:T(8,128)(2,1)S(1)}, bf16[4,192,384]{2,1,0:T(8,128)(2,1)}, u32[]{:S(2)}, u32[]{:S(2)}) collective-permute-start(bf16[4,192,384]{2,1,0:T(8,128)(2,1)S(1)} %add_convert_fusion.3), channel_id=1, source_target_pairs={{0,16},{1,9},{2,18},{3,11},{4,20},{5,13},{6,22},{7,15},{8,24},{9,1... | collective-permute-start | bytes 1769480 | tf_op jit(solution)/shard_map/cond/branch_1_fun/ppermute | solution.py:55
  228.7 20.6 %collective-permute-start.4 = (bf16[8,192,384]{2,1,0:T(8,128)(2,1)S(1)}, bf16[8,192,384]{2,1,0:T(8,128)(2,1)}, u32[]{:S(2)}, u32[]{:S(2)}) collective-permute-start(bf16[8,192,384]{2,1,0:T(8,128)(2,1)S(1)} %add_convert_fusion), channel_id=1, source_target_pairs={{0,8},{1,17},{2,10},{3,19},{4,12},{5,21},{6,14},{7,23},{8,0},{9,25... | collective-permute-start | bytes 3538952 | tf_op jit(solution)/shard_map/cond/branch_1_fun/ppermute | solution.py:55
  233.2 18.9 %collective-permute-start.19 = (bf16[1,192,384]{2,1,0:T(8,128)(2,1)}, bf16[1,192,384]{2,1,0:T(8,128)(2,1)}, u32[]{:S(2)}, u32[]{:S(2)}) collective-permute-start(bf16[1,192,384]{2,1,0:T(8,128)(2,1)} %get-tuple-element.258), channel_id=1, source_target_pairs={{0,6},{1,7},{2,4},{3,5},{4,2},{5,3},{6,0},{7,1},{8,14},{9,15},{10,... | collective-permute-start | bytes 442376 | tf_op jit(solution)/shard_map/cond/branch_1_fun/ppermute | solution.py:55
  233.9 18.2 %collective-permute-start.18 = (bf16[1,192,384]{2,1,0:T(8,128)(2,1)S(1)}, bf16[1,192,384]{2,1,0:T(8,128)(2,1)}, u32[]{:S(2)}, u32[]{:S(2)}) collective-permute-start(bf16[1,192,384]{2,1,0:T(8,128)(2,1)S(1)} %get-tuple-element.259), channel_id=1, source_target_pairs={{0,2},{1,3},{2,0},{3,1},{4,6},{5,7},{6,4},{7,5},{8,10},{9,11},{10,... | collective-permute-start | bytes 442376 | tf_op jit(solution)/shard_map/cond/branch_1_fun/ppermute | solution.py:55
  233.9 18.2 %collective-permute-start.17 = (bf16[1,192,384]{2,1,0:T(8,128)(2,1)S(1)}, bf16[1,192,384]{2,1,0:T(8,128)(2,1)}, u32[]{:S(2)}, u32[]{:S(2)}) collective-permute-start(bf16[1,192,384]{2,1,0:T(8,128)(2,1)S(1)} %get-tuple-element.260), channel_id=1, source_target_pairs={{0,4},{1,5},{2,6},{3,7},{4,0},{5,1},{6,2},{7,3},{8,12},{9,13},{10,... | collective-permute-start | bytes 442376 | tf_op jit(solution)/shard_map/cond/branch_1_fun/ppermute | solution.py:55
  250.7 9.9 %collective-permute-start.8 = (bf16[4,192,384]{2,1,0:T(8,128)(2,1)S(1)}, bf16[4,192,384]{2,1,0:T(8,128)(2,1)S(1)}, u32[]{:S(2)}, u32[]{:S(2)}) collective-permute-start(bf16[4,192,384]{2,1,0:T(8,128)(2,1)S(1)} %add_convert_fusion.2), channel_id=1, source_target_pairs={{0,16},{1,9},{2,18},{3,11},{4,20},{5,13},{6,22},{7,15},{8,24},{9,1... | collective-permute-start | bytes 1769480 | tf_op jit(solution)/shard_map/cond/branch_1_fun/ppermute | solution.py:55
  262.1 8.7 %collective-permute-start.15 = (bf16[1,192,384]{2,1,0:T(8,128)(2,1)S(1)}, bf16[1,192,384]{2,1,0:T(8,128)(2,1)S(1)}, u32[]{:S(2)}, u32[]{:S(2)}) collective-permute-start(bf16[1,192,384]{2,1,0:T(8,128)(2,1)S(1)} %get-tuple-element.255), channel_id=1, source_target_pairs={{0,6},{1,7},{2,4},{3,5},{4,2},{5,3},{6,0},{7,1},{8,14},{9,15},{10,... | collective-permute-start | bytes 442376 | tf_op jit(solution)/shard_map/cond/branch_1_fun/ppermute | solution.py:55
  264.8 11.9 %collective-permute-start.13 = (bf16[1,192,384]{2,1,0:T(8,128)(2,1)S(1)}, bf16[1,192,384]{2,1,0:T(8,128)(2,1)S(1)}, u32[]{:S(2)}, u32[]{:S(2)}) collective-permute-start(bf16[1,192,384]{2,1,0:T(8,128)(2,1)S(1)} %get-tuple-element.257), channel_id=1, source_target_pairs={{0,4},{1,5},{2,6},{3,7},{4,0},{5,1},{6,2},{7,3},{8,12},{9,13},{10,... | collective-permute-start | bytes 442376 | tf_op jit(solution)/shard_map/cond/branch_1_fun/ppermute | solution.py:55
  266.6 13.2 %collective-permute-start.20 = (f32[96,384]{1,0:T(8,128)S(1)}, f32[96,384]{1,0:T(8,128)S(1)}, u32[]{:S(2)}, u32[]{:S(2)}) collective-permute-start(f32[96,384]{1,0:T(8,128)S(1)} %get-tuple-element.262), channel_id=1, source_target_pairs={{0,1},{1,0},{2,3},{3,2},{4,5},{5,4},{6,7},{7,6},{8,9},{9,8},{10,11... | collective-permute-start | bytes 442376 | tf_op jit(solution)/shard_map/cond/branch_1_fun/ppermute | solution.py:51
  266.7 11.3 %collective-permute-start.9 = (bf16[4,16,768]{2,1,0:T(8,128)(2,1)S(1)}, bf16[4,16,768]{2,1,0:T(8,128)(2,1)S(1)}, u32[]{:S(2)}, u32[]{:S(2)}) collective-permute-start(bf16[4,16,768]{2,1,0:T(8,128)(2,1)S(1)} %constant_dynamic-update-slice_fusion), channel_id=1, source_target_pairs={{0,16},{1,9},{2,18},{3,11},{4,20},{5,13},{6,22},{7,15},{8,24},{9,1... | collective-permute-start | bytes 294920 | tf_op jit(solution)/shard_map/cond/branch_1_fun/ppermute | solution.py:55
  (43 other events, 494.2 us)
Sparse Core Ops, SparseCore 0:
  11.7 85.7 all-gather.1
  135.2 112.8 reduce-scatter.1

commit v3 on v2

v3 whole, which is shorter than its diff:
```python
from functools import partial
import math

import jax
import jax.numpy as jnp
from jax import lax
from jax.experimental import pallas as pl
from jax.experimental.pallas import tpu as pltpu
from jax.sharding import PartitionSpec as P

HEAD_DIM = 64
AXES = ("dp", "fsdp")
LANES = 384
CHIPS = 16
WIDTH = 768
FF = 3072
F32 = jnp.float32
BF16 = jnp.bfloat16
NEG = -1000000000.0


def sinusoid(timestep, half_width):
    frequency = jnp.exp(-math.log(10000.0) * jnp.arange(half_width, dtype=F32) / half_width)
    angles = timestep.astype(F32)[:, None] * frequency[None, :]
    return jnp.concatenate([jnp.cos(angles), jnp.sin(angles)], axis=-1)


def dot(left, right):
    return jnp.dot(left, right, preferred_element_type=F32)


def dot_last(left, right):
    return lax.dot_general(left, right, (((1,), (1,)), ((), ())), preferred_element_type=F32)


def dot_first(left, right):
    return lax.dot_general(left, right, (((0,), (0,)), ((), ())), preferred_element_type=F32)


def positions(masks):
    return [sum(masks[b] for b in range(4) if (p >> b) & 1) for p in range(CHIPS)]


LINE_FIRST = ((2, 1, 8, 4), (2, 1, 4, 8))
LINE_LATER = ((8, 2, 1, 4), (4, 2, 1, 8))


def core_swap(x):
    return lax.ppermute(x, AXES, [(i, i ^ 1) for i in range(2 * CHIPS)])


def chip_swap(x, position, order=LINE_FIRST):
    far = [positions(masks)[position] * 2 for masks in order]
    return lax.ppermute(x, AXES, [(i, i ^ far[i & 1]) for i in range(2 * CHIPS)])


def after(x, *others):
    return lax.optimization_barrier((x,) + others)[0]


def gather_line(piece):
    return jnp.concatenate([piece] + [chip_swap(piece, p) for p in (1, 2, 3)], axis=0)


def gather_plane(held):
    return jnp.concatenate([held, chip_swap(held, 4)], axis=0)


def together(outs, arrivals):
    return lax.optimization_barrier((outs, arrivals))


class Scatter:
    def __init__(self, theirs):
        self.parts = []
        self.steps = [(8,), (4,), (1, 2, 3)]
        self.theirs = theirs

    def swap(self):
        return [core_swap(self.theirs)]

    def land(self, brought, *own):
        self.parts += [*brought, *own]

    def sum(self, start, stop):
        total = self.parts[0][start:stop].astype(F32)
        for part in self.parts[1:]:
            total = total + part[start:stop].astype(F32)
        return total

    def send(self):
        self.at = self.steps.pop(0)
        size = 1 if len(self.at) == 3 else self.at[0]
        self.sent = [self.sum(p, p + size).astype(BF16) for p in self.at]
        return self.sent

    def fly(self):
        return [chip_swap(x, p) for x, p in zip(self.sent, self.at)]

    def total(self):
        return self.sum(0, 1)[0]


VMEM_SPEC = pl.BlockSpec(memory_space=pltpu.VMEM)
SMEM_SPEC = pl.BlockSpec(memory_space=pltpu.SMEM)
ANY_SPEC = pl.BlockSpec(memory_space=pl.ANY)


def tiles(rows, cols):
    return pl.BlockSpec((rows, cols), lambda i: (i, 0))


def columns(rows, cols):
    return pl.BlockSpec((rows, cols), lambda i: (0, i))


def fixed(*shape):
    return pl.BlockSpec(shape, lambda i: (0,) * len(shape))


def shaped(shape, dtype=BF16):
    return pltpu.HBM(shape, dtype)


def params(mib):
    return pltpu.CompilerParams(vmem_limit_bytes=mib * 1024 * 1024)


def kernel_call(*args, **kwargs):
    call = pl.pallas_call(*args, **kwargs)

    def run(*operands):
        return call(
            *[
                x
                if x.dtype == jnp.int32
                else pltpu.with_memory_space_constraint(x, pltpu.HBM)
                for x in operands
            ]
        )

    return run


def cost(flops, nbytes, transcendentals=0):
    return pl.CostEstimate(flops=flops, bytes_accessed=nbytes, transcendentals=transcendentals)


def ln_stats(v):
    center = v - jnp.mean(v, axis=-1, keepdims=True)
    scale = lax.rsqrt(jnp.mean(center * center, axis=-1, keepdims=True) + 1e-05)
    return center * scale, scale


def ln_back(y, gain, xhat, scale):
    yg = y * gain
    return scale * (
        yg - jnp.mean(yg, axis=-1, keepdims=True) - xhat * jnp.mean(yg * xhat, axis=-1, keepdims=True)
    )


def first_core(tab):
    return tab[64]


def each_piece(tab, parts, fn):
    core = first_core(tab)
    for side in (0, 1):
        half = core if side == 0 else 1 - core
        for group in (0, 1):
            part = parts[side * 2 + group]

            def body(q, _, part=part, side=side, group=group, half=half):
                chip = tab[side * CHIPS + group * 8 + q]
                fn(part.at[q], chip, half)
                return 0

            lax.fori_loop(0, 8, body, 0)


def rows_of(chip, size):
    return pl.ds(pl.multiple_of(chip * size, size), size)


def lanes_of(half, size, base=0):
    return pl.ds(pl.multiple_of(half * size + base, 128), LANES)


def fetch_pieces(tab, parts, rows, dst, sem):
    each_piece(
        tab,
        parts,
        lambda src, chip, half: pltpu.make_async_copy(
            src.at[pl.ds(0, rows), :], dst.at[chip, half], sem
        ).start(),
    )


def block(pieces, half, first, rows=48):
    return pieces[:, half, first : first + rows, :].reshape(CHIPS * rows, LANES)


def both_halves(pieces, first, rows=48):
    return jnp.concatenate([block(pieces, h, first, rows) for h in (0, 1)], axis=1)


def down_rows(pieces, j):
    return jnp.concatenate(
        [pieces[4 * j : 4 * j + 4, h].reshape(WIDTH, LANES) for h in (0, 1)], axis=1
    )


def qkv_columns(pieces, half):
    return jnp.concatenate([block(pieces, half, 48 * sec) for sec in range(3)], axis=1)


def finish(ref, sem):
    pltpu.make_async_copy(ref, ref, sem).wait()


def add_embed(x, embed, i):
    seqs = x.shape[0] // 128
    parts = [
        x[128 * k : 128 * k + 128].astype(F32) + embed[pl.ds(i * seqs + k, 1), :]
        for k in range(seqs)
    ]
    return jnp.concatenate(parts, axis=0)


def two_heads(x, low_half):
    none = jnp.zeros_like(x)
    return jnp.concatenate([jnp.where(low_half, x, none), jnp.where(low_half, none, x)], axis=0)


def side_by_side(x):
    return jnp.concatenate([x[:128], x[128:]], axis=1)


def pair_base(pair):
    return (pair // 3) * 3 * LANES + (pair % 3) * 128


def attention_rows(k, length, qkv_ref, probs_ref, att_ref):
    low_half = lax.broadcasted_iota(jnp.int32, (128, 128), 1) < HEAD_DIM
    keep = lax.broadcasted_iota(jnp.int32, (256, 128), 1) < length
    rows = slice(128 * k, 128 * k + 128)
    scores = []
    for pair in range(6):
        base = pair_base(pair)
        query = two_heads(qkv_ref[rows, base : base + 128], low_half)
        key = qkv_ref[rows, base + LANES : base + LANES + 128]
        scores.append(jnp.where(keep, dot_last(query, key) * HEAD_DIM ** (-0.5), NEG))
    probs = []
    for pair in range(6):
        shifted = jnp.exp(scores[pair] - jnp.max(scores[pair], axis=-1, keepdims=True))
        total = jnp.sum(shifted, axis=-1, keepdims=True)
        probs.append((shifted * (1.0 / total)).astype(BF16))
        first = 256 * (6 * k + pair)
        probs_ref[first : first + 256, :] = probs[pair]
    for pair in range(6):
        base = pair_base(pair) + 2 * LANES
        value = two_heads(qkv_ref[rows, base : base + 128], low_half)
        att_ref[rows, pair * 128 : pair * 128 + 128] = dot(
            side_by_side(probs[pair]), value
        ).astype(BF16)


def attention_kernel(
    tab, lens, sets, g_a, g_b, g_c, g_d, x_ref, feat_ref,
    normed_ref, qkv_ref, te_ref, vec_ref, seen_ref, probs_ref, att_ref,
    w, sem,
):
    i = pl.program_id(0)

    @pl.when(i == 0)
    def _():
        fetch_pieces(tab, (g_a, g_b, g_c, g_d), 192, w, sem)
        finish(w, sem)
        lane = lax.broadcasted_iota(jnp.int32, (128, WIDTH), 1)
        spread = (lax.broadcasted_iota(jnp.int32, (128, WIDTH), 0) == lane % 24).astype(BF16)
        vectors = jnp.zeros((16, WIDTH), F32)
        embed = jnp.zeros((8, WIDTH), F32)
        for owner in (0, 1):
            extra = block(w, owner, 176, 16)
            wide = dot(extra[:, 128:256], spread)
            chip = lax.broadcasted_iota(jnp.int32, (256, WIDTH), 0) // 16
            place = lax.broadcasted_iota(jnp.int32, (256, WIDTH), 1) // 24
            wide = jnp.where(place == chip * 2 + owner, wide, 0.0)
            vectors = vectors + jnp.sum(wide.reshape(CHIPS, 16, WIDTH), axis=0)
            pre = dot_last(feat_ref[...], extra[:, 0:128])
            hidden = (pre / (1.0 + jnp.exp(-pre))).astype(BF16)
            embed = embed + dot(hidden, both_halves(w, 144 + 16 * owner, 16))
            seen_ref[owner] = w[:, owner, 176:192, 256:]
        vec_ref[...] = vectors
        for s in range(8):
            chosen = jnp.where(sets[s // 4, s % 4] == 1, vectors[3:4, :], vectors[2:3, :])
            te_ref[s : s + 1, :] = embed[s : s + 1, :] + chosen

    xhat, _unused = ln_stats(add_embed(x_ref[...], te_ref, i))
    normed_ref[...] = (xhat * vec_ref[0:1, :]).astype(BF16)
    for half in (0, 1):
        cols = slice(half * 3 * LANES, (half + 1) * 3 * LANES)
        qkv_ref[:, cols] = dot(normed_ref[...], qkv_columns(w, half)).astype(BF16)
    for k in range(2):
        attention_rows(k, lens[i // 2, i % 2 * 2 + k], qkv_ref, probs_ref, att_ref)


def attention_forward(tab, lens, sets, pieces, rows, features):
    row = tiles(256, WIDTH)
    return kernel_call(
        attention_kernel,
        grid=(4,),
        out_shape=(
            shaped((1024, WIDTH)),
            shaped((1024, 3 * WIDTH)),
            shaped((8, WIDTH), F32),
            shaped((16, WIDTH), F32),
            shaped((2, CHIPS, 16, 128)),
            shaped((48 * 256, 128)),
            shaped((1024, WIDTH)),
        ),
        in_specs=[SMEM_SPEC] * 3 + [ANY_SPEC] * 4 + [row, fixed(8, 128)],
        out_specs=(
            row, tiles(256, 3 * WIDTH), fixed(8, WIDTH), fixed(16, WIDTH),
            fixed(2, CHIPS, 16, 128), tiles(12 * 256, 128), row,
        ),
        scratch_shapes=[pltpu.VMEM((CHIPS, 2, 192, LANES), BF16), pltpu.SemaphoreType.DMA],
        compiler_params=params(26),
        cost_estimate=cost(8_000_000_000, 20_000_000, 1_600_000),
        name="attention_forward",
    )(tab, lens, sets, *pieces, rows, features)


def gelu_parts(u):
    cdf = 0.5 + 0.5 * lax.erf(u * math.sqrt(0.5))
    return cdf, jnp.exp(u * u * -0.5) * (1.0 / math.sqrt(2.0 * math.pi))


def up_columns(pieces, j):
    first = 96 * (j % 2)
    return jnp.concatenate(
        [block(pieces, j // 2, first), block(pieces, j // 2, first + 48)], axis=1
    )


def half_of(tab, side):
    return first_core(tab) if side == 0 else 1 - first_core(tab)


def clamped(rows, cols):
    return pl.BlockSpec((rows, cols), lambda i: (jnp.minimum(i, 3), 0))


def down_grad_rows(tab, side, j, act, out_grad, out_ref):
    lanes = lanes_of(half_of(tab, side), LANES)
    grad = dot_first(act, out_grad[:, lanes]).astype(BF16)
    for k in range(4):
        place = tab[32 + side * CHIPS + j * 4 + k]
        out_ref[place, :, :] = grad[192 * k : 192 * k + 192, :]


def up_kernel(
    tab, u_a, u_b, u_c, u_d, out_grad_hbm, att_ref, x_ref, te_ref, vec_ref,
    mid_ref, two_ref, act_ref, slope_ref, theirs_ref,
    w, out_grad, kept, sem, sem_out_grad,
):
    i = pl.program_id(0)

    @pl.when(i == 0)
    def _():
        fetch_pieces(tab, (u_a, u_b, u_c, u_d), 240, w, sem)
        finish(w, sem)
        pltpu.make_async_copy(out_grad_hbm, out_grad, sem_out_grad).start()

    @pl.when(i < 4)
    def _():
        mid = add_embed(x_ref[...], te_ref, i) + dot(att_ref[...], both_halves(w, 192))
        mid_ref[...] = mid
        xhat, _unused = ln_stats(mid)
        two_ref[...] = (xhat * vec_ref[1:2, :]).astype(BF16)
        for j in range(4):
            cols = slice(j * WIDTH, (j + 1) * WIDTH)
            up = dot(two_ref[...], up_columns(w, j))
            cdf, density = gelu_parts(up)
            activated = (up * cdf).astype(BF16)
            act_ref[:, cols] = activated
            kept[j, rows_of(i, 256), :] = activated
            slope_ref[:, cols] = (cdf + up * density).astype(BF16)

    @pl.when(i == 4)
    def _():
        finish(out_grad, sem_out_grad)

    @pl.when(i >= 4)
    def _():
        down_grad_rows(tab, 1, i - 4, kept[i - 4], out_grad, theirs_ref)


def up_forward(tab, pieces, att, rows, out_grad, embed, vectors):
    row = clamped(256, WIDTH)
    wide = clamped(256, FF)
    return kernel_call(
        up_kernel,
        grid=(8,),
        out_shape=(
            shaped((1024, WIDTH), F32),
            shaped((1024, WIDTH)),
            shaped((1024, FF)),
            shaped((1024, FF)),
            pltpu.VMEM((CHIPS, 192, LANES), BF16),
        ),
        in_specs=[SMEM_SPEC] + [ANY_SPEC] * 5 + [row, row, fixed(8, WIDTH), fixed(16, WIDTH)],
        out_specs=(row, row, wide, wide, VMEM_SPEC),
        scratch_shapes=[
            pltpu.VMEM((CHIPS, 2, 240, LANES), BF16),
            pltpu.VMEM((1024, WIDTH), BF16),
            pltpu.VMEM((4, 1024, WIDTH), BF16),
            pltpu.SemaphoreType.DMA,
            pltpu.SemaphoreType.DMA,
        ],
        compiler_params=params(38),
        cost_estimate=cost(10_000_000_000, 30_000_000, 6_000_000),
        name="up_forward",
    )(tab, *pieces, out_grad, att, rows, embed, vectors)


def down_grad_kernel(tab, act_ref, out_grad_ref, out_ref):
    down_grad_rows(tab, 0, pl.program_id(0), act_ref[...], out_grad_ref, out_ref)


def down_grad(tab, act, out_grad):
    return kernel_call(
        down_grad_kernel,
        grid=(4,),
        out_shape=pltpu.VMEM((CHIPS, 192, LANES), BF16),
        in_specs=[SMEM_SPEC, columns(1024, WIDTH), fixed(1024, WIDTH)],
        out_specs=VMEM_SPEC,
        compiler_params=params(18),
        cost_estimate=cost(3_000_000_000, 10_000_000),
        name="down_grad",
    )(tab, act, out_grad)


def store_blocks(tab, side, target, first, part, lanes):
    for chip in range(CHIPS):
        place = tab[32 + side * CHIPS + chip]
        target[place, pl.ds(first, 48), :] = part[48 * chip : 48 * chip + 48, lanes]


def out_grad_rows(tab, side, att, branch, out_ref, part):
    lanes = lanes_of(half_of(tab, side), LANES)
    part[:, 0:LANES] = dot_first(att[...], branch[:, lanes]).astype(BF16)
    store_blocks(tab, side, out_ref, 192, part, slice(0, LANES))


def up_grad_rows(tab, side, j, two, grad_up, out_ref, part):
    part[...] = dot_first(two, grad_up).astype(BF16)
    for b in range(2):
        first = pl.multiple_of((2 * j + b) * 48, 48)
        store_blocks(tab, side, out_ref, first, part, slice(b * LANES, (b + 1) * LANES))


def up_grad_kernel(
    tab, att_hbm, branch_hbm, two_ref, grad_up_ref, out_ref,
    att, branch, part, sem_att, sem_branch,
):
    j = pl.program_id(0)

    @pl.when(j == 0)
    def _():
        pltpu.make_async_copy(att_hbm, att, sem_att).start()
        pltpu.make_async_copy(branch_hbm, branch, sem_branch).start()

    @pl.when(j < 2)
    def _():
        up_grad_rows(tab, 0, j, two_ref[...], grad_up_ref[...], out_ref, part)

    @pl.when(j == 2)
    def _():
        finish(att, sem_att)
        finish(branch, sem_branch)
        out_grad_rows(tab, 0, att, branch, out_ref, part)


def up_grad(tab, att, branch, two, grad_up):
    return kernel_call(
        up_grad_kernel,
        grid_spec=pltpu.PrefetchScalarGridSpec(
            num_scalar_prefetch=1,
            grid=(3,),
            in_specs=[
                ANY_SPEC,
                ANY_SPEC,
                pl.BlockSpec((1024, WIDTH), lambda j, tab: (0, 0)),
                pl.BlockSpec(
                    (1024, WIDTH), lambda j, tab: (0, half_of(tab, 0) * 2 + jnp.minimum(j, 1))
                ),
            ],
            out_specs=VMEM_SPEC,
            scratch_shapes=[pltpu.VMEM((1024, WIDTH), BF16)] * 2
            + [pltpu.VMEM((WIDTH, WIDTH), BF16)]
            + [pltpu.SemaphoreType.DMA] * 2,
        ),
        out_shape=pltpu.VMEM((CHIPS, 240, LANES), BF16),
        compiler_params=params(22),
        cost_estimate=cost(3_200_000_000, 11_000_000),
        name="up_grad",
    )(tab, att, branch, two, grad_up)


def mlp_backward_kernel(
    tab, down_tab, u_a, u_b, u_c, u_d, d_a, d_b, d_c, d_d, two_hbm, att_hbm,
    slope_ref, out_grad_ref, mid_ref, vec_ref,
    grad_mid_ref, branch_ref, grad_up_ref, grad_att_ref, gain_ref, theirs_ref,
    w, w_down, two, att, kept, kept_branch, part, sem, sem_down, sem_two, sem_att,
):
    i = pl.program_id(0)

    @pl.when(i == 0)
    def _():
        fetch_pieces(down_tab, (d_a, d_b, d_c, d_d), 192, w_down, sem_down)
        gain_ref[...] = jnp.zeros_like(gain_ref)
        finish(w_down, sem_down)
        fetch_pieces(tab, (u_a, u_b, u_c, u_d), 240, w, sem)
        pltpu.make_async_copy(two_hbm, two, sem_two).start()
        pltpu.make_async_copy(att_hbm, att, sem_att).start()

    @pl.when(i < 4)
    def _():
        for j in range(4):
            cols = slice(j * WIDTH, (j + 1) * WIDTH)
            grad_act = dot_last(out_grad_ref[...], down_rows(w_down, j))
            grad_up_ref[:, cols] = (grad_act * slope_ref[:, cols].astype(F32)).astype(BF16)

        @pl.when(i == 0)
        def _():
            finish(w, sem)

        y = jnp.zeros((256, WIDTH), F32)
        for j in range(4):
            cols = slice(j * WIDTH, (j + 1) * WIDTH)
            y = y + dot_last(grad_up_ref[:, cols], up_columns(w, j))
        theirs = pl.ds(pl.multiple_of(half_of(tab, 1) * 4 * LANES, 128), 4 * LANES)
        kept[rows_of(i, 256), :] = grad_up_ref[:, theirs]
        xhat, scale = ln_stats(mid_ref[...])
        grad = out_grad_ref[...].astype(F32) + ln_back(y, vec_ref[1:2, :], xhat, scale)
        grad_mid_ref[...] = grad
        branch_ref[...] = grad.astype(BF16)
        kept_branch[rows_of(i, 256), :] = branch_ref[...]
        gain_ref[...] += jnp.sum(y * xhat, axis=0, keepdims=True)
        grad_att_ref[...] = dot_last(branch_ref[...], both_halves(w, 192)).astype(BF16)

    @pl.when(i == 4)
    def _():
        finish(two, sem_two)
        finish(att, sem_att)
        out_grad_rows(tab, 1, att, kept_branch, theirs_ref, part)

    @pl.when(i >= 4)
    def _():
        cols = pl.ds(pl.multiple_of((i - 4) * WIDTH, WIDTH), WIDTH)
        up_grad_rows(tab, 1, i - 4, two[...], kept[:, cols], theirs_ref, part)


def mlp_backward(tab, down_tab, up_pieces, down_pieces, two, att, slope, out_grad, mid, vectors):
    row = clamped(256, WIDTH)
    wide = clamped(256, FF)
    return kernel_call(
        mlp_backward_kernel,
        grid=(6,),
        out_shape=(
            shaped((1024, WIDTH), F32),
            shaped((1024, WIDTH)),
            shaped((1024, FF)),
            shaped((1024, WIDTH)),
            shaped((1, WIDTH), F32),
            pltpu.VMEM((CHIPS, 240, LANES), BF16),
        ),
        in_specs=[SMEM_SPEC] * 2 + [ANY_SPEC] * 10 + [wide, row, row, fixed(16, WIDTH)],
        out_specs=(row, row, wide, row, fixed(1, WIDTH), VMEM_SPEC),
        scratch_shapes=[
            pltpu.VMEM((CHIPS, 2, 240, LANES), BF16),
            pltpu.VMEM((CHIPS, 2, 192, LANES), BF16),
            pltpu.VMEM((1024, WIDTH), BF16),
            pltpu.VMEM((1024, WIDTH), BF16),
            pltpu.VMEM((1024, 4 * LANES), BF16),
            pltpu.VMEM((1024, WIDTH), BF16),
            pltpu.VMEM((WIDTH, WIDTH), BF16),
        ]
        + [pltpu.SemaphoreType.DMA] * 4,
        compiler_params=params(46),
        cost_estimate=cost(18_000_000_000, 50_000_000),
        name="mlp_backward",
    )(tab, down_tab, *up_pieces, *down_pieces, two, att, slope, out_grad, mid, vectors)


def result_kernel(tab, d_a, d_b, d_c, d_d, act_ref, mid_ref, result_ref, w_down, sem):
    @pl.when(pl.program_id(0) == 0)
    def _():
        fetch_pieces(tab, (d_a, d_b, d_c, d_d), 192, w_down, sem)
        finish(w_down, sem)

    total = mid_ref[...]
    for j in range(4):
        total = total + dot(act_ref[:, j * WIDTH : (j + 1) * WIDTH], down_rows(w_down, j))
    result_ref[...] = total.astype(BF16)


def block_result(tab, pieces, act, mid):
    row = tiles(256, WIDTH)
    return kernel_call(
        result_kernel,
        grid=(4,),
        out_shape=shaped((1024, WIDTH)),
        in_specs=[SMEM_SPEC] + [ANY_SPEC] * 4 + [tiles(256, FF), row],
        out_specs=row,
        scratch_shapes=[pltpu.VMEM((CHIPS, 2, 192, LANES), BF16), pltpu.SemaphoreType.DMA],
        compiler_params=params(22),
        cost_estimate=cost(5_000_000_000, 16_000_000),
        name="block_result",
    )(tab, *pieces, act, mid)


def attention_backward_rows(k, qkv_ref, probs_ref, grad_att_ref, grad_qkv_ref):
    low_half = lax.broadcasted_iota(jnp.int32, (128, 128), 1) < HEAD_DIM
    rows = slice(128 * k, 128 * k + 128)

    def heads(ref, base):
        return two_heads(ref[rows, base : base + 128], low_half)

    def probs_of(pair):
        first = 256 * (6 * k + pair)
        return probs_ref[first : first + 256, :]

    grad_probs = []
    for pair in range(6):
        base = pair_base(pair) + 2 * LANES
        grad_probs.append(
            dot_last(heads(grad_att_ref, pair * 128), qkv_ref[rows, base : base + 128])
        )
    grad_scores = []
    for pair in range(6):
        probs = probs_of(pair).astype(F32)
        inner = jnp.sum(probs * grad_probs[pair], axis=-1, keepdims=True)
        grad_scores.append((probs * (grad_probs[pair] - inner)).astype(BF16))
    for pair in range(6):
        base = pair_base(pair)
        grad_query = dot(side_by_side(grad_scores[pair]), heads(qkv_ref, base + LANES))
        grad_key = dot_first(grad_scores[pair], heads(qkv_ref, base))
        grad_value = dot_first(probs_of(pair), heads(grad_att_ref, pair * 128))
        grad_query = (grad_query * HEAD_DIM ** (-0.5)).astype(BF16)
        grad_qkv_ref[rows, base : base + 128] = grad_query
        base = base + LANES
        grad_qkv_ref[rows, base : base + 128] = (grad_key * HEAD_DIM ** (-0.5)).astype(BF16)
        base = base + LANES
        grad_qkv_ref[rows, base : base + 128] = grad_value.astype(BF16)


def qkv_grad_rows(tab, side, normed, grad_qkv, out_ref, part):
    part[...] = dot_first(normed, grad_qkv).astype(BF16)
    for sec in range(3):
        store_blocks(tab, side, out_ref, 48 * sec, part, slice(sec * LANES, (sec + 1) * LANES))


def attention_backward_kernel(
    tab, normed_hbm, qkv_ref, probs_ref, grad_att_ref, grad_qkv_ref, theirs_ref,
    normed, kept, part, sem,
):
    i = pl.program_id(0)

    @pl.when(i == 0)
    def _():
        pltpu.make_async_copy(normed_hbm, normed, sem).start()

    @pl.when(i < 4)
    def _():
        for k in range(2):
            attention_backward_rows(k, qkv_ref, probs_ref, grad_att_ref, grad_qkv_ref)
        theirs = pl.ds(pl.multiple_of(half_of(tab, 1) * 3 * LANES, 128), 3 * LANES)
        kept[rows_of(i, 256), :] = grad_qkv_ref[:, theirs]

    @pl.when(i == 4)
    def _():
        finish(normed, sem)
        qkv_grad_rows(tab, 1, normed[...], kept[...], theirs_ref, part)


def attention_backward(tab, normed, qkv, probs, grad_att):
    wide = clamped(256, 3 * WIDTH)
    return kernel_call(
        attention_backward_kernel,
        grid=(5,),
        out_shape=(shaped((1024, 3 * WIDTH)), pltpu.VMEM((CHIPS, 144, LANES), BF16)),
        in_specs=[SMEM_SPEC, ANY_SPEC, wide, clamped(12 * 256, 128), clamped(256, WIDTH)],
        out_specs=(wide, VMEM_SPEC),
        scratch_shapes=[
            pltpu.VMEM((1024, WIDTH), BF16),
            pltpu.VMEM((1024, 3 * LANES), BF16),
            pltpu.VMEM((WIDTH, 3 * LANES), BF16),
            pltpu.SemaphoreType.DMA,
        ],
        compiler_params=params(28),
        cost_estimate=cost(11_000_000_000, 22_000_000),
        name="attention_backward",
    )(tab, normed, qkv, probs, grad_att)


def qkv_grad_kernel(tab, normed_ref, grad_qkv_ref, out_ref, part):
    qkv_grad_rows(tab, 0, normed_ref[...], grad_qkv_ref[...], out_ref, part)


def qkv_grad(tab, normed, grad_qkv):
    return kernel_call(
        qkv_grad_kernel,
        grid_spec=pltpu.PrefetchScalarGridSpec(
            num_scalar_prefetch=1,
            grid=(1,),
            in_specs=[
                pl.BlockSpec((1024, WIDTH), lambda i, tab: (0, 0)),
                pl.BlockSpec((1024, 3 * LANES), lambda i, tab: (0, half_of(tab, 0))),
            ],
            out_specs=VMEM_SPEC,
            scratch_shapes=[pltpu.VMEM((WIDTH, 3 * LANES), BF16)],
        ),
        out_shape=pltpu.VMEM((CHIPS, 144, LANES), BF16),
        compiler_params=params(22),
        cost_estimate=cost(2_000_000_000, 7_000_000),
        name="qkv_grad",
    )(tab, normed, grad_qkv)


def input_backward_kernel(
    tab, g_a, g_b, g_c, g_d, grad_qkv_ref, x_ref, te_ref, vec_ref, grad_mid_ref, gain_two_ref,
    input_ref, small_ref,
    w, sem,
):
    i = pl.program_id(0)

    @pl.when(i == 0)
    def _():
        fetch_pieces(tab, (g_a, g_b, g_c, g_d), 144, w, sem)
        small_ref[8:9, :] = jnp.zeros((1, WIDTH), F32)
        small_ref[9:10, :] = gain_two_ref[...]
        small_ref[10:16, :] = jnp.zeros((6, WIDTH), F32)
        finish(w, sem)

    y = jnp.zeros((256, WIDTH), F32)
    for half in (0, 1):
        cols = slice(half * 3 * LANES, (half + 1) * 3 * LANES)
        y = y + dot_last(grad_qkv_ref[:, cols], qkv_columns(w, half))
    xhat, scale = ln_stats(add_embed(x_ref[...], te_ref, i))
    grad = grad_mid_ref[...] + ln_back(y, vec_ref[0:1, :], xhat, scale)
    input_ref[...] = grad.astype(BF16)
    for s in range(2):
        small_ref[pl.ds(i * 2 + s, 1), :] = jnp.sum(
            grad[128 * s : 128 * s + 128], axis=0, keepdims=True
        )
    small_ref[8:9, :] += jnp.sum(y * xhat, axis=0, keepdims=True)


def input_backward(tab, pieces, grad_qkv, rows, embed, vectors, grad_mid, gain_two):
    row = tiles(256, WIDTH)
    return kernel_call(
        input_backward_kernel,
        grid=(4,),
        out_shape=(shaped((1024, WIDTH)), shaped((16, WIDTH), F32)),
        in_specs=[SMEM_SPEC]
        + [ANY_SPEC] * 4
        + [tiles(256, 3 * WIDTH), row, fixed(8, WIDTH), fixed(16, WIDTH), row, fixed(1, WIDTH)],
        out_specs=(row, fixed(16, WIDTH)),
        scratch_shapes=[pltpu.VMEM((CHIPS, 2, 144, LANES), BF16), pltpu.SemaphoreType.DMA],
        compiler_params=params(24),
        cost_estimate=cost(4_000_000_000, 18_000_000),
        name="input_backward",
    )(tab, *pieces, grad_qkv, rows, embed, vectors, grad_mid, gain_two)


def time_grads_kernel(tab, *refs):
    count = len(refs) - 10
    parts = refs[:count]
    wave_ref, hot_ref, hidden_ref, slope_ref, time_out_ref = refs[count : count + 5]
    tin_ref, tout_ref, sums_ref, every, sem = refs[count + 5 :]
    if count == 1:
        pltpu.make_async_copy(parts[0], every, sem).start()
    else:

        def fetch(src, chip, half):
            pltpu.make_async_copy(src, every.at[half * CHIPS + chip], sem).start()

        each_piece(tab, parts, fetch)
    finish(every, sem)
    grads = every[...].reshape(-1, WIDTH)
    tout_ref[...] = dot_first(hidden_ref[...], grads)
    grad_pre = dot_last(grads, time_out_ref[...]) * slope_ref[...]
    tin_ref[...] = dot_first(grad_pre.astype(BF16), wave_ref[...])
    sums_ref[...] = dot(hot_ref[...], grads)


def time_grads(tab, parts, wave, hot, hidden, slope, time_out):
    rows, width = time_out.shape
    devices = wave.shape[0] // 16
    return kernel_call(
        time_grads_kernel,
        out_shape=(
            shaped((rows, wave.shape[1]), F32), shaped((rows, width), F32), shaped((16, width), F32)
        ),
        in_specs=[SMEM_SPEC] + [ANY_SPEC] * len(parts) + [VMEM_SPEC] * 5,
        out_specs=(VMEM_SPEC,) * 3,
        scratch_shapes=[pltpu.VMEM((devices, 16, width), BF16), pltpu.SemaphoreType.DMA],
        compiler_params=params(40),
        cost_estimate=cost(50_000_000, 2_000_000),
        name="time_grads",
    )(tab, *parts, wave, hot, hidden, slope, time_out)


def pick(stacked, index):
    return lax.dynamic_index_in_dim(stacked, index, 0, keepdims=False)


def in_core_order(core, own, other, axis):
    return jnp.where(
        core == 0,
        jnp.concatenate([own, other], axis=axis),
        jnp.concatenate([other, own], axis=axis),
    )


def position_table(chip, core, order):
    index = jnp.arange(72, dtype=jnp.int32)
    side = jnp.bitwise_xor(core, (index // CHIPS) % 2)
    inner = index % CHIPS
    distance = jnp.bitwise_xor(inner, chip)
    there = jnp.zeros_like(index)
    back = jnp.zeros_like(index)
    for bit in range(4):
        mask = jnp.where(side == 0, order[0][bit], order[1][bit])
        there = there + jnp.where((inner >> bit) & 1 == 1, mask, 0)
        back = back + jnp.where(jnp.bitwise_and(distance, mask) != 0, 1 << bit, 0)
    moved = jnp.where(index < 32, jnp.bitwise_xor(there, chip), back)
    return jnp.where(index < 64, moved, core)


def lane_blocks(x, starts, step):
    return [
        jnp.concatenate([x[:, k + h * step : k + h * step + LANES] for k in starts], axis=0)
        for h in (0, 1)
    ]


def whole_columns(core, own, other, blocks):
    halves = (jnp.where(core == 0, own, other), jnp.where(core == 0, other, own))
    return [[half[24 * b : 24 * b + 24] for b in range(blocks)] for half in halves]


def swap_halves(halves, core):
    own = jnp.where(core == 0, halves[0], halves[1])
    return own, core_swap(jnp.where(core == 0, halves[1], halves[0]))


def join_rows(own, other, core, blocks):
    shape = (blocks, own.shape[0] // blocks, LANES)
    return in_core_order(core, own.reshape(shape), other.reshape(shape), 1).reshape(-1, LANES)


def split_rows(piece, blocks):
    rows = piece.reshape(blocks, 2, 24, LANES).transpose(1, 0, 2, 3)
    return rows.reshape(2, blocks * 24, LANES)


def pack_extra(time_in, vectors, ints):
    rows = time_in.shape[0]
    filler = jnp.zeros((rows, 128), BF16)
    vec = lax.dynamic_update_slice(filler, vectors, (0, 0))
    num = lax.dynamic_update_slice(filler, ints[None, :], (0, 0))
    return jnp.concatenate([time_in, vec, num], axis=1)


def split_time(timestep, dataset):
    steps = timestep.reshape(-1)
    return jnp.concatenate([steps // 64, steps % 64, dataset.reshape(-1)]).astype(BF16)


def gather_all(x):
    return lax.all_gather(x, AXES, axis=0, tiled=True)


def shards(
    block_input,
    out_grad,
    timestep,
    dataset,
    lengths,
    norm1_gain,
    qkv_weight,
    out_weight,
    norm2_gain,
    up_weight,
    down_weight,
    time_in,
    time_out,
    data_embed,
    devices,
):
    flat = lax.axis_index(AXES)
    exchange = devices == 2 * CHIPS
    vectors = jnp.concatenate([norm1_gain[None], norm2_gain[None], data_embed.T], axis=0)
    numbers = split_time(timestep, dataset)
    count = numbers.shape[0] // 3
    micros, seqs, seq_len, width = block_input.shape
    tokens = micros * seqs * seq_len
    x_rows = block_input.reshape(tokens, width)
    grad_rows = out_grad.reshape(tokens, width)
    features = sinusoid(timestep.reshape(-1), time_in.shape[1] // 2).astype(BF16)
    if exchange:
        core = flat & 1
        chip = flat >> 1

        wide = lane_blocks(qkv_weight, (0, WIDTH, 2 * WIDTH), LANES)
        slim = lane_blocks(time_out, (0,), LANES)
        own, other = swap_halves(
            [jnp.concatenate([x, y], axis=0) for x, y in zip(wide, slim)], core
        )
        attention_piece = jnp.concatenate(
            [
                join_rows(own[:72], other[:72], core, 3),
                join_rows(own[72:], other[72:], core, 1),
                pack_extra(time_in, vectors, numbers),
            ],
            axis=0,
        )[None]
        near = [chip_swap(attention_piece, p) for p in (1, 2, 3)]
        up_weight, out_weight, down_weight, flat = lax.optimization_barrier(
            (up_weight, out_weight, down_weight, flat, attention_piece)
        )[:4]
        tab = position_table(flat >> 1, flat & 1, LINE_FIRST)
        down_tab = position_table(flat >> 1, flat & 1, LINE_LATER)
        wide = lane_blocks(up_weight, range(0, 4 * LANES, LANES), 4 * LANES)
        slim = lane_blocks(out_weight, (0,), LANES)
        own, other = swap_halves(
            [jnp.concatenate([x, y], axis=0) for x, y in zip(wide, slim)], core
        )
        up_piece = jnp.concatenate(
            [join_rows(own[:96], other[:96], core, 4), join_rows(own[96:], other[96:], core, 1)],
            axis=0,
        )[None]
        own, other = swap_halves(lane_blocks(down_weight, (0,), LANES), core)
        down_piece = join_rows(own, other, core, 1)[None]
        down_pair = jnp.concatenate([down_piece, chip_swap(down_piece, 1, LINE_LATER)], axis=0)
        ready = (up_piece, down_pair, tab, down_tab, features)
        line = after(jnp.concatenate([attention_piece] + near, axis=0), *ready)
        plane = chip_swap(line, 4)
        up_near = [chip_swap(after(up_piece, line), p) for p in (1, 2, 3)]
        held = jnp.concatenate([line, plane], axis=0)
        far = chip_swap(held, 8)
        up_line = jnp.concatenate([up_piece] + [after(x, held) for x in up_near], axis=0)
        far = after(far, up_line)
        attention_pieces = (held, far, core_swap(held), core_swap(far))
        up_plane = chip_swap(after(up_line, far), 4)
        down_near = [chip_swap(after(down_pair, up_line), p, LINE_LATER) for p in (2, 4, 6)]
        up_held = jnp.concatenate([up_line, up_plane], axis=0)
        up_far = chip_swap(up_held, 8)
    else:
        tab = jnp.concatenate(
            [jnp.tile(jnp.arange(CHIPS, dtype=jnp.int32), 4), jnp.zeros((8,), jnp.int32)]
        )
        down_tab = tab
        full_qkv = gather_all(qkv_weight).reshape(CHIPS, 48, 3, 2, LANES)
        full_out = gather_all(out_weight).reshape(CHIPS, 48, 2, LANES)
        full_up = gather_all(up_weight).reshape(CHIPS, 48, 2, 4, LANES)
        full_down = gather_all(down_weight).reshape(CHIPS, 192, 2, LANES)
        full_tin = gather_all(time_in).reshape(CHIPS, 2, 16, 128)
        full_tout = gather_all(time_out).reshape(CHIPS, 32, 2, LANES)
        full_vec = lax.all_gather(vectors, AXES, axis=1, tiled=True).reshape(4, CHIPS, 2, 24)
        numbers_all = gather_all(numbers[None])
        extra = jnp.zeros((CHIPS, 2, 16, LANES), BF16)
        extra = extra.at[:, :, :, :128].set(full_tin)
        extra = extra.at[:, :, 0:4, 128:152].set(full_vec.transpose(1, 2, 0, 3))
        attention_pieces = []
        down_pieces = []
        up_pieces = []
        for half in (0, 1):
            wide = full_qkv[:, :, :, half].transpose(0, 2, 1, 3).reshape(CHIPS, 144, LANES)
            whole = jnp.concatenate([wide, full_tout[:, :, half], extra[:, half]], axis=1)
            attention_pieces += [whole[:8], whole[8:]]
            down_pieces += [full_down[:8, :, half], full_down[8:, :, half]]
            wide = full_up[:, :, half].transpose(0, 2, 1, 3).reshape(CHIPS, 192, LANES)
            whole = jnp.concatenate([wide, full_out[:, :, half]], axis=1)
            up_pieces += [whole[:8], whole[8:]]

    arrivals = []
    if exchange:
        x_rows = after(x_rows, up_held)
        arrivals = [up_far, down_near]
    forward = attention_forward(tab, lengths, dataset, attention_pieces, x_rows, features)
    (normed, qkv, embed, vecs, seen, probs, att), arrivals = together(forward, arrivals)
    seen = seen[:, :, 0, : 3 * count].reshape(2 * CHIPS, 3 * count) if exchange else numbers_all
    steps = seen[:, :count] * 64 + seen[:, count : 2 * count].astype(F32)
    wave = sinusoid(steps.reshape(-1), time_in.shape[1] // 2).astype(BF16)
    wave = jnp.pad(wave.reshape(devices, count, -1), ((0, 0), (0, 16 - count), (0, 0)))
    wave = wave.reshape(devices * 16, -1)
    which = jnp.pad(seen[:, 2 * count :], ((0, 0), (0, 16 - count))).reshape(-1)
    place = jnp.tile(jnp.arange(16), devices)
    hot = jnp.stack(
        [(place < count) & (which == 0), (place < count) & (which == 1), place == 8, place == 9]
    )
    hot = jnp.pad(hot.astype(BF16), ((0, 12), (0, 0)))
    pre = dot_last(wave, time_in)
    gate = 1.0 / (1.0 + jnp.exp(-pre))
    hidden = (pre * gate).astype(BF16)
    slope_pre = gate * (1.0 + pre * (1.0 - gate))
    if exchange:
        up_far, down_near = arrivals
        up_pieces = (up_held, up_far, core_swap(up_held), core_swap(up_far))
        down_held = jnp.concatenate([down_pair] + down_near, axis=0)
        att, wave, hot, hidden, slope_pre, down_held = lax.optimization_barrier(
            (att, wave, hot, hidden, slope_pre, down_held)
        )
        arrivals = chip_swap(down_held, 8, LINE_LATER)
    forward = up_forward(tab, up_pieces, att, x_rows, grad_rows, embed, vecs)
    (mid, two, act, slope, down_theirs), arrivals = together(forward, arrivals)
    if exchange:
        down_far = arrivals
        down_sum = Scatter(down_theirs)
        arrivals = [core_swap(down_held), core_swap(down_far)], down_sum.swap()
    down_mine, arrivals = together(down_grad(tab, act, grad_rows), arrivals)
    if exchange:
        down_pieces = (down_held, down_far, *arrivals[0])
        down_sum.land(arrivals[1], down_mine)
        slope = after(slope, *down_sum.send())
        arrivals = down_sum.fly()
    backward = mlp_backward(
        tab, down_tab, up_pieces, down_pieces, two, att, slope, grad_rows, mid, vecs
    )
    backward, arrivals = together(backward, arrivals)
    grad_mid, branch, grad_up, grad_att, gain_two, up_theirs = backward
    if exchange:
        down_sum.land(arrivals)
        up_sum = Scatter(up_theirs)
        grad_up = after(grad_up, *down_sum.send())
        arrivals = down_sum.fly(), up_sum.swap()
    up_mine, arrivals = together(up_grad(tab, att, branch, two, grad_up), arrivals)
    if exchange:
        down_sum.land(arrivals[0])
        up_sum.land(arrivals[1], up_mine)
        grad_att = after(grad_att, *up_sum.send(), *down_sum.send())
        arrivals = up_sum.fly(), down_sum.fly()
    backward = attention_backward(tab, normed, qkv, probs, grad_att)
    (grad_qkv, att_theirs), arrivals = together(backward, arrivals)
    if exchange:
        up_sum.land(arrivals[0])
        down_sum.land(arrivals[1])
        down_total = down_sum.total()
        att_sum = Scatter(att_theirs)
        grad_qkv = after(grad_qkv, *up_sum.send(), down_total)
        arrivals = up_sum.fly(), att_sum.swap()
    att_mine, arrivals = together(qkv_grad(tab, normed, grad_qkv), arrivals)
    if exchange:
        up_sum.land(arrivals[0])
        att_sum.land(arrivals[1], att_mine)
        grad_qkv = after(grad_qkv, *att_sum.send(), *up_sum.send())
        arrivals = att_sum.fly(), up_sum.fly()
    backward = input_backward(
        tab, attention_pieces, grad_qkv, x_rows, embed, vecs, grad_mid, gain_two
    )
    (grad_input, small), arrivals = together(backward, arrivals)

    small = small.astype(BF16)[None]
    if exchange:
        att_sum.land(arrivals[0])
        up_sum.land(arrivals[1])
        mid = after(mid, *att_sum.send(), small)
        arrivals = att_sum.fly(), [chip_swap(small, p) for p in (1, 2, 3)]
    result, arrivals = together(block_result(down_tab, down_pieces, act, mid), arrivals)
    if exchange:
        att_sum.land(arrivals[0])
        small_line = jnp.concatenate([small] + arrivals[1], axis=0)
        small_line = after(small_line, *att_sum.send())
        held = gather_plane(small_line)
        far = chip_swap(held, 8)
        every = (held, far, core_swap(held), core_swap(far))
        att_sum.land(att_sum.fly())
    else:
        every = (gather_all(small),)
    grad_tin, grad_tout, sums = time_grads(tab, every, wave, hot, hidden, slope_pre, time_out)
    own_cols = norm1_gain.shape[0]
    sums = lax.dynamic_slice_in_dim(sums, flat * own_cols, own_cols, 1)

    if exchange:
        own, other = swap_halves(after(down_total, result).reshape(2, 96, LANES), core)
        grad_down = in_core_order(core, own, other, 1)
        piece = after(up_sum.total(), result)
        out_rows = piece[192:].reshape(2, 24, LANES)
        own, other = swap_halves(
            jnp.concatenate([split_rows(piece[:192], 4), out_rows], axis=1), core
        )
        left, right = whole_columns(core, own, other, 5)
        grad_up_weight = jnp.concatenate(left[:4] + right[:4], axis=1)
        grad_out = jnp.concatenate([left[4], right[4]], axis=1)
        own, other = swap_halves(split_rows(att_sum.total(), 3), core)
        left, right = whole_columns(core, own, other, 3)
        grad_qkv_weight = jnp.concatenate(
            [side[sec] for sec in range(3) for side in (left, right)], axis=1
        )
    else:
        scatter = partial(lax.psum_scatter, axis_name=AXES, scatter_dimension=0, tiled=True)
        both = jnp.stack([down_mine, down_theirs]).astype(F32)
        grad_down = scatter(both.transpose(1, 2, 0, 3).reshape(FF, WIDTH))
        both = jnp.stack([up_mine, up_theirs]).astype(F32)
        grad_out = scatter(both[:, :, 192:].transpose(1, 2, 0, 3).reshape(WIDTH, WIDTH))
        both = both[:, :, :192].reshape(2, CHIPS, 4, 48, LANES)
        grad_up_weight = scatter(both.transpose(1, 3, 0, 2, 4).reshape(WIDTH, FF))
        both = jnp.stack([att_mine, att_theirs]).astype(F32).reshape(2, CHIPS, 3, 48, LANES)
        grad_qkv_weight = scatter(both.transpose(1, 3, 2, 0, 4).reshape(WIDTH, 3 * WIDTH))

    return (
        result.reshape(block_input.shape),
        grad_input.reshape(block_input.shape),
        sums[2],
        grad_qkv_weight,
        grad_out,
        sums[3],
        grad_up_weight,
        grad_down,
        grad_tin,
        grad_tout,
        sums[:2].T,
    )


def solution(mesh):
    devices = mesh.shape["dp"] * mesh.shape["fsdp"]
    seq_spec = P(None, AXES, None, None)
    int_spec = P(None, AXES)
    row_spec = P(AXES, None)
    in_specs = (seq_spec, seq_spec, int_spec, int_spec, int_spec, P(AXES), row_spec, row_spec, P(AXES))
    in_specs = in_specs + (row_spec,) * 5
    out_specs = (seq_spec, seq_spec, P(AXES), row_spec, row_spec, P(AXES)) + (row_spec,) * 5
    return jax.shard_map(
        partial(shards, devices=devices),
        mesh=mesh,
        in_specs=in_specs,
        out_specs=out_specs,
        check_vma=False,
    )
```

time: 298 us -> 269 us (0.903)
  waiting for transfers between devices: 82.7 us -> 52.2 us
  starting transfers between devices: 37.5 us -> 56.4 us
  between operations: 14.4 us -> 1.62 us
  other arithmetic: 20.8 us -> 17.1 us
    ppermute x25 -> x35, waiting for transfers between devices: 79 us -> 49 us  [chip_swap(): lax.ppermute(x, AXES, [(i, i ^ far[i & 1]) for i in range(2 * CHIPS)])]
    ppermute x25 -> x35, starting transfers between devices: 35 us -> 53 us  [chip_swap(): lax.ppermute(x, AXES, [(i, i ^ far[i & 1]) for i in range(2 * CHIPS)])]
    unnamed x34 -> x77, local copies, waits for them, and re-layouts: 2.19 us -> 8.41 us
    convert_element_type x8 -> x9, other arithmetic: 12.7 us -> 6.95 us  [send(): self.sent = [self.sum(p, p + size).astype(BF16) for p in self.at]]
    reshape x7 -> x0, local copies, waits for them, and re-layouts: 3.3 us -> none  [the longest x2 0.94 us: shards(): qkv_weight.reshape(24, 3, 2, LANES).transpose(2, 1, 0, 3)]
    pallas_call x9 -> x10, Pallas kernels: 121 us -> 123 us  [run(): call(*[x if x.dtype == jnp.int32 else pltpu.with_memory_space_constraint(...]
  transfers between devices with their start and end apart: 39 -> 52, of which waited for: 17 -> 17; matrix products, arithmetic and copies ran while one was open for 13% -> 8% of each run, Pallas kernels for 38% -> 45%
where the time goes in v3:
time: 269 us; the launch traced here: 268 us
  Pallas kernels  123 us (46%)
  starting transfers between devices  56.4 us (21%)
  waiting for transfers between devices  52.2 us (19%)
  other arithmetic  17.1 us (6%)
  local copies, waits for them, and re-layouts  16.8 us (6%)
    pallas_call x10, Pallas kernels, run(): call(*[x if x.dtype == jnp.int32 else pltpu.with_memory_space_constraint(...  123 us
    ppermute x35, starting transfers between devices, chip_swap(): lax.ppermute(x, AXES, [(i, i ^ far[i & 1]) for i in range(2 * CHIPS)])  53 us
    ppermute x35, waiting for transfers between devices, chip_swap(): lax.ppermute(x, AXES, [(i, i ^ far[i & 1]) for i in range(2 * CHIPS)])  49 us
    unnamed x77, local copies, waits for them, and re-layouts  8.41 us
    convert_element_type x9, other arithmetic, send(): self.sent = [self.sum(p, p + size).astype(BF16) for p in self.at]  6.95 us
  transfers between devices with their start and end apart: 52, of which 17 were waited for; matrix products, arithmetic and copies ran while one was open for 8% of the time, Pallas kernels for 45%

profile of v3, /device:TPU:0, one launch (start us, length us, event | category | flops | bytes accessed | tf_op | source)
XLA Modules:
  0.0 268.1 jit_solution(16159259602678558306)
XLA Ops:
  6.7 4.7 %collective-permute-start.3 = (bf16[1,192,384]{2,1,0:T(8,128)(2,1)S(1)}, bf16[1,192,384]{2,1,0:T(8,128)(2,1)S(1)}, u32[]{:S(2)}, u32[]{:S(2)}) collective-permute-start(bf16[1,192,384]{2,1,0:T(8,128)(2,1)S(1)} %maximum_bitcast_fusion.1), channel_id=1, source_target_pairs={{0,6},{1,7},{2,4},{3,5},{4,2},{5,3},{6,0},{7,1},{8,14},{9,15},{10,... | collective-permute-start | bytes 442376 | tf_op jit(solution)/shard_map/ppermute | solution.py:54
  16.3 3.9 %collective-permute-done.2 = bf16[1,192,384]{2,1,0:T(8,128)(2,1)S(1)} collective-permute-done((bf16[1,192,384]{2,1,0:T(8,128)(2,1)S(1)}, bf16[1,192,384]{2,1,0:T(8,128)(2,1)S(1)}, u32[]{:S(2)}, u32[]{:S(2)}) %collective-permute-start.2) | collective-permute-done | bytes 147488 | tf_op jit(solution)/shard_map/ppermute | solution.py:54
  20.2 4.4 %collective-permute-done.1 = bf16[1,192,384]{2,1,0:T(8,128)(2,1)S(1)} collective-permute-done((bf16[1,192,384]{2,1,0:T(8,128)(2,1)S(1)}, bf16[1,192,384]{2,1,0:T(8,128)(2,1)S(1)}, u32[]{:S(2)}, u32[]{:S(2)}) %collective-permute-start.1) | collective-permute-done | bytes 147488 | tf_op jit(solution)/shard_map/ppermute | solution.py:54
  26.3 8.3 %collective-permute-done.7 = bf16[4,192,384]{2,1,0:T(8,128)(2,1)S(1)} collective-permute-done((bf16[4,192,384]{2,1,0:T(8,128)(2,1)S(1)}, bf16[4,192,384]{2,1,0:T(8,128)(2,1)S(1)}, u32[]{:S(2)}, u32[]{:S(2)}) %collective-permute-start.7) | collective-permute-done | bytes 589856 | tf_op jit(solution)/shard_map/ppermute | solution.py:54
  36.3 2.5 collective-permute-start.11
  40.7 5.0 %collective-permute-done.11 = bf16[1,240,384]{2,1,0:T(8,128)(2,1)S(1)} collective-permute-done((bf16[1,240,384]{2,1,0:T(8,128)(2,1)S(1)}, bf16[1,240,384]{2,1,0:T(8,128)(2,1)S(1)}, u32[]{:S(2)}, u32[]{:S(2)}) %collective-permute-start.11) | collective-permute-done | bytes 184352 | tf_op jit(solution)/shard_map/ppermute | solution.py:54
  45.7 4.0 %collective-permute-done.10 = bf16[1,240,384]{2,1,0:T(8,128)(2,1)S(1)} collective-permute-done((bf16[1,240,384]{2,1,0:T(8,128)(2,1)S(1)}, bf16[1,240,384]{2,1,0:T(8,128)(2,1)S(1)}, u32[]{:S(2)}, u32[]{:S(2)}) %collective-permute-start.10) | collective-permute-done | bytes 184352 | tf_op jit(solution)/shard_map/ppermute | solution.py:54
  49.7 3.1 %collective-permute-done.9 = bf16[1,240,384]{2,1,0:T(8,128)(2,1)S(1)} collective-permute-done((bf16[1,240,384]{2,1,0:T(8,128)(2,1)S(1)}, bf16[1,240,384]{2,1,0:T(8,128)(2,1)S(1)}, u32[]{:S(2)}, u32[]{:S(2)}) %collective-permute-start.9) | collective-permute-done | bytes 184352 | tf_op jit(solution)/shard_map/ppermute | solution.py:54
  57.1 7.3 %collective-permute-done.14 = bf16[4,240,384]{2,1,0:T(8,128)(2,1)S(1)} collective-permute-done((bf16[4,240,384]{2,1,0:T(8,128)(2,1)S(1)}, bf16[4,240,384]{2,1,0:T(8,128)(2,1)S(1)}, u32[]{:S(2)}, u32[]{:S(2)}) %collective-permute-start.14) | collective-permute-done | bytes 737312 | tf_op jit(solution)/shard_map/ppermute | solution.py:54
  71.6 16.7 %attention_forward.1 = (bf16[1024,768]{1,0:T(8,128)(2,1)}, bf16[1024,2304]{1,0:T(8,128)(2,1)}, f32[8,768]{1,0:T(8,128)}, f32[16,768]{1,0:T(8,128)}, bf16[2,16,16...) custom-call(s32[72]{0:T(128)S(1)} %compare_select_fusion.23.tab, ...), custom_call_target="tpu_custom_call" | custom-call | flops 8000000000 | bytes 20000000 | tf_op jit(solution)/shard_map/attention_forward/pallas_call | solution.py:133
  96.8 21.4 %up_forward.1 = (f32[1024,768]{1,0:T(8,128)}, bf16[1024,768]{1,0:T(8,128)(2,1)}, bf16[1024,3072]{1,0:T(8,128)(2,1)}, bf16[1024,3072]{1,0:T(8,128)(2,1)}, bf16[16,192,384]{2,1,0:T(8,128)(2,1)S(1)}) custom-call(s32[72]{0:T(128)S(1)} %compare_select_fusion.23.tab, bf16[8,240,384]{2,1,0:T(8,128)(2,1)} %constant_dynamic-update-slice_fusion.12.u_a, ...), custom_call_target="tpu_custom_call" | custom-call | flops 10000000000 | bytes 30000000 | tf_op jit(solution)/shard_map/up_forward/pallas_call | solution.py:133
  119.0 6.5 %down_grad.1 = bf16[16,192,384]{2,1,0:T(8,128)(2,1)S(1)} custom-call(s32[72]{0:T(128)S(1)} %compare_select_fusion.23.tab, bf16[1024,3072]{1,0:T(8,128)(2,1)} %get-tuple-element.151.act_ref, bf16[1024,768]{1,0:T(8,128)(2,1)} %bitcast.82), custom_call_target="tpu_custom_call" | custom-call | flops 3000000000 | bytes 10000000 | tf_op jit(solution)/shard_map/down_grad/pallas_call | solution.py:133
  128.4 29.0 %mlp_backward.1 = (f32[1024,768]{1,0:T(8,128)}, bf16[1024,768]{1,0:T(8,128)(2,1)}, bf16[1024,3072]{1,0:T(8,128)(2,1)}, bf16[1024,768]{1,0:T(8,128)(2,1)}, f32[1,...) custom-call(s32[72]{0:T(128)S(1)} %compare_select_fusion.23.tab, s32[72]{0:T(128)S(1)} %compare_select_fusion.24.down_tab.tab, ...), custom_call_target="tpu_custom_call" | custom-call | flops 17999998976 | bytes 50000000 | tf_op jit(solution)/shard_map/mlp_backward/pallas_call | solution.py:133
  159.1 6.7 %up_grad.1 = bf16[16,240,384]{2,1,0:T(8,128)(2,1)S(1)} custom-call(s32[72]{0:T(128)S(1)} %compare_select_fusion.23.tab, bf16[1024,768]{1,0:T(8,128)(2,1)} %get-tuple-element.142.att_ref.att_hbm, bf16[1024,768]{1,0:T(8,128)(2,1)} %get-tuple-element.171.branch_hbm, bf16[1024,768]{1,0:T(8,128)(2,1)} %get-tuple-element.159.two_hbm.two_ref, ...), custom_call_target="tpu_custom_call" | custom-call | flops 3200000000 | bytes 11000000 | tf_op jit(solution)/shard_map/up_grad/pallas_call | solution.py:133
  169.7 5.1 %collective-permute-start.29 = (bf16[1,192,384]{2,1,0:T(8,128)(2,1)S(1)}, bf16[1,192,384]{2,1,0:T(8,128)(2,1)S(1)}, u32[]{:S(2)}, u32[]{:S(2)}) collective-permute-start(bf16[1,192,384]{2,1,0:T(8,128)(2,1)S(1)} %get-tuple-element.226), channel_id=1, source_target_pairs={{0,4},{1,5},{2,6},{3,7},{4,0},{5,1},{6,2},{7,3},{8,12},{9,13},{10,... | collective-permute-start | bytes 442376 | tf_op jit(solution)/shard_map/ppermute | solution.py:54
  177.2 12.3 %attention_backward.1 = (bf16[1024,2304]{1,0:T(8,128)(2,1)}, bf16[16,144,384]{2,1,0:T(8,128)(2,1)S(1)}) custom-call(s32[72]{0:T(128)S(1)} %compare_select_fusion.23.tab, bf16[1024,768]{1,0:T(8,128)(2,1)} %get-tuple-element.156.normed_hbm.normed_ref, bf16[1024,2304]{1,0:T(8,128)(2,1)} %get-tuple-element.157.qkv_ref, ...), custom_call_target="tpu_custom_call" | custom-call | flops 11000000512 | bytes 22000000 | tf_op jit(solution)/shard_map/attention_backward/pallas_call | solution.py:133
  192.3 5.1 %qkv_grad.1 = bf16[16,144,384]{2,1,0:T(8,128)(2,1)S(1)} custom-call(s32[72]{0:T(128)S(1)} %compare_select_fusion.23.tab, bf16[1024,768]{1,0:T(8,128)(2,1)} %get-tuple-element.156.normed_hbm.normed_ref, bf16[1024,2304]{1,0:T(8,128)(2,1)} %get-tuple-element.192.grad_qkv_ref), custom_call_target="tpu_custom_call" | custom-call | flops 2000000000 | bytes 7000000 | tf_op jit(solution)/shard_map/qkv_grad/pallas_call | solution.py:133
  197.4 4.8 %collective-permute-done.32 = bf16[4,240,384]{2,1,0:T(8,128)(2,1)S(1)} collective-permute-done((bf16[4,240,384]{2,1,0:T(8,128)(2,1)S(1)}, bf16[4,240,384]{2,1,0:T(8,128)(2,1)S(1)}, u32[]{:S(2)}, u32[]{:S(2)}) %collective-permute-start.32) | collective-permute-done | bytes 737312 | tf_op jit(solution)/shard_map/ppermute | solution.py:54
  207.3 2.9 %collective-permute-start.35 = (bf16[1,240,384]{2,1,0:T(8,128)(2,1)S(1)}, bf16[1,240,384]{2,1,0:T(8,128)(2,1)S(1)}, u32[]{:S(2)}, u32[]{:S(2)}) collective-permute-start(bf16[1,240,384]{2,1,0:T(8,128)(2,1)S(1)} %get-tuple-element.223), channel_id=1, source_target_pairs={{0,4},{1,5},{2,6},{3,7},{4,0},{5,1},{6,2},{7,3},{8,12},{9,13},{10,... | collective-permute-start | bytes 552968 | tf_op jit(solution)/shard_map/ppermute | solution.py:54
  212.5 10.7 %input_backward.1 = (bf16[1024,768]{1,0:T(8,128)(2,1)}, f32[16,768]{1,0:T(8,128)}) custom-call(s32[72]{0:T(128)S(1)} %compare_select_fusion.23.tab, bf16[8,192,384]{2,1,0:T(8,128)(2,1)} %copy-done.11, bf16[8,192,384]{2,1,0:T(8,128)(2,1)} %collective-permute-done.8.g_b, bf16[8,192,384]{2,1,0:T(8,128)(2,1)} %collective-permute-done.12.g_c, ...), custom_call_target="tpu_custom_call" | custom-call | flops 4000000000 | bytes 18000000 | tf_op jit(solution)/shard_map/input_backward/pallas_call | solution.py:133
  226.5 3.2 %collective-permute-start.39 = (bf16[1,16,768]{2,1,0:T(8,128)(2,1)S(1)}, bf16[1,16,768]{2,1,0:T(8,128)(2,1)S(1)}, u32[]{:S(2)}, u32[]{:S(2)}) collective-permute-start(bf16[1,16,768]{2,1,0:T(8,128)(2,1)S(1)} %convert_bitcast_fusion), channel_id=1, source_target_pairs={{0,4},{1,5},{2,6},{3,7},{4,0},{5,1},{6,2},{7,3},{8,12},{9,13},{10,... | collective-permute-start | bytes 73736 | tf_op jit(solution)/shard_map/ppermute | solution.py:54
  231.2 10.9 %block_result.1 = bf16[1024,768]{1,0:T(8,128)(2,1)} custom-call(s32[72]{0:T(128)S(1)} %compare_select_fusion.24.down_tab.tab, bf16[8,192,384]{2,1,0:T(8,128)(2,1)} %constant_dynamic-update-slice_fusion.17.d_a, bf16[8,192,384]{2,1,0:T(8,128)(2,1)} %copy-done.23, bf16[8,192,384]{2,1,0:T(8,128)(2,1)} %copy-done.24, bf16[8,192,384]{2,1,0:T(8,128)(2,1)} %copy-done.25, ...), custom_call_target="tpu_custom_call" | custom-call | flops 5000000000 | bytes 16000000 | tf_op jit(solution)/shard_map/block_result/pallas_call | solution.py:133
  249.9 3.8 %collective-permute-done.42 = bf16[4,16,768]{2,1,0:T(8,128)(2,1)S(1)} collective-permute-done((bf16[4,16,768]{2,1,0:T(8,128)(2,1)S(1)}, bf16[4,16,768]{2,1,0:T(8,128)(2,1)S(1)}, u32[]{:S(2)}, u32[]{:S(2)}) %collective-permute-start.42) | collective-permute-done | bytes 98336 | tf_op jit(solution)/shard_map/ppermute | solution.py:54
  261.6 3.7 %time_grads.1 = (f32[16,128]{1,0:T(8,128)}, f32[16,768]{1,0:T(8,128)}, f32[16,768]{1,0:T(8,128)}) custom-call(s32[72]{0:T(128)S(1)} %compare_select_fusion.23.tab, bf16[8,16,768]{2,1,0:T(8,128)(2,1)} %copy-done.10, bf16[8,16,768]{2,1,0:T(8,128)(2,1)} %copy-done.12, bf16[8,16,768]{2,1,0:T(8,128)(2,1)} %copy-done.13, bf16[8,16,768]{2,1,0:T(8,128)(2,1)} %copy-done.14, ...), custom_call_target="tpu_custom_call" | custom-call | flops 50000000 | bytes 2000000 | tf_op jit(solution)/shard_map/time_grads/pallas_call | solution.py:133
  (249 shorter events, 80.3 us)
Async XLA Ops:
  11.4 13.1 %collective-permute-start.1 = (bf16[1,192,384]{2,1,0:T(8,128)(2,1)S(1)}, bf16[1,192,384]{2,1,0:T(8,128)(2,1)S(1)}, u32[]{:S(2)}, u32[]{:S(2)}) collective-permute-start(bf16[1,192,384]{2,1,0:T(8,128)(2,1)S(1)} %maximum_bitcast_fusion.1), channel_id=1, source_target_pairs={{0,4},{1,5},{2,6},{3,7},{4,0},{5,1},{6,2},{7,3},{8,12},{9,13},{10,... | collective-permute-start | bytes 442376 | tf_op jit(solution)/shard_map/ppermute | solution.py:54
  34.8 18.2 %collective-permute-start.8 = (bf16[8,192,384]{2,1,0:T(8,128)(2,1)S(1)}, bf16[8,192,384]{2,1,0:T(8,128)(2,1)}, u32[]{:S(2)}, u32[]{:S(2)}) collective-permute-start(bf16[8,192,384]{2,1,0:T(8,128)(2,1)S(1)} %constant_dynamic-update-slice_fusion.10.g_a), channel_id=1, source_target_pairs={{0,8},{1,17},{2,10},{3,19},{4,12},{5,21},{6,14},{7,23},{8,0},{9,25... | collective-permute-start | bytes 3538952 | tf_op jit(solution)/shard_map/ppermute | solution.py:54
  38.8 14.0 %collective-permute-start.9 = (bf16[1,240,384]{2,1,0:T(8,128)(2,1)S(1)}, bf16[1,240,384]{2,1,0:T(8,128)(2,1)S(1)}, u32[]{:S(2)}, u32[]{:S(2)}) collective-permute-start(bf16[1,240,384]{2,1,0:T(8,128)(2,1)S(1)} %maximum_bitcast_fusion), channel_id=1, source_target_pairs={{0,4},{1,5},{2,6},{3,7},{4,0},{5,1},{6,2},{7,3},{8,12},{9,13},{10,... | collective-permute-start | bytes 552968 | tf_op jit(solution)/shard_map/ppermute | solution.py:54
  54.5 15.6 %collective-permute-start.12 = (bf16[8,192,384]{2,1,0:T(8,128)(2,1)S(1)}, bf16[8,192,384]{2,1,0:T(8,128)(2,1)}, u32[]{:S(2)}, u32[]{:S(2)}) collective-permute-start(bf16[8,192,384]{2,1,0:T(8,128)(2,1)S(1)} %constant_dynamic-update-slice_fusion.10.g_a), channel_id=1, source_target_pairs={{0,1},{1,0},{2,3},{3,2},{4,5},{5,4},{6,7},{7,6},{8,9},{9,8},{10,11... | collective-permute-start | bytes 3538952 | tf_op jit(solution)/shard_map/ppermute | solution.py:49
  54.6 17.1 %collective-permute-start.13 = (bf16[8,192,384]{2,1,0:T(8,128)(2,1)}, bf16[8,192,384]{2,1,0:T(8,128)(2,1)}, u32[]{:S(2)}, u32[]{:S(2)}) collective-permute-start(bf16[8,192,384]{2,1,0:T(8,128)(2,1)} %collective-permute-done.8.g_b), channel_id=1, source_target_pairs={{0,1},{1,0},{2,3},{3,2},{4,5},{5,4},{6,7},{7,6},{8,9},{9,8},{10,11... | collective-permute-start | bytes 3538952 | tf_op jit(solution)/shard_map/ppermute | solution.py:49
  65.4 23.0 %collective-permute-start.15 = (bf16[8,240,384]{2,1,0:T(8,128)(2,1)}, bf16[8,240,384]{2,1,0:T(8,128)(2,1)}, u32[]{:S(2)}, u32[]{:S(2)}) collective-permute-start(bf16[8,240,384]{2,1,0:T(8,128)(2,1)} %constant_dynamic-update-slice_fusion.12.u_a), channel_id=1, source_target_pairs={{0,8},{1,17},{2,10},{3,19},{4,12},{5,21},{6,14},{7,23},{8,0},{9,25... | collective-permute-start | bytes 4423688 | tf_op jit(solution)/shard_map/ppermute | solution.py:54
  67.2 21.1 %collective-permute-start.16 = (bf16[2,192,384]{2,1,0:T(8,128)(2,1)S(1)}, bf16[2,192,384]{2,1,0:T(8,128)(2,1)S(1)}, u32[]{:S(2)}, u32[]{:S(2)}) collective-permute-start(bf16[2,192,384]{2,1,0:T(8,128)(2,1)S(1)} %pad_maximum_fusion.2), channel_id=1, source_target_pairs={{0,4},{1,5},{2,6},{3,7},{4,0},{5,1},{6,2},{7,3},{8,12},{9,13},{10,... | collective-permute-start | bytes 884744 | tf_op jit(solution)/shard_map/ppermute | solution.py:54
  67.8 20.5 %collective-permute-start.17 = (bf16[2,192,384]{2,1,0:T(8,128)(2,1)S(1)}, bf16[2,192,384]{2,1,0:T(8,128)(2,1)S(1)}, u32[]{:S(2)}, u32[]{:S(2)}) collective-permute-start(bf16[2,192,384]{2,1,0:T(8,128)(2,1)S(1)} %pad_maximum_fusion.2), channel_id=1, source_target_pairs={{0,2},{1,3},{2,0},{3,1},{4,6},{5,7},{6,4},{7,5},{8,10},{9,11},{10,... | collective-permute-start | bytes 884744 | tf_op jit(solution)/shard_map/ppermute | solution.py:54
  70.1 18.2 %collective-permute-start.18 = (bf16[2,192,384]{2,1,0:T(8,128)(2,1)S(1)}, bf16[2,192,384]{2,1,0:T(8,128)(2,1)S(1)}, u32[]{:S(2)}, u32[]{:S(2)}) collective-permute-start(bf16[2,192,384]{2,1,0:T(8,128)(2,1)S(1)} %pad_maximum_fusion.2), channel_id=1, source_target_pairs={{0,6},{1,7},{2,4},{3,5},{4,2},{5,3},{6,0},{7,1},{8,14},{9,15},{10,... | collective-permute-start | bytes 884744 | tf_op jit(solution)/shard_map/ppermute | solution.py:54
  71.6 24.1 %collective-permute-start.19 = (bf16[8,240,384]{2,1,0:T(8,128)(2,1)}, bf16[8,240,384]{2,1,0:T(8,128)(2,1)}, u32[]{:S(2)}, u32[]{:S(2)}) collective-permute-start(bf16[8,240,384]{2,1,0:T(8,128)(2,1)} %constant_dynamic-update-slice_fusion.12.u_a), channel_id=1, source_target_pairs={{0,1},{1,0},{2,3},{3,2},{4,5},{5,4},{6,7},{7,6},{8,9},{9,8},{10,11... | collective-permute-start | bytes 4423688 | tf_op jit(solution)/shard_map/ppermute | solution.py:49
  94.6 23.7 %collective-permute-start.21 = (bf16[8,192,384]{2,1,0:T(8,128)(2,1)}, bf16[8,192,384]{2,1,0:T(8,128)(2,1)S(1)}, u32[]{:S(2)}, u32[]{:S(2)}) collective-permute-start(bf16[8,192,384]{2,1,0:T(8,128)(2,1)} %constant_dynamic-update-slice_fusion.17.d_a), channel_id=1, source_target_pairs={{0,8},{1,17},{2,10},{3,19},{4,12},{5,21},{6,14},{7,23},{8,0},{9,25... | collective-permute-start | bytes 3538952 | tf_op jit(solution)/shard_map/ppermute | solution.py:54
  127.5 30.0 %collective-permute-start.25 = (bf16[8,192,384]{2,1,0:T(8,128)(2,1)S(1)}, bf16[8,192,384]{2,1,0:T(8,128)(2,1)S(1)}, u32[]{:S(2)}, u32[]{:S(2)}) collective-permute-start(bf16[8,192,384]{2,1,0:T(8,128)(2,1)S(1)} %add_convert_fusion.1), channel_id=1, source_target_pairs={{0,8},{1,17},{2,10},{3,19},{4,12},{5,21},{6,14},{7,23},{8,0},{9,25... | collective-permute-start | bytes 3538952 | tf_op jit(solution)/shard_map/ppermute | solution.py:54
  168.3 21.4 %collective-permute-start.28 = (bf16[8,240,384]{2,1,0:T(8,128)(2,1)S(1)}, bf16[8,240,384]{2,1,0:T(8,128)(2,1)S(1)}, u32[]{:S(2)}, u32[]{:S(2)}) collective-permute-start(bf16[8,240,384]{2,1,0:T(8,128)(2,1)S(1)} %add_convert_fusion), channel_id=1, source_target_pairs={{0,8},{1,17},{2,10},{3,19},{4,12},{5,21},{6,14},{7,23},{8,0},{9,25... | collective-permute-start | bytes 4423688 | tf_op jit(solution)/shard_map/ppermute | solution.py:54
  169.7 19.8 %collective-permute-start.29 = (bf16[1,192,384]{2,1,0:T(8,128)(2,1)S(1)}, bf16[1,192,384]{2,1,0:T(8,128)(2,1)S(1)}, u32[]{:S(2)}, u32[]{:S(2)}) collective-permute-start(bf16[1,192,384]{2,1,0:T(8,128)(2,1)S(1)} %get-tuple-element.226), channel_id=1, source_target_pairs={{0,4},{1,5},{2,6},{3,7},{4,0},{5,1},{6,2},{7,3},{8,12},{9,13},{10,... | collective-permute-start | bytes 442376 | tf_op jit(solution)/shard_map/ppermute | solution.py:54
  174.9 14.7 %collective-permute-start.30 = (bf16[1,192,384]{2,1,0:T(8,128)(2,1)S(1)}, bf16[1,192,384]{2,1,0:T(8,128)(2,1)S(1)}, u32[]{:S(2)}, u32[]{:S(2)}) collective-permute-start(bf16[1,192,384]{2,1,0:T(8,128)(2,1)S(1)} %get-tuple-element.225), channel_id=1, source_target_pairs={{0,2},{1,3},{2,0},{3,1},{4,6},{5,7},{6,4},{7,5},{8,10},{9,11},{10,... | collective-permute-start | bytes 442376 | tf_op jit(solution)/shard_map/ppermute | solution.py:54
  174.9 14.7 %collective-permute-start.31 = (bf16[1,192,384]{2,1,0:T(8,128)(2,1)S(1)}, bf16[1,192,384]{2,1,0:T(8,128)(2,1)S(1)}, u32[]{:S(2)}, u32[]{:S(2)}) collective-permute-start(bf16[1,192,384]{2,1,0:T(8,128)(2,1)S(1)} %get-tuple-element.224), channel_id=1, source_target_pairs={{0,6},{1,7},{2,4},{3,5},{4,2},{5,3},{6,0},{7,1},{8,14},{9,15},{10,... | collective-permute-start | bytes 442376 | tf_op jit(solution)/shard_map/ppermute | solution.py:54
  204.0 19.6 %collective-permute-start.34 = (bf16[8,144,384]{2,1,0:T(8,128)(2,1)}, bf16[8,144,384]{2,1,0:T(8,128)(2,1)}, u32[]{:S(2)}, u32[]{:S(2)}) collective-permute-start(bf16[8,144,384]{2,1,0:T(8,128)(2,1)} %add_convert_fusion.2), channel_id=1, source_target_pairs={{0,8},{1,17},{2,10},{3,19},{4,12},{5,21},{6,14},{7,23},{8,0},{9,25... | collective-permute-start | bytes 2654216 | tf_op jit(solution)/shard_map/ppermute | solution.py:54
  207.3 16.0 %collective-permute-start.35 = (bf16[1,240,384]{2,1,0:T(8,128)(2,1)S(1)}, bf16[1,240,384]{2,1,0:T(8,128)(2,1)S(1)}, u32[]{:S(2)}, u32[]{:S(2)}) collective-permute-start(bf16[1,240,384]{2,1,0:T(8,128)(2,1)S(1)} %get-tuple-element.223), channel_id=1, source_target_pairs={{0,4},{1,5},{2,6},{3,7},{4,0},{5,1},{6,2},{7,3},{8,12},{9,13},{10,... | collective-permute-start | bytes 552968 | tf_op jit(solution)/shard_map/ppermute | solution.py:54
  210.1 13.1 %collective-permute-start.36 = (bf16[1,240,384]{2,1,0:T(8,128)(2,1)S(1)}, bf16[1,240,384]{2,1,0:T(8,128)(2,1)S(1)}, u32[]{:S(2)}, u32[]{:S(2)}) collective-permute-start(bf16[1,240,384]{2,1,0:T(8,128)(2,1)S(1)} %get-tuple-element.222), channel_id=1, source_target_pairs={{0,2},{1,3},{2,0},{3,1},{4,6},{5,7},{6,4},{7,5},{8,10},{9,11},{10,... | collective-permute-start | bytes 552968 | tf_op jit(solution)/shard_map/ppermute | solution.py:54
  210.2 13.4 %collective-permute-start.37 = (bf16[1,240,384]{2,1,0:T(8,128)(2,1)S(1)}, bf16[1,240,384]{2,1,0:T(8,128)(2,1)S(1)}, u32[]{:S(2)}, u32[]{:S(2)}) collective-permute-start(bf16[1,240,384]{2,1,0:T(8,128)(2,1)S(1)} %get-tuple-element.221), channel_id=1, source_target_pairs={{0,6},{1,7},{2,4},{3,5},{4,2},{5,3},{6,0},{7,1},{8,14},{9,15},{10,... | collective-permute-start | bytes 552968 | tf_op jit(solution)/shard_map/ppermute | solution.py:54
  224.9 18.5 %collective-permute-start.38 = (bf16[4,144,384]{2,1,0:T(8,128)(2,1)S(1)}, bf16[4,144,384]{2,1,0:T(8,128)(2,1)S(1)}, u32[]{:S(2)}, u32[]{:S(2)}) collective-permute-start(bf16[4,144,384]{2,1,0:T(8,128)(2,1)S(1)} %add_convert_fusion.5), channel_id=1, source_target_pairs={{0,16},{1,9},{2,18},{3,11},{4,20},{5,13},{6,22},{7,15},{8,24},{9,1... | collective-permute-start | bytes 1327112 | tf_op jit(solution)/shard_map/ppermute | solution.py:54
  226.5 16.8 %collective-permute-start.39 = (bf16[1,16,768]{2,1,0:T(8,128)(2,1)S(1)}, bf16[1,16,768]{2,1,0:T(8,128)(2,1)S(1)}, u32[]{:S(2)}, u32[]{:S(2)}) collective-permute-start(bf16[1,16,768]{2,1,0:T(8,128)(2,1)S(1)} %convert_bitcast_fusion), channel_id=1, source_target_pairs={{0,4},{1,5},{2,6},{3,7},{4,0},{5,1},{6,2},{7,3},{8,12},{9,13},{10,... | collective-permute-start | bytes 73736 | tf_op jit(solution)/shard_map/ppermute | solution.py:54
  229.7 13.6 %collective-permute-start.40 = (bf16[1,16,768]{2,1,0:T(8,128)(2,1)S(1)}, bf16[1,16,768]{2,1,0:T(8,128)(2,1)S(1)}, u32[]{:S(2)}, u32[]{:S(2)}) collective-permute-start(bf16[1,16,768]{2,1,0:T(8,128)(2,1)S(1)} %convert_bitcast_fusion), channel_id=1, source_target_pairs={{0,2},{1,3},{2,0},{3,1},{4,6},{5,7},{6,4},{7,5},{8,10},{9,11},{10,... | collective-permute-start | bytes 73736 | tf_op jit(solution)/shard_map/ppermute | solution.py:54
  229.7 13.6 %collective-permute-start.41 = (bf16[1,16,768]{2,1,0:T(8,128)(2,1)S(1)}, bf16[1,16,768]{2,1,0:T(8,128)(2,1)S(1)}, u32[]{:S(2)}, u32[]{:S(2)}) collective-permute-start(bf16[1,16,768]{2,1,0:T(8,128)(2,1)S(1)} %convert_bitcast_fusion), channel_id=1, source_target_pairs={{0,6},{1,7},{2,4},{3,5},{4,2},{5,3},{6,0},{7,1},{8,14},{9,15},{10,... | collective-permute-start | bytes 73736 | tf_op jit(solution)/shard_map/ppermute | solution.py:54
  (54 other events, 410.2 us)

commit v4 on v3

--- a/solution.py
+++ b/solution.py
@@ -92,7 +92,8 @@
         self.at = self.steps.pop(0)
         size = 1 if len(self.at) == 3 else self.at[0]
         self.sent = [self.sum(p, p + size).astype(BF16) for p in self.at]
-        return self.sent
+        self.parts = [self.sum(0, size)]
+        return [*self.sent, self.parts[0]]
 
     def fly(self):
         return [chip_swap(x, p) for x, p in zip(self.sent, self.at)]
@@ -122,22 +123,30 @@
     return pltpu.HBM(shape, dtype)
 
 
+def local(shape, dtype=BF16):
+    return pltpu.VMEM(shape, dtype)
+
+
 def params(mib):
     return pltpu.CompilerParams(vmem_limit_bytes=mib * 1024 * 1024)
 
 
-def kernel_call(*args, **kwargs):
-    call = pl.pallas_call(*args, **kwargs)
+def kernel_call(kernel, **kwargs):
+    call = pl.pallas_call(kernel, **kwargs)
+    if "grid_spec" in kwargs:
+        grid_spec = kwargs["grid_spec"]
+        specs = [SMEM_SPEC] * grid_spec.num_scalar_prefetch + list(grid_spec.in_specs)
+    else:
+        specs = kwargs["in_specs"]
+
+    def place(x, spec):
+        if spec is SMEM_SPEC:
+            return x
+        space = pltpu.VMEM if spec is VMEM_SPEC else pltpu.HBM
+        return pltpu.with_memory_space_constraint(x, space)
 
     def run(*operands):
-        return call(
-            *[
-                x
-                if x.dtype == jnp.int32
-                else pltpu.with_memory_space_constraint(x, pltpu.HBM)
-                for x in operands
-            ]
-        )
+        return call(*[place(x, spec) for x, spec in zip(operands, specs, strict=True)])
 
     return run
 
@@ -186,12 +195,12 @@
     return pl.ds(pl.multiple_of(half * size + base, 128), LANES)
 
 
-def fetch_pieces(tab, parts, rows, dst, sem):
+def fetch_pieces(tab, parts, rows, dst, sem, first=0):
     each_piece(
         tab,
         parts,
         lambda src, chip, half: pltpu.make_async_copy(
-            src.at[pl.ds(0, rows), :], dst.at[chip, half], sem
+            src.at[pl.ds(first, rows), :], dst.at[chip, half], sem
         ).start(),
     )
 
@@ -268,20 +277,21 @@
 def attention_kernel(
     tab, lens, sets, g_a, g_b, g_c, g_d, x_ref, feat_ref,
     normed_ref, qkv_ref, te_ref, vec_ref, seen_ref, probs_ref, att_ref,
-    w, sem,
+    w, w_time, sem, sem_time,
 ):
     i = pl.program_id(0)
 
     @pl.when(i == 0)
     def _():
-        fetch_pieces(tab, (g_a, g_b, g_c, g_d), 192, w, sem)
-        finish(w, sem)
+        fetch_pieces(tab, (g_a, g_b, g_c, g_d), 48, w_time, sem_time, 144)
+        fetch_pieces(tab, (g_a, g_b, g_c, g_d), 144, w, sem)
+        finish(w_time, sem_time)
         lane = lax.broadcasted_iota(jnp.int32, (128, WIDTH), 1)
         spread = (lax.broadcasted_iota(jnp.int32, (128, WIDTH), 0) == lane % 24).astype(BF16)
         vectors = jnp.zeros((16, WIDTH), F32)
         embed = jnp.zeros((8, WIDTH), F32)
         for owner in (0, 1):
-            extra = block(w, owner, 176, 16)
+            extra = block(w_time, owner, 32, 16)
             wide = dot(extra[:, 128:256], spread)
             chip = lax.broadcasted_iota(jnp.int32, (256, WIDTH), 0) // 16
             place = lax.broadcasted_iota(jnp.int32, (256, WIDTH), 1) // 24
@@ -289,8 +299,8 @@
             vectors = vectors + jnp.sum(wide.reshape(CHIPS, 16, WIDTH), axis=0)
             pre = dot_last(feat_ref[...], extra[:, 0:128])
             hidden = (pre / (1.0 + jnp.exp(-pre))).astype(BF16)
-            embed = embed + dot(hidden, both_halves(w, 144 + 16 * owner, 16))
-            seen_ref[owner] = w[:, owner, 176:192, 256:]
+            embed = embed + dot(hidden, both_halves(w_time, 16 * owner, 16))
+            seen_ref[owner] = w_time[:, owner, 32:48, 256:]
         vec_ref[...] = vectors
         for s in range(8):
             chosen = jnp.where(sets[s // 4, s % 4] == 1, vectors[3:4, :], vectors[2:3, :])
@@ -298,6 +308,11 @@
 
     xhat, _unused = ln_stats(add_embed(x_ref[...], te_ref, i))
     normed_ref[...] = (xhat * vec_ref[0:1, :]).astype(BF16)
+
+    @pl.when(i == 0)
+    def _():
+        finish(w, sem)
+
     for half in (0, 1):
         cols = slice(half * 3 * LANES, (half + 1) * 3 * LANES)
         qkv_ref[:, cols] = dot(normed_ref[...], qkv_columns(w, half)).astype(BF16)
@@ -324,7 +339,12 @@
             row, tiles(256, 3 * WIDTH), fixed(8, WIDTH), fixed(16, WIDTH),
             fixed(2, CHIPS, 16, 128), tiles(12 * 256, 128), row,
         ),
-        scratch_shapes=[pltpu.VMEM((CHIPS, 2, 192, LANES), BF16), pltpu.SemaphoreType.DMA],
+        scratch_shapes=[
+            pltpu.VMEM((CHIPS, 2, 144, LANES), BF16),
+            pltpu.VMEM((CHIPS, 2, 48, LANES), BF16),
+            pltpu.SemaphoreType.DMA,
+            pltpu.SemaphoreType.DMA,
+        ],
         compiler_params=params(26),
         cost_estimate=cost(8_000_000_000, 20_000_000, 1_600_000),
         name="attention_forward",
@@ -360,9 +380,9 @@
 
 
 def up_kernel(
-    tab, u_a, u_b, u_c, u_d, out_grad_hbm, att_ref, x_ref, te_ref, vec_ref,
+    tab, u_a, u_b, u_c, u_d, out_grad_ref, att_ref, x_ref, te_ref, vec_ref,
     mid_ref, two_ref, act_ref, slope_ref, theirs_ref,
-    w, out_grad, kept, sem, sem_out_grad,
+    w, sem,
 ):
     i = pl.program_id(0)
 
@@ -370,72 +390,72 @@
     def _():
         fetch_pieces(tab, (u_a, u_b, u_c, u_d), 240, w, sem)
         finish(w, sem)
-        pltpu.make_async_copy(out_grad_hbm, out_grad, sem_out_grad).start()
 
     @pl.when(i < 4)
     def _():
+        rows = rows_of(i, 256)
         mid = add_embed(x_ref[...], te_ref, i) + dot(att_ref[...], both_halves(w, 192))
         mid_ref[...] = mid
         xhat, _unused = ln_stats(mid)
-        two_ref[...] = (xhat * vec_ref[1:2, :]).astype(BF16)
+        two = (xhat * vec_ref[1:2, :]).astype(BF16)
+        two_ref[...] = two
         for j in range(4):
-            cols = slice(j * WIDTH, (j + 1) * WIDTH)
-            up = dot(two_ref[...], up_columns(w, j))
+            up = dot(two, up_columns(w, j))
             cdf, density = gelu_parts(up)
-            activated = (up * cdf).astype(BF16)
-            act_ref[:, cols] = activated
-            kept[j, rows_of(i, 256), :] = activated
-            slope_ref[:, cols] = (cdf + up * density).astype(BF16)
-
-    @pl.when(i == 4)
-    def _():
-        finish(out_grad, sem_out_grad)
+            act_ref[j, rows, :] = (up * cdf).astype(BF16)
+            slope_ref[j, rows, :] = (cdf + up * density).astype(BF16)
 
     @pl.when(i >= 4)
     def _():
-        down_grad_rows(tab, 1, i - 4, kept[i - 4], out_grad, theirs_ref)
+        down_grad_rows(tab, 1, i - 4, act_ref[i - 4], out_grad_ref, theirs_ref)
 
 
 def up_forward(tab, pieces, att, rows, out_grad, embed, vectors):
     row = clamped(256, WIDTH)
-    wide = clamped(256, FF)
     return kernel_call(
         up_kernel,
         grid=(8,),
         out_shape=(
             shaped((1024, WIDTH), F32),
             shaped((1024, WIDTH)),
-            shaped((1024, FF)),
-            shaped((1024, FF)),
-            pltpu.VMEM((CHIPS, 192, LANES), BF16),
+            local((4, 1024, WIDTH)),
+            local((4, 1024, WIDTH)),
+            local((CHIPS, 192, LANES)),
         ),
-        in_specs=[SMEM_SPEC] + [ANY_SPEC] * 5 + [row, row, fixed(8, WIDTH), fixed(16, WIDTH)],
-        out_specs=(row, row, wide, wide, VMEM_SPEC),
-        scratch_shapes=[
-            pltpu.VMEM((CHIPS, 2, 240, LANES), BF16),
-            pltpu.VMEM((1024, WIDTH), BF16),
-            pltpu.VMEM((4, 1024, WIDTH), BF16),
-            pltpu.SemaphoreType.DMA,
-            pltpu.SemaphoreType.DMA,
-        ],
-        compiler_params=params(38),
+        in_specs=[SMEM_SPEC]
+        + [ANY_SPEC] * 4
+        + [VMEM_SPEC, row, row, fixed(8, WIDTH), fixed(16, WIDTH)],
+        out_specs=(row, row) + (VMEM_SPEC,) * 3,
+        scratch_shapes=[pltpu.VMEM((CHIPS, 2, 240, LANES), BF16), pltpu.SemaphoreType.DMA],
+        compiler_params=params(26),
         cost_estimate=cost(10_000_000_000, 30_000_000, 6_000_000),
         name="up_forward",
     )(tab, *pieces, out_grad, att, rows, embed, vectors)
 
 
-def down_grad_kernel(tab, act_ref, out_grad_ref, out_ref):
-    down_grad_rows(tab, 0, pl.program_id(0), act_ref[...], out_grad_ref, out_ref)
+def down_grad_kernel(tab, act_ref, out_grad_ref, out_ref, act_hbm, sem):
+    j = pl.program_id(0)
+
+    @pl.when(j == 0)
+    def _():
+        pltpu.make_async_copy(act_ref, act_hbm, sem).start()
+
+    down_grad_rows(tab, 0, j, act_ref[j], out_grad_ref, out_ref)
+
+    @pl.when(j == 3)
+    def _():
+        pltpu.make_async_copy(act_ref, act_hbm, sem).wait()
 
 
 def down_grad(tab, act, out_grad):
     return kernel_call(
         down_grad_kernel,
         grid=(4,),
-        out_shape=pltpu.VMEM((CHIPS, 192, LANES), BF16),
-        in_specs=[SMEM_SPEC, columns(1024, WIDTH), fixed(1024, WIDTH)],
-        out_specs=VMEM_SPEC,
-        compiler_params=params(18),
+        out_shape=(local((CHIPS, 192, LANES)), shaped((4, 1024, WIDTH))),
+        in_specs=[SMEM_SPEC] + [VMEM_SPEC] * 2,
+        out_specs=(VMEM_SPEC, ANY_SPEC),
+        scratch_shapes=[pltpu.SemaphoreType.DMA],
+        compiler_params=params(12),
         cost_estimate=cost(3_000_000_000, 10_000_000),
         name="down_grad",
     )(tab, act, out_grad)
@@ -461,64 +481,50 @@
 
 
 def up_grad_kernel(
-    tab, att_hbm, branch_hbm, two_ref, grad_up_ref, out_ref,
-    att, branch, part, sem_att, sem_branch,
+    tab, att_hbm, two_hbm, branch_ref, grad_up_ref, out_ref, att, two, part, sem_att, sem_two
 ):
     j = pl.program_id(0)
 
     @pl.when(j == 0)
     def _():
         pltpu.make_async_copy(att_hbm, att, sem_att).start()
-        pltpu.make_async_copy(branch_hbm, branch, sem_branch).start()
-
-    @pl.when(j < 2)
-    def _():
-        up_grad_rows(tab, 0, j, two_ref[...], grad_up_ref[...], out_ref, part)
-
-    @pl.when(j == 2)
-    def _():
+        pltpu.make_async_copy(two_hbm, two, sem_two).start()
         finish(att, sem_att)
-        finish(branch, sem_branch)
-        out_grad_rows(tab, 0, att, branch, out_ref, part)
+        out_grad_rows(tab, 0, att, branch_ref, out_ref, part)
+        finish(two, sem_two)
+
+    @pl.when(j > 0)
+    def _():
+        up_grad_rows(tab, 0, j - 1, two[...], grad_up_ref[j - 1], out_ref, part)
 
 
 def up_grad(tab, att, branch, two, grad_up):
     return kernel_call(
         up_grad_kernel,
-        grid_spec=pltpu.PrefetchScalarGridSpec(
-            num_scalar_prefetch=1,
-            grid=(3,),
-            in_specs=[
-                ANY_SPEC,
-                ANY_SPEC,
-                pl.BlockSpec((1024, WIDTH), lambda j, tab: (0, 0)),
-                pl.BlockSpec(
-                    (1024, WIDTH), lambda j, tab: (0, half_of(tab, 0) * 2 + jnp.minimum(j, 1))
-                ),
-            ],
-            out_specs=VMEM_SPEC,
-            scratch_shapes=[pltpu.VMEM((1024, WIDTH), BF16)] * 2
-            + [pltpu.VMEM((WIDTH, WIDTH), BF16)]
-            + [pltpu.SemaphoreType.DMA] * 2,
-        ),
-        out_shape=pltpu.VMEM((CHIPS, 240, LANES), BF16),
-        compiler_params=params(22),
+        grid=(3,),
+        out_shape=local((CHIPS, 240, LANES)),
+        in_specs=[SMEM_SPEC] + [ANY_SPEC] * 2 + [VMEM_SPEC] * 2,
+        out_specs=VMEM_SPEC,
+        scratch_shapes=[pltpu.VMEM((1024, WIDTH), BF16)] * 2
+        + [pltpu.VMEM((WIDTH, WIDTH), BF16)]
+        + [pltpu.SemaphoreType.DMA] * 2,
+        compiler_params=params(16),
         cost_estimate=cost(3_200_000_000, 11_000_000),
         name="up_grad",
-    )(tab, att, branch, two, grad_up)
+    )(tab, att, two, branch, grad_up)
 
 
 def mlp_backward_kernel(
-    tab, down_tab, u_a, u_b, u_c, u_d, d_a, d_b, d_c, d_d, two_hbm, att_hbm,
-    slope_ref, out_grad_ref, mid_ref, vec_ref,
-    grad_mid_ref, branch_ref, grad_up_ref, grad_att_ref, gain_ref, theirs_ref,
-    w, w_down, two, att, kept, kept_branch, part, sem, sem_down, sem_two, sem_att,
+    tab, later_tab, u_a, u_b, u_c, u_d, d_a, d_b, d_c, d_d,
+    two_hbm, att_hbm, slope_ref, out_grad_ref, mid_ref, vec_ref,
+    grad_mid_ref, branch_ref, mine_up_ref, grad_att_ref, gain_ref, theirs_ref,
+    w, w_down, two, att, theirs_up, grad_up, part, sem, sem_down, sem_two, sem_att,
 ):
     i = pl.program_id(0)
 
     @pl.when(i == 0)
     def _():
-        fetch_pieces(down_tab, (d_a, d_b, d_c, d_d), 192, w_down, sem_down)
+        fetch_pieces(later_tab, (d_a, d_b, d_c, d_d), 192, w_down, sem_down)
         gain_ref[...] = jnp.zeros_like(gain_ref)
         finish(w_down, sem_down)
         fetch_pieces(tab, (u_a, u_b, u_c, u_d), 240, w, sem)
@@ -527,10 +533,10 @@
 
     @pl.when(i < 4)
     def _():
+        rows = rows_of(i, 256)
         for j in range(4):
-            cols = slice(j * WIDTH, (j + 1) * WIDTH)
-            grad_act = dot_last(out_grad_ref[...], down_rows(w_down, j))
-            grad_up_ref[:, cols] = (grad_act * slope_ref[:, cols].astype(F32)).astype(BF16)
+            grad_act = dot_last(out_grad_ref[rows, :], down_rows(w_down, j))
+            grad_up[j] = (grad_act * slope_ref[j, rows, :].astype(F32)).astype(BF16)
 
         @pl.when(i == 0)
         def _():
@@ -538,95 +544,73 @@
 
         y = jnp.zeros((256, WIDTH), F32)
         for j in range(4):
-            cols = slice(j * WIDTH, (j + 1) * WIDTH)
-            y = y + dot_last(grad_up_ref[:, cols], up_columns(w, j))
-        theirs = pl.ds(pl.multiple_of(half_of(tab, 1) * 4 * LANES, 128), 4 * LANES)
-        kept[rows_of(i, 256), :] = grad_up_ref[:, theirs]
+            y = y + dot_last(grad_up[j], up_columns(w, j))
+        mine = half_of(tab, 0)
+        for j in range(2):
+            mine_up_ref[j, rows, :] = grad_up[2 * mine + j]
+            theirs_up[j, rows, :] = grad_up[2 - 2 * mine + j]
         xhat, scale = ln_stats(mid_ref[...])
-        grad = out_grad_ref[...].astype(F32) + ln_back(y, vec_ref[1:2, :], xhat, scale)
+        grad = out_grad_ref[rows, :].astype(F32) + ln_back(y, vec_ref[1:2, :], xhat, scale)
         grad_mid_ref[...] = grad
-        branch_ref[...] = grad.astype(BF16)
-        kept_branch[rows_of(i, 256), :] = branch_ref[...]
+        branch = grad.astype(BF16)
+        branch_ref[rows, :] = branch
         gain_ref[...] += jnp.sum(y * xhat, axis=0, keepdims=True)
-        grad_att_ref[...] = dot_last(branch_ref[...], both_halves(w, 192)).astype(BF16)
+        grad_att_ref[rows, :] = dot_last(branch, both_halves(w, 192)).astype(BF16)
 
     @pl.when(i == 4)
     def _():
         finish(two, sem_two)
         finish(att, sem_att)
-        out_grad_rows(tab, 1, att, kept_branch, theirs_ref, part)
+        out_grad_rows(tab, 1, att, branch_ref, theirs_ref, part)
 
     @pl.when(i >= 4)
     def _():
-        cols = pl.ds(pl.multiple_of((i - 4) * WIDTH, WIDTH), WIDTH)
-        up_grad_rows(tab, 1, i - 4, two[...], kept[:, cols], theirs_ref, part)
-
-
-def mlp_backward(tab, down_tab, up_pieces, down_pieces, two, att, slope, out_grad, mid, vectors):
-    row = clamped(256, WIDTH)
-    wide = clamped(256, FF)
+        up_grad_rows(tab, 1, i - 4, two[...], theirs_up[i - 4], theirs_ref, part)
+
+
+def mlp_backward(
+    tab, later_tab, up_pieces, down_pieces, two, att, slope, out_grad, mid, vectors
+):
     return kernel_call(
         mlp_backward_kernel,
         grid=(6,),
         out_shape=(
             shaped((1024, WIDTH), F32),
-            shaped((1024, WIDTH)),
-            shaped((1024, FF)),
-            shaped((1024, WIDTH)),
-            shaped((1, WIDTH), F32),
-            pltpu.VMEM((CHIPS, 240, LANES), BF16),
+            local((1024, WIDTH)),
+            local((2, 1024, WIDTH)),
+            local((1024, WIDTH)),
+            local((1, WIDTH), F32),
+            local((CHIPS, 240, LANES)),
         ),
-        in_specs=[SMEM_SPEC] * 2 + [ANY_SPEC] * 10 + [wide, row, row, fixed(16, WIDTH)],
-        out_specs=(row, row, wide, row, fixed(1, WIDTH), VMEM_SPEC),
+        in_specs=[SMEM_SPEC] * 2
+        + [ANY_SPEC] * 10
+        + [VMEM_SPEC] * 2
+        + [clamped(256, WIDTH), fixed(16, WIDTH)],
+        out_specs=(clamped(256, WIDTH),) + (VMEM_SPEC,) * 5,
         scratch_shapes=[
             pltpu.VMEM((CHIPS, 2, 240, LANES), BF16),
             pltpu.VMEM((CHIPS, 2, 192, LANES), BF16),
             pltpu.VMEM((1024, WIDTH), BF16),
             pltpu.VMEM((1024, WIDTH), BF16),
-            pltpu.VMEM((1024, 4 * LANES), BF16),
-            pltpu.VMEM((1024, WIDTH), BF16),
+            pltpu.VMEM((2, 1024, WIDTH), BF16),
+            pltpu.VMEM((4, 256, WIDTH), BF16),
             pltpu.VMEM((WIDTH, WIDTH), BF16),
         ]
         + [pltpu.SemaphoreType.DMA] * 4,
-        compiler_params=params(46),
+        compiler_params=params(38),
         cost_estimate=cost(18_000_000_000, 50_000_000),
         name="mlp_backward",
-    )(tab, down_tab, *up_pieces, *down_pieces, two, att, slope, out_grad, mid, vectors)
-
-
-def result_kernel(tab, d_a, d_b, d_c, d_d, act_ref, mid_ref, result_ref, w_down, sem):
-    @pl.when(pl.program_id(0) == 0)
-    def _():
-        fetch_pieces(tab, (d_a, d_b, d_c, d_d), 192, w_down, sem)
-        finish(w_down, sem)
-
-    total = mid_ref[...]
-    for j in range(4):
-        total = total + dot(act_ref[:, j * WIDTH : (j + 1) * WIDTH], down_rows(w_down, j))
-    result_ref[...] = total.astype(BF16)
-
-
-def block_result(tab, pieces, act, mid):
-    row = tiles(256, WIDTH)
-    return kernel_call(
-        result_kernel,
-        grid=(4,),
-        out_shape=shaped((1024, WIDTH)),
-        in_specs=[SMEM_SPEC] + [ANY_SPEC] * 4 + [tiles(256, FF), row],
-        out_specs=row,
-        scratch_shapes=[pltpu.VMEM((CHIPS, 2, 192, LANES), BF16), pltpu.SemaphoreType.DMA],
-        compiler_params=params(22),
-        cost_estimate=cost(5_000_000_000, 16_000_000),
-        name="block_result",
-    )(tab, *pieces, act, mid)
-
-
-def attention_backward_rows(k, qkv_ref, probs_ref, grad_att_ref, grad_qkv_ref):
+    )(tab, later_tab, *up_pieces, *down_pieces, two, att, slope, out_grad, mid, vectors)
+
+
+def attention_backward_rows(k, first_row, qkv_ref, probs_ref, grad_att_ref, grad_qkv_ref):
     low_half = lax.broadcasted_iota(jnp.int32, (128, 128), 1) < HEAD_DIM
     rows = slice(128 * k, 128 * k + 128)
+    whole_rows = pl.ds(pl.multiple_of(first_row, 128), 128)
 
     def heads(ref, base):
-        return two_heads(ref[rows, base : base + 128], low_half)
+        where = whole_rows if ref is grad_att_ref else rows
+        return two_heads(ref[where, base : base + 128], low_half)
 
     def probs_of(pair):
         first = 256 * (6 * k + pair)
@@ -663,7 +647,7 @@
 
 
 def attention_backward_kernel(
-    tab, normed_hbm, qkv_ref, probs_ref, grad_att_ref, grad_qkv_ref, theirs_ref,
+    tab, normed_hbm, qkv_ref, probs_ref, grad_att_ref, grad_qkv_ref, mine_ref, theirs_ref,
     normed, kept, part, sem,
 ):
     i = pl.program_id(0)
@@ -675,9 +659,12 @@
     @pl.when(i < 4)
     def _():
         for k in range(2):
-            attention_backward_rows(k, qkv_ref, probs_ref, grad_att_ref, grad_qkv_ref)
-        theirs = pl.ds(pl.multiple_of(half_of(tab, 1) * 3 * LANES, 128), 3 * LANES)
-        kept[rows_of(i, 256), :] = grad_qkv_ref[:, theirs]
+            attention_backward_rows(
+                k, i * 256 + 128 * k, qkv_ref, probs_ref, grad_att_ref, grad_qkv_ref
+            )
+        for side, target in enumerate((mine_ref, kept)):
+            lanes = pl.ds(pl.multiple_of(half_of(tab, side) * 3 * LANES, 128), 3 * LANES)
+            target[rows_of(i, 256), :] = grad_qkv_ref[:, lanes]
 
     @pl.when(i == 4)
     def _():
@@ -690,9 +677,11 @@
     return kernel_call(
         attention_backward_kernel,
         grid=(5,),
-        out_shape=(shaped((1024, 3 * WIDTH)), pltpu.VMEM((CHIPS, 144, LANES), BF16)),
-        in_specs=[SMEM_SPEC, ANY_SPEC, wide, clamped(12 * 256, 128), clamped(256, WIDTH)],
-        out_specs=(wide, VMEM_SPEC),
+        out_shape=(
+            shaped((1024, 3 * WIDTH)), local((1024, 3 * LANES)), local((CHIPS, 144, LANES))
+        ),
+        in_specs=[SMEM_SPEC, ANY_SPEC, wide, clamped(12 * 256, 128), VMEM_SPEC],
+        out_specs=(wide, VMEM_SPEC, VMEM_SPEC),
         scratch_shapes=[
             pltpu.VMEM((1024, WIDTH), BF16),
             pltpu.VMEM((1024, 3 * LANES), BF16),
@@ -705,28 +694,45 @@
     )(tab, normed, qkv, probs, grad_att)
 
 
-def qkv_grad_kernel(tab, normed_ref, grad_qkv_ref, out_ref, part):
-    qkv_grad_rows(tab, 0, normed_ref[...], grad_qkv_ref[...], out_ref, part)
-
-
-def qkv_grad(tab, normed, grad_qkv):
+def qkv_grad_kernel(
+    tab, later_tab, d_a, d_b, d_c, d_d, normed_ref, grad_qkv_ref, act_ref, mid_ref,
+    out_ref, result_ref,
+    part, w_down, sem,
+):
+    i = pl.program_id(0)
+
+    @pl.when(i == 0)
+    def _():
+        fetch_pieces(later_tab, (d_a, d_b, d_c, d_d), 192, w_down, sem)
+        qkv_grad_rows(tab, 0, normed_ref[...], grad_qkv_ref[...], out_ref, part)
+        finish(w_down, sem)
+
+    @pl.when(i > 0)
+    def _():
+        total = mid_ref[...]
+        for j in range(4):
+            total = total + dot(act_ref[j], down_rows(w_down, j))
+        result_ref[...] = total.astype(BF16)
+
+
+def qkv_grad(tab, later_tab, pieces, normed, grad_qkv, act, mid):
+    row = pl.BlockSpec((256, WIDTH), lambda i: (jnp.maximum(i - 1, 0), 0))
+    wide = pl.BlockSpec((4, 256, WIDTH), lambda i: (0, jnp.maximum(i - 1, 0), 0))
     return kernel_call(
         qkv_grad_kernel,
-        grid_spec=pltpu.PrefetchScalarGridSpec(
-            num_scalar_prefetch=1,
-            grid=(1,),
-            in_specs=[
-                pl.BlockSpec((1024, WIDTH), lambda i, tab: (0, 0)),
-                pl.BlockSpec((1024, 3 * LANES), lambda i, tab: (0, half_of(tab, 0))),
-            ],
-            out_specs=VMEM_SPEC,
-            scratch_shapes=[pltpu.VMEM((WIDTH, 3 * LANES), BF16)],
-        ),
-        out_shape=pltpu.VMEM((CHIPS, 144, LANES), BF16),
-        compiler_params=params(22),
-        cost_estimate=cost(2_000_000_000, 7_000_000),
+        grid=(5,),
+        out_shape=(local((CHIPS, 144, LANES)), shaped((1024, WIDTH))),
+        in_specs=[SMEM_SPEC] * 2 + [ANY_SPEC] * 4 + [fixed(1024, WIDTH), VMEM_SPEC, wide, row],
+        out_specs=(VMEM_SPEC, row),
+        scratch_shapes=[
+            pltpu.VMEM((WIDTH, 3 * LANES), BF16),
+            pltpu.VMEM((CHIPS, 2, 192, LANES), BF16),
+            pltpu.SemaphoreType.DMA,
+        ],
+        compiler_params=params(26),
+        cost_estimate=cost(7_000_000_000, 22_000_000),
         name="qkv_grad",
-    )(tab, normed, grad_qkv)
+    )(tab, later_tab, *pieces, normed, grad_qkv, act, mid)
 
 
 def input_backward_kernel(
@@ -763,13 +769,13 @@
     return kernel_call(
         input_backward_kernel,
         grid=(4,),
-        out_shape=(shaped((1024, WIDTH)), shaped((16, WIDTH), F32)),
+        out_shape=(shaped((1024, WIDTH)), local((16, WIDTH), F32)),
         in_specs=[SMEM_SPEC]
         + [ANY_SPEC] * 4
-        + [tiles(256, 3 * WIDTH), row, fixed(8, WIDTH), fixed(16, WIDTH), row, fixed(1, WIDTH)],
-        out_specs=(row, fixed(16, WIDTH)),
+        + [tiles(256, 3 * WIDTH), row, fixed(8, WIDTH), fixed(16, WIDTH), row, VMEM_SPEC],
+        out_specs=(row, VMEM_SPEC),
         scratch_shapes=[pltpu.VMEM((CHIPS, 2, 144, LANES), BF16), pltpu.SemaphoreType.DMA],
-        compiler_params=params(24),
+        compiler_params=params(20),
         cost_estimate=cost(4_000_000_000, 18_000_000),
         name="input_backward",
     )(tab, *pieces, grad_qkv, rows, embed, vectors, grad_mid, gain_two)
@@ -802,7 +808,7 @@
     return kernel_call(
         time_grads_kernel,
         out_shape=(
-            shaped((rows, wave.shape[1]), F32), shaped((rows, width), F32), shaped((16, width), F32)
+            shaped((rows, wave.shape[1]), F32), shaped((rows, width), F32), local((16, width), F32)
         ),
         in_specs=[SMEM_SPEC] + [ANY_SPEC] * len(parts) + [VMEM_SPEC] * 5,
         out_specs=(VMEM_SPEC,) * 3,
@@ -933,7 +939,7 @@
             (up_weight, out_weight, down_weight, flat, attention_piece)
         )[:4]
         tab = position_table(flat >> 1, flat & 1, LINE_FIRST)
-        down_tab = position_table(flat >> 1, flat & 1, LINE_LATER)
+        later_tab = position_table(flat >> 1, flat & 1, LINE_LATER)
         wide = lane_blocks(up_weight, range(0, 4 * LANES, LANES), 4 * LANES)
         slim = lane_blocks(out_weight, (0,), LANES)
         own, other = swap_halves(
@@ -946,24 +952,27 @@
         own, other = swap_halves(lane_blocks(down_weight, (0,), LANES), core)
         down_piece = join_rows(own, other, core, 1)[None]
         down_pair = jnp.concatenate([down_piece, chip_swap(down_piece, 1, LINE_LATER)], axis=0)
-        ready = (up_piece, down_pair, tab, down_tab, features)
+        ready = (up_piece, down_pair, tab, later_tab, features)
         line = after(jnp.concatenate([attention_piece] + near, axis=0), *ready)
         plane = chip_swap(line, 4)
-        up_near = [chip_swap(after(up_piece, line), p) for p in (1, 2, 3)]
+        up_near = [chip_swap(after(up_piece, line), p) for p in (1, 2)]
+        plane, up_near = together(plane, up_near)
         held = jnp.concatenate([line, plane], axis=0)
         far = chip_swap(held, 8)
-        up_line = jnp.concatenate([up_piece] + [after(x, held) for x in up_near], axis=0)
-        far = after(far, up_line)
+        up_near.append(chip_swap(after(up_piece, plane), 3))
+        up_line = jnp.concatenate([up_piece] + up_near, axis=0)
+        up_plane = chip_swap(up_line, 4)
+        down_near = [chip_swap(after(down_pair, up_line), 2, LINE_LATER)]
+        (far, up_plane), down_near = together((far, up_plane), down_near)
         attention_pieces = (held, far, core_swap(held), core_swap(far))
-        up_plane = chip_swap(after(up_line, far), 4)
-        down_near = [chip_swap(after(down_pair, up_line), p, LINE_LATER) for p in (2, 4, 6)]
         up_held = jnp.concatenate([up_line, up_plane], axis=0)
         up_far = chip_swap(up_held, 8)
+        down_last = [chip_swap(after(down_pair, up_held), p, LINE_LATER) for p in (4, 6)]
     else:
         tab = jnp.concatenate(
             [jnp.tile(jnp.arange(CHIPS, dtype=jnp.int32), 4), jnp.zeros((8,), jnp.int32)]
         )
-        down_tab = tab
+        later_tab = tab
         full_qkv = gather_all(qkv_weight).reshape(CHIPS, 48, 3, 2, LANES)
         full_out = gather_all(out_weight).reshape(CHIPS, 48, 2, LANES)
         full_up = gather_all(up_weight).reshape(CHIPS, 48, 2, 4, LANES)
@@ -990,7 +999,7 @@
     arrivals = []
     if exchange:
         x_rows = after(x_rows, up_held)
-        arrivals = [up_far, down_near]
+        arrivals = [up_far]
     forward = attention_forward(tab, lengths, dataset, attention_pieces, x_rows, features)
     (normed, qkv, embed, vecs, seen, probs, att), arrivals = together(forward, arrivals)
     seen = seen[:, :, 0, : 3 * count].reshape(2 * CHIPS, 3 * count) if exchange else numbers_all
@@ -1009,7 +1018,8 @@
     hidden = (pre * gate).astype(BF16)
     slope_pre = gate * (1.0 + pre * (1.0 - gate))
     if exchange:
-        up_far, down_near = arrivals
+        (up_far,) = arrivals
+        down_near = down_near + [after(x, embed) for x in down_last]
         up_pieces = (up_held, up_far, core_swap(up_held), core_swap(up_far))
         down_held = jnp.concatenate([down_pair] + down_near, axis=0)
         att, wave, hot, hidden, slope_pre, down_held = lax.optimization_barrier(
@@ -1022,14 +1032,14 @@
         down_far = arrivals
         down_sum = Scatter(down_theirs)
         arrivals = [core_swap(down_held), core_swap(down_far)], down_sum.swap()
-    down_mine, arrivals = together(down_grad(tab, act, grad_rows), arrivals)
+    (down_mine, act), arrivals = together(down_grad(tab, act, grad_rows), arrivals)
     if exchange:
         down_pieces = (down_held, down_far, *arrivals[0])
         down_sum.land(arrivals[1], down_mine)
         slope = after(slope, *down_sum.send())
         arrivals = down_sum.fly()
     backward = mlp_backward(
-        tab, down_tab, up_pieces, down_pieces, two, att, slope, grad_rows, mid, vecs
+        tab, later_tab, up_pieces, down_pieces, two, att, slope, grad_rows, mid, vecs
     )
     backward, arrivals = together(backward, arrivals)
     grad_mid, branch, grad_up, grad_att, gain_two, up_theirs = backward
@@ -1045,15 +1055,16 @@
         grad_att = after(grad_att, *up_sum.send(), *down_sum.send())
         arrivals = up_sum.fly(), down_sum.fly()
     backward = attention_backward(tab, normed, qkv, probs, grad_att)
-    (grad_qkv, att_theirs), arrivals = together(backward, arrivals)
+    (grad_qkv, mine_qkv, att_theirs), arrivals = together(backward, arrivals)
     if exchange:
         up_sum.land(arrivals[0])
         down_sum.land(arrivals[1])
         down_total = down_sum.total()
         att_sum = Scatter(att_theirs)
-        grad_qkv = after(grad_qkv, *up_sum.send(), down_total)
+        mine_qkv = after(mine_qkv, *up_sum.send(), down_total)
         arrivals = up_sum.fly(), att_sum.swap()
-    att_mine, arrivals = together(qkv_grad(tab, normed, grad_qkv), arrivals)
+    backward = qkv_grad(tab, later_tab, down_pieces, normed, mine_qkv, act, mid)
+    (att_mine, result), arrivals = together(backward, arrivals)
     if exchange:
         up_sum.land(arrivals[0])
         att_sum.land(arrivals[1], att_mine)
@@ -1068,14 +1079,12 @@
     if exchange:
         att_sum.land(arrivals[0])
         up_sum.land(arrivals[1])
-        mid = after(mid, *att_sum.send(), small)
-        arrivals = att_sum.fly(), [chip_swap(small, p) for p in (1, 2, 3)]
-    result, arrivals = together(block_result(down_tab, down_pieces, act, mid), arrivals)
-    if exchange:
-        att_sum.land(arrivals[0])
-        small_line = jnp.concatenate([small] + arrivals[1], axis=0)
-        small_line = after(small_line, *att_sum.send())
+        att_sum.send()
+        brought, near = together(att_sum.fly(), [chip_swap(small, p) for p in (1, 2, 3)])
+        att_sum.land(brought)
+        small_line = jnp.concatenate([small] + near, axis=0)
         held = gather_plane(small_line)
+        att_sum.send()
         far = chip_swap(held, 8)
         every = (held, far, core_swap(held), core_swap(far))
         att_sum.land(att_sum.fly())
@@ -1086,9 +1095,9 @@
     sums = lax.dynamic_slice_in_dim(sums, flat * own_cols, own_cols, 1)
 
     if exchange:
-        own, other = swap_halves(after(down_total, result).reshape(2, 96, LANES), core)
+        own, other = swap_halves(after(down_total, small_line).reshape(2, 96, LANES), core)
         grad_down = in_core_order(core, own, other, 1)
-        piece = after(up_sum.total(), result)
+        piece = after(up_sum.total(), small_line)
         out_rows = piece[192:].reshape(2, 24, LANES)
         own, other = swap_halves(
             jnp.concatenate([split_rows(piece[:192], 4), out_rows], axis=1), core

time: 269 us -> 250 us (0.929)
  Pallas kernels: 123 us -> 112 us
  starting transfers between devices: 56.4 us -> 48.9 us
  waiting for transfers between devices: 52.2 us -> 57.4 us
    pallas_call x10 -> x9, Pallas kernels: 123 us -> 112 us  [run(): call(*[place(x, spec) for x, spec in zip(operands, specs, strict=True)])]
    ppermute x35, starting transfers between devices: 53 us -> 45.1 us  [chip_swap(): lax.ppermute(x, AXES, [(i, i ^ far[i & 1]) for i in range(2 * CHIPS)])]
    convert_element_type x9 -> x1, other arithmetic: 6.95 us -> 0.09 us  [send(): self.sent = [self.sum(p, p + size).astype(BF16) for p in self.at]]
    add x1 -> x9, other arithmetic: 1 us -> 6.61 us  [sum(): total = total + part[start:stop].astype(F32)]
    ppermute x35, waiting for transfers between devices: 49 us -> 51.9 us  [chip_swap(): lax.ppermute(x, AXES, [(i, i ^ far[i & 1]) for i in range(2 * CHIPS)])]
    unnamed x77 -> x81, local copies, waits for them, and re-layouts: 8.41 us -> 8.33 us
  transfers between devices with their start and end apart: 52 -> 52, of which waited for: 17 -> 20; matrix products, arithmetic and copies ran while one was open for 8% -> 7% of each run, Pallas kernels for 45% -> 44%
where the time goes in v4:
time: 250 us; the launch traced here: 249 us
  Pallas kernels  112 us (45%)
  waiting for transfers between devices  57.4 us (23%)
  starting transfers between devices  48.9 us (20%)
  local copies, waits for them, and re-layouts  14.5 us (6%)
  other arithmetic  14.5 us (6%)
    pallas_call x9, Pallas kernels, run(): call(*[place(x, spec) for x, spec in zip(operands, specs, strict=True)])  112 us
    ppermute x35, waiting for transfers between devices, chip_swap(): lax.ppermute(x, AXES, [(i, i ^ far[i & 1]) for i in range(2 * CHIPS)])  51.9 us
    ppermute x35, starting transfers between devices, chip_swap(): lax.ppermute(x, AXES, [(i, i ^ far[i & 1]) for i in range(2 * CHIPS)])  45.1 us
    unnamed x81, local copies, waits for them, and re-layouts  8.33 us
    add x9, other arithmetic, sum(): total = total + part[start:stop].astype(F32)  6.61 us
    ppermute x17, waiting for transfers between devices, core_swap(): return lax.ppermute(x, AXES, [(i, i ^ 1) for i in range(2 * CHIPS)])  5.55 us
  transfers between devices with their start and end apart: 52, of which 20 were waited for; matrix products, arithmetic and copies ran while one was open for 7% of the time, Pallas kernels for 44%

profile of v4, /device:TPU:0, one launch (start us, length us, event | category | flops | bytes accessed | tf_op | source)
XLA Modules:
  0.0 249.4 jit_solution(4463826514238127298)
XLA Ops:
  6.7 4.7 %collective-permute-start.3 = (bf16[1,192,384]{2,1,0:T(8,128)(2,1)S(1)}, bf16[1,192,384]{2,1,0:T(8,128)(2,1)S(1)}, u32[]{:S(2)}, u32[]{:S(2)}) collective-permute-start(bf16[1,192,384]{2,1,0:T(8,128)(2,1)S(1)} %maximum_bitcast_fusion.1), channel_id=1, source_target_pairs={{0,6},{1,7},{2,4},{3,5},{4,2},{5,3},{6,0},{7,1},{8,14},{9,15},{10,... | collective-permute-start | bytes 442376 | tf_op jit(solution)/shard_map/ppermute | solution.py:54
  16.3 3.9 %collective-permute-done.2 = bf16[1,192,384]{2,1,0:T(8,128)(2,1)S(1)} collective-permute-done((bf16[1,192,384]{2,1,0:T(8,128)(2,1)S(1)}, bf16[1,192,384]{2,1,0:T(8,128)(2,1)S(1)}, u32[]{:S(2)}, u32[]{:S(2)}) %collective-permute-start.2) | collective-permute-done | bytes 147488 | tf_op jit(solution)/shard_map/ppermute | solution.py:54
  20.2 4.4 %collective-permute-done.1 = bf16[1,192,384]{2,1,0:T(8,128)(2,1)S(1)} collective-permute-done((bf16[1,192,384]{2,1,0:T(8,128)(2,1)S(1)}, bf16[1,192,384]{2,1,0:T(8,128)(2,1)S(1)}, u32[]{:S(2)}, u32[]{:S(2)}) %collective-permute-start.1) | collective-permute-done | bytes 147488 | tf_op jit(solution)/shard_map/ppermute | solution.py:54
  26.8 2.6 %collective-permute-start.9 = (bf16[1,240,384]{2,1,0:T(8,128)(2,1)S(1)}, bf16[1,240,384]{2,1,0:T(8,128)(2,1)S(1)}, u32[]{:S(2)}, u32[]{:S(2)}) collective-permute-start(bf16[1,240,384]{2,1,0:T(8,128)(2,1)S(1)} %maximum_bitcast_fusion), channel_id=1, source_target_pairs={{0,2},{1,3},{2,0},{3,1},{4,6},{5,7},{6,4},{7,5},{8,10},{9,11},{10,... | collective-permute-start | bytes 552968 | tf_op jit(solution)/shard_map/ppermute | solution.py:54
  29.4 7.6 %collective-permute-done.8 = bf16[1,240,384]{2,1,0:T(8,128)(2,1)S(1)} collective-permute-done((bf16[1,240,384]{2,1,0:T(8,128)(2,1)S(1)}, bf16[1,240,384]{2,1,0:T(8,128)(2,1)S(1)}, u32[]{:S(2)}, u32[]{:S(2)}) %collective-permute-start.8) | collective-permute-done | bytes 184352 | tf_op jit(solution)/shard_map/ppermute | solution.py:54
  39.4 7.5 %collective-permute-done.11 = bf16[1,240,384]{2,1,0:T(8,128)(2,1)S(1)} collective-permute-done((bf16[1,240,384]{2,1,0:T(8,128)(2,1)S(1)}, bf16[1,240,384]{2,1,0:T(8,128)(2,1)S(1)}, u32[]{:S(2)}, u32[]{:S(2)}) %collective-permute-start.11) | collective-permute-done | bytes 184352 | tf_op jit(solution)/shard_map/ppermute | solution.py:54
  47.5 2.3 collective-permute-start.13
  50.5 12.5 %collective-permute-done.13 = bf16[2,192,384]{2,1,0:T(8,128)(2,1)S(1)} collective-permute-done((bf16[2,192,384]{2,1,0:T(8,128)(2,1)S(1)}, bf16[2,192,384]{2,1,0:T(8,128)(2,1)S(1)}, u32[]{:S(2)}, u32[]{:S(2)}) %collective-permute-start.13) | collective-permute-done | bytes 294944 | tf_op jit(solution)/shard_map/ppermute | solution.py:54
  70.9 16.0 %attention_forward.1 = (bf16[1024,768]{1,0:T(8,128)(2,1)}, bf16[1024,2304]{1,0:T(8,128)(2,1)}, f32[8,768]{1,0:T(8,128)}, f32[16,768]{1,0:T(8,128)}, bf16[2,16,16...) custom-call(s32[72]{0:T(128)S(1)} %compare_select_fusion.24.tab, ...), custom_call_target="tpu_custom_call" | custom-call | flops 8000000000 | bytes 20000000 | tf_op jit(solution)/shard_map/attention_forward/pallas_call | solution.py:149
  92.8 20.3 %up_forward.1 = (f32[1024,768]{1,0:T(8,128)}, bf16[1024,768]{1,0:T(8,128)(2,1)}, bf16[4,1024,768]{2,1,0:T(8,128)(2,1)S(1)}, bf16[4,1024,768]{2,1,0:T(8,128)(2,1)S(1)}, bf16[16,192,384]{2,1,0:T(8,128)(2,1)S(1)}) custom-call(s32[72]{0:T(128)S(1)} %compare_select_fusion.24.tab, bf16[8,240,384]{2,1,0:T(8,128)(2,1)} %constant_dynamic-update-slice_fusion.12.u_a, ...), custom_call_target="tpu_custom_call" | custom-call | flops 10000000000 | bytes 30000000 | tf_op jit(solution)/shard_map/up_forward/pallas_call | solution.py:149
  114.1 4.6 %down_grad.1 = (bf16[16,192,384]{2,1,0:T(8,128)(2,1)S(1)}, bf16[4,1024,768]{2,1,0:T(8,128)(2,1)}) custom-call(s32[72]{0:T(128)S(1)} %compare_select_fusion.24.tab, bf16[4,1024,768]{2,1,0:T(8,128)(2,1)S(1)} %get-tuple-element.160.act_ref, bf16[1024,768]{1,0:T(8,128)(2,1)S(1)} %bitcast.63), custom_call_target="tpu_custom_call" | custom-call | flops 3000000000 | bytes 10000000 | tf_op jit(solution)/shard_map/down_grad/pallas_call | solution.py:149
  124.4 27.2 %mlp_backward.1 = (f32[1024,768]{1,0:T(8,128)}, bf16[1024,768]{1,0:T(8,128)(2,1)S(1)}, bf16[2,1024,768]{2,1,0:T(8,128)(2,1)S(1)}, bf16[1024,768]{1,0:T(8,128)(2,...) custom-call(s32[72]{0:T(128)} %copy-done.1, s32[72]{0:T(128)} %compare_select_fusion.23.later_tab, ...), custom_call_target="tpu_custom_call" | custom-call | flops 17999998976 | bytes 50000000 | tf_op jit(solution)/shard_map/mlp_backward/pallas_call | solution.py:149
  152.2 6.2 %up_grad.1 = bf16[16,240,384]{2,1,0:T(8,128)(2,1)S(1)} custom-call(s32[72]{0:T(128)S(1)} %copy-done.2, bf16[1024,768]{1,0:T(8,128)(2,1)} %get-tuple-element.152.att_ref.att_hbm, bf16[1024,768]{1,0:T(8,128)(2,1)} %get-tuple-element.169.two_hbm, bf16[1024,768]{1,0:T(8,128)(2,1)S(1)} %get-tuple-element.182.branch_ref, ...), custom_call_target="tpu_custom_call" | custom-call | flops 3200000000 | bytes 11000000 | tf_op jit(solution)/shard_map/up_grad/pallas_call | solution.py:149
  158.5 3.6 %collective-permute-done.26 = bf16[4,192,384]{2,1,0:T(8,128)(2,1)S(1)} collective-permute-done((bf16[4,192,384]{2,1,0:T(8,128)(2,1)S(1)}, bf16[4,192,384]{2,1,0:T(8,128)(2,1)S(1)}, u32[]{:S(2)}, u32[]{:S(2)}) %collective-permute-start.26) | collective-permute-done | bytes 589856 | tf_op jit(solution)/shard_map/ppermute | solution.py:54
  167.8 12.2 %attention_backward.1 = (bf16[1024,2304]{1,0:T(8,128)(2,1)}, bf16[1024,1152]{1,0:T(8,128)(2,1)S(1)}, bf16[16,144,384]{2,1,0:T(8,128)(2,1)S(1)}) custom-call(s32[72]{0:T(128)S(1)} %copy-done.2, bf16[1024,768]{1,0:T(8,128)(2,1)} %get-tuple-element.166.normed_hbm.normed_ref, bf16[1024,2304]{1,0:T(8,128)(2,1)} %get-tuple-element.167.qkv_ref, ...), custom_call_target="tpu_custom_call" | custom-call | flops 11000000512 | bytes 22000000 | tf_op jit(solution)/shard_map/attention_backward/pallas_call | solution.py:149
  180.1 2.2 collective-permute-done.28
  183.8 12.0 %qkv_grad.1 = (bf16[16,144,384]{2,1,0:T(8,128)(2,1)S(1)}, bf16[1024,768]{1,0:T(8,128)(2,1)}) custom-call(s32[72]{0:T(128)S(1)} %copy-done.2, s32[72]{0:T(128)S(1)} %copy-done.6, bf16[8,192,384]{2,1,0:T(8,128)(2,1)} %copy-done.19, bf16[8,192,384]{2,1,0:T(8,128)(2,1)} %copy-done.24, bf16[8,192,384]{2,1,0:T(8,128)(2,1)} %copy-done.25, ...), custom_call_target="tpu_custom_call" | custom-call | flops 7000000000 | bytes 22000000 | tf_op jit(solution)/shard_map/qkv_grad/pallas_call | solution.py:149
  204.4 10.7 %input_backward.1 = (bf16[1024,768]{1,0:T(8,128)(2,1)}, f32[16,768]{1,0:T(8,128)S(1)}) custom-call(s32[72]{0:T(128)S(1)} %copy-done.2, bf16[8,192,384]{2,1,0:T(8,128)(2,1)} %copy-done.10, bf16[8,192,384]{2,1,0:T(8,128)(2,1)} %collective-permute-done.10.g_b, bf16[8,192,384]{2,1,0:T(8,128)(2,1)} %collective-permute-done.14.g_c, ...), custom_call_target="tpu_custom_call" | custom-call | flops 4000000000 | bytes 18000000 | tf_op jit(solution)/shard_map/input_backward/pallas_call | solution.py:149
  218.2 4.6 %collective-permute-start.39 = (bf16[1,16,768]{2,1,0:T(8,128)(2,1)S(1)}, bf16[1,16,768]{2,1,0:T(8,128)(2,1)S(1)}, u32[]{:S(2)}, u32[]{:S(2)}) collective-permute-start(bf16[1,16,768]{2,1,0:T(8,128)(2,1)S(1)} %get-tuple-element.234), channel_id=1, source_target_pairs={{0,4},{1,5},{2,6},{3,7},{4,0},{5,1},{6,2},{7,3},{8,12},{9,13},{10,... | collective-permute-start | bytes 73736 | tf_op jit(solution)/shard_map/ppermute | solution.py:54
  224.7 2.0 collective-permute-done.40
  232.0 2.5 collective-permute-start.46
  235.2 2.2 collective-permute-done.48
  237.8 2.9 %collective-permute-done.46 = bf16[1,144,384]{2,1,0:T(8,128)(2,1)S(1)} collective-permute-done((bf16[1,144,384]{2,1,0:T(8,128)(2,1)S(1)}, bf16[1,144,384]{2,1,0:T(8,128)(2,1)S(1)}, u32[]{:S(2)}, u32[]{:S(2)}) %collective-permute-start.46) | collective-permute-done | bytes 110624 | tf_op jit(solution)/shard_map/ppermute | solution.py:54
  245.2 3.0 %time_grads.1 = (f32[16,128]{1,0:T(8,128)}, f32[16,768]{1,0:T(8,128)}, f32[16,768]{1,0:T(8,128)S(1)}) custom-call(s32[72]{0:T(128)S(1)} %copy-done.2, bf16[8,16,768]{2,1,0:T(8,128)(2,1)} %copy-done.11, bf16[8,16,768]{2,1,0:T(8,128)(2,1)} %copy-done.12, bf16[8,16,768]{2,1,0:T(8,128)(2,1)} %copy-done.13, bf16[8,16,768]{2,1,0:T(8,128)(2,1)} %copy-done.14, ...), custom_call_target="tpu_custom_call" | custom-call | flops 50000000 | bytes 2000000 | tf_op jit(solution)/shard_map/time_grads/pallas_call | solution.py:149
  (252 shorter events, 70.1 us)
Async XLA Ops:
  11.4 13.1 %collective-permute-start.1 = (bf16[1,192,384]{2,1,0:T(8,128)(2,1)S(1)}, bf16[1,192,384]{2,1,0:T(8,128)(2,1)S(1)}, u32[]{:S(2)}, u32[]{:S(2)}) collective-permute-start(bf16[1,192,384]{2,1,0:T(8,128)(2,1)S(1)} %maximum_bitcast_fusion.1), channel_id=1, source_target_pairs={{0,4},{1,5},{2,6},{3,7},{4,0},{5,1},{6,2},{7,3},{8,12},{9,13},{10,... | collective-permute-start | bytes 442376 | tf_op jit(solution)/shard_map/ppermute | solution.py:54
  24.7 12.5 %collective-permute-start.7 = (bf16[4,192,384]{2,1,0:T(8,128)(2,1)S(1)}, bf16[4,192,384]{2,1,0:T(8,128)(2,1)S(1)}, u32[]{:S(2)}, u32[]{:S(2)}) collective-permute-start(bf16[4,192,384]{2,1,0:T(8,128)(2,1)S(1)} %pad_maximum_fusion.1), channel_id=1, source_target_pairs={{0,16},{1,9},{2,18},{3,11},{4,20},{5,13},{6,22},{7,15},{8,24},{9,1... | collective-permute-start | bytes 1769480 | tf_op jit(solution)/shard_map/ppermute | solution.py:54
  26.3 10.7 %collective-permute-start.8 = (bf16[1,240,384]{2,1,0:T(8,128)(2,1)S(1)}, bf16[1,240,384]{2,1,0:T(8,128)(2,1)S(1)}, u32[]{:S(2)}, u32[]{:S(2)}) collective-permute-start(bf16[1,240,384]{2,1,0:T(8,128)(2,1)S(1)} %maximum_bitcast_fusion), channel_id=1, source_target_pairs={{0,4},{1,5},{2,6},{3,7},{4,0},{5,1},{6,2},{7,3},{8,12},{9,13},{10,... | collective-permute-start | bytes 552968 | tf_op jit(solution)/shard_map/ppermute | solution.py:54
  37.3 25.6 %collective-permute-start.10 = (bf16[8,192,384]{2,1,0:T(8,128)(2,1)S(1)}, bf16[8,192,384]{2,1,0:T(8,128)(2,1)}, u32[]{:S(2)}, u32[]{:S(2)}) collective-permute-start(bf16[8,192,384]{2,1,0:T(8,128)(2,1)S(1)} %constant_dynamic-update-slice_fusion.10.g_a), channel_id=1, source_target_pairs={{0,8},{1,17},{2,10},{3,19},{4,12},{5,21},{6,14},{7,23},{8,0},{9,25... | collective-permute-start | bytes 3538952 | tf_op jit(solution)/shard_map/ppermute | solution.py:54
  47.0 15.9 %collective-permute-start.12 = (bf16[4,240,384]{2,1,0:T(8,128)(2,1)S(1)}, bf16[4,240,384]{2,1,0:T(8,128)(2,1)S(1)}, u32[]{:S(2)}, u32[]{:S(2)}) collective-permute-start(bf16[4,240,384]{2,1,0:T(8,128)(2,1)S(1)} %pad_maximum_fusion), channel_id=1, source_target_pairs={{0,16},{1,9},{2,18},{3,11},{4,20},{5,13},{6,22},{7,15},{8,24},{9,1... | collective-permute-start | bytes 2211848 | tf_op jit(solution)/shard_map/ppermute | solution.py:54
  47.5 15.4 %collective-permute-start.13 = (bf16[2,192,384]{2,1,0:T(8,128)(2,1)S(1)}, bf16[2,192,384]{2,1,0:T(8,128)(2,1)S(1)}, u32[]{:S(2)}, u32[]{:S(2)}) collective-permute-start(bf16[2,192,384]{2,1,0:T(8,128)(2,1)S(1)} %pad_maximum_fusion.2), channel_id=1, source_target_pairs={{0,4},{1,5},{2,6},{3,7},{4,0},{5,1},{6,2},{7,3},{8,12},{9,13},{10,... | collective-permute-start | bytes 884744 | tf_op jit(solution)/shard_map/ppermute | solution.py:54
  50.5 20.4 %collective-permute-start.14 = (bf16[8,192,384]{2,1,0:T(8,128)(2,1)S(1)}, bf16[8,192,384]{2,1,0:T(8,128)(2,1)}, u32[]{:S(2)}, u32[]{:S(2)}) collective-permute-start(bf16[8,192,384]{2,1,0:T(8,128)(2,1)S(1)} %constant_dynamic-update-slice_fusion.10.g_a), channel_id=1, source_target_pairs={{0,1},{1,0},{2,3},{3,2},{4,5},{5,4},{6,7},{7,6},{8,9},{9,8},{10,11... | collective-permute-start | bytes 3538952 | tf_op jit(solution)/shard_map/ppermute | solution.py:49
  66.0 21.0 %collective-permute-start.16 = (bf16[8,240,384]{2,1,0:T(8,128)(2,1)}, bf16[8,240,384]{2,1,0:T(8,128)(2,1)}, u32[]{:S(2)}, u32[]{:S(2)}) collective-permute-start(bf16[8,240,384]{2,1,0:T(8,128)(2,1)} %constant_dynamic-update-slice_fusion.12.u_a), channel_id=1, source_target_pairs={{0,8},{1,17},{2,10},{3,19},{4,12},{5,21},{6,14},{7,23},{8,0},{9,25... | collective-permute-start | bytes 4423688 | tf_op jit(solution)/shard_map/ppermute | solution.py:54
  68.6 19.6 %collective-permute-start.17 = (bf16[2,192,384]{2,1,0:T(8,128)(2,1)S(1)}, bf16[2,192,384]{2,1,0:T(8,128)(2,1)S(1)}, u32[]{:S(2)}, u32[]{:S(2)}) collective-permute-start(bf16[2,192,384]{2,1,0:T(8,128)(2,1)S(1)} %pad_maximum_fusion.2), channel_id=1, source_target_pairs={{0,2},{1,3},{2,0},{3,1},{4,6},{5,7},{6,4},{7,5},{8,10},{9,11},{10,... | collective-permute-start | bytes 884744 | tf_op jit(solution)/shard_map/ppermute | solution.py:54
  68.6 19.6 %collective-permute-start.18 = (bf16[2,192,384]{2,1,0:T(8,128)(2,1)S(1)}, bf16[2,192,384]{2,1,0:T(8,128)(2,1)S(1)}, u32[]{:S(2)}, u32[]{:S(2)}) collective-permute-start(bf16[2,192,384]{2,1,0:T(8,128)(2,1)S(1)} %pad_maximum_fusion.2), channel_id=1, source_target_pairs={{0,6},{1,7},{2,4},{3,5},{4,2},{5,3},{6,0},{7,1},{8,14},{9,15},{10,... | collective-permute-start | bytes 884744 | tf_op jit(solution)/shard_map/ppermute | solution.py:54
  70.9 19.3 %collective-permute-start.19 = (bf16[8,240,384]{2,1,0:T(8,128)(2,1)}, bf16[8,240,384]{2,1,0:T(8,128)(2,1)}, u32[]{:S(2)}, u32[]{:S(2)}) collective-permute-start(bf16[8,240,384]{2,1,0:T(8,128)(2,1)} %constant_dynamic-update-slice_fusion.12.u_a), channel_id=1, source_target_pairs={{0,1},{1,0},{2,3},{3,2},{4,5},{5,4},{6,7},{7,6},{8,9},{9,8},{10,11... | collective-permute-start | bytes 4423688 | tf_op jit(solution)/shard_map/ppermute | solution.py:49
  89.8 23.4 %collective-permute-start.21 = (bf16[8,192,384]{2,1,0:T(8,128)(2,1)S(1)}, bf16[8,192,384]{2,1,0:T(8,128)(2,1)S(1)}, u32[]{:S(2)}, u32[]{:S(2)}) collective-permute-start(bf16[8,192,384]{2,1,0:T(8,128)(2,1)S(1)} %constant_dynamic-update-slice_fusion.17.d_a), channel_id=1, source_target_pairs={{0,8},{1,17},{2,10},{3,19},{4,12},{5,21},{6,14},{7,23},{8,0},{9,25... | collective-permute-start | bytes 3538952 | tf_op jit(solution)/shard_map/ppermute | solution.py:54
  122.1 29.4 %collective-permute-start.25 = (bf16[8,192,384]{2,1,0:T(8,128)(2,1)S(1)}, bf16[8,192,384]{2,1,0:T(8,128)(2,1)S(1)}, u32[]{:S(2)}, u32[]{:S(2)}) collective-permute-start(bf16[8,192,384]{2,1,0:T(8,128)(2,1)S(1)} %get-tuple-element.240), channel_id=1, source_target_pairs={{0,8},{1,17},{2,10},{3,19},{4,12},{5,21},{6,14},{7,23},{8,0},{9,25... | collective-permute-start | bytes 3538952 | tf_op jit(solution)/shard_map/ppermute | solution.py:54
  162.8 19.4 %collective-permute-start.28 = (bf16[8,240,384]{2,1,0:T(8,128)(2,1)S(1)}, bf16[8,240,384]{2,1,0:T(8,128)(2,1)S(1)}, u32[]{:S(2)}, u32[]{:S(2)}) collective-permute-start(bf16[8,240,384]{2,1,0:T(8,128)(2,1)S(1)} %get-tuple-element.238), channel_id=1, source_target_pairs={{0,8},{1,17},{2,10},{3,19},{4,12},{5,21},{6,14},{7,23},{8,0},{9,25... | collective-permute-start | bytes 4423688 | tf_op jit(solution)/shard_map/ppermute | solution.py:54
  163.4 16.7 %collective-permute-start.29 = (bf16[1,192,384]{2,1,0:T(8,128)(2,1)S(1)}, bf16[1,192,384]{2,1,0:T(8,128)(2,1)S(1)}, u32[]{:S(2)}, u32[]{:S(2)}) collective-permute-start(bf16[1,192,384]{2,1,0:T(8,128)(2,1)S(1)} %get-tuple-element.256), channel_id=1, source_target_pairs={{0,4},{1,5},{2,6},{3,7},{4,0},{5,1},{6,2},{7,3},{8,12},{9,13},{10,... | collective-permute-start | bytes 442376 | tf_op jit(solution)/shard_map/ppermute | solution.py:54
  165.4 14.7 %collective-permute-start.30 = (bf16[1,192,384]{2,1,0:T(8,128)(2,1)S(1)}, bf16[1,192,384]{2,1,0:T(8,128)(2,1)S(1)}, u32[]{:S(2)}, u32[]{:S(2)}) collective-permute-start(bf16[1,192,384]{2,1,0:T(8,128)(2,1)S(1)} %get-tuple-element.255), channel_id=1, source_target_pairs={{0,2},{1,3},{2,0},{3,1},{4,6},{5,7},{6,4},{7,5},{8,10},{9,11},{10,... | collective-permute-start | bytes 442376 | tf_op jit(solution)/shard_map/ppermute | solution.py:54
  166.3 13.8 %collective-permute-start.31 = (bf16[1,192,384]{2,1,0:T(8,128)(2,1)S(1)}, bf16[1,192,384]{2,1,0:T(8,128)(2,1)S(1)}, u32[]{:S(2)}, u32[]{:S(2)}) collective-permute-start(bf16[1,192,384]{2,1,0:T(8,128)(2,1)S(1)} %get-tuple-element.254), channel_id=1, source_target_pairs={{0,6},{1,7},{2,4},{3,5},{4,2},{5,3},{6,0},{7,1},{8,14},{9,15},{10,... | collective-permute-start | bytes 442376 | tf_op jit(solution)/shard_map/ppermute | solution.py:54
  182.2 13.5 %collective-permute-start.33 = (bf16[16,144,384]{2,1,0:T(8,128)(2,1)S(1)}, bf16[16,144,384]{2,1,0:T(8,128)(2,1)S(1)}, u32[]{:S(2)}, u32[]{:S(2)}) collective-permute-start(bf16[16,144,384]{2,1,0:T(8,128)(2,1)S(1)} %get-tuple-element.203), channel_id=1, source_target_pairs={{0,1},{1,0},{2,3},{3,2},{4,5},{5,4},{6,7},{7,6},{8,9},{9,8},{10,11... | collective-permute-start | bytes 5308424 | tf_op jit(solution)/shard_map/ppermute | solution.py:49
  183.7 12.0 %collective-permute-start.32 = (bf16[4,240,384]{2,1,0:T(8,128)(2,1)S(1)}, bf16[4,240,384]{2,1,0:T(8,128)(2,1)S(1)}, u32[]{:S(2)}, u32[]{:S(2)}) collective-permute-start(bf16[4,240,384]{2,1,0:T(8,128)(2,1)S(1)} %get-tuple-element.242), channel_id=1, source_target_pairs={{0,16},{1,9},{2,18},{3,11},{4,20},{5,13},{6,22},{7,15},{8,24},{9,1... | collective-permute-start | bytes 2211848 | tf_op jit(solution)/shard_map/ppermute | solution.py:54
  196.6 19.1 %collective-permute-start.34 = (bf16[8,144,384]{2,1,0:T(8,128)(2,1)S(1)}, bf16[8,144,384]{2,1,0:T(8,128)(2,1)}, u32[]{:S(2)}, u32[]{:S(2)}) collective-permute-start(bf16[8,144,384]{2,1,0:T(8,128)(2,1)S(1)} %get-tuple-element.244), channel_id=1, source_target_pairs={{0,8},{1,17},{2,10},{3,19},{4,12},{5,21},{6,14},{7,23},{8,0},{9,25... | collective-permute-start | bytes 2654216 | tf_op jit(solution)/shard_map/ppermute | solution.py:54
  200.0 15.2 %collective-permute-start.35 = (bf16[1,240,384]{2,1,0:T(8,128)(2,1)S(1)}, bf16[1,240,384]{2,1,0:T(8,128)(2,1)S(1)}, u32[]{:S(2)}, u32[]{:S(2)}) collective-permute-start(bf16[1,240,384]{2,1,0:T(8,128)(2,1)S(1)} %get-tuple-element.252), channel_id=1, source_target_pairs={{0,4},{1,5},{2,6},{3,7},{4,0},{5,1},{6,2},{7,3},{8,12},{9,13},{10,... | collective-permute-start | bytes 552968 | tf_op jit(solution)/shard_map/ppermute | solution.py:54
  201.7 13.5 %collective-permute-start.36 = (bf16[1,240,384]{2,1,0:T(8,128)(2,1)S(1)}, bf16[1,240,384]{2,1,0:T(8,128)(2,1)S(1)}, u32[]{:S(2)}, u32[]{:S(2)}) collective-permute-start(bf16[1,240,384]{2,1,0:T(8,128)(2,1)S(1)} %get-tuple-element.251), channel_id=1, source_target_pairs={{0,2},{1,3},{2,0},{3,1},{4,6},{5,7},{6,4},{7,5},{8,10},{9,11},{10,... | collective-permute-start | bytes 552968 | tf_op jit(solution)/shard_map/ppermute | solution.py:54
  202.9 12.9 %collective-permute-start.37 = (bf16[1,240,384]{2,1,0:T(8,128)(2,1)S(1)}, bf16[1,240,384]{2,1,0:T(8,128)(2,1)S(1)}, u32[]{:S(2)}, u32[]{:S(2)}) collective-permute-start(bf16[1,240,384]{2,1,0:T(8,128)(2,1)S(1)} %get-tuple-element.250), channel_id=1, source_target_pairs={{0,6},{1,7},{2,4},{3,5},{4,2},{5,3},{6,0},{7,1},{8,14},{9,15},{10,... | collective-permute-start | bytes 552968 | tf_op jit(solution)/shard_map/ppermute | solution.py:54
  217.1 11.3 %collective-permute-start.38 = (bf16[4,144,384]{2,1,0:T(8,128)(2,1)S(1)}, bf16[4,144,384]{2,1,0:T(8,128)(2,1)S(1)}, u32[]{:S(2)}, u32[]{:S(2)}) collective-permute-start(bf16[4,144,384]{2,1,0:T(8,128)(2,1)S(1)} %get-tuple-element.248), channel_id=1, source_target_pairs={{0,16},{1,9},{2,18},{3,11},{4,20},{5,13},{6,22},{7,15},{8,24},{9,1... | collective-permute-start | bytes 1327112 | tf_op jit(solution)/shard_map/ppermute | solution.py:54
  (55 other events, 459.1 us)

commit v5 on v4

--- a/solution.py
+++ b/solution.py
@@ -214,9 +214,8 @@
 
 
 def down_rows(pieces, j):
-    return jnp.concatenate(
-        [pieces[4 * j : 4 * j + 4, h].reshape(WIDTH, LANES) for h in (0, 1)], axis=1
-    )
+    chips = pl.ds(4 * j, 4)
+    return jnp.concatenate([pieces[chips, h].reshape(WIDTH, LANES) for h in (0, 1)], axis=1)
 
 
 def qkv_columns(pieces, half):
@@ -249,28 +248,32 @@
     return (pair // 3) * 3 * LANES + (pair % 3) * 128
 
 
-def attention_rows(k, length, qkv_ref, probs_ref, att_ref):
+def attention_tile(lengths, qkv_ref, probs_ref, att_ref):
     low_half = lax.broadcasted_iota(jnp.int32, (128, 128), 1) < HEAD_DIM
-    keep = lax.broadcasted_iota(jnp.int32, (256, 128), 1) < length
-    rows = slice(128 * k, 128 * k + 128)
+    lane = lax.broadcasted_iota(jnp.int32, (256, 128), 1)
+    keep = [lane < length for length in lengths]
+    units = [(k, pair) for k in range(2) for pair in range(6)]
+
+    def part(k, pair, section):
+        base = pair_base(pair) + section * LANES
+        return qkv_ref[128 * k : 128 * k + 128, base : base + 128]
+
     scores = []
-    for pair in range(6):
-        base = pair_base(pair)
-        query = two_heads(qkv_ref[rows, base : base + 128], low_half)
-        key = qkv_ref[rows, base + LANES : base + LANES + 128]
-        scores.append(jnp.where(keep, dot_last(query, key) * HEAD_DIM ** (-0.5), NEG))
+    for k, pair in units:
+        query = two_heads(part(k, pair, 0), low_half)
+        score = dot_last(query, part(k, pair, 1)) * HEAD_DIM ** (-0.5)
+        scores.append(jnp.where(keep[k], score, NEG))
     probs = []
-    for pair in range(6):
-        shifted = jnp.exp(scores[pair] - jnp.max(scores[pair], axis=-1, keepdims=True))
+    for (k, pair), score in zip(units, scores):
+        shifted = jnp.exp(score - jnp.max(score, axis=-1, keepdims=True))
         total = jnp.sum(shifted, axis=-1, keepdims=True)
         probs.append((shifted * (1.0 / total)).astype(BF16))
         first = 256 * (6 * k + pair)
-        probs_ref[first : first + 256, :] = probs[pair]
-    for pair in range(6):
-        base = pair_base(pair) + 2 * LANES
-        value = two_heads(qkv_ref[rows, base : base + 128], low_half)
-        att_ref[rows, pair * 128 : pair * 128 + 128] = dot(
-            side_by_side(probs[pair]), value
+        probs_ref[first : first + 256, :] = probs[-1]
+    for (k, pair), prob in zip(units, probs):
+        value = two_heads(part(k, pair, 2), low_half)
+        att_ref[128 * k : 128 * k + 128, pair * 128 : pair * 128 + 128] = dot(
+            side_by_side(prob), value
         ).astype(BF16)
 
 
@@ -316,8 +319,8 @@
     for half in (0, 1):
         cols = slice(half * 3 * LANES, (half + 1) * 3 * LANES)
         qkv_ref[:, cols] = dot(normed_ref[...], qkv_columns(w, half)).astype(BF16)
-    for k in range(2):
-        attention_rows(k, lens[i // 2, i % 2 * 2 + k], qkv_ref, probs_ref, att_ref)
+    lengths = [lens[i // 2, i % 2 * 2 + k] for k in range(2)]
+    attention_tile(lengths, qkv_ref, probs_ref, att_ref)
 
 
 def attention_forward(tab, lens, sets, pieces, rows, features):
@@ -356,10 +359,9 @@
     return cdf, jnp.exp(u * u * -0.5) * (1.0 / math.sqrt(2.0 * math.pi))
 
 
-def up_columns(pieces, j):
-    first = 96 * (j % 2)
+def up_columns(pieces, half, j):
     return jnp.concatenate(
-        [block(pieces, j // 2, first), block(pieces, j // 2, first + 48)], axis=1
+        [block(pieces, half, 96 * j), block(pieces, half, 96 * j + 48)], axis=1
     )
 
 
@@ -382,28 +384,35 @@
 def up_kernel(
     tab, u_a, u_b, u_c, u_d, out_grad_ref, att_ref, x_ref, te_ref, vec_ref,
     mid_ref, two_ref, act_ref, slope_ref, theirs_ref,
-    w, sem,
+    w, w_out, sem, sem_out,
 ):
     i = pl.program_id(0)
-
-    @pl.when(i == 0)
-    def _():
-        fetch_pieces(tab, (u_a, u_b, u_c, u_d), 240, w, sem)
-        finish(w, sem)
-
-    @pl.when(i < 4)
-    def _():
+    parts = (u_a, u_b, u_c, u_d)
+
+    def token_rows(arrived):
         rows = rows_of(i, 256)
-        mid = add_embed(x_ref[...], te_ref, i) + dot(att_ref[...], both_halves(w, 192))
+        mid = add_embed(x_ref[...], te_ref, i) + dot(att_ref[...], both_halves(w_out, 0))
         mid_ref[...] = mid
         xhat, _unused = ln_stats(mid)
         two = (xhat * vec_ref[1:2, :]).astype(BF16)
         two_ref[...] = two
+        arrived()
         for j in range(4):
-            up = dot(two, up_columns(w, j))
+            up = dot(two, up_columns(w, j // 2, j % 2))
             cdf, density = gelu_parts(up)
             act_ref[j, rows, :] = (up * cdf).astype(BF16)
             slope_ref[j, rows, :] = (cdf + up * density).astype(BF16)
+
+    @pl.when(i == 0)
+    def _():
+        fetch_pieces(tab, parts, 48, w_out, sem_out, 192)
+        fetch_pieces(tab, parts, 192, w, sem)
+        finish(w_out, sem_out)
+        token_rows(lambda: finish(w, sem))
+
+    @pl.when((i > 0) & (i < 4))
+    def _():
+        token_rows(lambda: None)
 
     @pl.when(i >= 4)
     def _():
@@ -426,14 +435,19 @@
         + [ANY_SPEC] * 4
         + [VMEM_SPEC, row, row, fixed(8, WIDTH), fixed(16, WIDTH)],
         out_specs=(row, row) + (VMEM_SPEC,) * 3,
-        scratch_shapes=[pltpu.VMEM((CHIPS, 2, 240, LANES), BF16), pltpu.SemaphoreType.DMA],
+        scratch_shapes=[
+            pltpu.VMEM((CHIPS, 2, 192, LANES), BF16),
+            pltpu.VMEM((CHIPS, 2, 48, LANES), BF16),
+            pltpu.SemaphoreType.DMA,
+            pltpu.SemaphoreType.DMA,
+        ],
         compiler_params=params(26),
         cost_estimate=cost(10_000_000_000, 30_000_000, 6_000_000),
         name="up_forward",
     )(tab, *pieces, out_grad, att, rows, embed, vectors)
 
 
-def down_grad_kernel(tab, act_ref, out_grad_ref, out_ref, act_hbm, sem):
+def down_grad_kernel(tab, act_ref, out_grad_ref, _slope, out_ref, act_hbm, _slope_out, sem):
     j = pl.program_id(0)
 
     @pl.when(j == 0)
@@ -447,18 +461,21 @@
         pltpu.make_async_copy(act_ref, act_hbm, sem).wait()
 
 
-def down_grad(tab, act, out_grad):
+def down_grad(tab, act, out_grad, slope):
     return kernel_call(
         down_grad_kernel,
         grid=(4,),
-        out_shape=(local((CHIPS, 192, LANES)), shaped((4, 1024, WIDTH))),
-        in_specs=[SMEM_SPEC] + [VMEM_SPEC] * 2,
-        out_specs=(VMEM_SPEC, ANY_SPEC),
+        out_shape=(
+            local((CHIPS, 192, LANES)), shaped((4, 1024, WIDTH)), local((4, 1024, WIDTH))
+        ),
+        in_specs=[SMEM_SPEC] + [VMEM_SPEC] * 3,
+        out_specs=(VMEM_SPEC, ANY_SPEC, VMEM_SPEC),
+        input_output_aliases={3: 2},
         scratch_shapes=[pltpu.SemaphoreType.DMA],
         compiler_params=params(12),
         cost_estimate=cost(3_000_000_000, 10_000_000),
         name="down_grad",
-    )(tab, act, out_grad)
+    )(tab, act, out_grad, slope)
 
 
 def store_blocks(tab, side, target, first, part, lanes):
@@ -518,9 +535,14 @@
     tab, later_tab, u_a, u_b, u_c, u_d, d_a, d_b, d_c, d_d,
     two_hbm, att_hbm, slope_ref, out_grad_ref, mid_ref, vec_ref,
     grad_mid_ref, branch_ref, mine_up_ref, grad_att_ref, gain_ref, theirs_ref,
-    w, w_down, two, att, theirs_up, grad_up, part, sem, sem_down, sem_two, sem_att,
+    w, w_down, two, att, theirs_up, part, sem, sem_down, sem_two, sem_att,
 ):
     i = pl.program_id(0)
+    grad_up = [
+        (half_of(tab, side), j, target)
+        for side, target in enumerate((mine_up_ref, theirs_up))
+        for j in range(2)
+    ]
 
     @pl.when(i == 0)
     def _():
@@ -528,27 +550,27 @@
         gain_ref[...] = jnp.zeros_like(gain_ref)
         finish(w_down, sem_down)
         fetch_pieces(tab, (u_a, u_b, u_c, u_d), 240, w, sem)
+
+    @pl.when(i < 4)
+    def _():
+        rows = rows_of(i, 256)
+        for half, j, target in grad_up:
+            grad_act = dot_last(out_grad_ref[rows, :], down_rows(w_down, 2 * half + j))
+            slope = slope_ref[2 * half + j, rows, :].astype(F32)
+            target[j, rows, :] = (grad_act * slope).astype(BF16)
+
+    @pl.when(i == 4)
+    def _():
+        finish(w, sem)
         pltpu.make_async_copy(two_hbm, two, sem_two).start()
         pltpu.make_async_copy(att_hbm, att, sem_att).start()
 
-    @pl.when(i < 4)
-    def _():
-        rows = rows_of(i, 256)
-        for j in range(4):
-            grad_act = dot_last(out_grad_ref[rows, :], down_rows(w_down, j))
-            grad_up[j] = (grad_act * slope_ref[j, rows, :].astype(F32)).astype(BF16)
-
-        @pl.when(i == 0)
-        def _():
-            finish(w, sem)
-
+    @pl.when((i >= 4) & (i < 8))
+    def _():
+        rows = rows_of(i - 4, 256)
         y = jnp.zeros((256, WIDTH), F32)
-        for j in range(4):
-            y = y + dot_last(grad_up[j], up_columns(w, j))
-        mine = half_of(tab, 0)
-        for j in range(2):
-            mine_up_ref[j, rows, :] = grad_up[2 * mine + j]
-            theirs_up[j, rows, :] = grad_up[2 - 2 * mine + j]
+        for half, j, target in grad_up:
+            y = y + dot_last(target[j, rows, :], up_columns(w, half, j))
         xhat, scale = ln_stats(mid_ref[...])
         grad = out_grad_ref[rows, :].astype(F32) + ln_back(y, vec_ref[1:2, :], xhat, scale)
         grad_mid_ref[...] = grad
@@ -557,23 +579,24 @@
         gain_ref[...] += jnp.sum(y * xhat, axis=0, keepdims=True)
         grad_att_ref[rows, :] = dot_last(branch, both_halves(w, 192)).astype(BF16)
 
-    @pl.when(i == 4)
+    @pl.when(i == 8)
     def _():
         finish(two, sem_two)
         finish(att, sem_att)
         out_grad_rows(tab, 1, att, branch_ref, theirs_ref, part)
 
-    @pl.when(i >= 4)
-    def _():
-        up_grad_rows(tab, 1, i - 4, two[...], theirs_up[i - 4], theirs_ref, part)
+    @pl.when(i >= 8)
+    def _():
+        up_grad_rows(tab, 1, i - 8, two[...], theirs_up[i - 8], theirs_ref, part)
 
 
 def mlp_backward(
     tab, later_tab, up_pieces, down_pieces, two, att, slope, out_grad, mid, vectors
 ):
+    row = pl.BlockSpec((256, WIDTH), lambda i: (jnp.clip(i - 4, 0, 3), 0))
     return kernel_call(
         mlp_backward_kernel,
-        grid=(6,),
+        grid=(10,),
         out_shape=(
             shaped((1024, WIDTH), F32),
             local((1024, WIDTH)),
@@ -585,15 +608,14 @@
         in_specs=[SMEM_SPEC] * 2
         + [ANY_SPEC] * 10
         + [VMEM_SPEC] * 2
-        + [clamped(256, WIDTH), fixed(16, WIDTH)],
-        out_specs=(clamped(256, WIDTH),) + (VMEM_SPEC,) * 5,
+        + [row, fixed(16, WIDTH)],
+        out_specs=(row,) + (VMEM_SPEC,) * 5,
         scratch_shapes=[
             pltpu.VMEM((CHIPS, 2, 240, LANES), BF16),
             pltpu.VMEM((CHIPS, 2, 192, LANES), BF16),
             pltpu.VMEM((1024, WIDTH), BF16),
             pltpu.VMEM((1024, WIDTH), BF16),
             pltpu.VMEM((2, 1024, WIDTH), BF16),
-            pltpu.VMEM((4, 256, WIDTH), BF16),
             pltpu.VMEM((WIDTH, WIDTH), BF16),
         ]
         + [pltpu.SemaphoreType.DMA] * 4,
@@ -603,41 +625,41 @@
     )(tab, later_tab, *up_pieces, *down_pieces, two, att, slope, out_grad, mid, vectors)
 
 
-def attention_backward_rows(k, first_row, qkv_ref, probs_ref, grad_att_ref, grad_qkv_ref):
+def attention_backward_tile(first_row, qkv_ref, probs_ref, grad_att_ref, grad_qkv_ref):
     low_half = lax.broadcasted_iota(jnp.int32, (128, 128), 1) < HEAD_DIM
-    rows = slice(128 * k, 128 * k + 128)
-    whole_rows = pl.ds(pl.multiple_of(first_row, 128), 128)
-
-    def heads(ref, base):
-        where = whole_rows if ref is grad_att_ref else rows
-        return two_heads(ref[where, base : base + 128], low_half)
-
-    def probs_of(pair):
+    units = [(k, pair) for k in range(2) for pair in range(6)]
+
+    def rows(k):
+        return slice(128 * k, 128 * k + 128)
+
+    def part(k, pair, section):
+        base = pair_base(pair) + section * LANES
+        return qkv_ref[rows(k), base : base + 128]
+
+    def up(k, pair):
+        whole = pl.ds(pl.multiple_of(first_row + 128 * k, 128), 128)
+        return two_heads(grad_att_ref[whole, pair * 128 : pair * 128 + 128], low_half)
+
+    def probs_of(k, pair):
         first = 256 * (6 * k + pair)
         return probs_ref[first : first + 256, :]
 
-    grad_probs = []
-    for pair in range(6):
-        base = pair_base(pair) + 2 * LANES
-        grad_probs.append(
-            dot_last(heads(grad_att_ref, pair * 128), qkv_ref[rows, base : base + 128])
-        )
+    def store(k, pair, section, value):
+        base = pair_base(pair) + section * LANES
+        grad_qkv_ref[rows(k), base : base + 128] = value.astype(BF16)
+
+    grad_probs = [dot_last(up(k, pair), part(k, pair, 2)) for k, pair in units]
     grad_scores = []
-    for pair in range(6):
-        probs = probs_of(pair).astype(F32)
-        inner = jnp.sum(probs * grad_probs[pair], axis=-1, keepdims=True)
-        grad_scores.append((probs * (grad_probs[pair] - inner)).astype(BF16))
-    for pair in range(6):
-        base = pair_base(pair)
-        grad_query = dot(side_by_side(grad_scores[pair]), heads(qkv_ref, base + LANES))
-        grad_key = dot_first(grad_scores[pair], heads(qkv_ref, base))
-        grad_value = dot_first(probs_of(pair), heads(grad_att_ref, pair * 128))
-        grad_query = (grad_query * HEAD_DIM ** (-0.5)).astype(BF16)
-        grad_qkv_ref[rows, base : base + 128] = grad_query
-        base = base + LANES
-        grad_qkv_ref[rows, base : base + 128] = (grad_key * HEAD_DIM ** (-0.5)).astype(BF16)
-        base = base + LANES
-        grad_qkv_ref[rows, base : base + 128] = grad_value.astype(BF16)
+    for (k, pair), grad in zip(units, grad_probs):
+        probs = probs_of(k, pair).astype(F32)
+        inner = jnp.sum(probs * grad, axis=-1, keepdims=True)
+        grad_scores.append((probs * (grad - inner)).astype(BF16))
+    for (k, pair), grad in zip(units, grad_scores):
+        grad_query = dot(side_by_side(grad), two_heads(part(k, pair, 1), low_half))
+        store(k, pair, 0, grad_query * HEAD_DIM ** (-0.5))
+        grad_key = dot_first(grad, two_heads(part(k, pair, 0), low_half))
+        store(k, pair, 1, grad_key * HEAD_DIM ** (-0.5))
+        store(k, pair, 2, dot_first(probs_of(k, pair), up(k, pair)))
 
 
 def qkv_grad_rows(tab, side, normed, grad_qkv, out_ref, part):
@@ -658,10 +680,7 @@
 
     @pl.when(i < 4)
     def _():
-        for k in range(2):
-            attention_backward_rows(
-                k, i * 256 + 128 * k, qkv_ref, probs_ref, grad_att_ref, grad_qkv_ref
-            )
+        attention_backward_tile(i * 256, qkv_ref, probs_ref, grad_att_ref, grad_qkv_ref)
         for side, target in enumerate((mine_ref, kept)):
             lanes = pl.ds(pl.multiple_of(half_of(tab, side) * 3 * LANES, 128), 3 * LANES)
             target[rows_of(i, 256), :] = grad_qkv_ref[:, lanes]
@@ -781,42 +800,66 @@
     )(tab, *pieces, grad_qkv, rows, embed, vectors, grad_mid, gain_two)
 
 
-def time_grads_kernel(tab, *refs):
-    count = len(refs) - 10
-    parts = refs[:count]
-    wave_ref, hot_ref, hidden_ref, slope_ref, time_out_ref = refs[count : count + 5]
-    tin_ref, tout_ref, sums_ref, every, sem = refs[count + 5 :]
-    if count == 1:
-        pltpu.make_async_copy(parts[0], every, sem).start()
-    else:
-
-        def fetch(src, chip, half):
-            pltpu.make_async_copy(src, every.at[half * CHIPS + chip], sem).start()
-
-        each_piece(tab, parts, fetch)
+def finish_kernel(
+    tab, e_a, e_b, e_c, e_d, wave_ref, hot_ref, hidden_ref, slope_ref, time_out_ref,
+    down_ref, down_other, up_ref, up_other, qkv_ref, qkv_other,
+    tin_out, tout_out, one_out, two_out, data_out, down_out, up_out, out_out, qkv_out,
+    every, sem,
+):
+    each_piece(
+        tab,
+        (e_a, e_b, e_c, e_d),
+        lambda src, chip, half: pltpu.make_async_copy(
+            src, every.at[half * CHIPS + chip], sem
+        ).start(),
+    )
+    core = first_core(tab)
+    for half, down, up, qkv in (
+        (core, down_ref, up_ref, qkv_ref), (1 - core, down_other, up_other, qkv_other)
+    ):
+        down_out[:, lanes_of(half, LANES)] = down[pl.ds(pl.multiple_of(96 * core, 8), 96), :]
+        for b in range(4):
+            up_out[:, lanes_of(half, 4 * LANES, b * LANES)] = up[pl.ds(pl.multiple_of(48 * b + 24 * core, 8), 24), :]
+        out_out[:, lanes_of(half, LANES)] = up[pl.ds(pl.multiple_of(192 + 24 * core, 8), 24), :]
+        for sec in range(3):
+            qkv_out[:, lanes_of(half, LANES, sec * WIDTH)] = qkv[pl.ds(pl.multiple_of(48 * sec + 24 * core, 8), 24), :]
     finish(every, sem)
     grads = every[...].reshape(-1, WIDTH)
-    tout_ref[...] = dot_first(hidden_ref[...], grads)
+    tout_out[...] = dot_first(hidden_ref[...], grads)
     grad_pre = dot_last(grads, time_out_ref[...]) * slope_ref[...]
-    tin_ref[...] = dot_first(grad_pre.astype(BF16), wave_ref[...])
-    sums_ref[...] = dot(hot_ref[...], grads)
-
-
-def time_grads(tab, parts, wave, hot, hidden, slope, time_out):
+    tin_out[...] = dot_first(grad_pre.astype(BF16), wave_ref[...])
+    first = tab[68] * 24
+    lane = lax.broadcasted_iota(jnp.int32, (WIDTH, 128), 0)
+    place = lax.broadcasted_iota(jnp.int32, (WIDTH, 128), 1)
+    own = dot(grads, ((lane == place + first) & (place < 24)).astype(BF16)).astype(BF16)
+    sums = dot(hot_ref[...], own)
+    data_out[...] = sums[0:2, 0:24]
+    one_out[...] = sums[2:3, 0:24]
+    two_out[...] = sums[3:4, 0:24]
+
+
+def finish_grads(tab, parts, wave, hot, hidden, slope, time_out, pieces):
     rows, width = time_out.shape
-    devices = wave.shape[0] // 16
     return kernel_call(
-        time_grads_kernel,
+        finish_kernel,
         out_shape=(
-            shaped((rows, wave.shape[1]), F32), shaped((rows, width), F32), local((16, width), F32)
+            shaped((rows, wave.shape[1]), F32),
+            shaped((rows, width), F32),
+            shaped((1, 24), F32),
+            shaped((1, 24), F32),
+            shaped((2, 24), F32),
+            shaped((96, WIDTH), F32),
+            shaped((24, FF), F32),
+            shaped((24, WIDTH), F32),
+            shaped((24, 3 * WIDTH), F32),
         ),
-        in_specs=[SMEM_SPEC] + [ANY_SPEC] * len(parts) + [VMEM_SPEC] * 5,
-        out_specs=(VMEM_SPEC,) * 3,
-        scratch_shapes=[pltpu.VMEM((devices, 16, width), BF16), pltpu.SemaphoreType.DMA],
-        compiler_params=params(40),
-        cost_estimate=cost(50_000_000, 2_000_000),
-        name="time_grads",
-    )(tab, *parts, wave, hot, hidden, slope, time_out)
+        in_specs=[SMEM_SPEC] + [ANY_SPEC] * 4 + [VMEM_SPEC] * 11,
+        out_specs=(VMEM_SPEC,) * 9,
+        scratch_shapes=[pltpu.VMEM((2 * CHIPS, 16, width), BF16), pltpu.SemaphoreType.DMA],
+        compiler_params=params(16),
+        cost_estimate=cost(50_000_000, 4_000_000),
+        name="finish_grads",
+    )(tab, *parts, wave, hot, hidden, slope, time_out, *pieces)
 
 
 def pick(stacked, index):
@@ -843,7 +886,7 @@
         there = there + jnp.where((inner >> bit) & 1 == 1, mask, 0)
         back = back + jnp.where(jnp.bitwise_and(distance, mask) != 0, 1 << bit, 0)
     moved = jnp.where(index < 32, jnp.bitwise_xor(there, chip), back)
-    return jnp.where(index < 64, moved, core)
+    return jnp.where(index < 64, moved, jnp.where(index < 68, core, 2 * chip + core))
 
 
 def lane_blocks(x, starts, step):
@@ -853,11 +896,6 @@
     ]
 
 
-def whole_columns(core, own, other, blocks):
-    halves = (jnp.where(core == 0, own, other), jnp.where(core == 0, other, own))
-    return [[half[24 * b : 24 * b + 24] for b in range(blocks)] for half in halves]
-
-
 def swap_halves(halves, core):
     own = jnp.where(core == 0, halves[0], halves[1])
     return own, core_swap(jnp.where(core == 0, halves[1], halves[0]))
@@ -866,11 +904,6 @@
 def join_rows(own, other, core, blocks):
     shape = (blocks, own.shape[0] // blocks, LANES)
     return in_core_order(core, own.reshape(shape), other.reshape(shape), 1).reshape(-1, LANES)
-
-
-def split_rows(piece, blocks):
-    rows = piece.reshape(blocks, 2, 24, LANES).transpose(1, 0, 2, 3)
-    return rows.reshape(2, blocks * 24, LANES)
 
 
 def pack_extra(time_in, vectors, ints):
@@ -960,14 +993,14 @@
         held = jnp.concatenate([line, plane], axis=0)
         far = chip_swap(held, 8)
         up_near.append(chip_swap(after(up_piece, plane), 3))
-        up_line = jnp.concatenate([up_piece] + up_near, axis=0)
+        up_line = lax.optimization_barrier(jnp.concatenate([up_piece] + up_near, axis=0))
         up_plane = chip_swap(up_line, 4)
-        down_near = [chip_swap(after(down_pair, up_line), 2, LINE_LATER)]
+        down_near = [chip_swap(after(down_pair, up_line), p, LINE_LATER) for p in (2, 4)]
         (far, up_plane), down_near = together((far, up_plane), down_near)
         attention_pieces = (held, far, core_swap(held), core_swap(far))
         up_held = jnp.concatenate([up_line, up_plane], axis=0)
         up_far = chip_swap(up_held, 8)
-        down_last = [chip_swap(after(down_pair, up_held), p, LINE_LATER) for p in (4, 6)]
+        down_last = chip_swap(after(down_pair, up_held), 6, LINE_LATER)
     else:
         tab = jnp.concatenate(
             [jnp.tile(jnp.arange(CHIPS, dtype=jnp.int32), 4), jnp.zeros((8,), jnp.int32)]
@@ -1019,9 +1052,9 @@
     slope_pre = gate * (1.0 + pre * (1.0 - gate))
     if exchange:
         (up_far,) = arrivals
-        down_near = down_near + [after(x, embed) for x in down_last]
+        down_near = [after(x, embed) for x in [down_pair] + down_near + [down_last]]
         up_pieces = (up_held, up_far, core_swap(up_held), core_swap(up_far))
-        down_held = jnp.concatenate([down_pair] + down_near, axis=0)
+        down_held = jnp.concatenate(down_near, axis=0)
         att, wave, hot, hidden, slope_pre, down_held = lax.optimization_barrier(
             (att, wave, hot, hidden, slope_pre, down_held)
         )
@@ -1032,7 +1065,7 @@
         down_far = arrivals
         down_sum = Scatter(down_theirs)
         arrivals = [core_swap(down_held), core_swap(down_far)], down_sum.swap()
-    (down_mine, act), arrivals = together(down_grad(tab, act, grad_rows), arrivals)
+    (down_mine, act, slope), arrivals = together(down_grad(tab, act, grad_rows, slope), arrivals)
     if exchange:
         down_pieces = (down_held, down_far, *arrivals[0])
         down_sum.land(arrivals[1], down_mine)
@@ -1069,7 +1102,8 @@
         up_sum.land(arrivals[0])
         att_sum.land(arrivals[1], att_mine)
         grad_qkv = after(grad_qkv, *att_sum.send(), *up_sum.send())
-        arrivals = att_sum.fly(), up_sum.fly()
+        *up_near, up_last = up_sum.fly()
+        arrivals = att_sum.fly(), up_near
     backward = input_backward(
         tab, attention_pieces, grad_qkv, x_rows, embed, vecs, grad_mid, gain_two
     )
@@ -1080,37 +1114,32 @@
         att_sum.land(arrivals[0])
         up_sum.land(arrivals[1])
         att_sum.send()
-        brought, near = together(att_sum.fly(), [chip_swap(small, p) for p in (1, 2, 3)])
+        near = [chip_swap(small, p) for p in (1, 2, 3)]
+        brought, near = together(att_sum.fly(), near)
         att_sum.land(brought)
         small_line = jnp.concatenate([small] + near, axis=0)
         held = gather_plane(small_line)
         att_sum.send()
         far = chip_swap(held, 8)
         every = (held, far, core_swap(held), core_swap(far))
-        att_sum.land(att_sum.fly())
+        brought, up_last = together(att_sum.fly(), up_last)
+        att_sum.land(brought)
+        up_sum.land([up_last])
+        sums = after(down_total, small_line), after(up_sum.total(), small_line), att_sum.total()
+        pieces = [x for total in sums for x in (total, core_swap(total))]
+        finished = finish_grads(
+            tab, every, wave, hot, hidden, slope_pre, time_out, pieces
+        )
+        grad_tin, grad_tout, gain_one, gain_two, grad_data, *weights = finished
+        grad_down, grad_up_weight, grad_out, grad_qkv_weight = weights
     else:
-        every = (gather_all(small),)
-    grad_tin, grad_tout, sums = time_grads(tab, every, wave, hot, hidden, slope_pre, time_out)
-    own_cols = norm1_gain.shape[0]
-    sums = lax.dynamic_slice_in_dim(sums, flat * own_cols, own_cols, 1)
-
-    if exchange:
-        own, other = swap_halves(after(down_total, small_line).reshape(2, 96, LANES), core)
-        grad_down = in_core_order(core, own, other, 1)
-        piece = after(up_sum.total(), small_line)
-        out_rows = piece[192:].reshape(2, 24, LANES)
-        own, other = swap_halves(
-            jnp.concatenate([split_rows(piece[:192], 4), out_rows], axis=1), core
-        )
-        left, right = whole_columns(core, own, other, 5)
-        grad_up_weight = jnp.concatenate(left[:4] + right[:4], axis=1)
-        grad_out = jnp.concatenate([left[4], right[4]], axis=1)
-        own, other = swap_halves(split_rows(att_sum.total(), 3), core)
-        left, right = whole_columns(core, own, other, 3)
-        grad_qkv_weight = jnp.concatenate(
-            [side[sec] for sec in range(3) for side in (left, right)], axis=1
-        )
-    else:
+        every = gather_all(small).reshape(devices * 16, width)
+        grad_tout = dot_first(hidden, every)
+        grad_pre = dot_last(every, time_out) * slope_pre
+        grad_tin = dot_first(grad_pre.astype(BF16), wave)
+        own_cols = norm1_gain.shape[0]
+        sums = lax.dynamic_slice_in_dim(dot(hot, every), flat * own_cols, own_cols, 1)
+        grad_data, gain_one, gain_two = sums[0:2], sums[2], sums[3]
         scatter = partial(lax.psum_scatter, axis_name=AXES, scatter_dimension=0, tiled=True)
         both = jnp.stack([down_mine, down_theirs]).astype(F32)
         grad_down = scatter(both.transpose(1, 2, 0, 3).reshape(FF, WIDTH))
@@ -1124,15 +1153,15 @@
     return (
         result.reshape(block_input.shape),
         grad_input.reshape(block_input.shape),
-        sums[2],
+        gain_one.reshape(-1),
         grad_qkv_weight,
         grad_out,
-        sums[3],
+        gain_two.reshape(-1),
         grad_up_weight,
         grad_down,
         grad_tin,
         grad_tout,
-        sums[:2].T,
+        grad_data.T,
     )
 
 

time: 250 us -> 237 us (0.948)
  other arithmetic: 14.5 us -> 7.99 us
  local copies, waits for them, and re-layouts: 14.5 us -> 8.32 us
  waiting for transfers between devices: 57.4 us -> 60.3 us
    unnamed x81 -> x49, local copies, waits for them, and re-layouts: 8.33 us -> 3.63 us
    add x9 -> x8, other arithmetic: 6.61 us -> 2.6 us  [sum(): total = total + part[start:stop].astype(F32)]
    ppermute x35, waiting for transfers between devices: 51.9 us -> 54.9 us  [chip_swap(): lax.ppermute(x, AXES, [(i, i ^ far[i & 1]) for i in range(2 * CHIPS)])]
    pallas_call x9, Pallas kernels: 112 us -> 110 us  [run(): call(*[place(x, spec) for x, spec in zip(operands, specs, strict=True)])]
  transfers between devices with their start and end apart: 52 -> 52, of which waited for: 20 -> 21; matrix products, arithmetic and copies ran while one was open for 7% -> 4% of each run, Pallas kernels for 44% -> 45%
where the time goes in v5:
time: 237 us; the launch traced here: 236 us
  Pallas kernels  110 us (46%)
  waiting for transfers between devices  60.3 us (25%)
  starting transfers between devices  48.4 us (20%)
  local copies, waits for them, and re-layouts  8.32 us (4%)
  other arithmetic  7.99 us (3%)
    pallas_call x9, Pallas kernels, run(): call(*[place(x, spec) for x, spec in zip(operands, specs, strict=True)])  110 us
    ppermute x35, waiting for transfers between devices, chip_swap(): lax.ppermute(x, AXES, [(i, i ^ far[i & 1]) for i in range(2 * CHIPS)])  54.9 us
    ppermute x35, starting transfers between devices, chip_swap(): lax.ppermute(x, AXES, [(i, i ^ far[i & 1]) for i in range(2 * CHIPS)])  45.3 us
    ppermute x17, waiting for transfers between devices, core_swap(): return lax.ppermute(x, AXES, [(i, i ^ 1) for i in range(2 * CHIPS)])  5.44 us
  transfers between devices with their start and end apart: 52, of which 21 were waited for; matrix products, arithmetic and copies ran while one was open for 4% of the time, Pallas kernels for 45%

profile of v5, /device:TPU:0, one launch (start us, length us, event | category | flops | bytes accessed | tf_op | source)
XLA Modules:
  0.0 236.4 jit_solution(18032933178338696371)
XLA Ops:
  6.7 4.7 %collective-permute-start.3 = (bf16[1,192,384]{2,1,0:T(8,128)(2,1)S(1)}, bf16[1,192,384]{2,1,0:T(8,128)(2,1)S(1)}, u32[]{:S(2)}, u32[]{:S(2)}) collective-permute-start(bf16[1,192,384]{2,1,0:T(8,128)(2,1)S(1)} %maximum_bitcast_fusion.1), channel_id=1, source_target_pairs={{0,6},{1,7},{2,4},{3,5},{4,2},{5,3},{6,0},{7,1},{8,14},{9,15},{10,... | collective-permute-start | bytes 442376 | tf_op jit(solution)/shard_map/ppermute | solution.py:54
  16.5 3.7 %collective-permute-done.2 = bf16[1,192,384]{2,1,0:T(8,128)(2,1)S(1)} collective-permute-done((bf16[1,192,384]{2,1,0:T(8,128)(2,1)S(1)}, bf16[1,192,384]{2,1,0:T(8,128)(2,1)S(1)}, u32[]{:S(2)}, u32[]{:S(2)}) %collective-permute-start.2) | collective-permute-done | bytes 147488 | tf_op jit(solution)/shard_map/ppermute | solution.py:54
  20.2 4.4 %collective-permute-done.1 = bf16[1,192,384]{2,1,0:T(8,128)(2,1)S(1)} collective-permute-done((bf16[1,192,384]{2,1,0:T(8,128)(2,1)S(1)}, bf16[1,192,384]{2,1,0:T(8,128)(2,1)S(1)}, u32[]{:S(2)}, u32[]{:S(2)}) %collective-permute-start.1) | collective-permute-done | bytes 147488 | tf_op jit(solution)/shard_map/ppermute | solution.py:54
  26.8 2.6 %collective-permute-start.9 = (bf16[1,240,384]{2,1,0:T(8,128)(2,1)S(1)}, bf16[1,240,384]{2,1,0:T(8,128)(2,1)S(1)}, u32[]{:S(2)}, u32[]{:S(2)}) collective-permute-start(bf16[1,240,384]{2,1,0:T(8,128)(2,1)S(1)} %maximum_bitcast_fusion), channel_id=1, source_target_pairs={{0,2},{1,3},{2,0},{3,1},{4,6},{5,7},{6,4},{7,5},{8,10},{9,11},{10,... | collective-permute-start | bytes 552968 | tf_op jit(solution)/shard_map/ppermute | solution.py:54
  30.2 6.8 %collective-permute-done.8 = bf16[1,240,384]{2,1,0:T(8,128)(2,1)S(1)} collective-permute-done((bf16[1,240,384]{2,1,0:T(8,128)(2,1)S(1)}, bf16[1,240,384]{2,1,0:T(8,128)(2,1)S(1)}, u32[]{:S(2)}, u32[]{:S(2)}) %collective-permute-start.8) | collective-permute-done | bytes 184352 | tf_op jit(solution)/shard_map/ppermute | solution.py:54
  40.1 7.5 %collective-permute-done.11 = bf16[1,240,384]{2,1,0:T(8,128)(2,1)S(1)} collective-permute-done((bf16[1,240,384]{2,1,0:T(8,128)(2,1)S(1)}, bf16[1,240,384]{2,1,0:T(8,128)(2,1)S(1)}, u32[]{:S(2)}, u32[]{:S(2)}) %collective-permute-start.11) | collective-permute-done | bytes 184352 | tf_op jit(solution)/shard_map/ppermute | solution.py:54
  48.3 2.2 collective-permute-start.13
  50.5 13.3 %collective-permute-done.13 = bf16[2,192,384]{2,1,0:T(8,128)(2,1)S(1)} collective-permute-done((bf16[2,192,384]{2,1,0:T(8,128)(2,1)S(1)}, bf16[2,192,384]{2,1,0:T(8,128)(2,1)S(1)}, u32[]{:S(2)}, u32[]{:S(2)}) %collective-permute-start.13) | collective-permute-done | bytes 294944 | tf_op jit(solution)/shard_map/ppermute | solution.py:54
  68.2 15.3 %attention_forward.1 = (bf16[1024,768]{1,0:T(8,128)(2,1)}, bf16[1024,2304]{1,0:T(8,128)(2,1)}, f32[8,768]{1,0:T(8,128)}, f32[16,768]{1,0:T(8,128)}, bf16[2,16,16...) custom-call(s32[72]{0:T(128)S(1)} %compare_select_fusion.25.tab, ...), custom_call_target="tpu_custom_call" | custom-call | flops 8000000000 | bytes 20000000 | tf_op jit(solution)/shard_map/attention_forward/pallas_call | solution.py:149
  89.3 19.7 %up_forward.1 = (f32[1024,768]{1,0:T(8,128)}, bf16[1024,768]{1,0:T(8,128)(2,1)}, bf16[4,1024,768]{2,1,0:T(8,128)(2,1)S(1)}, bf16[4,1024,768]{2,1,0:T(8,128)(2,1)S(1)}, bf16[16,192,384]{2,1,0:T(8,128)(2,1)S(1)}) custom-call(s32[72]{0:T(128)S(1)} %compare_select_fusion.25.tab, bf16[8,240,384]{2,1,0:T(8,128)(2,1)} %copy-done.7, ...), custom_call_target="tpu_custom_call" | custom-call | flops 10000000000 | bytes 30000000 | tf_op jit(solution)/shard_map/up_forward/pallas_call | solution.py:149
  109.7 4.6 %down_grad.1 = (bf16[16,192,384]{2,1,0:T(8,128)(2,1)S(1)}, bf16[4,1024,768]{2,1,0:T(8,128)(2,1)}, bf16[4,1024,768]{2,1,0:T(8,128)(2,1)S(1)}) custom-call(s32[72]{0:T(128)S(1)} %compare_select_fusion.25.tab, bf16[4,1024,768]{2,1,0:T(8,128)(2,1)S(1)} %get-tuple-element.177.act_ref, bf16[1024,768]{1,0:T(8,128)(2,1)S(1)} %bitcast.41, ...), custom_call_target="tpu_custom_call", output_to_operand_aliasing={{2}: (3, {})} | custom-call | flops 3000000000 | bytes 10000000 | tf_op jit(solution)/shard_map/down_grad/pallas_call | solution.py:149
  119.7 26.1 %mlp_backward.1 = (f32[1024,768]{1,0:T(8,128)}, bf16[1024,768]{1,0:T(8,128)(2,1)S(1)}, bf16[2,1024,768]{2,1,0:T(8,128)(2,1)S(1)}, bf16[1024,768]{1,0:T(8,128)(2,...) custom-call(s32[72]{0:T(128)} %copy-done.2, s32[72]{0:T(128)} %compare_select_fusion.24.later_tab, ...), custom_call_target="tpu_custom_call" | custom-call | flops 17999998976 | bytes 50000000 | tf_op jit(solution)/shard_map/mlp_backward/pallas_call | solution.py:149
  146.5 6.2 %up_grad.1 = bf16[16,240,384]{2,1,0:T(8,128)(2,1)S(1)} custom-call(s32[72]{0:T(128)S(1)} %copy-done.3, bf16[1024,768]{1,0:T(8,128)(2,1)} %get-tuple-element.169.att_ref.att_hbm, bf16[1024,768]{1,0:T(8,128)(2,1)} %get-tuple-element.188.two_hbm, bf16[1024,768]{1,0:T(8,128)(2,1)S(1)} %get-tuple-element.201.branch_ref, ...), custom_call_target="tpu_custom_call" | custom-call | flops 3200000000 | bytes 11000000 | tf_op jit(solution)/shard_map/up_grad/pallas_call | solution.py:149
  152.7 3.4 %collective-permute-done.26 = bf16[4,192,384]{2,1,0:T(8,128)(2,1)S(1)} collective-permute-done((bf16[4,192,384]{2,1,0:T(8,128)(2,1)S(1)}, bf16[4,192,384]{2,1,0:T(8,128)(2,1)S(1)}, u32[]{:S(2)}, u32[]{:S(2)}) %collective-permute-start.26) | collective-permute-done | bytes 589856 | tf_op jit(solution)/shard_map/ppermute | solution.py:54
  157.4 2.2 collective-permute-start.30
  159.6 2.2 collective-permute-start.31
  161.8 11.5 %attention_backward.1 = (bf16[1024,2304]{1,0:T(8,128)(2,1)}, bf16[1024,1152]{1,0:T(8,128)(2,1)S(1)}, bf16[16,144,384]{2,1,0:T(8,128)(2,1)S(1)}) custom-call(s32[72]{0:T(128)S(1)} %copy-done.3, bf16[1024,768]{1,0:T(8,128)(2,1)} %get-tuple-element.185.normed_hbm.normed_ref, bf16[1024,2304]{1,0:T(8,128)(2,1)} %get-tuple-element.186.qkv_ref, ...), custom_call_target="tpu_custom_call" | custom-call | flops 11000000512 | bytes 22000000 | tf_op jit(solution)/shard_map/attention_backward/pallas_call | solution.py:149
  173.3 2.9 %collective-permute-done.28 = bf16[8,240,384]{2,1,0:T(8,128)(2,1)S(1)} collective-permute-done((bf16[8,240,384]{2,1,0:T(8,128)(2,1)S(1)}, bf16[8,240,384]{2,1,0:T(8,128)(2,1)S(1)}, u32[]{:S(2)}, u32[]{:S(2)}) %collective-permute-start.28) | collective-permute-done | bytes 1474592 | tf_op jit(solution)/shard_map/ppermute | solution.py:54
  176.8 12.0 %qkv_grad.1 = (bf16[16,144,384]{2,1,0:T(8,128)(2,1)S(1)}, bf16[1024,768]{1,0:T(8,128)(2,1)}) custom-call(s32[72]{0:T(128)S(1)} %copy-done.3, s32[72]{0:T(128)S(1)} %copy-done.4, bf16[8,192,384]{2,1,0:T(8,128)(2,1)} %copy-done.8, bf16[8,192,384]{2,1,0:T(8,128)(2,1)} %copy-done.17, bf16[8,192,384]{2,1,0:T(8,128)(2,1)} %copy-done.18, ...), custom_call_target="tpu_custom_call" | custom-call | flops 7000000000 | bytes 22000000 | tf_op jit(solution)/shard_map/qkv_grad/pallas_call | solution.py:149
  192.5 10.7 %input_backward.1 = (bf16[1024,768]{1,0:T(8,128)(2,1)}, f32[16,768]{1,0:T(8,128)S(1)}) custom-call(s32[72]{0:T(128)S(1)} %copy-done.3, bf16[8,192,384]{2,1,0:T(8,128)(2,1)} %constant_dynamic-update-slice_fusion.10.g_a, bf16[8,192,384]{2,1,0:T(8,128)(2,1)} %collective-permute-done.10.g_b, bf16[8,192,384]{2,1,0:T(8,128)(2,1)} %collective-permute-done.15.g_c, ...), custom_call_target="tpu_custom_call" | custom-call | flops 4000000000 | bytes 18000000 | tf_op jit(solution)/shard_map/input_backward/pallas_call | solution.py:149
  218.5 2.3 collective-permute-start.48
  221.7 2.3 collective-permute-done.47
  224.0 4.9 %collective-permute-done.48 = bf16[1,144,384]{2,1,0:T(8,128)(2,1)S(1)} collective-permute-done((bf16[1,144,384]{2,1,0:T(8,128)(2,1)S(1)}, bf16[1,144,384]{2,1,0:T(8,128)(2,1)S(1)}, u32[]{:S(2)}, u32[]{:S(2)}) %collective-permute-start.48) | collective-permute-done | bytes 110624 | tf_op jit(solution)/shard_map/ppermute | solution.py:54
  232.7 3.5 %finish_grads.1 = (f32[16,128]{1,0:T(8,128)}, f32[16,768]{1,0:T(8,128)}, f32[1,24]{1,0:T(1,128)}, f32[1,24]{1,0:T(1,128)}, f32[2,24]{1,0:T(2,128)}, /*index=5*/f...) custom-call(s32[72]{0:T(128)S(1)} %copy-done.3, bf16[8,16,768]{2,1,0:T(8,128)(2,1)} %copy-done.9, ...), custom_call_target="tpu_custom_call" | custom-call | flops 50000000 | bytes 4000000 | tf_op jit(solution)/shard_map/finish_grads/pallas_call | solution.py:149
  (205 shorter events, 59.9 us)
Async XLA Ops:
  11.4 13.1 %collective-permute-start.1 = (bf16[1,192,384]{2,1,0:T(8,128)(2,1)S(1)}, bf16[1,192,384]{2,1,0:T(8,128)(2,1)S(1)}, u32[]{:S(2)}, u32[]{:S(2)}) collective-permute-start(bf16[1,192,384]{2,1,0:T(8,128)(2,1)S(1)} %maximum_bitcast_fusion.1), channel_id=1, source_target_pairs={{0,4},{1,5},{2,6},{3,7},{4,0},{5,1},{6,2},{7,3},{8,12},{9,13},{10,... | collective-permute-start | bytes 442376 | tf_op jit(solution)/shard_map/ppermute | solution.py:54
  24.7 12.5 %collective-permute-start.7 = (bf16[4,192,384]{2,1,0:T(8,128)(2,1)S(1)}, bf16[4,192,384]{2,1,0:T(8,128)(2,1)S(1)}, u32[]{:S(2)}, u32[]{:S(2)}) collective-permute-start(bf16[4,192,384]{2,1,0:T(8,128)(2,1)S(1)} %pad_maximum_fusion.3), channel_id=1, source_target_pairs={{0,16},{1,9},{2,18},{3,11},{4,20},{5,13},{6,22},{7,15},{8,24},{9,1... | collective-permute-start | bytes 1769480 | tf_op jit(solution)/shard_map/ppermute | solution.py:54
  26.3 10.7 %collective-permute-start.8 = (bf16[1,240,384]{2,1,0:T(8,128)(2,1)S(1)}, bf16[1,240,384]{2,1,0:T(8,128)(2,1)S(1)}, u32[]{:S(2)}, u32[]{:S(2)}) collective-permute-start(bf16[1,240,384]{2,1,0:T(8,128)(2,1)S(1)} %maximum_bitcast_fusion), channel_id=1, source_target_pairs={{0,4},{1,5},{2,6},{3,7},{4,0},{5,1},{6,2},{7,3},{8,12},{9,13},{10,... | collective-permute-start | bytes 552968 | tf_op jit(solution)/shard_map/ppermute | solution.py:54
  38.1 26.9 %collective-permute-start.10 = (bf16[8,192,384]{2,1,0:T(8,128)(2,1)}, bf16[8,192,384]{2,1,0:T(8,128)(2,1)}, u32[]{:S(2)}, u32[]{:S(2)}) collective-permute-start(bf16[8,192,384]{2,1,0:T(8,128)(2,1)} %constant_dynamic-update-slice_fusion.10.g_a), channel_id=1, source_target_pairs={{0,8},{1,17},{2,10},{3,19},{4,12},{5,21},{6,14},{7,23},{8,0},{9,25... | collective-permute-start | bytes 3538952 | tf_op jit(solution)/shard_map/ppermute | solution.py:54
  47.8 17.2 %collective-permute-start.12 = (bf16[4,240,384]{2,1,0:T(8,128)(2,1)S(1)}, bf16[4,240,384]{2,1,0:T(8,128)(2,1)S(1)}, u32[]{:S(2)}, u32[]{:S(2)}) collective-permute-start(bf16[4,240,384]{2,1,0:T(8,128)(2,1)S(1)} %pad_maximum_fusion.2), channel_id=1, source_target_pairs={{0,16},{1,9},{2,18},{3,11},{4,20},{5,13},{6,22},{7,15},{8,24},{9,1... | collective-permute-start | bytes 2211848 | tf_op jit(solution)/shard_map/ppermute | solution.py:54
  48.3 15.5 %collective-permute-start.13 = (bf16[2,192,384]{2,1,0:T(8,128)(2,1)S(1)}, bf16[2,192,384]{2,1,0:T(8,128)(2,1)S(1)}, u32[]{:S(2)}, u32[]{:S(2)}) collective-permute-start(bf16[2,192,384]{2,1,0:T(8,128)(2,1)S(1)} %pad_maximum_fusion.4), channel_id=1, source_target_pairs={{0,4},{1,5},{2,6},{3,7},{4,0},{5,1},{6,2},{7,3},{8,12},{9,13},{10,... | collective-permute-start | bytes 884744 | tf_op jit(solution)/shard_map/ppermute | solution.py:54
  50.5 14.5 %collective-permute-start.14 = (bf16[2,192,384]{2,1,0:T(8,128)(2,1)S(1)}, bf16[2,192,384]{2,1,0:T(8,128)(2,1)S(1)}, u32[]{:S(2)}, u32[]{:S(2)}) collective-permute-start(bf16[2,192,384]{2,1,0:T(8,128)(2,1)S(1)} %pad_maximum_fusion.4), channel_id=1, source_target_pairs={{0,2},{1,3},{2,0},{3,1},{4,6},{5,7},{6,4},{7,5},{8,10},{9,11},{10,... | collective-permute-start | bytes 884744 | tf_op jit(solution)/shard_map/ppermute | solution.py:54
  50.5 17.1 %collective-permute-start.15 = (bf16[8,192,384]{2,1,0:T(8,128)(2,1)}, bf16[8,192,384]{2,1,0:T(8,128)(2,1)}, u32[]{:S(2)}, u32[]{:S(2)}) collective-permute-start(bf16[8,192,384]{2,1,0:T(8,128)(2,1)} %constant_dynamic-update-slice_fusion.10.g_a), channel_id=1, source_target_pairs={{0,1},{1,0},{2,3},{3,2},{4,5},{5,4},{6,7},{7,6},{8,9},{9,8},{10,11... | collective-permute-start | bytes 3538952 | tf_op jit(solution)/shard_map/ppermute | solution.py:49
  65.2 19.5 %collective-permute-start.17 = (bf16[8,240,384]{2,1,0:T(8,128)(2,1)S(1)}, bf16[8,240,384]{2,1,0:T(8,128)(2,1)}, u32[]{:S(2)}, u32[]{:S(2)}) collective-permute-start(bf16[8,240,384]{2,1,0:T(8,128)(2,1)S(1)} %pad_maximum_fusion.u_a), channel_id=1, source_target_pairs={{0,8},{1,17},{2,10},{3,19},{4,12},{5,21},{6,14},{7,23},{8,0},{9,25... | collective-permute-start | bytes 4423688 | tf_op jit(solution)/shard_map/ppermute | solution.py:54
  67.1 21.8 %collective-permute-start.19 = (bf16[8,240,384]{2,1,0:T(8,128)(2,1)S(1)}, bf16[8,240,384]{2,1,0:T(8,128)(2,1)}, u32[]{:S(2)}, u32[]{:S(2)}) collective-permute-start(bf16[8,240,384]{2,1,0:T(8,128)(2,1)S(1)} %pad_maximum_fusion.u_a), channel_id=1, source_target_pairs={{0,1},{1,0},{2,3},{3,2},{4,5},{5,4},{6,7},{7,6},{8,9},{9,8},{10,11... | collective-permute-start | bytes 4423688 | tf_op jit(solution)/shard_map/ppermute | solution.py:49
  67.2 18.7 %collective-permute-start.18 = (bf16[2,192,384]{2,1,0:T(8,128)(2,1)S(1)}, bf16[2,192,384]{2,1,0:T(8,128)(2,1)S(1)}, u32[]{:S(2)}, u32[]{:S(2)}) collective-permute-start(bf16[2,192,384]{2,1,0:T(8,128)(2,1)S(1)} %pad_maximum_fusion.4), channel_id=1, source_target_pairs={{0,6},{1,7},{2,4},{3,5},{4,2},{5,3},{6,0},{7,1},{8,14},{9,15},{10,... | collective-permute-start | bytes 884744 | tf_op jit(solution)/shard_map/ppermute | solution.py:54
  87.1 21.9 %collective-permute-start.21 = (bf16[8,192,384]{2,1,0:T(8,128)(2,1)S(1)}, bf16[8,192,384]{2,1,0:T(8,128)(2,1)S(1)}, u32[]{:S(2)}, u32[]{:S(2)}) collective-permute-start(bf16[8,192,384]{2,1,0:T(8,128)(2,1)S(1)} %pad_maximum_fusion.1.d_a), channel_id=1, source_target_pairs={{0,8},{1,17},{2,10},{3,19},{4,12},{5,21},{6,14},{7,23},{8,0},{9,25... | collective-permute-start | bytes 3538952 | tf_op jit(solution)/shard_map/ppermute | solution.py:54
  118.0 27.8 %collective-permute-start.25 = (bf16[8,192,384]{2,1,0:T(8,128)(2,1)S(1)}, bf16[8,192,384]{2,1,0:T(8,128)(2,1)S(1)}, u32[]{:S(2)}, u32[]{:S(2)}) collective-permute-start(bf16[8,192,384]{2,1,0:T(8,128)(2,1)S(1)} %get-tuple-element.266), channel_id=1, source_target_pairs={{0,8},{1,17},{2,10},{3,19},{4,12},{5,21},{6,14},{7,23},{8,0},{9,25... | collective-permute-start | bytes 3538952 | tf_op jit(solution)/shard_map/ppermute | solution.py:54
  156.8 19.4 %collective-permute-start.28 = (bf16[8,240,384]{2,1,0:T(8,128)(2,1)S(1)}, bf16[8,240,384]{2,1,0:T(8,128)(2,1)S(1)}, u32[]{:S(2)}, u32[]{:S(2)}) collective-permute-start(bf16[8,240,384]{2,1,0:T(8,128)(2,1)S(1)} %get-tuple-element.264), channel_id=1, source_target_pairs={{0,8},{1,17},{2,10},{3,19},{4,12},{5,21},{6,14},{7,23},{8,0},{9,25... | collective-permute-start | bytes 4423688 | tf_op jit(solution)/shard_map/ppermute | solution.py:54
  157.3 15.9 %collective-permute-start.29 = (bf16[1,192,384]{2,1,0:T(8,128)(2,1)S(1)}, bf16[1,192,384]{2,1,0:T(8,128)(2,1)S(1)}, u32[]{:S(2)}, u32[]{:S(2)}) collective-permute-start(bf16[1,192,384]{2,1,0:T(8,128)(2,1)S(1)} %get-tuple-element.282), channel_id=1, source_target_pairs={{0,4},{1,5},{2,6},{3,7},{4,0},{5,1},{6,2},{7,3},{8,12},{9,13},{10,... | collective-permute-start | bytes 442376 | tf_op jit(solution)/shard_map/ppermute | solution.py:54
  157.4 15.8 %collective-permute-start.30 = (bf16[1,192,384]{2,1,0:T(8,128)(2,1)S(1)}, bf16[1,192,384]{2,1,0:T(8,128)(2,1)S(1)}, u32[]{:S(2)}, u32[]{:S(2)}) collective-permute-start(bf16[1,192,384]{2,1,0:T(8,128)(2,1)S(1)} %get-tuple-element.281), channel_id=1, source_target_pairs={{0,2},{1,3},{2,0},{3,1},{4,6},{5,7},{6,4},{7,5},{8,10},{9,11},{10,... | collective-permute-start | bytes 442376 | tf_op jit(solution)/shard_map/ppermute | solution.py:54
  159.6 13.7 %collective-permute-start.31 = (bf16[1,192,384]{2,1,0:T(8,128)(2,1)S(1)}, bf16[1,192,384]{2,1,0:T(8,128)(2,1)S(1)}, u32[]{:S(2)}, u32[]{:S(2)}) collective-permute-start(bf16[1,192,384]{2,1,0:T(8,128)(2,1)S(1)} %get-tuple-element.280), channel_id=1, source_target_pairs={{0,6},{1,7},{2,4},{3,5},{4,2},{5,3},{6,0},{7,1},{8,14},{9,15},{10,... | collective-permute-start | bytes 442376 | tf_op jit(solution)/shard_map/ppermute | solution.py:54
  176.2 12.7 %collective-permute-start.33 = (bf16[16,144,384]{2,1,0:T(8,128)(2,1)S(1)}, bf16[16,144,384]{2,1,0:T(8,128)(2,1)S(1)}, u32[]{:S(2)}, u32[]{:S(2)}) collective-permute-start(bf16[16,144,384]{2,1,0:T(8,128)(2,1)S(1)} %get-tuple-element.222), channel_id=1, source_target_pairs={{0,1},{1,0},{2,3},{3,2},{4,5},{5,4},{6,7},{7,6},{8,9},{9,8},{10,11... | collective-permute-start | bytes 5308424 | tf_op jit(solution)/shard_map/ppermute | solution.py:49
  176.5 12.4 %collective-permute-start.32 = (bf16[4,240,384]{2,1,0:T(8,128)(2,1)S(1)}, bf16[4,240,384]{2,1,0:T(8,128)(2,1)S(1)}, u32[]{:S(2)}, u32[]{:S(2)}) collective-permute-start(bf16[4,240,384]{2,1,0:T(8,128)(2,1)S(1)} %get-tuple-element.268), channel_id=1, source_target_pairs={{0,16},{1,9},{2,18},{3,11},{4,20},{5,13},{6,22},{7,15},{8,24},{9,1... | collective-permute-start | bytes 2211848 | tf_op jit(solution)/shard_map/ppermute | solution.py:54
  189.2 14.0 %collective-permute-start.34 = (bf16[8,144,384]{2,1,0:T(8,128)(2,1)S(1)}, bf16[8,144,384]{2,1,0:T(8,128)(2,1)S(1)}, u32[]{:S(2)}, u32[]{:S(2)}) collective-permute-start(bf16[8,144,384]{2,1,0:T(8,128)(2,1)S(1)} %get-tuple-element.270), channel_id=1, source_target_pairs={{0,8},{1,17},{2,10},{3,19},{4,12},{5,21},{6,14},{7,23},{8,0},{9,25... | collective-permute-start | bytes 2654216 | tf_op jit(solution)/shard_map/ppermute | solution.py:54
  191.1 12.1 %collective-permute-start.35 = (bf16[1,240,384]{2,1,0:T(8,128)(2,1)S(1)}, bf16[1,240,384]{2,1,0:T(8,128)(2,1)S(1)}, u32[]{:S(2)}, u32[]{:S(2)}) collective-permute-start(bf16[1,240,384]{2,1,0:T(8,128)(2,1)S(1)} %get-tuple-element.278), channel_id=1, source_target_pairs={{0,4},{1,5},{2,6},{3,7},{4,0},{5,1},{6,2},{7,3},{8,12},{9,13},{10,... | collective-permute-start | bytes 552968 | tf_op jit(solution)/shard_map/ppermute | solution.py:54
  191.2 12.1 %collective-permute-start.36 = (bf16[1,240,384]{2,1,0:T(8,128)(2,1)S(1)}, bf16[1,240,384]{2,1,0:T(8,128)(2,1)S(1)}, u32[]{:S(2)}, u32[]{:S(2)}) collective-permute-start(bf16[1,240,384]{2,1,0:T(8,128)(2,1)S(1)} %get-tuple-element.277), channel_id=1, source_target_pairs={{0,2},{1,3},{2,0},{3,1},{4,6},{5,7},{6,4},{7,5},{8,10},{9,11},{10,... | collective-permute-start | bytes 552968 | tf_op jit(solution)/shard_map/ppermute | solution.py:54
  209.5 11.3 %collective-permute-start.49 = (bf16[1,240,384]{2,1,0:T(8,128)(2,1)S(1)}, bf16[1,240,384]{2,1,0:T(8,128)(2,1)S(1)}, u32[]{:S(2)}, u32[]{:S(2)}) collective-permute-start(bf16[1,240,384]{2,1,0:T(8,128)(2,1)S(1)} %get-tuple-element.276), channel_id=1, source_target_pairs={{0,6},{1,7},{2,4},{3,5},{4,2},{5,3},{6,0},{7,1},{8,14},{9,15},{10,... | collective-permute-start | bytes 552968 | tf_op jit(solution)/shard_map/ppermute | solution.py:54
  215.1 16.2 %collective-permute-start.45 = (f32[192,384]{1,0:T(8,128)S(1)}, f32[192,384]{1,0:T(8,128)S(1)}, u32[]{:S(2)}, u32[]{:S(2)}) collective-permute-start(f32[192,384]{1,0:T(8,128)S(1)} %add_bitcast_fusion.1.down_ref), channel_id=1, source_target_pairs={{0,1},{1,0},{2,3},{3,2},{4,5},{5,4},{6,7},{7,6},{8,9},{9,8},{10,11... | collective-permute-start | bytes 884744 | tf_op jit(solution)/shard_map/ppermute | solution.py:49
  (48 other events, 441.1 us)

commit v6 on v5

--- a/solution.py
+++ b/solution.py
@@ -801,14 +801,14 @@
 
 
 def finish_kernel(
-    tab, e_a, e_b, e_c, e_d, wave_ref, hot_ref, hidden_ref, slope_ref, time_out_ref,
+    tab, e_mine, e_theirs, wave_ref, hot_ref, hidden_ref, slope_ref, time_out_ref,
     down_ref, down_other, up_ref, up_other, qkv_ref, qkv_other,
     tin_out, tout_out, one_out, two_out, data_out, down_out, up_out, out_out, qkv_out,
     every, sem,
 ):
     each_piece(
         tab,
-        (e_a, e_b, e_c, e_d),
+        [e.at[pl.ds(first, 8)] for e in (e_mine, e_theirs) for first in (0, 8)],
         lambda src, chip, half: pltpu.make_async_copy(
             src, every.at[half * CHIPS + chip], sem
         ).start(),
@@ -853,7 +853,7 @@
             shaped((24, WIDTH), F32),
             shaped((24, 3 * WIDTH), F32),
         ),
-        in_specs=[SMEM_SPEC] + [ANY_SPEC] * 4 + [VMEM_SPEC] * 11,
+        in_specs=[SMEM_SPEC] + [ANY_SPEC] * 2 + [VMEM_SPEC] * 11,
         out_specs=(VMEM_SPEC,) * 9,
         scratch_shapes=[pltpu.VMEM((2 * CHIPS, 16, width), BF16), pltpu.SemaphoreType.DMA],
         compiler_params=params(16),
@@ -1118,11 +1118,13 @@
         brought, near = together(att_sum.fly(), near)
         att_sum.land(brought)
         small_line = jnp.concatenate([small] + near, axis=0)
-        held = gather_plane(small_line)
         att_sum.send()
-        far = chip_swap(held, 8)
-        every = (held, far, core_swap(held), core_swap(far))
-        brought, up_last = together(att_sum.fly(), up_last)
+        brought = att_sum.fly()
+        small_line, brought[1] = lax.optimization_barrier((small_line, brought[1]))
+        plane = [small_line] + [chip_swap(small_line, p) for p in (4, 8, 12)]
+        every = jnp.concatenate(plane, axis=0)
+        every = every, core_swap(every)
+        brought, up_last = together(brought, up_last)
         att_sum.land(brought)
         up_sum.land([up_last])
         sums = after(down_total, small_line), after(up_sum.total(), small_line), att_sum.total()

time: 237 us -> 236 us (level)
  waiting for transfers between devices: 60.3 us -> 57.6 us
    ppermute x35 -> x36, waiting for transfers between devices: 54.9 us -> 52.2 us  [chip_swap(): lax.ppermute(x, AXES, [(i, i ^ far[i & 1]) for i in range(2 * CHIPS)])]
    ppermute x35 -> x36, starting transfers between devices: 45.3 us -> 46.3 us  [chip_swap(): lax.ppermute(x, AXES, [(i, i ^ far[i & 1]) for i in range(2 * CHIPS)])]
    ppermute x17 -> x16, waiting for transfers between devices: 5.44 us -> 5.45 us  [core_swap(): return lax.ppermute(x, AXES, [(i, i ^ 1) for i in range(2 * CHIPS)])]
  transfers between devices with their start and end apart: 52 -> 52, of which waited for: 21 -> 20; matrix products, arithmetic and copies ran while one was open for 4% -> 4% of each run, Pallas kernels for 45% -> 45%
where the time goes in v6:
time: 236 us; the launch traced here: 235 us
  Pallas kernels  110 us (47%)
  waiting for transfers between devices  57.6 us (24%)
  starting transfers between devices  49.5 us (21%)
  other arithmetic  7.99 us (3%)
  local copies, waits for them, and re-layouts  7.98 us (3%)
    pallas_call x9, Pallas kernels, run(): call(*[place(x, spec) for x, spec in zip(operands, specs, strict=True)])  110 us
    ppermute x36, waiting for transfers between devices, chip_swap(): lax.ppermute(x, AXES, [(i, i ^ far[i & 1]) for i in range(2 * CHIPS)])  52.2 us
    ppermute x36, starting transfers between devices, chip_swap(): lax.ppermute(x, AXES, [(i, i ^ far[i & 1]) for i in range(2 * CHIPS)])  46.3 us
    ppermute x16, waiting for transfers between devices, core_swap(): return lax.ppermute(x, AXES, [(i, i ^ 1) for i in range(2 * CHIPS)])  5.45 us
  transfers between devices with their start and end apart: 52, of which 20 were waited for; matrix products, arithmetic and copies ran while one was open for 4% of the time, Pallas kernels for 45%

profile of v6, /device:TPU:0, one launch (start us, length us, event | category | flops | bytes accessed | tf_op | source)
XLA Modules:
  0.0 234.6 jit_solution(12513774458732092328)
XLA Ops:
  6.7 4.7 %collective-permute-start.3 = (bf16[1,192,384]{2,1,0:T(8,128)(2,1)S(1)}, bf16[1,192,384]{2,1,0:T(8,128)(2,1)S(1)}, u32[]{:S(2)}, u32[]{:S(2)}) collective-permute-start(bf16[1,192,384]{2,1,0:T(8,128)(2,1)S(1)} %maximum_bitcast_fusion.1), channel_id=1, source_target_pairs={{0,6},{1,7},{2,4},{3,5},{4,2},{5,3},{6,0},{7,1},{8,14},{9,15},{10,... | collective-permute-start | bytes 442376 | tf_op jit(solution)/shard_map/ppermute | solution.py:54
  16.5 3.7 %collective-permute-done.2 = bf16[1,192,384]{2,1,0:T(8,128)(2,1)S(1)} collective-permute-done((bf16[1,192,384]{2,1,0:T(8,128)(2,1)S(1)}, bf16[1,192,384]{2,1,0:T(8,128)(2,1)S(1)}, u32[]{:S(2)}, u32[]{:S(2)}) %collective-permute-start.2) | collective-permute-done | bytes 147488 | tf_op jit(solution)/shard_map/ppermute | solution.py:54
  20.2 4.4 %collective-permute-done.1 = bf16[1,192,384]{2,1,0:T(8,128)(2,1)S(1)} collective-permute-done((bf16[1,192,384]{2,1,0:T(8,128)(2,1)S(1)}, bf16[1,192,384]{2,1,0:T(8,128)(2,1)S(1)}, u32[]{:S(2)}, u32[]{:S(2)}) %collective-permute-start.1) | collective-permute-done | bytes 147488 | tf_op jit(solution)/shard_map/ppermute | solution.py:54
  26.8 2.6 %collective-permute-start.9 = (bf16[1,240,384]{2,1,0:T(8,128)(2,1)S(1)}, bf16[1,240,384]{2,1,0:T(8,128)(2,1)S(1)}, u32[]{:S(2)}, u32[]{:S(2)}) collective-permute-start(bf16[1,240,384]{2,1,0:T(8,128)(2,1)S(1)} %maximum_bitcast_fusion), channel_id=1, source_target_pairs={{0,2},{1,3},{2,0},{3,1},{4,6},{5,7},{6,4},{7,5},{8,10},{9,11},{10,... | collective-permute-start | bytes 552968 | tf_op jit(solution)/shard_map/ppermute | solution.py:54
  30.2 6.8 %collective-permute-done.8 = bf16[1,240,384]{2,1,0:T(8,128)(2,1)S(1)} collective-permute-done((bf16[1,240,384]{2,1,0:T(8,128)(2,1)S(1)}, bf16[1,240,384]{2,1,0:T(8,128)(2,1)S(1)}, u32[]{:S(2)}, u32[]{:S(2)}) %collective-permute-start.8) | collective-permute-done | bytes 184352 | tf_op jit(solution)/shard_map/ppermute | solution.py:54
  40.1 7.5 %collective-permute-done.11 = bf16[1,240,384]{2,1,0:T(8,128)(2,1)S(1)} collective-permute-done((bf16[1,240,384]{2,1,0:T(8,128)(2,1)S(1)}, bf16[1,240,384]{2,1,0:T(8,128)(2,1)S(1)}, u32[]{:S(2)}, u32[]{:S(2)}) %collective-permute-start.11) | collective-permute-done | bytes 184352 | tf_op jit(solution)/shard_map/ppermute | solution.py:54
  48.3 2.2 collective-permute-start.13
  50.5 13.3 %collective-permute-done.13 = bf16[2,192,384]{2,1,0:T(8,128)(2,1)S(1)} collective-permute-done((bf16[2,192,384]{2,1,0:T(8,128)(2,1)S(1)}, bf16[2,192,384]{2,1,0:T(8,128)(2,1)S(1)}, u32[]{:S(2)}, u32[]{:S(2)}) %collective-permute-start.13) | collective-permute-done | bytes 294944 | tf_op jit(solution)/shard_map/ppermute | solution.py:54
  68.2 15.3 %attention_forward.1 = (bf16[1024,768]{1,0:T(8,128)(2,1)}, bf16[1024,2304]{1,0:T(8,128)(2,1)}, f32[8,768]{1,0:T(8,128)}, f32[16,768]{1,0:T(8,128)}, bf16[2,16,16...) custom-call(s32[72]{0:T(128)S(1)} %compare_select_fusion.25.tab, ...), custom_call_target="tpu_custom_call" | custom-call | flops 8000000000 | bytes 20000000 | tf_op jit(solution)/shard_map/attention_forward/pallas_call | solution.py:149
  89.3 19.7 %up_forward.1 = (f32[1024,768]{1,0:T(8,128)}, bf16[1024,768]{1,0:T(8,128)(2,1)}, bf16[4,1024,768]{2,1,0:T(8,128)(2,1)S(1)}, bf16[4,1024,768]{2,1,0:T(8,128)(2,1)S(1)}, bf16[16,192,384]{2,1,0:T(8,128)(2,1)S(1)}) custom-call(s32[72]{0:T(128)S(1)} %compare_select_fusion.25.tab, bf16[8,240,384]{2,1,0:T(8,128)(2,1)} %copy-done.7, ...), custom_call_target="tpu_custom_call" | custom-call | flops 10000000000 | bytes 30000000 | tf_op jit(solution)/shard_map/up_forward/pallas_call | solution.py:149
  109.7 4.6 %down_grad.1 = (bf16[16,192,384]{2,1,0:T(8,128)(2,1)S(1)}, bf16[4,1024,768]{2,1,0:T(8,128)(2,1)}, bf16[4,1024,768]{2,1,0:T(8,128)(2,1)S(1)}) custom-call(s32[72]{0:T(128)S(1)} %compare_select_fusion.25.tab, bf16[4,1024,768]{2,1,0:T(8,128)(2,1)S(1)} %get-tuple-element.179.act_ref, bf16[1024,768]{1,0:T(8,128)(2,1)S(1)} %bitcast.40, ...), custom_call_target="tpu_custom_call", output_to_operand_aliasing={{2}: (3, {})} | custom-call | flops 3000000000 | bytes 10000000 | tf_op jit(solution)/shard_map/down_grad/pallas_call | solution.py:149
  119.7 26.1 %mlp_backward.1 = (f32[1024,768]{1,0:T(8,128)}, bf16[1024,768]{1,0:T(8,128)(2,1)S(1)}, bf16[2,1024,768]{2,1,0:T(8,128)(2,1)S(1)}, bf16[1024,768]{1,0:T(8,128)(2,...) custom-call(s32[72]{0:T(128)} %copy-done.2, s32[72]{0:T(128)} %compare_select_fusion.24.later_tab, ...), custom_call_target="tpu_custom_call" | custom-call | flops 17999998976 | bytes 50000000 | tf_op jit(solution)/shard_map/mlp_backward/pallas_call | solution.py:149
  146.4 6.2 %up_grad.1 = bf16[16,240,384]{2,1,0:T(8,128)(2,1)S(1)} custom-call(s32[72]{0:T(128)S(1)} %copy-done.3, bf16[1024,768]{1,0:T(8,128)(2,1)} %get-tuple-element.171.att_ref.att_hbm, bf16[1024,768]{1,0:T(8,128)(2,1)} %get-tuple-element.190.two_hbm, bf16[1024,768]{1,0:T(8,128)(2,1)S(1)} %get-tuple-element.203.branch_ref, ...), custom_call_target="tpu_custom_call" | custom-call | flops 3200000000 | bytes 11000000 | tf_op jit(solution)/shard_map/up_grad/pallas_call | solution.py:149
  152.7 3.4 %collective-permute-done.26 = bf16[4,192,384]{2,1,0:T(8,128)(2,1)S(1)} collective-permute-done((bf16[4,192,384]{2,1,0:T(8,128)(2,1)S(1)}, bf16[4,192,384]{2,1,0:T(8,128)(2,1)S(1)}, u32[]{:S(2)}, u32[]{:S(2)}) %collective-permute-start.26) | collective-permute-done | bytes 589856 | tf_op jit(solution)/shard_map/ppermute | solution.py:54
  157.4 2.2 collective-permute-start.30
  161.8 11.4 %attention_backward.1 = (bf16[1024,2304]{1,0:T(8,128)(2,1)}, bf16[1024,1152]{1,0:T(8,128)(2,1)S(1)}, bf16[16,144,384]{2,1,0:T(8,128)(2,1)S(1)}) custom-call(s32[72]{0:T(128)S(1)} %copy-done.3, bf16[1024,768]{1,0:T(8,128)(2,1)} %get-tuple-element.187.normed_hbm.normed_ref, bf16[1024,2304]{1,0:T(8,128)(2,1)} %get-tuple-element.188.qkv_ref, ...), custom_call_target="tpu_custom_call" | custom-call | flops 11000000512 | bytes 22000000 | tf_op jit(solution)/shard_map/attention_backward/pallas_call | solution.py:149
  173.2 2.9 %collective-permute-done.28 = bf16[8,240,384]{2,1,0:T(8,128)(2,1)S(1)} collective-permute-done((bf16[8,240,384]{2,1,0:T(8,128)(2,1)S(1)}, bf16[8,240,384]{2,1,0:T(8,128)(2,1)S(1)}, u32[]{:S(2)}, u32[]{:S(2)}) %collective-permute-start.28) | collective-permute-done | bytes 1474592 | tf_op jit(solution)/shard_map/ppermute | solution.py:54
  176.8 12.0 %qkv_grad.1 = (bf16[16,144,384]{2,1,0:T(8,128)(2,1)S(1)}, bf16[1024,768]{1,0:T(8,128)(2,1)}) custom-call(s32[72]{0:T(128)S(1)} %copy-done.3, s32[72]{0:T(128)S(1)} %copy-done.4, bf16[8,192,384]{2,1,0:T(8,128)(2,1)} %copy-done.8, bf16[8,192,384]{2,1,0:T(8,128)(2,1)} %copy-done.15, bf16[8,192,384]{2,1,0:T(8,128)(2,1)} %copy-done.16, ...), custom_call_target="tpu_custom_call" | custom-call | flops 7000000000 | bytes 22000000 | tf_op jit(solution)/shard_map/qkv_grad/pallas_call | solution.py:149
  192.6 10.7 %input_backward.1 = (bf16[1024,768]{1,0:T(8,128)(2,1)}, f32[16,768]{1,0:T(8,128)S(1)}) custom-call(s32[72]{0:T(128)S(1)} %copy-done.3, bf16[8,192,384]{2,1,0:T(8,128)(2,1)} %constant_dynamic-update-slice_fusion.10.g_a, bf16[8,192,384]{2,1,0:T(8,128)(2,1)} %collective-permute-done.10.g_b, bf16[8,192,384]{2,1,0:T(8,128)(2,1)} %collective-permute-done.15.g_c, ...), custom_call_target="tpu_custom_call" | custom-call | flops 4000000000 | bytes 18000000 | tf_op jit(solution)/shard_map/input_backward/pallas_call | solution.py:149
  216.1 2.2 collective-permute-start.48
  218.4 2.4 %collective-permute-done.41 = bf16[1,144,384]{2,1,0:T(8,128)(2,1)S(1)} collective-permute-done((bf16[1,144,384]{2,1,0:T(8,128)(2,1)S(1)}, bf16[1,144,384]{2,1,0:T(8,128)(2,1)S(1)}, u32[]{:S(2)}, u32[]{:S(2)}) %collective-permute-start.41) | collective-permute-done | bytes 110624 | tf_op jit(solution)/shard_map/ppermute | solution.py:54
  221.8 2.4 %collective-permute-start.44 = (bf16[4,16,768]{2,1,0:T(8,128)(2,1)S(1)}, bf16[4,16,768]{2,1,0:T(8,128)(2,1)S(1)}, u32[]{:S(2)}, u32[]{:S(2)}) collective-permute-start(bf16[4,16,768]{2,1,0:T(8,128)(2,1)S(1)} %pad_maximum_fusion.5), channel_id=1, source_target_pairs={{0,24},{1,25},{2,26},{3,27},{4,28},{5,29},{6,30},{7,31},{8,16},{9,... | collective-permute-start | bytes 294920 | tf_op jit(solution)/shard_map/ppermute | solution.py:54
  224.3 2.4 %collective-permute-done.47 = bf16[1,144,384]{2,1,0:T(8,128)(2,1)S(1)} collective-permute-done((bf16[1,144,384]{2,1,0:T(8,128)(2,1)S(1)}, bf16[1,144,384]{2,1,0:T(8,128)(2,1)S(1)}, u32[]{:S(2)}, u32[]{:S(2)}) %collective-permute-start.47) | collective-permute-done | bytes 110624 | tf_op jit(solution)/shard_map/ppermute | solution.py:54
  230.8 3.5 %finish_grads.1 = (f32[16,128]{1,0:T(8,128)}, f32[16,768]{1,0:T(8,128)}, f32[1,24]{1,0:T(1,128)}, f32[1,24]{1,0:T(1,128)}, f32[2,24]{1,0:T(2,128)}, /*index=5*/f...) custom-call(s32[72]{0:T(128)S(1)} %copy-done.3, bf16[16,16,768]{2,1,0:T(8,128)(2,1)} %copy-done.9, ...), custom_call_target="tpu_custom_call" | custom-call | flops 50000000 | bytes 4000000 | tf_op jit(solution)/shard_map/finish_grads/pallas_call | solution.py:149
  (201 shorter events, 60.2 us)
Async XLA Ops:
  11.4 13.1 %collective-permute-start.1 = (bf16[1,192,384]{2,1,0:T(8,128)(2,1)S(1)}, bf16[1,192,384]{2,1,0:T(8,128)(2,1)S(1)}, u32[]{:S(2)}, u32[]{:S(2)}) collective-permute-start(bf16[1,192,384]{2,1,0:T(8,128)(2,1)S(1)} %maximum_bitcast_fusion.1), channel_id=1, source_target_pairs={{0,4},{1,5},{2,6},{3,7},{4,0},{5,1},{6,2},{7,3},{8,12},{9,13},{10,... | collective-permute-start | bytes 442376 | tf_op jit(solution)/shard_map/ppermute | solution.py:54
  24.7 12.5 %collective-permute-start.7 = (bf16[4,192,384]{2,1,0:T(8,128)(2,1)S(1)}, bf16[4,192,384]{2,1,0:T(8,128)(2,1)S(1)}, u32[]{:S(2)}, u32[]{:S(2)}) collective-permute-start(bf16[4,192,384]{2,1,0:T(8,128)(2,1)S(1)} %pad_maximum_fusion.3), channel_id=1, source_target_pairs={{0,16},{1,9},{2,18},{3,11},{4,20},{5,13},{6,22},{7,15},{8,24},{9,1... | collective-permute-start | bytes 1769480 | tf_op jit(solution)/shard_map/ppermute | solution.py:54
  26.3 10.7 %collective-permute-start.8 = (bf16[1,240,384]{2,1,0:T(8,128)(2,1)S(1)}, bf16[1,240,384]{2,1,0:T(8,128)(2,1)S(1)}, u32[]{:S(2)}, u32[]{:S(2)}) collective-permute-start(bf16[1,240,384]{2,1,0:T(8,128)(2,1)S(1)} %maximum_bitcast_fusion), channel_id=1, source_target_pairs={{0,4},{1,5},{2,6},{3,7},{4,0},{5,1},{6,2},{7,3},{8,12},{9,13},{10,... | collective-permute-start | bytes 552968 | tf_op jit(solution)/shard_map/ppermute | solution.py:54
  38.1 26.9 %collective-permute-start.10 = (bf16[8,192,384]{2,1,0:T(8,128)(2,1)}, bf16[8,192,384]{2,1,0:T(8,128)(2,1)}, u32[]{:S(2)}, u32[]{:S(2)}) collective-permute-start(bf16[8,192,384]{2,1,0:T(8,128)(2,1)} %constant_dynamic-update-slice_fusion.10.g_a), channel_id=1, source_target_pairs={{0,8},{1,17},{2,10},{3,19},{4,12},{5,21},{6,14},{7,23},{8,0},{9,25... | collective-permute-start | bytes 3538952 | tf_op jit(solution)/shard_map/ppermute | solution.py:54
  47.7 17.2 %collective-permute-start.12 = (bf16[4,240,384]{2,1,0:T(8,128)(2,1)S(1)}, bf16[4,240,384]{2,1,0:T(8,128)(2,1)S(1)}, u32[]{:S(2)}, u32[]{:S(2)}) collective-permute-start(bf16[4,240,384]{2,1,0:T(8,128)(2,1)S(1)} %pad_maximum_fusion.2), channel_id=1, source_target_pairs={{0,16},{1,9},{2,18},{3,11},{4,20},{5,13},{6,22},{7,15},{8,24},{9,1... | collective-permute-start | bytes 2211848 | tf_op jit(solution)/shard_map/ppermute | solution.py:54
  48.3 15.5 %collective-permute-start.13 = (bf16[2,192,384]{2,1,0:T(8,128)(2,1)S(1)}, bf16[2,192,384]{2,1,0:T(8,128)(2,1)S(1)}, u32[]{:S(2)}, u32[]{:S(2)}) collective-permute-start(bf16[2,192,384]{2,1,0:T(8,128)(2,1)S(1)} %pad_maximum_fusion.4), channel_id=1, source_target_pairs={{0,4},{1,5},{2,6},{3,7},{4,0},{5,1},{6,2},{7,3},{8,12},{9,13},{10,... | collective-permute-start | bytes 884744 | tf_op jit(solution)/shard_map/ppermute | solution.py:54
  50.5 14.5 %collective-permute-start.14 = (bf16[2,192,384]{2,1,0:T(8,128)(2,1)S(1)}, bf16[2,192,384]{2,1,0:T(8,128)(2,1)S(1)}, u32[]{:S(2)}, u32[]{:S(2)}) collective-permute-start(bf16[2,192,384]{2,1,0:T(8,128)(2,1)S(1)} %pad_maximum_fusion.4), channel_id=1, source_target_pairs={{0,2},{1,3},{2,0},{3,1},{4,6},{5,7},{6,4},{7,5},{8,10},{9,11},{10,... | collective-permute-start | bytes 884744 | tf_op jit(solution)/shard_map/ppermute | solution.py:54
  50.5 17.1 %collective-permute-start.15 = (bf16[8,192,384]{2,1,0:T(8,128)(2,1)}, bf16[8,192,384]{2,1,0:T(8,128)(2,1)}, u32[]{:S(2)}, u32[]{:S(2)}) collective-permute-start(bf16[8,192,384]{2,1,0:T(8,128)(2,1)} %constant_dynamic-update-slice_fusion.10.g_a), channel_id=1, source_target_pairs={{0,1},{1,0},{2,3},{3,2},{4,5},{5,4},{6,7},{7,6},{8,9},{9,8},{10,11... | collective-permute-start | bytes 3538952 | tf_op jit(solution)/shard_map/ppermute | solution.py:49
  65.2 19.5 %collective-permute-start.17 = (bf16[8,240,384]{2,1,0:T(8,128)(2,1)S(1)}, bf16[8,240,384]{2,1,0:T(8,128)(2,1)}, u32[]{:S(2)}, u32[]{:S(2)}) collective-permute-start(bf16[8,240,384]{2,1,0:T(8,128)(2,1)S(1)} %pad_maximum_fusion.u_a), channel_id=1, source_target_pairs={{0,8},{1,17},{2,10},{3,19},{4,12},{5,21},{6,14},{7,23},{8,0},{9,25... | collective-permute-start | bytes 4423688 | tf_op jit(solution)/shard_map/ppermute | solution.py:54
  67.1 21.7 %collective-permute-start.19 = (bf16[8,240,384]{2,1,0:T(8,128)(2,1)S(1)}, bf16[8,240,384]{2,1,0:T(8,128)(2,1)}, u32[]{:S(2)}, u32[]{:S(2)}) collective-permute-start(bf16[8,240,384]{2,1,0:T(8,128)(2,1)S(1)} %pad_maximum_fusion.u_a), channel_id=1, source_target_pairs={{0,1},{1,0},{2,3},{3,2},{4,5},{5,4},{6,7},{7,6},{8,9},{9,8},{10,11... | collective-permute-start | bytes 4423688 | tf_op jit(solution)/shard_map/ppermute | solution.py:49
  67.1 18.7 %collective-permute-start.18 = (bf16[2,192,384]{2,1,0:T(8,128)(2,1)S(1)}, bf16[2,192,384]{2,1,0:T(8,128)(2,1)S(1)}, u32[]{:S(2)}, u32[]{:S(2)}) collective-permute-start(bf16[2,192,384]{2,1,0:T(8,128)(2,1)S(1)} %pad_maximum_fusion.4), channel_id=1, source_target_pairs={{0,6},{1,7},{2,4},{3,5},{4,2},{5,3},{6,0},{7,1},{8,14},{9,15},{10,... | collective-permute-start | bytes 884744 | tf_op jit(solution)/shard_map/ppermute | solution.py:54
  87.1 21.9 %collective-permute-start.21 = (bf16[8,192,384]{2,1,0:T(8,128)(2,1)S(1)}, bf16[8,192,384]{2,1,0:T(8,128)(2,1)S(1)}, u32[]{:S(2)}, u32[]{:S(2)}) collective-permute-start(bf16[8,192,384]{2,1,0:T(8,128)(2,1)S(1)} %pad_maximum_fusion.1.d_a), channel_id=1, source_target_pairs={{0,8},{1,17},{2,10},{3,19},{4,12},{5,21},{6,14},{7,23},{8,0},{9,25... | collective-permute-start | bytes 3538952 | tf_op jit(solution)/shard_map/ppermute | solution.py:54
  118.0 27.8 %collective-permute-start.25 = (bf16[8,192,384]{2,1,0:T(8,128)(2,1)S(1)}, bf16[8,192,384]{2,1,0:T(8,128)(2,1)S(1)}, u32[]{:S(2)}, u32[]{:S(2)}) collective-permute-start(bf16[8,192,384]{2,1,0:T(8,128)(2,1)S(1)} %get-tuple-element.268), channel_id=1, source_target_pairs={{0,8},{1,17},{2,10},{3,19},{4,12},{5,21},{6,14},{7,23},{8,0},{9,25... | collective-permute-start | bytes 3538952 | tf_op jit(solution)/shard_map/ppermute | solution.py:54
  156.7 19.4 %collective-permute-start.28 = (bf16[8,240,384]{2,1,0:T(8,128)(2,1)S(1)}, bf16[8,240,384]{2,1,0:T(8,128)(2,1)S(1)}, u32[]{:S(2)}, u32[]{:S(2)}) collective-permute-start(bf16[8,240,384]{2,1,0:T(8,128)(2,1)S(1)} %get-tuple-element.266), channel_id=1, source_target_pairs={{0,8},{1,17},{2,10},{3,19},{4,12},{5,21},{6,14},{7,23},{8,0},{9,25... | collective-permute-start | bytes 4423688 | tf_op jit(solution)/shard_map/ppermute | solution.py:54
  157.3 15.9 %collective-permute-start.29 = (bf16[1,192,384]{2,1,0:T(8,128)(2,1)S(1)}, bf16[1,192,384]{2,1,0:T(8,128)(2,1)S(1)}, u32[]{:S(2)}, u32[]{:S(2)}) collective-permute-start(bf16[1,192,384]{2,1,0:T(8,128)(2,1)S(1)} %get-tuple-element.284), channel_id=1, source_target_pairs={{0,4},{1,5},{2,6},{3,7},{4,0},{5,1},{6,2},{7,3},{8,12},{9,13},{10,... | collective-permute-start | bytes 442376 | tf_op jit(solution)/shard_map/ppermute | solution.py:54
  157.4 15.8 %collective-permute-start.30 = (bf16[1,192,384]{2,1,0:T(8,128)(2,1)S(1)}, bf16[1,192,384]{2,1,0:T(8,128)(2,1)S(1)}, u32[]{:S(2)}, u32[]{:S(2)}) collective-permute-start(bf16[1,192,384]{2,1,0:T(8,128)(2,1)S(1)} %get-tuple-element.283), channel_id=1, source_target_pairs={{0,2},{1,3},{2,0},{3,1},{4,6},{5,7},{6,4},{7,5},{8,10},{9,11},{10,... | collective-permute-start | bytes 442376 | tf_op jit(solution)/shard_map/ppermute | solution.py:54
  159.6 13.6 %collective-permute-start.31 = (bf16[1,192,384]{2,1,0:T(8,128)(2,1)S(1)}, bf16[1,192,384]{2,1,0:T(8,128)(2,1)S(1)}, u32[]{:S(2)}, u32[]{:S(2)}) collective-permute-start(bf16[1,192,384]{2,1,0:T(8,128)(2,1)S(1)} %get-tuple-element.282), channel_id=1, source_target_pairs={{0,6},{1,7},{2,4},{3,5},{4,2},{5,3},{6,0},{7,1},{8,14},{9,15},{10,... | collective-permute-start | bytes 442376 | tf_op jit(solution)/shard_map/ppermute | solution.py:54
  176.2 12.7 %collective-permute-start.33 = (bf16[16,144,384]{2,1,0:T(8,128)(2,1)S(1)}, bf16[16,144,384]{2,1,0:T(8,128)(2,1)S(1)}, u32[]{:S(2)}, u32[]{:S(2)}) collective-permute-start(bf16[16,144,384]{2,1,0:T(8,128)(2,1)S(1)} %get-tuple-element.224), channel_id=1, source_target_pairs={{0,1},{1,0},{2,3},{3,2},{4,5},{5,4},{6,7},{7,6},{8,9},{9,8},{10,11... | collective-permute-start | bytes 5308424 | tf_op jit(solution)/shard_map/ppermute | solution.py:49
  176.4 12.4 %collective-permute-start.32 = (bf16[4,240,384]{2,1,0:T(8,128)(2,1)S(1)}, bf16[4,240,384]{2,1,0:T(8,128)(2,1)S(1)}, u32[]{:S(2)}, u32[]{:S(2)}) collective-permute-start(bf16[4,240,384]{2,1,0:T(8,128)(2,1)S(1)} %get-tuple-element.270), channel_id=1, source_target_pairs={{0,16},{1,9},{2,18},{3,11},{4,20},{5,13},{6,22},{7,15},{8,24},{9,1... | collective-permute-start | bytes 2211848 | tf_op jit(solution)/shard_map/ppermute | solution.py:54
  189.3 14.0 %collective-permute-start.34 = (bf16[8,144,384]{2,1,0:T(8,128)(2,1)S(1)}, bf16[8,144,384]{2,1,0:T(8,128)(2,1)S(1)}, u32[]{:S(2)}, u32[]{:S(2)}) collective-permute-start(bf16[8,144,384]{2,1,0:T(8,128)(2,1)S(1)} %get-tuple-element.272), channel_id=1, source_target_pairs={{0,8},{1,17},{2,10},{3,19},{4,12},{5,21},{6,14},{7,23},{8,0},{9,25... | collective-permute-start | bytes 2654216 | tf_op jit(solution)/shard_map/ppermute | solution.py:54
  191.1 12.1 %collective-permute-start.35 = (bf16[1,240,384]{2,1,0:T(8,128)(2,1)S(1)}, bf16[1,240,384]{2,1,0:T(8,128)(2,1)S(1)}, u32[]{:S(2)}, u32[]{:S(2)}) collective-permute-start(bf16[1,240,384]{2,1,0:T(8,128)(2,1)S(1)} %get-tuple-element.280), channel_id=1, source_target_pairs={{0,4},{1,5},{2,6},{3,7},{4,0},{5,1},{6,2},{7,3},{8,12},{9,13},{10,... | collective-permute-start | bytes 552968 | tf_op jit(solution)/shard_map/ppermute | solution.py:54
  191.2 12.1 %collective-permute-start.36 = (bf16[1,240,384]{2,1,0:T(8,128)(2,1)S(1)}, bf16[1,240,384]{2,1,0:T(8,128)(2,1)S(1)}, u32[]{:S(2)}, u32[]{:S(2)}) collective-permute-start(bf16[1,240,384]{2,1,0:T(8,128)(2,1)S(1)} %get-tuple-element.279), channel_id=1, source_target_pairs={{0,2},{1,3},{2,0},{3,1},{4,6},{5,7},{6,4},{7,5},{8,10},{9,11},{10,... | collective-permute-start | bytes 552968 | tf_op jit(solution)/shard_map/ppermute | solution.py:54
  209.5 12.3 %collective-permute-start.49 = (bf16[1,240,384]{2,1,0:T(8,128)(2,1)S(1)}, bf16[1,240,384]{2,1,0:T(8,128)(2,1)S(1)}, u32[]{:S(2)}, u32[]{:S(2)}) collective-permute-start(bf16[1,240,384]{2,1,0:T(8,128)(2,1)S(1)} %get-tuple-element.278), channel_id=1, source_target_pairs={{0,6},{1,7},{2,4},{3,5},{4,2},{5,3},{6,0},{7,1},{8,14},{9,15},{10,... | collective-permute-start | bytes 552968 | tf_op jit(solution)/shard_map/ppermute | solution.py:54
  214.0 12.7 %collective-permute-start.47 = (bf16[1,144,384]{2,1,0:T(8,128)(2,1)S(1)}, bf16[1,144,384]{2,1,0:T(8,128)(2,1)S(1)}, u32[]{:S(2)}, u32[]{:S(2)}) collective-permute-start(bf16[1,144,384]{2,1,0:T(8,128)(2,1)S(1)} %get-tuple-element.286), channel_id=1, source_target_pairs={{0,4},{1,5},{2,6},{3,7},{4,0},{5,1},{6,2},{7,3},{8,12},{9,13},{10,... | collective-permute-start | bytes 331784 | tf_op jit(solution)/shard_map/ppermute | solution.py:54
  (46 other events, 428.3 us)

commit v7 on v6

--- a/solution.py
+++ b/solution.py
@@ -1115,8 +1115,7 @@
         up_sum.land(arrivals[1])
         att_sum.send()
         near = [chip_swap(small, p) for p in (1, 2, 3)]
-        brought, near = together(att_sum.fly(), near)
-        att_sum.land(brought)
+        att_sum.land(att_sum.fly())
         small_line = jnp.concatenate([small] + near, axis=0)
         att_sum.send()
         brought = att_sum.fly()
@@ -1124,9 +1123,8 @@
         plane = [small_line] + [chip_swap(small_line, p) for p in (4, 8, 12)]
         every = jnp.concatenate(plane, axis=0)
         every = every, core_swap(every)
-        brought, up_last = together(brought, up_last)
         att_sum.land(brought)
-        up_sum.land([up_last])
+        up_sum.land([after(up_last, small_line)])
         sums = after(down_total, small_line), after(up_sum.total(), small_line), att_sum.total()
         pieces = [x for total in sums for x in (total, core_swap(total))]
         finished = finish_grads(

time: 236 us -> 235 us (level)
  starting transfers between devices: 49.5 us -> 46.9 us
  transfers between devices with their start and end apart: 52 -> 52, of which waited for: 20 -> 23; matrix products, arithmetic and copies ran while one was open for 4% -> 4% of each run, Pallas kernels for 45% -> 45%
where the time goes in v7:
time: 235 us; the launch traced here: 234 us
  Pallas kernels  110 us (47%)
  waiting for transfers between devices  59.3 us (25%)
  starting transfers between devices  46.9 us (20%)
  local copies, waits for them, and re-layouts  7.98 us (3%)
  other arithmetic  7.98 us (3%)
    pallas_call x9, Pallas kernels, run(): call(*[place(x, spec) for x, spec in zip(operands, specs, strict=True)])  110 us
    ppermute x36, waiting for transfers between devices, chip_swap(): lax.ppermute(x, AXES, [(i, i ^ far[i & 1]) for i in range(2 * CHIPS)])  53.8 us
    ppermute x36, starting transfers between devices, chip_swap(): lax.ppermute(x, AXES, [(i, i ^ far[i & 1]) for i in range(2 * CHIPS)])  44.8 us
    ppermute x16, waiting for transfers between devices, core_swap(): return lax.ppermute(x, AXES, [(i, i ^ 1) for i in range(2 * CHIPS)])  5.53 us
  transfers between devices with their start and end apart: 52, of which 23 were waited for; matrix products, arithmetic and copies ran while one was open for 4% of the time, Pallas kernels for 45%

profile of v7, /device:TPU:0, one launch (start us, length us, event | category | flops | bytes accessed | tf_op | source)
XLA Modules:
  0.0 233.6 jit_solution(3004314206645472412)
XLA Ops:
  6.7 4.7 %collective-permute-start.3 = (bf16[1,192,384]{2,1,0:T(8,128)(2,1)S(1)}, bf16[1,192,384]{2,1,0:T(8,128)(2,1)S(1)}, u32[]{:S(2)}, u32[]{:S(2)}) collective-permute-start(bf16[1,192,384]{2,1,0:T(8,128)(2,1)S(1)} %maximum_bitcast_fusion.1), channel_id=1, source_target_pairs={{0,6},{1,7},{2,4},{3,5},{4,2},{5,3},{6,0},{7,1},{8,14},{9,15},{10,... | collective-permute-start | bytes 442376 | tf_op jit(solution)/shard_map/ppermute | solution.py:54
  16.5 3.7 %collective-permute-done.2 = bf16[1,192,384]{2,1,0:T(8,128)(2,1)S(1)} collective-permute-done((bf16[1,192,384]{2,1,0:T(8,128)(2,1)S(1)}, bf16[1,192,384]{2,1,0:T(8,128)(2,1)S(1)}, u32[]{:S(2)}, u32[]{:S(2)}) %collective-permute-start.2) | collective-permute-done | bytes 147488 | tf_op jit(solution)/shard_map/ppermute | solution.py:54
  20.2 4.4 %collective-permute-done.1 = bf16[1,192,384]{2,1,0:T(8,128)(2,1)S(1)} collective-permute-done((bf16[1,192,384]{2,1,0:T(8,128)(2,1)S(1)}, bf16[1,192,384]{2,1,0:T(8,128)(2,1)S(1)}, u32[]{:S(2)}, u32[]{:S(2)}) %collective-permute-start.1) | collective-permute-done | bytes 147488 | tf_op jit(solution)/shard_map/ppermute | solution.py:54
  26.8 2.6 %collective-permute-start.9 = (bf16[1,240,384]{2,1,0:T(8,128)(2,1)S(1)}, bf16[1,240,384]{2,1,0:T(8,128)(2,1)S(1)}, u32[]{:S(2)}, u32[]{:S(2)}) collective-permute-start(bf16[1,240,384]{2,1,0:T(8,128)(2,1)S(1)} %maximum_bitcast_fusion), channel_id=1, source_target_pairs={{0,2},{1,3},{2,0},{3,1},{4,6},{5,7},{6,4},{7,5},{8,10},{9,11},{10,... | collective-permute-start | bytes 552968 | tf_op jit(solution)/shard_map/ppermute | solution.py:54
  30.2 6.8 %collective-permute-done.8 = bf16[1,240,384]{2,1,0:T(8,128)(2,1)S(1)} collective-permute-done((bf16[1,240,384]{2,1,0:T(8,128)(2,1)S(1)}, bf16[1,240,384]{2,1,0:T(8,128)(2,1)S(1)}, u32[]{:S(2)}, u32[]{:S(2)}) %collective-permute-start.8) | collective-permute-done | bytes 184352 | tf_op jit(solution)/shard_map/ppermute | solution.py:54
  40.1 7.5 %collective-permute-done.11 = bf16[1,240,384]{2,1,0:T(8,128)(2,1)S(1)} collective-permute-done((bf16[1,240,384]{2,1,0:T(8,128)(2,1)S(1)}, bf16[1,240,384]{2,1,0:T(8,128)(2,1)S(1)}, u32[]{:S(2)}, u32[]{:S(2)}) %collective-permute-start.11) | collective-permute-done | bytes 184352 | tf_op jit(solution)/shard_map/ppermute | solution.py:54
  48.3 2.2 collective-permute-start.13
  50.5 13.3 %collective-permute-done.13 = bf16[2,192,384]{2,1,0:T(8,128)(2,1)S(1)} collective-permute-done((bf16[2,192,384]{2,1,0:T(8,128)(2,1)S(1)}, bf16[2,192,384]{2,1,0:T(8,128)(2,1)S(1)}, u32[]{:S(2)}, u32[]{:S(2)}) %collective-permute-start.13) | collective-permute-done | bytes 294944 | tf_op jit(solution)/shard_map/ppermute | solution.py:54
  68.2 15.3 %attention_forward.1 = (bf16[1024,768]{1,0:T(8,128)(2,1)}, bf16[1024,2304]{1,0:T(8,128)(2,1)}, f32[8,768]{1,0:T(8,128)}, f32[16,768]{1,0:T(8,128)}, bf16[2,16,16...) custom-call(s32[72]{0:T(128)S(1)} %compare_select_fusion.25.tab, ...), custom_call_target="tpu_custom_call" | custom-call | flops 8000000000 | bytes 20000000 | tf_op jit(solution)/shard_map/attention_forward/pallas_call | solution.py:149
  89.3 19.7 %up_forward.1 = (f32[1024,768]{1,0:T(8,128)}, bf16[1024,768]{1,0:T(8,128)(2,1)}, bf16[4,1024,768]{2,1,0:T(8,128)(2,1)S(1)}, bf16[4,1024,768]{2,1,0:T(8,128)(2,1)S(1)}, bf16[16,192,384]{2,1,0:T(8,128)(2,1)S(1)}) custom-call(s32[72]{0:T(128)S(1)} %compare_select_fusion.25.tab, bf16[8,240,384]{2,1,0:T(8,128)(2,1)} %copy-done.7, ...), custom_call_target="tpu_custom_call" | custom-call | flops 10000000000 | bytes 30000000 | tf_op jit(solution)/shard_map/up_forward/pallas_call | solution.py:149
  109.7 4.6 %down_grad.1 = (bf16[16,192,384]{2,1,0:T(8,128)(2,1)S(1)}, bf16[4,1024,768]{2,1,0:T(8,128)(2,1)}, bf16[4,1024,768]{2,1,0:T(8,128)(2,1)S(1)}) custom-call(s32[72]{0:T(128)S(1)} %compare_select_fusion.25.tab, bf16[4,1024,768]{2,1,0:T(8,128)(2,1)S(1)} %get-tuple-element.172.act_ref, bf16[1024,768]{1,0:T(8,128)(2,1)S(1)} %bitcast.40, ...), custom_call_target="tpu_custom_call", output_to_operand_aliasing={{2}: (3, {})} | custom-call | flops 3000000000 | bytes 10000000 | tf_op jit(solution)/shard_map/down_grad/pallas_call | solution.py:149
  119.7 26.1 %mlp_backward.1 = (f32[1024,768]{1,0:T(8,128)}, bf16[1024,768]{1,0:T(8,128)(2,1)S(1)}, bf16[2,1024,768]{2,1,0:T(8,128)(2,1)S(1)}, bf16[1024,768]{1,0:T(8,128)(2,...) custom-call(s32[72]{0:T(128)} %copy-done.2, s32[72]{0:T(128)} %compare_select_fusion.24.later_tab, ...), custom_call_target="tpu_custom_call" | custom-call | flops 17999998976 | bytes 50000000 | tf_op jit(solution)/shard_map/mlp_backward/pallas_call | solution.py:149
  146.4 6.2 %up_grad.1 = bf16[16,240,384]{2,1,0:T(8,128)(2,1)S(1)} custom-call(s32[72]{0:T(128)S(1)} %copy-done.3, bf16[1024,768]{1,0:T(8,128)(2,1)} %get-tuple-element.164.att_ref.att_hbm, bf16[1024,768]{1,0:T(8,128)(2,1)} %get-tuple-element.183.two_hbm, bf16[1024,768]{1,0:T(8,128)(2,1)S(1)} %get-tuple-element.196.branch_ref, ...), custom_call_target="tpu_custom_call" | custom-call | flops 3200000000 | bytes 11000000 | tf_op jit(solution)/shard_map/up_grad/pallas_call | solution.py:149
  152.7 3.4 %collective-permute-done.26 = bf16[4,192,384]{2,1,0:T(8,128)(2,1)S(1)} collective-permute-done((bf16[4,192,384]{2,1,0:T(8,128)(2,1)S(1)}, bf16[4,192,384]{2,1,0:T(8,128)(2,1)S(1)}, u32[]{:S(2)}, u32[]{:S(2)}) %collective-permute-start.26) | collective-permute-done | bytes 589856 | tf_op jit(solution)/shard_map/ppermute | solution.py:54
  157.4 2.2 collective-permute-start.30
  159.6 2.2 collective-permute-start.31
  161.8 11.4 %attention_backward.1 = (bf16[1024,2304]{1,0:T(8,128)(2,1)}, bf16[1024,1152]{1,0:T(8,128)(2,1)S(1)}, bf16[16,144,384]{2,1,0:T(8,128)(2,1)S(1)}) custom-call(s32[72]{0:T(128)S(1)} %copy-done.3, bf16[1024,768]{1,0:T(8,128)(2,1)} %get-tuple-element.180.normed_hbm.normed_ref, bf16[1024,2304]{1,0:T(8,128)(2,1)} %get-tuple-element.181.qkv_ref, ...), custom_call_target="tpu_custom_call" | custom-call | flops 11000000512 | bytes 22000000 | tf_op jit(solution)/shard_map/attention_backward/pallas_call | solution.py:149
  173.2 2.9 %collective-permute-done.28 = bf16[8,240,384]{2,1,0:T(8,128)(2,1)S(1)} collective-permute-done((bf16[8,240,384]{2,1,0:T(8,128)(2,1)S(1)}, bf16[8,240,384]{2,1,0:T(8,128)(2,1)S(1)}, u32[]{:S(2)}, u32[]{:S(2)}) %collective-permute-start.28) | collective-permute-done | bytes 1474592 | tf_op jit(solution)/shard_map/ppermute | solution.py:54
  176.8 12.0 %qkv_grad.1 = (bf16[16,144,384]{2,1,0:T(8,128)(2,1)S(1)}, bf16[1024,768]{1,0:T(8,128)(2,1)}) custom-call(s32[72]{0:T(128)S(1)} %copy-done.3, s32[72]{0:T(128)S(1)} %copy-done.4, bf16[8,192,384]{2,1,0:T(8,128)(2,1)} %copy-done.8, bf16[8,192,384]{2,1,0:T(8,128)(2,1)} %copy-done.15, bf16[8,192,384]{2,1,0:T(8,128)(2,1)} %copy-done.16, ...), custom_call_target="tpu_custom_call" | custom-call | flops 7000000000 | bytes 22000000 | tf_op jit(solution)/shard_map/qkv_grad/pallas_call | solution.py:149
  192.6 10.7 %input_backward.1 = (bf16[1024,768]{1,0:T(8,128)(2,1)}, f32[16,768]{1,0:T(8,128)S(1)}) custom-call(s32[72]{0:T(128)S(1)} %copy-done.3, bf16[8,192,384]{2,1,0:T(8,128)(2,1)} %constant_dynamic-update-slice_fusion.10.g_a, bf16[8,192,384]{2,1,0:T(8,128)(2,1)} %collective-permute-done.10.g_b, bf16[8,192,384]{2,1,0:T(8,128)(2,1)} %collective-permute-done.15.g_c, ...), custom_call_target="tpu_custom_call" | custom-call | flops 4000000000 | bytes 18000000 | tf_op jit(solution)/shard_map/input_backward/pallas_call | solution.py:149
  205.1 2.2 collective-permute-start.47
  208.9 2.7 %collective-permute-start.37 = (bf16[1,16,768]{2,1,0:T(8,128)(2,1)S(1)}, bf16[1,16,768]{2,1,0:T(8,128)(2,1)S(1)}, u32[]{:S(2)}, u32[]{:S(2)}) collective-permute-start(bf16[1,16,768]{2,1,0:T(8,128)(2,1)S(1)} %convert_bitcast_fusion), channel_id=1, source_target_pairs={{0,4},{1,5},{2,6},{3,7},{4,0},{5,1},{6,2},{7,3},{8,12},{9,13},{10,... | collective-permute-start | bytes 73736 | tf_op jit(solution)/shard_map/ppermute | solution.py:54
  213.9 2.9 %collective-permute-done.37 = bf16[1,16,768]{2,1,0:T(8,128)(2,1)S(1)} collective-permute-done((bf16[1,16,768]{2,1,0:T(8,128)(2,1)S(1)}, bf16[1,16,768]{2,1,0:T(8,128)(2,1)S(1)}, u32[]{:S(2)}, u32[]{:S(2)}) %collective-permute-start.37) | collective-permute-done | bytes 24608 | tf_op jit(solution)/shard_map/ppermute | solution.py:54
  229.9 3.5 %finish_grads.1 = (f32[16,128]{1,0:T(8,128)}, f32[16,768]{1,0:T(8,128)}, f32[1,24]{1,0:T(1,128)}, f32[1,24]{1,0:T(1,128)}, f32[2,24]{1,0:T(2,128)}, /*index=5*/f...) custom-call(s32[72]{0:T(128)S(1)} %copy-done.3, bf16[16,16,768]{2,1,0:T(8,128)(2,1)} %copy-done.9, ...), custom_call_target="tpu_custom_call" | custom-call | flops 50000000 | bytes 4000000 | tf_op jit(solution)/shard_map/finish_grads/pallas_call | solution.py:149
  (201 shorter events, 58.8 us)
Async XLA Ops:
  11.4 13.1 %collective-permute-start.1 = (bf16[1,192,384]{2,1,0:T(8,128)(2,1)S(1)}, bf16[1,192,384]{2,1,0:T(8,128)(2,1)S(1)}, u32[]{:S(2)}, u32[]{:S(2)}) collective-permute-start(bf16[1,192,384]{2,1,0:T(8,128)(2,1)S(1)} %maximum_bitcast_fusion.1), channel_id=1, source_target_pairs={{0,4},{1,5},{2,6},{3,7},{4,0},{5,1},{6,2},{7,3},{8,12},{9,13},{10,... | collective-permute-start | bytes 442376 | tf_op jit(solution)/shard_map/ppermute | solution.py:54
  24.7 12.5 %collective-permute-start.7 = (bf16[4,192,384]{2,1,0:T(8,128)(2,1)S(1)}, bf16[4,192,384]{2,1,0:T(8,128)(2,1)S(1)}, u32[]{:S(2)}, u32[]{:S(2)}) collective-permute-start(bf16[4,192,384]{2,1,0:T(8,128)(2,1)S(1)} %pad_maximum_fusion.3), channel_id=1, source_target_pairs={{0,16},{1,9},{2,18},{3,11},{4,20},{5,13},{6,22},{7,15},{8,24},{9,1... | collective-permute-start | bytes 1769480 | tf_op jit(solution)/shard_map/ppermute | solution.py:54
  26.3 10.7 %collective-permute-start.8 = (bf16[1,240,384]{2,1,0:T(8,128)(2,1)S(1)}, bf16[1,240,384]{2,1,0:T(8,128)(2,1)S(1)}, u32[]{:S(2)}, u32[]{:S(2)}) collective-permute-start(bf16[1,240,384]{2,1,0:T(8,128)(2,1)S(1)} %maximum_bitcast_fusion), channel_id=1, source_target_pairs={{0,4},{1,5},{2,6},{3,7},{4,0},{5,1},{6,2},{7,3},{8,12},{9,13},{10,... | collective-permute-start | bytes 552968 | tf_op jit(solution)/shard_map/ppermute | solution.py:54
  26.8 10.4 %collective-permute-start.9 = (bf16[1,240,384]{2,1,0:T(8,128)(2,1)S(1)}, bf16[1,240,384]{2,1,0:T(8,128)(2,1)S(1)}, u32[]{:S(2)}, u32[]{:S(2)}) collective-permute-start(bf16[1,240,384]{2,1,0:T(8,128)(2,1)S(1)} %maximum_bitcast_fusion), channel_id=1, source_target_pairs={{0,2},{1,3},{2,0},{3,1},{4,6},{5,7},{6,4},{7,5},{8,10},{9,11},{10,... | collective-permute-start | bytes 552968 | tf_op jit(solution)/shard_map/ppermute | solution.py:54
  38.1 26.9 %collective-permute-start.10 = (bf16[8,192,384]{2,1,0:T(8,128)(2,1)}, bf16[8,192,384]{2,1,0:T(8,128)(2,1)}, u32[]{:S(2)}, u32[]{:S(2)}) collective-permute-start(bf16[8,192,384]{2,1,0:T(8,128)(2,1)} %constant_dynamic-update-slice_fusion.10.g_a), channel_id=1, source_target_pairs={{0,8},{1,17},{2,10},{3,19},{4,12},{5,21},{6,14},{7,23},{8,0},{9,25... | collective-permute-start | bytes 3538952 | tf_op jit(solution)/shard_map/ppermute | solution.py:54
  47.7 17.2 %collective-permute-start.12 = (bf16[4,240,384]{2,1,0:T(8,128)(2,1)S(1)}, bf16[4,240,384]{2,1,0:T(8,128)(2,1)S(1)}, u32[]{:S(2)}, u32[]{:S(2)}) collective-permute-start(bf16[4,240,384]{2,1,0:T(8,128)(2,1)S(1)} %pad_maximum_fusion.2), channel_id=1, source_target_pairs={{0,16},{1,9},{2,18},{3,11},{4,20},{5,13},{6,22},{7,15},{8,24},{9,1... | collective-permute-start | bytes 2211848 | tf_op jit(solution)/shard_map/ppermute | solution.py:54
  48.3 15.5 %collective-permute-start.13 = (bf16[2,192,384]{2,1,0:T(8,128)(2,1)S(1)}, bf16[2,192,384]{2,1,0:T(8,128)(2,1)S(1)}, u32[]{:S(2)}, u32[]{:S(2)}) collective-permute-start(bf16[2,192,384]{2,1,0:T(8,128)(2,1)S(1)} %pad_maximum_fusion.4), channel_id=1, source_target_pairs={{0,4},{1,5},{2,6},{3,7},{4,0},{5,1},{6,2},{7,3},{8,12},{9,13},{10,... | collective-permute-start | bytes 884744 | tf_op jit(solution)/shard_map/ppermute | solution.py:54
  50.5 14.5 %collective-permute-start.14 = (bf16[2,192,384]{2,1,0:T(8,128)(2,1)S(1)}, bf16[2,192,384]{2,1,0:T(8,128)(2,1)S(1)}, u32[]{:S(2)}, u32[]{:S(2)}) collective-permute-start(bf16[2,192,384]{2,1,0:T(8,128)(2,1)S(1)} %pad_maximum_fusion.4), channel_id=1, source_target_pairs={{0,2},{1,3},{2,0},{3,1},{4,6},{5,7},{6,4},{7,5},{8,10},{9,11},{10,... | collective-permute-start | bytes 884744 | tf_op jit(solution)/shard_map/ppermute | solution.py:54
  50.5 17.1 %collective-permute-start.15 = (bf16[8,192,384]{2,1,0:T(8,128)(2,1)}, bf16[8,192,384]{2,1,0:T(8,128)(2,1)}, u32[]{:S(2)}, u32[]{:S(2)}) collective-permute-start(bf16[8,192,384]{2,1,0:T(8,128)(2,1)} %constant_dynamic-update-slice_fusion.10.g_a), channel_id=1, source_target_pairs={{0,1},{1,0},{2,3},{3,2},{4,5},{5,4},{6,7},{7,6},{8,9},{9,8},{10,11... | collective-permute-start | bytes 3538952 | tf_op jit(solution)/shard_map/ppermute | solution.py:49
  65.2 19.5 %collective-permute-start.17 = (bf16[8,240,384]{2,1,0:T(8,128)(2,1)S(1)}, bf16[8,240,384]{2,1,0:T(8,128)(2,1)}, u32[]{:S(2)}, u32[]{:S(2)}) collective-permute-start(bf16[8,240,384]{2,1,0:T(8,128)(2,1)S(1)} %pad_maximum_fusion.u_a), channel_id=1, source_target_pairs={{0,8},{1,17},{2,10},{3,19},{4,12},{5,21},{6,14},{7,23},{8,0},{9,25... | collective-permute-start | bytes 4423688 | tf_op jit(solution)/shard_map/ppermute | solution.py:54
  67.1 21.7 %collective-permute-start.19 = (bf16[8,240,384]{2,1,0:T(8,128)(2,1)S(1)}, bf16[8,240,384]{2,1,0:T(8,128)(2,1)}, u32[]{:S(2)}, u32[]{:S(2)}) collective-permute-start(bf16[8,240,384]{2,1,0:T(8,128)(2,1)S(1)} %pad_maximum_fusion.u_a), channel_id=1, source_target_pairs={{0,1},{1,0},{2,3},{3,2},{4,5},{5,4},{6,7},{7,6},{8,9},{9,8},{10,11... | collective-permute-start | bytes 4423688 | tf_op jit(solution)/shard_map/ppermute | solution.py:49
  67.1 18.7 %collective-permute-start.18 = (bf16[2,192,384]{2,1,0:T(8,128)(2,1)S(1)}, bf16[2,192,384]{2,1,0:T(8,128)(2,1)S(1)}, u32[]{:S(2)}, u32[]{:S(2)}) collective-permute-start(bf16[2,192,384]{2,1,0:T(8,128)(2,1)S(1)} %pad_maximum_fusion.4), channel_id=1, source_target_pairs={{0,6},{1,7},{2,4},{3,5},{4,2},{5,3},{6,0},{7,1},{8,14},{9,15},{10,... | collective-permute-start | bytes 884744 | tf_op jit(solution)/shard_map/ppermute | solution.py:54
  87.1 21.9 %collective-permute-start.21 = (bf16[8,192,384]{2,1,0:T(8,128)(2,1)S(1)}, bf16[8,192,384]{2,1,0:T(8,128)(2,1)S(1)}, u32[]{:S(2)}, u32[]{:S(2)}) collective-permute-start(bf16[8,192,384]{2,1,0:T(8,128)(2,1)S(1)} %pad_maximum_fusion.1.d_a), channel_id=1, source_target_pairs={{0,8},{1,17},{2,10},{3,19},{4,12},{5,21},{6,14},{7,23},{8,0},{9,25... | collective-permute-start | bytes 3538952 | tf_op jit(solution)/shard_map/ppermute | solution.py:54
  118.0 27.8 %collective-permute-start.25 = (bf16[8,192,384]{2,1,0:T(8,128)(2,1)S(1)}, bf16[8,192,384]{2,1,0:T(8,128)(2,1)S(1)}, u32[]{:S(2)}, u32[]{:S(2)}) collective-permute-start(bf16[8,192,384]{2,1,0:T(8,128)(2,1)S(1)} %get-tuple-element.254), channel_id=1, source_target_pairs={{0,8},{1,17},{2,10},{3,19},{4,12},{5,21},{6,14},{7,23},{8,0},{9,25... | collective-permute-start | bytes 3538952 | tf_op jit(solution)/shard_map/ppermute | solution.py:54
  156.7 19.4 %collective-permute-start.28 = (bf16[8,240,384]{2,1,0:T(8,128)(2,1)S(1)}, bf16[8,240,384]{2,1,0:T(8,128)(2,1)S(1)}, u32[]{:S(2)}, u32[]{:S(2)}) collective-permute-start(bf16[8,240,384]{2,1,0:T(8,128)(2,1)S(1)} %get-tuple-element.252), channel_id=1, source_target_pairs={{0,8},{1,17},{2,10},{3,19},{4,12},{5,21},{6,14},{7,23},{8,0},{9,25... | collective-permute-start | bytes 4423688 | tf_op jit(solution)/shard_map/ppermute | solution.py:54
  157.3 15.9 %collective-permute-start.29 = (bf16[1,192,384]{2,1,0:T(8,128)(2,1)S(1)}, bf16[1,192,384]{2,1,0:T(8,128)(2,1)S(1)}, u32[]{:S(2)}, u32[]{:S(2)}) collective-permute-start(bf16[1,192,384]{2,1,0:T(8,128)(2,1)S(1)} %get-tuple-element.270), channel_id=1, source_target_pairs={{0,4},{1,5},{2,6},{3,7},{4,0},{5,1},{6,2},{7,3},{8,12},{9,13},{10,... | collective-permute-start | bytes 442376 | tf_op jit(solution)/shard_map/ppermute | solution.py:54
  157.4 15.8 %collective-permute-start.30 = (bf16[1,192,384]{2,1,0:T(8,128)(2,1)S(1)}, bf16[1,192,384]{2,1,0:T(8,128)(2,1)S(1)}, u32[]{:S(2)}, u32[]{:S(2)}) collective-permute-start(bf16[1,192,384]{2,1,0:T(8,128)(2,1)S(1)} %get-tuple-element.269), channel_id=1, source_target_pairs={{0,2},{1,3},{2,0},{3,1},{4,6},{5,7},{6,4},{7,5},{8,10},{9,11},{10,... | collective-permute-start | bytes 442376 | tf_op jit(solution)/shard_map/ppermute | solution.py:54
  159.6 13.6 %collective-permute-start.31 = (bf16[1,192,384]{2,1,0:T(8,128)(2,1)S(1)}, bf16[1,192,384]{2,1,0:T(8,128)(2,1)S(1)}, u32[]{:S(2)}, u32[]{:S(2)}) collective-permute-start(bf16[1,192,384]{2,1,0:T(8,128)(2,1)S(1)} %get-tuple-element.268), channel_id=1, source_target_pairs={{0,6},{1,7},{2,4},{3,5},{4,2},{5,3},{6,0},{7,1},{8,14},{9,15},{10,... | collective-permute-start | bytes 442376 | tf_op jit(solution)/shard_map/ppermute | solution.py:54
  176.2 12.7 %collective-permute-start.33 = (bf16[16,144,384]{2,1,0:T(8,128)(2,1)S(1)}, bf16[16,144,384]{2,1,0:T(8,128)(2,1)S(1)}, u32[]{:S(2)}, u32[]{:S(2)}) collective-permute-start(bf16[16,144,384]{2,1,0:T(8,128)(2,1)S(1)} %get-tuple-element.217), channel_id=1, source_target_pairs={{0,1},{1,0},{2,3},{3,2},{4,5},{5,4},{6,7},{7,6},{8,9},{9,8},{10,11... | collective-permute-start | bytes 5308424 | tf_op jit(solution)/shard_map/ppermute | solution.py:49
  176.4 12.4 %collective-permute-start.32 = (bf16[4,240,384]{2,1,0:T(8,128)(2,1)S(1)}, bf16[4,240,384]{2,1,0:T(8,128)(2,1)S(1)}, u32[]{:S(2)}, u32[]{:S(2)}) collective-permute-start(bf16[4,240,384]{2,1,0:T(8,128)(2,1)S(1)} %get-tuple-element.256), channel_id=1, source_target_pairs={{0,16},{1,9},{2,18},{3,11},{4,20},{5,13},{6,22},{7,15},{8,24},{9,1... | collective-permute-start | bytes 2211848 | tf_op jit(solution)/shard_map/ppermute | solution.py:54
  189.3 14.0 %collective-permute-start.34 = (bf16[8,144,384]{2,1,0:T(8,128)(2,1)S(1)}, bf16[8,144,384]{2,1,0:T(8,128)(2,1)S(1)}, u32[]{:S(2)}, u32[]{:S(2)}) collective-permute-start(bf16[8,144,384]{2,1,0:T(8,128)(2,1)S(1)} %get-tuple-element.258), channel_id=1, source_target_pairs={{0,8},{1,17},{2,10},{3,19},{4,12},{5,21},{6,14},{7,23},{8,0},{9,25... | collective-permute-start | bytes 2654216 | tf_op jit(solution)/shard_map/ppermute | solution.py:54
  191.1 12.1 %collective-permute-start.35 = (bf16[1,240,384]{2,1,0:T(8,128)(2,1)S(1)}, bf16[1,240,384]{2,1,0:T(8,128)(2,1)S(1)}, u32[]{:S(2)}, u32[]{:S(2)}) collective-permute-start(bf16[1,240,384]{2,1,0:T(8,128)(2,1)S(1)} %get-tuple-element.266), channel_id=1, source_target_pairs={{0,4},{1,5},{2,6},{3,7},{4,0},{5,1},{6,2},{7,3},{8,12},{9,13},{10,... | collective-permute-start | bytes 552968 | tf_op jit(solution)/shard_map/ppermute | solution.py:54
  191.2 12.1 %collective-permute-start.36 = (bf16[1,240,384]{2,1,0:T(8,128)(2,1)S(1)}, bf16[1,240,384]{2,1,0:T(8,128)(2,1)S(1)}, u32[]{:S(2)}, u32[]{:S(2)}) collective-permute-start(bf16[1,240,384]{2,1,0:T(8,128)(2,1)S(1)} %get-tuple-element.265), channel_id=1, source_target_pairs={{0,2},{1,3},{2,0},{3,1},{4,6},{5,7},{6,4},{7,5},{8,10},{9,11},{10,... | collective-permute-start | bytes 552968 | tf_op jit(solution)/shard_map/ppermute | solution.py:54
  205.1 15.8 %collective-permute-start.47 = (bf16[1,240,384]{2,1,0:T(8,128)(2,1)S(1)}, bf16[1,240,384]{2,1,0:T(8,128)(2,1)S(1)}, u32[]{:S(2)}, u32[]{:S(2)}) collective-permute-start(bf16[1,240,384]{2,1,0:T(8,128)(2,1)S(1)} %get-tuple-element.264), channel_id=1, source_target_pairs={{0,6},{1,7},{2,4},{3,5},{4,2},{5,3},{6,0},{7,1},{8,14},{9,15},{10,... | collective-permute-start | bytes 552968 | tf_op jit(solution)/shard_map/ppermute | solution.py:54
  (46 other events, 428.3 us)
